TPU v7x, 32 devices: a whole 2x2x4 slice. The times are simulated.
32 devices in a mesh: grp: 2 (over x), exp: 16 (over z, y, core).
Axes of the slice: x: 2, y: 2, z: 4, core: 2. Of those that a mesh axis runs over, the one named last changes fastest.
Arguments:
- resid: bfloat16 [32, 2048], P(('grp', 'exp')), parts along dimension 0, may hold values from -6 to 6
- queries: bfloat16 [32, 2048], P(('grp', 'exp')), parts along dimension 0, may hold values from -6 to 6
- incoming_key_value: bfloat16 [32, 512], P(('grp', 'exp')), parts along dimension 0, may hold values from -6 to 6
- key_value_cache: bfloat16 [16, 3072, 512], P('grp', 'exp'), parts along dimension 0, may hold values from -6 to 6
- lengths: int32 [16], P('grp'), parts along dimension 0, may hold values from 384 to 3072, as said below
- norm_scale_vector: float32 [2048], replicated, may hold values from 0.1 to 1.9
- expert_choice: int32 [32, 8], P(('grp', 'exp')), parts along dimension 0, may hold values from 0 to 15, all different within a row; in each aligned block of 16 rows (0 to 15, 16 to 31, ...) at most 16 rows name the same one
- router_probability: float32 [32, 8], P(('grp', 'exp')), parts along dimension 0, may hold values from 0.05 to 1
- gate_weight: bfloat16 [16, 2048, 768], P('exp'), may hold values from -0.125 to 0.125
- up_weight: bfloat16 [16, 2048, 768], P('exp'), may hold values from -0.125 to 0.125
- down_weight: bfloat16 [16, 768, 2048], P('exp'), may hold values from -0.21875 to 0.21875
- adapter_model: bfloat16 [16, 96, 2048], P(None, None, 'exp'), may hold values from -0.41992188 to 0.41992188
- adapter_hidden: bfloat16 [16, 96, 768], P(None, None, 'exp'), may hold values from -0.41992188 to 0.41992188
Outputs:
- layer_out: bfloat16 [32, 2048], P(('grp', 'exp')), parts along dimension 0
There are 2 independent parts, one for each index of `grp`. A program takes and returns all parts, laid end to end along the dimension named above; an argument that names none is the same for every part. Nothing has to cross between parts.
Inputs may be any that keep to these rules, and one draw needn't show every extreme that they name: `lengths`: every sequence keeps at least 384 cached positions, and some sequence has all 3072. `expert_choice`: no expert is named by more than 16 tokens of a group, a bound that some block reaches.
All inputs are finite; a program needn't handle non-finite values.
Results may differ from a plain program's by a relative error of at most 0.0062.
The roundings to bfloat16 on the way count: a program that leaves them out, or rounds other values in their place, can miss the bound.
Values may be sent and summed in bfloat16 or wider, within the bound.
No kernel may reach another device: no remote copies, remote signals or barrier semaphores. Data moves between devices by JAX's collectives and lax.ppermute only.
A program may use at most 64 MiB of HBM per device.

v0:
```python
import jax
import jax.numpy as jnp
from jax import lax
from jax.sharding import PartitionSpec as P

QUERY_HEADS = 16
KEY_VALUE_HEADS = 2
HEAD_WIDTH = 128
ADAPTER_RANK = 32


floor_score = -1e30
epsilon = 1e-06


def expert_pass(rows, gate_fold, up_fold, down_fold):
    gate_part = jnp.dot(rows, gate_fold, preferred_element_type=jnp.float32)
    up_part = jnp.dot(rows, up_fold, preferred_element_type=jnp.float32)
    act = (jax.nn.silu(gate_part) * up_part).astype(jnp.bfloat16)
    return jnp.dot(act, down_fold, preferred_element_type=jnp.float32)


def body(
    resid,
    queries,
    incoming_key_value,
    key_value_cache,
    lengths,
    norm_scale_vector,
    expert_choice,
    router_probability,
    gate_weight,
    up_weight,
    down_weight,
    adapter_model,
    adapter_hidden,
):
    got_model, got_hidden = (
        lax.all_to_all(adapter_model, "exp", split_axis=0, concat_axis=2, tiled=True),
        lax.all_to_all(adapter_hidden, "exp", split_axis=0, concat_axis=2, tiled=True),
    )
    grouped_heads = QUERY_HEADS // KEY_VALUE_HEADS
    key_value_width = KEY_VALUE_HEADS * HEAD_WIDTH
    inv_root = HEAD_WIDTH ** (-0.5)
    token_share = resid.shape[0]
    sequence_total = key_value_cache.shape[0]
    block_length = key_value_cache.shape[1]
    where_dev = lax.axis_index("exp")
    query_rows_all, all_new = (
        lax.all_gather(queries, "exp", axis=0, tiled=True),
        lax.all_gather(incoming_key_value, "exp", axis=0, tiled=True),
    )
    tokens = query_rows_all.shape[0]
    query_head_rows = query_rows_all.reshape(
        sequence_total, 2, KEY_VALUE_HEADS, grouped_heads, HEAD_WIDTH
    )
    stored_keys = key_value_cache[:, :, :key_value_width].reshape(
        sequence_total, block_length, KEY_VALUE_HEADS, HEAD_WIDTH
    )
    stored_values = key_value_cache[:, :, key_value_width:].reshape(
        sequence_total, block_length, KEY_VALUE_HEADS, HEAD_WIDTH
    )
    scores = (
        jnp.einsum(
            "spgih,scgh->spgic", query_head_rows, stored_keys, preferred_element_type=jnp.float32
        )
        * inv_root
    )
    positions = where_dev * block_length + jnp.arange(block_length, dtype=jnp.int32)
    in_range = (positions[None, :] < lengths[:, None])[:, None, None, None, :]
    scores = jnp.where(in_range, scores, floor_score)
    block_max = jnp.max(scores, axis=-1)
    weights = jnp.where(in_range, jnp.exp(scores - block_max[..., None]), 0.0).astype(jnp.bfloat16)
    block_sum = jnp.sum(weights, axis=-1, dtype=jnp.float32)
    block_acc = jnp.einsum(
        "spgic,scgh->spgih", weights, stored_values, preferred_element_type=jnp.float32
    )
    maxima = block_max.reshape(tokens, QUERY_HEADS)
    totals = block_sum.reshape(tokens, QUERY_HEADS)
    sums_flat = block_acc.reshape(tokens, QUERY_HEADS, HEAD_WIDTH)
    got_max, got_sum, got_acc = (
        lax.all_to_all(maxima, "exp", split_axis=0, concat_axis=0, tiled=True),
        lax.all_to_all(totals, "exp", split_axis=0, concat_axis=0, tiled=True),
        lax.all_to_all(
            sums_flat.reshape(tokens, QUERY_HEADS * HEAD_WIDTH),
            "exp",
            split_axis=0,
            concat_axis=0,
            tiled=True,
        ),
    )
    got_max = got_max.reshape(-1, token_share, QUERY_HEADS)
    got_sum = got_sum.reshape(-1, token_share, QUERY_HEADS)
    got_acc = got_acc.reshape(-1, token_share, QUERY_HEADS, HEAD_WIDTH)
    cache_max = jnp.max(got_max, axis=0)
    factor = jnp.exp(got_max - cache_max[None])
    cache_sum = jnp.sum(factor * got_sum, axis=0)
    cache_acc = jnp.sum(factor[..., None] * got_acc, axis=0)
    own_ids = where_dev * token_share + jnp.arange(token_share, dtype=jnp.int32)
    token_pair_rows = all_new.reshape(sequence_total, 2, 2 * key_value_width)[own_ids // 2]
    step_index = own_ids % 2
    incoming_keys = token_pair_rows[:, :, :key_value_width].reshape(
        token_share, 2, KEY_VALUE_HEADS, HEAD_WIDTH
    )
    incoming_values = token_pair_rows[:, :, key_value_width:].reshape(
        token_share, 2, KEY_VALUE_HEADS, HEAD_WIDTH
    )
    sequence_query = queries.reshape(token_share, KEY_VALUE_HEADS, grouped_heads, HEAD_WIDTH)
    new_scores = (
        jnp.einsum(
            "tgih,tjgh->tgij", sequence_query, incoming_keys, preferred_element_type=jnp.float32
        )
        * inv_root
    )
    new_mask = (jnp.arange(2, dtype=jnp.int32)[None, :] <= step_index[:, None])[:, None, None, :]
    new_scores = jnp.where(new_mask, new_scores, floor_score)
    new_max = jnp.max(new_scores, axis=-1)
    new_weights = jnp.where(new_mask, jnp.exp(new_scores - new_max[..., None]), 0.0).astype(
        jnp.bfloat16
    )
    new_sum = jnp.sum(new_weights, axis=-1, dtype=jnp.float32).reshape(token_share, QUERY_HEADS)
    new_acc = jnp.einsum(
        "tgij,tjgh->tgih", new_weights, incoming_values, preferred_element_type=jnp.float32
    ).reshape(token_share, QUERY_HEADS, HEAD_WIDTH)
    new_max = new_max.reshape(token_share, QUERY_HEADS)
    highest = jnp.maximum(cache_max, new_max)
    cache_share = jnp.exp(cache_max - highest)
    fresh_share = jnp.exp(new_max - highest)
    denominator = cache_sum * cache_share + new_sum * fresh_share
    context = (cache_acc * cache_share[..., None] + new_acc * fresh_share[..., None]) / denominator[
        ..., None
    ]
    hidden = resid.astype(jnp.float32) + context.reshape(token_share, QUERY_HEADS * HEAD_WIDTH)
    normed = (
        hidden
        * lax.rsqrt(jnp.mean(hidden * hidden, axis=-1, keepdims=True) + epsilon)
        * norm_scale_vector
    ).astype(jnp.bfloat16)
    exp_dev = gate_weight.shape[0]
    expert_total = exp_dev * lax.axis_size("exp")
    shares = router_probability / jnp.sum(router_probability, axis=-1, keepdims=True)
    picks = (
        expert_choice[:, :, None] == jnp.arange(expert_total, dtype=jnp.int32)[None, None, :]
    ).astype(jnp.float32)
    gates = jnp.sum(shares[:, :, None] * picks, axis=1).astype(jnp.bfloat16)
    all_rows, all_gates = (
        lax.all_gather(normed, "exp", axis=0, tiled=True),
        lax.all_gather(gates, "exp", axis=0, tiled=True),
    )
    gate_fold = (
        gate_weight.astype(jnp.float32)
        + jnp.einsum(
            "erd,erf->edf",
            got_model[:, 0:ADAPTER_RANK],
            got_hidden[:, 0:ADAPTER_RANK],
            preferred_element_type=jnp.float32,
        )
    ).astype(jnp.bfloat16)
    up_fold = (
        up_weight.astype(jnp.float32)
        + jnp.einsum(
            "erd,erf->edf",
            got_model[:, ADAPTER_RANK : 2 * ADAPTER_RANK],
            got_hidden[:, ADAPTER_RANK : 2 * ADAPTER_RANK],
            preferred_element_type=jnp.float32,
        )
    ).astype(jnp.bfloat16)
    down_fold = (
        down_weight.astype(jnp.float32)
        + jnp.einsum(
            "erf,erd->efd",
            got_hidden[:, 2 * ADAPTER_RANK : 3 * ADAPTER_RANK],
            got_model[:, 2 * ADAPTER_RANK : 3 * ADAPTER_RANK],
            preferred_element_type=jnp.float32,
        )
    ).astype(jnp.bfloat16)
    column_index = lax.dynamic_index_in_dim(all_gates, where_dev * exp_dev + 0, 1, keepdims=False)
    output = expert_pass(all_rows, gate_fold[0], up_fold[0], down_fold[0])
    contrib = output * column_index.astype(jnp.float32)[:, None]
    moe = lax.psum_scatter(contrib, "exp", scatter_dimension=0, tiled=True)
    return (hidden + moe).astype(jnp.bfloat16)


def solution(mesh):
    return jax.shard_map(
        body,
        mesh=mesh,
        in_specs=(
            P(("grp", "exp"), None),
            P(("grp", "exp"), None),
            P(("grp", "exp"), None),
            P("grp", "exp", None),
            P("grp"),
            P(),
            P(("grp", "exp"), None),
            P(("grp", "exp"), None),
            P("exp", None, None),
            P("exp", None, None),
            P("exp", None, None),
            P(None, None, "exp"),
            P(None, None, "exp"),
        ),
        out_specs=P(("grp", "exp"), None),
        check_vma=False,
    )
```

profile of v0, /device:TPU:0, one launch (start us, length us, event | category | flops | bytes accessed | tf_op | source)
XLA Modules:
  0.0 272.5 jit_solution(8954489989387986293)
XLA Ops:
  6.5 2.4 fusion.39
  9.0 0.2 reshape.409
  9.2 23.4 %all-gather.1 = bf16[16,1,2048]{2,1,0:T(2,128)(2,1)S(1)} all-gather(bf16[1,1,2048]{2,1,0:T(2,128)(2,1)S(1)} %bitcast.144), channel_id=1, replica_groups=mesh['grp'=2,'exp'=16] {'exp'}, dimensions={0}, use_global_device_ids=true | all-gather | bytes 69632 | tf_op jit(solution)/shard_map/all_gather | solution.py:50
  32.6 0.4 reduce.14
  33.1 0.6 fusion.42
  33.7 0.7 all_to_all.44
  34.4 3.5 %all-to-all-start = ((f32[16,1,16]{2,1,0:T(1,128)}), f32[16,1,16]{2,1,0:T(1,128)S(1)}, u32[]{:S(2)}, u32[]{:S(2)}) async-start(f32[16,1,16]{2,1,0:T(1,128)} %bitcast.3), calls=%async_computation | async-start | bytes 16384 | tf_op jit(solution)/shard_map/all_to_all | solution.py:82
  38.0 21.7 %all-gather.2 = bf16[16,1,512]{2,1,0:T(2,128)(2,1)S(1)} all-gather(bf16[1,1,512]{2,1,0:T(2,128)(2,1)S(1)} %bitcast.150), channel_id=1, replica_groups=mesh['grp'=2,'exp'=16] {'exp'}, dimensions={0}, use_global_device_ids=true | all-gather | bytes 17408 | tf_op jit(solution)/shard_map/all_gather | solution.py:51
  59.7 0.1 reduce.15
  59.9 2.9 %reshape.411 = bf16[8,192,2,128]{3,2,1,0:T(2,128)(2,1)} reshape(bf16[8,192,256]{2,1,0:T(8,128)(2,1)} %get-tuple-element.25) | data formatting | bytes 1572864 | tf_op jit(solution)/shard_map/reshape | solution.py:60
  62.7 0.6 reduce_sum.71
  63.3 1.2 divide_bitcast_fusion
  64.6 0.1 fusion.41
  64.7 0.7 convert_reduce_fusion.2
  65.4 0.8 fusion.31
  66.1 1.5 convolution_bitcast_fusion
  67.6 0.9 convert_reduce_fusion
  68.6 0.7 all_to_all.48
  69.3 3.5 %all-to-all-start.2 = ((f32[16,1,16]{2,1,0:T(1,128)}), f32[16,1,16]{2,1,0:T(1,128)S(1)}, u32[]{:S(2)}, u32[]{:S(2)}) async-start(f32[16,1,16]{2,1,0:T(1,128)} %bitcast.20), calls=%async_computation.2 | async-start | bytes 16384 | tf_op jit(solution)/shard_map/all_to_all | solution.py:83
  72.8 0.8 select_reduce_fusion
  73.5 0.7 reshape.415
  74.3 0.7 reshape.418
  75.0 0.6 copy.49
  75.7 0.6 fusion.40
  76.8 0.2 dynamic-update-slice.1
  77.1 0.1 reshape.448
  77.2 33.8 %all-reduce.1 = bf16[16,16]{1,0:T(8,128)(2,1)S(1)} all-reduce(bf16[16,16]{1,0:T(8,128)(2,1)S(1)} %reshape.448), channel_id=2, replica_groups=mesh['grp'=2,'exp'=16] {'exp'}, use_global_device_ids=true, to_apply=%add | all-reduce | flops 256 | bytes 1024
  111.0 0.8 convert_reduce_fusion.1
  111.8 3.5 %all-to-all-start.1 = ((f32[16,1,2048]{2,1,0:T(1,128)}), f32[16,1,2048]{2,1,0:T(1,128)S(1)}, u32[]{:S(2)}, u32[]{:S(2)}) async-start(f32[16,1,2048]{2,1,0:T(1,128)} %bitcast.8), calls=%async_computation.1 | async-start | bytes 262144 | tf_op jit(solution)/shard_map/all_to_all | solution.py:84
  115.4 0.5 multiply_add_fusion
  115.9 7.3 %all-to-all-done.1 = f32[16,1,2048]{2,1,0:T(1,128)S(1)} async-done(((f32[16,1,2048]{2,1,0:T(1,128)}), f32[16,1,2048]{2,1,0:T(1,128)S(1)}, u32[]{:S(2)}, u32[]{:S(2)}) %all-to-all-start.1) | async-done | bytes 131104 | tf_op jit(solution)/shard_map/all_to_all | solution.py:84
  123.2 0.6 copy-done.3
  123.9 3.6 %all-to-all-start.3 = ((bf16[16,96,128]{2,1,0:T(8,128)(2,1)}), bf16[16,96,128]{2,1,0:T(8,128)(2,1)S(1)}, u32[]{:S(2)}, u32[]{:S(2)}) async-start(bf16[16,96,128]{2,1,0:T(8,128)(2,1)} %param.24), calls=%async_computation.3 | async-start | bytes 786432 | tf_op jit(solution)/shard_map/all_to_all | solution.py:39
  127.4 0.1 mul.142
  127.5 1.1 multiply_reduce_fusion
  128.6 0.7 mul.147
  129.5 1.4 multiply_reduce_fusion.1
  131.5 0.7 convert_bitcast_fusion
  132.2 23.4 %all-gather.3 = bf16[16,1,2048]{2,1,0:T(2,128)(2,1)} all-gather(bf16[1,1,2048]{2,1,0:T(2,128)(2,1)S(1)} %convert_bitcast_fusion), channel_id=1, replica_groups=mesh['grp'=2,'exp'=16] {'exp'}, dimensions={0}, use_global_device_ids=true | all-gather | bytes 69632 | tf_op jit(solution)/shard_map/all_gather | solution.py:147
  155.7 0.7 copy-done.2
  156.4 3.5 %all-to-all-start.4 = ((bf16[16,96,48]{1,2,0:T(8,128)(2,1)}), bf16[16,96,48]{1,2,0:T(8,128)(2,1)S(1)}, u32[]{:S(2)}, u32[]{:S(2)}) async-start(bf16[16,96,48]{1,2,0:T(8,128)(2,1)} %param.25), calls=%async_computation.4 | async-start | bytes 393216 | tf_op jit(solution)/shard_map/all_to_all | solution.py:40
  160.0 1.8 copy_bitcast_fusion
  161.8 7.1 %all-to-all-done.4 = bf16[16,96,48]{1,2,0:T(8,128)(2,1)S(1)} async-done(((bf16[16,96,48]{1,2,0:T(8,128)(2,1)}), bf16[16,96,48]{1,2,0:T(8,128)(2,1)S(1)}, u32[]{:S(2)}, u32[]{:S(2)}) %all-to-all-start.4) | async-done | bytes 147488 | tf_op jit(solution)/shard_map/all_to_all | solution.py:40
  168.9 2.4 fusion.7
  171.3 4.2 %fusion.17 = bf16[16,768]{1,0:T(8,128)(2,1)} fusion(bf16[1,2048,768]{2,1,0:T(8,128)(2,1)} %param.22, bf16[1,96,768]{1,2,0:T(8,128)(2,1)S(1)} %bitcast.135, bf16[1,96,2048]{2,1,0:T(8,128)(2,1)} %copy_bitcast_fusion, f32[16,768]{1,0:T(8,128)S(1)} %fusion.7, bf16[16,1,2048]{2,1,0:T(2,128)(2,1)S(1)} %copy-done.4), kind=kOutput, calls=%fused_computation.18 | convolution fusion | flops 155787264 | bytes 3563520 | tf_op jit(solution)/shard_map/dot_general | solution.py:18
  175.5 3.0 %fusion.9 = f32[16,2048]{1,0:T(8,128)} fusion(bf16[16,768]{1,0:T(8,128)(2,1)} %fusion.17, bf16[1,768,2048]{2,1,0:T(8,128)(2,1)S(1)} %copy-done.1, bf16[1,96,768]{1,2,0:T(8,128)(2,1)S(1)} %bitcast.136, bf16[1,96,2048]{2,1,0:T(8,128)(2,1)} %copy_bitcast_fusion, f32[16]{0:T(128)S(1)} %copy-done.9), kind=kOutput, calls=%fused_computation.12 | convolution fusion | flops 155746304 | bytes 3579968 | tf_op jit(solution)/shard_map/dot_general | solution.py:20
  178.5 85.1 %all-reduce.5.cloned.1.call-done = f32[16,2048]{1,0:T(8,128)} async-done(((f32[16,2048]{1,0:T(8,128)}), f32[16,2048]{1,0:T(8,128)}) %all-reduce.5.cloned.1.call-update) | async-done | bytes 131088
  263.6 2.1 fusion.29
  (42 shorter events, 0.5 us)
Async XLA Ops:
  6.5 2.7 copy-start.6
  6.5 26.5 %copy-start.11 = (s32[8]{0:T(128)S(1)}, s32[8]{0:T(128)}, u32[]{:S(2)}) copy-start(s32[8]{0:T(128)} %param.17) | copy-start | bytes 100
  6.5 31.4 %copy-start.7 = (bf16[1,512]{1,0:T(2,128)(2,1)S(1)}, bf16[1,512]{1,0:T(2,128)(2,1)}, u32[]{:S(2)}) copy-start(bf16[1,512]{1,0:T(2,128)(2,1)} %param.15) | copy-start | bytes 3076
  9.0 53.8 %copy-start.12 = (f32[1,8]{1,0:T(1,128)S(1)}, f32[1,8]{1,0:T(1,128)}, u32[]{:S(2)}) copy-start(f32[1,8]{1,0:T(1,128)} %param.20) | copy-start | bytes 100
  9.2 66.5 %copy-start.8 = (u32[32]{0:T(128)S(1)}, u32[32]{0:T(128)}, u32[]{:S(2)}) copy-start(u32[32]{0:T(128)} %constant.96) | copy-start | bytes 388
  33.7 26.1 %copy-start.5 = (f32[8,2,2,8]{3,1,2,0:T(2,128)}, f32[8,2,2,8]{3,1,2,0:T(2,128)S(1)}, u32[]{:S(2)}) copy-start(f32[8,2,2,8]{3,1,2,0:T(2,128)S(1)} %get-tuple-element.31) | copy-start | bytes 3076
  34.4 34.9 %all-to-all-start = ((f32[16,1,16]{2,1,0:T(1,128)}), f32[16,1,16]{2,1,0:T(1,128)S(1)}, u32[]{:S(2)}, u32[]{:S(2)}) async-start(f32[16,1,16]{2,1,0:T(1,128)} %bitcast.3), calls=%async_computation | async-start | bytes 16384 | tf_op jit(solution)/shard_map/all_to_all | solution.py:82
  59.9 109.1 %copy-start = (bf16[1,2048,768]{2,1,0:T(8,128)(2,1)S(1)}, bf16[1,2048,768]{2,1,0:T(8,128)(2,1)}, u32[]{:S(2)}) copy-start(bf16[1,2048,768]{2,1,0:T(8,128)(2,1)} %param.21) | copy-start | bytes 9437188
  64.7 1.4 copy-start.10
  69.3 42.5 %all-to-all-start.2 = ((f32[16,1,16]{2,1,0:T(1,128)}), f32[16,1,16]{2,1,0:T(1,128)S(1)}, u32[]{:S(2)}, u32[]{:S(2)}) async-start(f32[16,1,16]{2,1,0:T(1,128)} %bitcast.20), calls=%async_computation.2 | async-start | bytes 16384 | tf_op jit(solution)/shard_map/all_to_all | solution.py:83
  111.8 11.4 %all-to-all-start.1 = ((f32[16,1,2048]{2,1,0:T(1,128)}), f32[16,1,2048]{2,1,0:T(1,128)S(1)}, u32[]{:S(2)}, u32[]{:S(2)}) async-start(f32[16,1,2048]{2,1,0:T(1,128)} %bitcast.8), calls=%async_computation.1 | async-start | bytes 262144 | tf_op jit(solution)/shard_map/all_to_all | solution.py:84
  123.2 0.6 copy-start.3
  123.9 31.8 %all-to-all-start.3 = ((bf16[16,96,128]{2,1,0:T(8,128)(2,1)}), bf16[16,96,128]{2,1,0:T(8,128)(2,1)S(1)}, u32[]{:S(2)}, u32[]{:S(2)}) async-start(bf16[16,96,128]{2,1,0:T(8,128)(2,1)} %param.24), calls=%async_computation.3 | async-start | bytes 786432 | tf_op jit(solution)/shard_map/all_to_all | solution.py:39
  155.7 0.7 copy-start.2
  156.4 12.5 %all-to-all-start.4 = ((bf16[16,96,48]{1,2,0:T(8,128)(2,1)}), bf16[16,96,48]{1,2,0:T(8,128)(2,1)S(1)}, u32[]{:S(2)}, u32[]{:S(2)}) async-start(bf16[16,96,48]{1,2,0:T(8,128)(2,1)} %param.25), calls=%async_computation.4 | async-start | bytes 393216 | tf_op jit(solution)/shard_map/all_to_all | solution.py:40
  160.0 11.3 %copy-start.4 = (bf16[16,1,2048]{2,1,0:T(2,128)(2,1)S(1)}, bf16[16,1,2048]{2,1,0:T(2,128)(2,1)}, u32[]{:S(2)}) copy-start(bf16[16,1,2048]{2,1,0:T(2,128)(2,1)} %all-gather.3) | copy-start | bytes 196612
  160.0 103.6 %all-reduce.5.cloned.1.call-start = ((), (), s32[]{:S(2)}) async-start(), calls=%async_computation.5 | async-start | bytes 262144
  168.9 6.6 %copy-start.9 = (f32[16]{0:T(128)S(1)}, f32[16]{0:T(128)}, u32[]{:S(2)}) copy-start(f32[16]{0:T(128)} %convert_reduce_fusion.1) | copy-start | bytes 196
  171.3 4.2 %copy-start.1 = (bf16[1,768,2048]{2,1,0:T(8,128)(2,1)S(1)}, bf16[1,768,2048]{2,1,0:T(8,128)(2,1)}, u32[]{:S(2)}) copy-start(bf16[1,768,2048]{2,1,0:T(8,128)(2,1)} %param.23) | copy-start | bytes 9437188
Sparse Core Ops, SparseCore 0:
  178.6 84.9 all-reduce.4
where the time goes:
time: 275 us; the launch traced here: 273 us
  blocking collectives  102 us (37%)
  waiting for transfers between devices  99.6 us (36%)
  starting transfers between devices  17.6 us (6%)
  between operations  14.9 us (5%)
  local copies, waits for them, and re-layouts  14.1 us (5%)
  matrix products  12.5 us (5%)
  other arithmetic  11.3 us (4%)
    unnamed x2, waiting for transfers between devices  85.2 us
    unnamed x1, blocking collectives  33.8 us
    all_gather x1, blocking collectives, body(): lax.all_gather(normed, 'exp', axis=0, tiled=True)  23.4 us
    all_gather x1, blocking collectives, body(): lax.all_gather(queries, 'exp', axis=0, tiled=True)  23.4 us
    all_gather x1, blocking collectives, body(): lax.all_gather(incoming_key_value, 'exp', axis=0, tiled=True)  21.7 us
    all_to_all x1, waiting for transfers between devices, body(): lax.all_to_all(sums_flat.reshape(tokens, QUERY_HEADS * HEAD_WIDTH), 'exp'...  7.33 us
    all_to_all x1, waiting for transfers between devices, body(): lax.all_to_all(adapter_hidden, 'exp', split_axis=0, concat_axis=2, tiled=...  7.1 us
  transfers between devices with their start and end apart: 6, of which 3 were waited for; matrix products, arithmetic and copies ran while one was open for 7% of the time, Pallas kernels for 0%

commit v1 on v0

v1 whole, which is shorter than its diff:
```python
import functools

import jax
import jax.numpy as jnp
from jax import lax
from jax.experimental import pallas as pl
from jax.experimental.pallas import tpu as pltpu
from jax.sharding import PartitionSpec as P

QUERY_HEADS = 16
KEY_VALUE_HEADS = 2
HEAD_WIDTH = 128
ADAPTER_RANK = 32
GROUPED = QUERY_HEADS // KEY_VALUE_HEADS
KEY_VALUE_WIDTH = KEY_VALUE_HEADS * HEAD_WIDTH
INV_ROOT = HEAD_WIDTH ** (-0.5)
STAT_ROWS = 8
PART_ROWS = QUERY_HEADS + STAT_ROWS

floor_score = -1e30
epsilon = 1e-06

VMEM_LIMIT = 48 * 1024 * 1024
VMEM = pl.BlockSpec(memory_space=pltpu.VMEM)
SMEM = pl.BlockSpec(memory_space=pltpu.SMEM)
PARAMS = pltpu.CompilerParams(vmem_limit_bytes=VMEM_LIMIT)


def iota(shape, dim):
    return lax.broadcasted_iota(jnp.int32, shape, dim)


def attend_kernel(lengths, offset, query, cache, part):
    sequences, block, _ = cache.shape
    rows = 2 * QUERY_HEADS
    first_group = (iota((rows, HEAD_WIDTH), 0) % QUERY_HEADS) < GROUPED
    diagonal = iota((QUERY_HEADS, HEAD_WIDTH), 0) == iota((QUERY_HEADS, HEAD_WIDTH), 1)
    stat_row = iota((STAT_ROWS, HEAD_WIDTH), 0)
    positions = offset[0] + iota((rows, block), 1)

    def step(s, carry):
        both = query[pl.ds(2 * s, 2)].reshape(rows, HEAD_WIDTH)
        zero = jnp.zeros_like(both)
        wide = jnp.concatenate(
            [jnp.where(first_group, both, zero), jnp.where(first_group, zero, both)], axis=1
        )
        keys = cache[s, :, :KEY_VALUE_WIDTH]
        values = cache[s, :, KEY_VALUE_WIDTH:]
        scores = (
            lax.dot_general(
                wide, keys, (((1,), (1,)), ((), ())), preferred_element_type=jnp.float32
            )
            * INV_ROOT
        )
        valid = positions < lengths[s]
        scores = jnp.where(valid, scores, floor_score)
        top = jnp.max(scores, axis=1, keepdims=True)
        weights = jnp.where(valid, jnp.exp(scores - top), 0.0).astype(jnp.bfloat16)
        total = jnp.sum(weights.astype(jnp.float32), axis=1, keepdims=True)
        acc = jnp.dot(weights, values, preferred_element_type=jnp.float32)
        acc = jnp.where(first_group, acc[:, :HEAD_WIDTH], acc[:, HEAD_WIDTH:])
        for p in range(2):
            cut = slice(p * QUERY_HEADS, (p + 1) * QUERY_HEADS)
            part[2 * s + p, :QUERY_HEADS] = acc[cut]
            top_row = jnp.sum(jnp.where(diagonal, top[cut], 0.0), axis=0, keepdims=True)
            sum_row = jnp.sum(jnp.where(diagonal, total[cut], 0.0), axis=0, keepdims=True)
            part[2 * s + p, QUERY_HEADS:] = jnp.where(
                stat_row == 0, top_row, jnp.where(stat_row == 1, sum_row, 0.0)
            )
        return carry

    if sequences <= 8:
        for s in range(sequences):
            step(s, 0)
    else:
        lax.fori_loop(0, sequences, step, 0)


def merge_kernel(
    me, got, query, own, partner, resid, scale, choice, probability, hidden_out, normed_out, gates_out
):
    sources = got.shape[0]
    first_group = iota((QUERY_HEADS, HEAD_WIDTH), 0) < GROUPED

    def by_head(rows, at):
        return jnp.where(first_group, rows[at : at + 1], rows[at + 1 : at + 2])

    q = query[...].astype(jnp.float32)
    own_rows = own[...].astype(jnp.float32)
    partner_rows = partner[...].astype(jnp.float32)
    second = lax.rem(me[0], 2) == 1
    own_score = jnp.sum(q * by_head(own_rows, 0), axis=1, keepdims=True) * INV_ROOT
    partner_score = jnp.sum(q * by_head(partner_rows, 0), axis=1, keepdims=True) * INV_ROOT
    partner_score = jnp.where(second, partner_score, floor_score)
    new_max = jnp.maximum(own_score, partner_score)
    own_weight = jnp.exp(own_score - new_max).astype(jnp.bfloat16).astype(jnp.float32)
    partner_weight = jnp.where(second, jnp.exp(partner_score - new_max), 0.0)
    partner_weight = partner_weight.astype(jnp.bfloat16).astype(jnp.float32)
    new_sum = own_weight + partner_weight
    new_acc = own_weight * by_head(own_rows, 2) + partner_weight * by_head(partner_rows, 2)

    stats = got[:, QUERY_HEADS:, :]
    maxima = stats[:, 0, :].T[:QUERY_HEADS]
    totals = stats[:, 1, :].T[:QUERY_HEADS]
    top = jnp.maximum(jnp.max(maxima, axis=1, keepdims=True), new_max)
    share = jnp.exp(maxima - top)
    fresh = jnp.exp(new_max - top)
    denominator = jnp.sum(share * totals, axis=1, keepdims=True) + fresh * new_sum
    numerator = fresh * new_acc
    for c in range(sources):
        numerator = numerator + share[:, c : c + 1] * got[c, :QUERY_HEADS, :]
    hidden = resid[...].astype(jnp.float32) + numerator / denominator
    width = QUERY_HEADS * HEAD_WIDTH
    squares = jnp.sum(jnp.sum(hidden * hidden, axis=1, keepdims=True), axis=0, keepdims=True)
    normed = hidden * lax.rsqrt(squares / width + epsilon) * scale[...]
    hidden_out[...] = hidden
    normed_out[...] = normed.astype(jnp.bfloat16)

    p = probability[...]
    shares = p / jnp.sum(p, axis=1, keepdims=True)
    lanes = iota(gates_out.shape, 1)
    gates = jnp.zeros(gates_out.shape, jnp.float32)
    for k in range(p.shape[1]):
        gates = gates + jnp.where(choice[:, k : k + 1] == lanes, shares[:, k : k + 1], 0.0)
    gates_out[...] = gates.astype(jnp.bfloat16).astype(jnp.float32)


def dot_pair(value, factor):
    high = value.astype(jnp.bfloat16)
    low = (value - high.astype(jnp.float32)).astype(jnp.bfloat16)
    return jnp.dot(high, factor, preferred_element_type=jnp.float32) + jnp.dot(
        low, factor, preferred_element_type=jnp.float32
    )


def expert_kernel(rows, gate_w, up_w, down_w, model, hidden, out):
    tokens = rows.shape[0]
    x = rows[...].astype(jnp.float32).reshape(tokens, -1).astype(jnp.bfloat16)
    r = ADAPTER_RANK
    mixed = lax.dot_general(
        x, model[: 2 * r], (((1,), (1,)), ((), ())), preferred_element_type=jnp.float32
    )
    gate = jnp.dot(x, gate_w[...], preferred_element_type=jnp.float32)
    gate = gate + dot_pair(mixed[:, :r], hidden[:r])
    up = jnp.dot(x, up_w[...], preferred_element_type=jnp.float32)
    up = up + dot_pair(mixed[:, r:], hidden[r : 2 * r])
    act = (gate / (1.0 + jnp.exp(-gate)) * up).astype(jnp.bfloat16)
    lowered = lax.dot_general(
        act, hidden[2 * r :], (((1,), (1,)), ((), ())), preferred_element_type=jnp.float32
    )
    result = jnp.dot(act, down_w[...], preferred_element_type=jnp.float32)
    result = result + dot_pair(lowered, model[2 * r :])
    for j in range(QUERY_HEADS):
        out[:, j, :] = result[:, j * HEAD_WIDTH : (j + 1) * HEAD_WIDTH]


def finish_kernel(hidden, gates, got, out):
    total = hidden[...]
    for c in range(got.shape[0]):
        total = total + gates[:, c : c + 1] * got[c]
    out[...] = total.astype(jnp.bfloat16)


def call(kernel, shapes, specs, *args):
    return pl.pallas_call(
        kernel,
        out_shape=shapes,
        in_specs=specs,
        out_specs=jax.tree.map(lambda _: VMEM, shapes),
        compiler_params=PARAMS,
    )(*args)


def exchange(parts):
    return lax.all_to_all(parts, "exp", split_axis=0, concat_axis=0, tiled=True)


def body(
    resid,
    queries,
    incoming_key_value,
    key_value_cache,
    lengths,
    norm_scale_vector,
    expert_choice,
    router_probability,
    gate_weight,
    up_weight,
    down_weight,
    adapter_model,
    adapter_hidden,
):
    n = lax.axis_size("exp")
    me = lax.axis_index("exp").astype(jnp.int32)
    heads = (QUERY_HEADS, HEAD_WIDTH)
    shape = jax.ShapeDtypeStruct
    block = key_value_cache.shape[1]

    query = queries.reshape(heads)
    fresh = incoming_key_value.reshape(2 * KEY_VALUE_HEADS, HEAD_WIDTH)
    partner = lax.ppermute(fresh, "exp", [(t, t ^ 1) for t in range(n)])
    all_queries = exchange(jnp.broadcast_to(query[None], (n,) + heads))
    part = call(
        attend_kernel,
        shape((n, PART_ROWS, HEAD_WIDTH), jnp.float32),
        [SMEM, SMEM, VMEM, VMEM],
        lengths,
        (me * block).reshape(1),
        all_queries,
        key_value_cache,
    )
    got = exchange(part)
    hidden, normed, gates = call(
        merge_kernel,
        (
            shape(heads, jnp.float32),
            shape(heads, jnp.bfloat16),
            shape((1, max(n, HEAD_WIDTH)), jnp.float32),
        ),
        [SMEM] + [VMEM] * 8,
        me.reshape(1),
        got,
        query,
        fresh,
        partner,
        resid.reshape(heads),
        norm_scale_vector.reshape(heads),
        expert_choice,
        router_probability,
    )
    rows = exchange(jnp.broadcast_to(normed[None], (n,) + heads))
    model = lax.all_to_all(adapter_model, "exp", split_axis=0, concat_axis=2, tiled=True)
    inner = lax.all_to_all(adapter_hidden, "exp", split_axis=0, concat_axis=2, tiled=True)
    out = call(
        expert_kernel,
        shape((n,) + heads, jnp.float32),
        [VMEM] * 6,
        rows,
        gate_weight[0],
        up_weight[0],
        down_weight[0],
        model[0],
        inner[0],
    )
    final = call(
        finish_kernel, shape(heads, jnp.bfloat16), [VMEM] * 3, hidden, gates, exchange(out)
    )
    return final.reshape(1, QUERY_HEADS * HEAD_WIDTH)


def solution(mesh):
    return jax.shard_map(
        body,
        mesh=mesh,
        in_specs=(
            P(("grp", "exp"), None),
            P(("grp", "exp"), None),
            P(("grp", "exp"), None),
            P("grp", "exp", None),
            P("grp"),
            P(),
            P(("grp", "exp"), None),
            P(("grp", "exp"), None),
            P("exp", None, None),
            P("exp", None, None),
            P("exp", None, None),
            P(None, None, "exp"),
            P(None, None, "exp"),
        ),
        out_specs=P(("grp", "exp"), None),
        check_vma=False,
    )
```

time: 275 us -> 86.4 us (0.31)
  waiting for transfers between devices: 99.6 us -> 16.2 us
  blocking collectives: 102 us -> 36.3 us
  between operations: 14.9 us -> 0.09 us
  matrix products: 12.5 us -> 0 us
  other arithmetic: 11.3 us -> 2.31 us
  Pallas kernels: 0 us -> 8.79 us
  local copies, waits for them, and re-layouts: 14.1 us -> 9.19 us
  starting transfers between devices: 17.6 us -> 12.8 us
    unnamed x2 -> x0, waiting for transfers between devices: 85.2 us -> none
    all_gather x3 -> x0, blocking collectives: 68.6 us -> none  [the longest x1 23.4 us: body(): lax.all_gather(normed, 'exp', axis=0, tiled=True)]
    all_to_all x0 -> x3, blocking collectives: none -> 36.3 us  [exchange(): return lax.all_to_all(parts, 'exp', split_axis=0, concat_axis=0, tiled=True)]
    unnamed x1 -> x0, blocking collectives: 33.8 us -> none
    dot_general x7 -> x0, matrix products: 12.5 us -> none  [the longest x1 4.17 us: expert_pass(): up_part = jnp.dot(rows, up_fold, preferred_element_type=jnp.float32)]
    pallas_call x0 -> x4, Pallas kernels: none -> 8.79 us  [call(): pl.pallas_call(kernel, out_shape=shapes, in_specs=specs, out_specs=jax.tr...]
    all_to_all x1, waiting for transfers between devices: 0.01 us -> 7.85 us  [body(): lax.all_to_all(adapter_model, 'exp', split_axis=0, concat_axis=2, tiled=T...]
    all_to_all x3 -> x1, starting transfers between devices: 10.5 us -> 4.13 us  [exchange(): return lax.all_to_all(parts, 'exp', split_axis=0, concat_axis=0, tiled=True)]
  transfers between devices with their start and end apart: 6 -> 4, of which waited for: 3 -> 4; matrix products, arithmetic and copies ran while one was open for 7% -> 5% of each run, Pallas kernels for 0% -> 4%
where the time goes in v1:
time: 86.4 us; the launch traced here: 85.7 us
  blocking collectives  36.3 us (42%)
  waiting for transfers between devices  16.2 us (19%)
  starting transfers between devices  12.8 us (15%)
  local copies, waits for them, and re-layouts  9.19 us (11%)
  Pallas kernels  8.79 us (10%)
  other arithmetic  2.31 us (3%)
    all_to_all x3, blocking collectives, exchange(): return lax.all_to_all(parts, 'exp', split_axis=0, concat_axis=0, tiled=True)  36.3 us
    pallas_call x4, Pallas kernels, call(): pl.pallas_call(kernel, out_shape=shapes, in_specs=specs, out_specs=jax.tr...  8.79 us
    all_to_all x1, waiting for transfers between devices, body(): lax.all_to_all(adapter_model, 'exp', split_axis=0, concat_axis=2, tiled=T...  7.85 us
    unnamed x16, local copies, waits for them, and re-layouts  5.69 us
    all_to_all x1, waiting for transfers between devices, body(): lax.all_to_all(adapter_hidden, 'exp', split_axis=0, concat_axis=2, tiled=...  4.25 us
    all_to_all x1, starting transfers between devices, body(): lax.all_to_all(adapter_model, 'exp', split_axis=0, concat_axis=2, tiled=T...  4.22 us
    all_to_all x1, starting transfers between devices, body(): lax.all_to_all(adapter_hidden, 'exp', split_axis=0, concat_axis=2, tiled=...  4.17 us
    all_to_all x1, starting transfers between devices, exchange(): return lax.all_to_all(parts, 'exp', split_axis=0, concat_axis=0, tiled=True)  4.13 us
  transfers between devices with their start and end apart: 4, of which 4 were waited for; matrix products, arithmetic and copies ran while one was open for 5% of the time, Pallas kernels for 4%

profile of v1, /device:TPU:0, one launch (start us, length us, event | category | flops | bytes accessed | tf_op | source)
XLA Modules:
  0.0 85.7 jit_solution(3035227502183972471)
XLA Ops:
  0.0 0.0 copy-start
  0.0 0.9 %reduce = bf16[2048]{0:T(1024)(128)(2,1)S(1)} reduce(bf16[1,2048]{1,0:T(2,128)(2,1)} %param.14, bf16[]{:T(256)} %constant.14), dimensions={0}, to_apply=%param.14.reduce_sub_computation | reduce | bytes 8194 | tf_op args[1]
  0.9 14.2 %all_to_all.50.query = bf16[16,16,128]{2,1,0:T(8,128)(2,1)S(1)} all-to-all(bf16[16,16,128]{2,1,0:T(8,128)(2,1)S(1)} %broadcast_in_dim.14), channel_id=1, replica_groups=mesh['grp'=2,'exp'=16] {'exp'}, dimensions={0} | all-to-all | bytes 131072 | tf_op jit(solution)/shard_map/all_to_all | solution.py:175
  15.1 4.2 %all-to-all-start.4 = ((bf16[16,96,48]{1,2,0:T(8,128)(2,1)}), bf16[16,96,48]{1,2,0:T(8,128)(2,1)}, u32[]{:S(2)}, u32[]{:S(2)}) async-start(bf16[16,96,48]{1,2,0:T(8,128)(2,1)} %param.25), calls=%async_computation.4 | async-start | bytes 393216 | tf_op jit(solution)/shard_map/all_to_all | solution.py:233
  19.3 0.0 copy-start.1
  19.3 1.4 %copy-done.1 = bf16[8,192,512]{2,1,0:T(8,128)(2,1)S(1)} copy-done((bf16[8,192,512]{2,1,0:T(8,128)(2,1)S(1)}, bf16[8,192,512]{2,1,0:T(8,128)(2,1)}, u32[]{:S(2)}) %copy-start.1) | copy-done | bytes 1572888
  20.7 0.0 copy-start.4
  20.7 0.7 copy-done.4
  21.4 2.7 %shard_map.127 = f32[16,24,128]{2,1,0:T(8,128)S(1)} custom-call(s32[8]{0:T(128)S(1)} %copy-done.4, s32[1]{0:T(128)} %bitcast.1.offset, bf16[16,16,128]{2,1,0:T(8,128)(2,1)S(1)} %all_to_all.50.query, bf16[8,192,512]{2,1,0:T(8,128)(2,1)S(1)} %copy-done.1), custom_call_target="tpu_custom_call" | custom-call | tf_op jit(solution)/shard_map/pallas_call | solution.py:165
  24.1 4.3 %all-to-all-done.4 = bf16[16,96,48]{1,2,0:T(8,128)(2,1)} async-done(((bf16[16,96,48]{1,2,0:T(8,128)(2,1)}), bf16[16,96,48]{1,2,0:T(8,128)(2,1)}, u32[]{:S(2)}, u32[]{:S(2)}) %all-to-all-start.4) | async-done | bytes 147488 | tf_op jit(solution)/shard_map/all_to_all | solution.py:233
  28.3 11.6 %all_to_all.51.got = f32[16,24,128]{2,1,0:T(8,128)S(1)} all-to-all(f32[16,24,128]{2,1,0:T(8,128)S(1)} %shard_map.127), channel_id=1, replica_groups=mesh['grp'=2,'exp'=16] {'exp'}, dimensions={0} | all-to-all | bytes 393216 | tf_op jit(solution)/shard_map/all_to_all | solution.py:175
  39.9 4.2 %all-to-all-start.3 = ((bf16[16,96,128]{2,1,0:T(8,128)(2,1)}), bf16[16,96,128]{2,1,0:T(8,128)(2,1)}, u32[]{:S(2)}, u32[]{:S(2)}) async-start(bf16[16,96,128]{2,1,0:T(8,128)(2,1)} %param.24), calls=%async_computation.3 | async-start | bytes 786432 | tf_op jit(solution)/shard_map/all_to_all | solution.py:232
  44.1 0.7 reduce.1
  44.8 0.3 collective-permute-start
  45.1 0.7 reduce.2
  45.8 0.2 collective-permute-done.partner
  46.0 0.0 copy-start.3
  46.0 0.7 copy-done.3
  46.7 0.0 copy-start.5
  46.7 0.7 copy-done.5
  47.4 0.0 copy-start.6
  47.4 0.7 copy-done.6
  48.0 0.4 shard_map.128
  48.5 7.9 %all-to-all-done.3 = bf16[16,96,128]{2,1,0:T(8,128)(2,1)} async-done(((bf16[16,96,128]{2,1,0:T(8,128)(2,1)}), bf16[16,96,128]{2,1,0:T(8,128)(2,1)}, u32[]{:S(2)}, u32[]{:S(2)}) %all-to-all-start.3) | async-done | bytes 393248 | tf_op jit(solution)/shard_map/all_to_all | solution.py:232
  56.3 0.6 broadcast_in_dim.15
  57.0 4.1 %all-to-all-start.2 = ((bf16[16,16,128]{2,1,0:T(8,128)(2,1)}), bf16[16,16,128]{2,1,0:T(8,128)(2,1)}, u32[]{:S(2)}, u32[]{:S(2)}) async-start(bf16[16,16,128]{2,1,0:T(8,128)(2,1)} %broadcast_in_dim.15), calls=%async_computation.2 | async-start | bytes 131072 | tf_op jit(solution)/shard_map/all_to_all | solution.py:175
  61.1 1.7 %copy.17.hidden = bf16[96,768]{1,0:T(8,128)(2,1)} copy(bf16[96,768]{0,1:T(8,128)(2,1)} %bitcast.10) | data formatting | bytes 294912 | tf_op jit(solution)/shard_map/squeeze | solution.py:243
  62.8 1.1 %copy.16 = bf16[1,96,16,128]{3,2,1,0:T(8,128)(2,1)S(1)} copy(bf16[1,96,16,128]{3,1,2,0:T(8,128)(2,1)} %bitcast.7) | data formatting | bytes 786432 | tf_op jit(solution)/shard_map/all_to_all | solution.py:232
  63.9 0.1 copy.22
  64.1 3.9 %all-to-all-done.2.rows = bf16[16,16,128]{2,1,0:T(8,128)(2,1)} async-done(((bf16[16,16,128]{2,1,0:T(8,128)(2,1)}), bf16[16,16,128]{2,1,0:T(8,128)(2,1)}, u32[]{:S(2)}, u32[]{:S(2)}) %all-to-all-start.2) | async-done | bytes 65568 | tf_op jit(solution)/shard_map/all_to_all | solution.py:175
  68.0 0.0 copy-done
  68.0 0.0 copy-start.2
  68.0 0.9 %copy-done.2 = bf16[96,768]{1,0:T(8,128)(2,1)S(1)} copy-done((bf16[96,768]{1,0:T(8,128)(2,1)S(1)}, bf16[96,768]{1,0:T(8,128)(2,1)}, u32[]{:S(2)}) %copy-start.2) | copy-done | bytes 147480
  68.9 5.6 %shard_map.129 = f32[16,16,128]{2,1,0:T(8,128)S(1)} custom-call(bf16[16,16,128]{2,1,0:T(8,128)(2,1)} %all-to-all-done.2.rows, bf16[2048,768]{1,0:T(8,128)(2,1)S(1)} %bitcast.27, bf16[2048,768]{1,0:T(8,128)(2,1)} %bitcast.36, bf16[768,2048]{1,0:T(8,128)(2,1)} %bitcast.37, bf16[96,2048]{1,0:T(8,128)(2,1)S(1)} %bitcast.28, bf16[96,768]{1,0:T(8,128)(2,1)S(1)} %copy-done.2), custom_call_target="tpu_custom_call" | custom-call | tf_op jit(solution)/shard_map/pallas_call | solution.py:165
  74.5 10.5 %all_to_all.52.got = f32[16,16,128]{2,1,0:T(8,128)S(1)} all-to-all(f32[16,16,128]{2,1,0:T(8,128)S(1)} %shard_map.129), channel_id=1, replica_groups=mesh['grp'=2,'exp'=16] {'exp'}, dimensions={0} | all-to-all | bytes 262144 | tf_op jit(solution)/shard_map/all_to_all | solution.py:175
  85.0 0.1 shard_map.130
  85.1 0.6 copy.23
  (1 shorter events, 0.0 us)
Async XLA Ops:
  0.0 68.0 %copy-start = (bf16[1,2048,768]{2,1,0:T(8,128)(2,1)S(1)}, bf16[1,2048,768]{2,1,0:T(8,128)(2,1)}, u32[]{:S(2)}) copy-start(bf16[1,2048,768]{2,1,0:T(8,128)(2,1)} %param.21) | copy-start | bytes 9437188
  15.1 13.2 %all-to-all-start.4 = ((bf16[16,96,48]{1,2,0:T(8,128)(2,1)}), bf16[16,96,48]{1,2,0:T(8,128)(2,1)}, u32[]{:S(2)}, u32[]{:S(2)}) async-start(bf16[16,96,48]{1,2,0:T(8,128)(2,1)} %param.25), calls=%async_computation.4 | async-start | bytes 393216 | tf_op jit(solution)/shard_map/all_to_all | solution.py:233
  19.3 1.4 %copy-start.1 = (bf16[8,192,512]{2,1,0:T(8,128)(2,1)S(1)}, bf16[8,192,512]{2,1,0:T(8,128)(2,1)}, u32[]{:S(2)}) copy-start(bf16[8,192,512]{2,1,0:T(8,128)(2,1)} %cache.1) | copy-start | bytes 4718596
  20.7 0.7 copy-start.4
  39.9 16.4 %all-to-all-start.3 = ((bf16[16,96,128]{2,1,0:T(8,128)(2,1)}), bf16[16,96,128]{2,1,0:T(8,128)(2,1)}, u32[]{:S(2)}, u32[]{:S(2)}) async-start(bf16[16,96,128]{2,1,0:T(8,128)(2,1)} %param.24), calls=%async_computation.3 | async-start | bytes 786432 | tf_op jit(solution)/shard_map/all_to_all | solution.py:232
  44.8 1.2 %collective-permute-start = (bf16[4,128]{1,0:T(4,128)(2,1)S(1)}, bf16[4,128]{1,0:T(4,128)(2,1)S(1)}, u32[]{:S(2)}, u32[]{:S(2)}) collective-permute-start(bf16[4,128]{1,0:T(4,128)(2,1)S(1)} %bitcast.34), channel_id=1, source_target_pairs={{0,1},{1,0},{2,3},{3,2},{4,5},{5,4},{6,7},{7,6},{8,9},{9,8},{10,11... | collective-permute-start | bytes 3080 | tf_op jit(solution)/shard_map/ppermute | solution.py:201
  46.0 0.7 copy-start.3
  46.7 0.7 copy-start.5
  47.4 0.7 copy-start.6
  57.0 11.0 %all-to-all-start.2 = ((bf16[16,16,128]{2,1,0:T(8,128)(2,1)}), bf16[16,16,128]{2,1,0:T(8,128)(2,1)}, u32[]{:S(2)}, u32[]{:S(2)}) async-start(bf16[16,16,128]{2,1,0:T(8,128)(2,1)} %broadcast_in_dim.15), calls=%async_computation.2 | async-start | bytes 131072 | tf_op jit(solution)/shard_map/all_to_all | solution.py:175
  68.0 0.9 %copy-start.2 = (bf16[96,768]{1,0:T(8,128)(2,1)S(1)}, bf16[96,768]{1,0:T(8,128)(2,1)}, u32[]{:S(2)}) copy-start(bf16[96,768]{1,0:T(8,128)(2,1)} %copy.17.hidden) | copy-start | bytes 442372

commit v2 on v1

v2 whole, which is shorter than its diff:
```python
import functools

import jax
import jax.numpy as jnp
from jax import lax
from jax.experimental import pallas as pl
from jax.experimental.pallas import tpu as pltpu
from jax.sharding import PartitionSpec as P

QUERY_HEADS = 16
KEY_VALUE_HEADS = 2
HEAD_WIDTH = 128
ADAPTER_RANK = 32
GROUPED = QUERY_HEADS // KEY_VALUE_HEADS
KEY_VALUE_WIDTH = KEY_VALUE_HEADS * HEAD_WIDTH
WIDTH = QUERY_HEADS * HEAD_WIDTH
INV_ROOT = HEAD_WIDTH ** (-0.5)
NEW_ROW = QUERY_HEADS
GATE_ROW = NEW_ROW + 2 * KEY_VALUE_HEADS
MESSAGE = (2 * QUERY_HEADS, HEAD_WIDTH)
HEADS = (QUERY_HEADS, HEAD_WIDTH)

floor_score = -1e30
epsilon = 1e-06

VMEM = pl.BlockSpec(memory_space=pltpu.VMEM)
SMEM = pl.BlockSpec(memory_space=pltpu.SMEM)
shape = jax.ShapeDtypeStruct


def call(kernel, shapes, specs, *args, limit=8):
    return pl.pallas_call(
        kernel,
        out_shape=shapes,
        in_specs=specs,
        out_specs=jax.tree.map(lambda _: VMEM, shapes),
        compiler_params=pltpu.CompilerParams(vmem_limit_bytes=limit * 1024 * 1024),
    )(*args)


def iota(dims, dim):
    return lax.broadcasted_iota(jnp.int32, dims, dim)


def as_rows(line, rows):
    return jnp.concatenate(
        [line[:, j * HEAD_WIDTH : (j + 1) * HEAD_WIDTH] for j in range(rows)], axis=0
    )


def stages_of(n):
    sizes, stride, found = [], 1, []
    while stride < n:
        size = 4 if n // stride % 4 == 0 else 2
        found.append((stride, size))
        stride *= size
    return found


def swap(value, n, distance):
    return lax.ppermute(value, "exp", [(t, t ^ distance) for t in range(n)])


def join_kernel(*refs):
    out = refs[-1]
    step = refs[0].shape[0]
    for k, ref in enumerate(refs[:-1]):
        out[k * step : (k + 1) * step] = ref[...]


def gather(block, n):
    pieces = [block]
    for index, (stride, size) in enumerate(stages_of(n)):
        if index:
            rows = sum(piece.shape[0] for piece in pieces)
            block = call(
                join_kernel,
                shape((rows,) + block.shape[1:], block.dtype),
                [VMEM] * len(pieces),
                *pieces,
            )
        pieces = [block] + [swap(block, n, k * stride) for k in range(1, size)]
    return pieces


def pack_kernel(query, new, choice, probability, out):
    q = as_rows(query[...].astype(jnp.float32), QUERY_HEADS)
    fresh = as_rows(new[...].astype(jnp.float32), 2 * KEY_VALUE_HEADS)
    p = probability[...]
    shares = p / jnp.sum(p, axis=1, keepdims=True)
    lanes = iota((1, HEAD_WIDTH), 1)
    gates = jnp.zeros((1, HEAD_WIDTH), jnp.float32)
    for k in range(p.shape[1]):
        gates = gates + jnp.where(choice[:, k : k + 1] == lanes, shares[:, k : k + 1], 0.0)
    rest = jnp.zeros((MESSAGE[0] - GATE_ROW - 1, HEAD_WIDTH), jnp.float32)
    out[0] = jnp.concatenate([q, fresh, gates, rest], axis=0).astype(jnp.bfloat16)


def encode(top, total, acc):
    lanes = iota(HEADS, 1)
    stats = jnp.zeros(HEADS, jnp.float32)
    for at, value in ((0, top), (3, total)):
        for k in range(3):
            part = value.astype(jnp.bfloat16).astype(jnp.float32)
            stats = jnp.where(lanes == at + k, part, stats)
            value = value - part
    return jnp.concatenate([acc, stats], axis=0).astype(jnp.bfloat16)


def decode(message):
    value = message.astype(jnp.float32)
    acc, stats = value[:QUERY_HEADS], value[QUERY_HEADS:]
    top = stats[:, 0:1] + stats[:, 1:2] + stats[:, 2:3]
    total = stats[:, 3:4] + stats[:, 4:5] + stats[:, 5:6]
    return top, total, acc


def merged(messages, extra=None):
    parts = [decode(message) for message in messages] + ([extra] if extra else [])
    top = functools.reduce(jnp.maximum, [part[0] for part in parts])
    total, acc = 0.0, 0.0
    for peak, amount, value in parts:
        share = jnp.exp(peak - top)
        total = total + share * amount
        acc = acc + share * value
    return top, total, acc


def attend_kernel(lengths, me, *refs, pieces, outs):
    got, cache, parts = refs[:pieces], refs[pieces], refs[pieces + 1 :]
    sequences, block, _ = cache.shape
    held = got[0].shape[0]
    rows = 2 * QUERY_HEADS
    first_group = (iota((rows, HEAD_WIDTH), 0) % QUERY_HEADS) < GROUPED
    positions = me[0] * block + iota((rows, block), 1)
    for u in range(sequences):
        s = lax.shift_right_logical(me[0], 1) ^ u
        source, at = got[2 * u // held], 2 * u % held
        both = jnp.concatenate([source[at, :QUERY_HEADS], source[at + 1, :QUERY_HEADS]], axis=0)
        zero = jnp.zeros_like(both)
        wide = jnp.concatenate(
            [jnp.where(first_group, both, zero), jnp.where(first_group, zero, both)], axis=1
        )
        keys = cache[s, :, :KEY_VALUE_WIDTH]
        values = cache[s, :, KEY_VALUE_WIDTH:]
        scores = (
            lax.dot_general(
                wide, keys, (((1,), (1,)), ((), ())), preferred_element_type=jnp.float32
            )
            * INV_ROOT
        )
        valid = positions < lengths[s]
        scores = jnp.where(valid, scores, floor_score)
        top = jnp.max(scores, axis=1, keepdims=True)
        weights = jnp.where(valid, jnp.exp(scores - top), 0.0).astype(jnp.bfloat16)
        total = jnp.sum(weights.astype(jnp.float32), axis=1, keepdims=True)
        acc = jnp.dot(weights, values, preferred_element_type=jnp.float32)
        acc = jnp.where(first_group, acc[:, :HEAD_WIDTH], acc[:, HEAD_WIDTH:])
        for p in range(2):
            cut = slice(p * QUERY_HEADS, (p + 1) * QUERY_HEADS)
            slot = 2 * u + p
            parts[slot % outs][slot // outs] = encode(top[cut], total[cut], acc[cut])


def merge_kernel(*refs, pieces, outs):
    got, parts = refs[:pieces], refs[pieces:]
    for slot in range(got[0].shape[0]):
        parts[slot % outs][slot // outs] = encode(*merged([ref[slot] for ref in got]))


def token_kernel(me, own, partner, resid, scale, *refs, pieces):
    got, (hidden_out, normed_out) = refs[:pieces], refs[pieces:]
    first_group = iota(HEADS, 0) < GROUPED

    def by_head(rows, at):
        return jnp.where(first_group, rows[at : at + 1], rows[at + 1 : at + 2])

    mine = own[0].astype(jnp.float32)
    other = partner[0].astype(jnp.float32)
    q = mine[:QUERY_HEADS]
    mine, other = mine[NEW_ROW:GATE_ROW], other[NEW_ROW:GATE_ROW]
    second = me[0] % 2 == 1
    own_score = jnp.sum(q * by_head(mine, 0), axis=1, keepdims=True) * INV_ROOT
    other_score = jnp.sum(q * by_head(other, 0), axis=1, keepdims=True) * INV_ROOT
    other_score = jnp.where(second, other_score, floor_score)
    new_max = jnp.maximum(own_score, other_score)
    own_weight = jnp.exp(own_score - new_max).astype(jnp.bfloat16).astype(jnp.float32)
    other_weight = jnp.where(second, jnp.exp(other_score - new_max), 0.0)
    other_weight = other_weight.astype(jnp.bfloat16).astype(jnp.float32)
    new_acc = own_weight * by_head(mine, 2) + other_weight * by_head(other, 2)
    _, total, acc = merged(
        [ref[0] for ref in got], (new_max, own_weight + other_weight, new_acc)
    )
    hidden = as_rows(resid[...].astype(jnp.float32), QUERY_HEADS) + acc / total
    squares = jnp.sum(jnp.sum(hidden * hidden, axis=1, keepdims=True), axis=0, keepdims=True)
    normed = hidden * lax.rsqrt(squares / WIDTH + epsilon) * scale[...]
    hidden_out[...] = hidden
    normed_out[0] = normed.astype(jnp.bfloat16)


def dot_pair(value, factor, contract):
    high = value.astype(jnp.bfloat16)
    low = (value - high.astype(jnp.float32)).astype(jnp.bfloat16)
    both = lax.dot_general(
        jnp.concatenate([high, low], axis=0),
        factor,
        (((1,), (contract,)), ((), ())),
        preferred_element_type=jnp.float32,
    )
    return both[: value.shape[0]] + both[value.shape[0] :]


def expert_kernel(me, gate_w, up_w, down_w, model, inner, *refs, pieces, outs):
    got, routes, parts = refs[:pieces], refs[pieces : 2 * pieces], refs[2 * pieces :]
    x = jnp.concatenate([ref[...].astype(jnp.float32) for ref in got], axis=0)
    tokens = x.shape[0]
    x = x.reshape(tokens, WIDTH).astype(jnp.bfloat16)
    r = ADAPTER_RANK
    mixed = lax.dot_general(
        x, model[: 2 * r], (((1,), (1,)), ((), ())), preferred_element_type=jnp.float32
    )
    gate = jnp.dot(x, gate_w[...], preferred_element_type=jnp.float32)
    gate = gate + dot_pair(mixed[:, :r], inner[:, :r], 1)
    up = jnp.dot(x, up_w[...], preferred_element_type=jnp.float32)
    up = up + dot_pair(mixed[:, r:], inner[:, r : 2 * r], 1)
    act = (gate / (1.0 + jnp.exp(-gate)) * up).astype(jnp.bfloat16)
    lowered = jnp.dot(act, inner[:, 2 * r : 3 * r], preferred_element_type=jnp.float32)
    result = jnp.dot(act, down_w[...], preferred_element_type=jnp.float32)
    result = result + dot_pair(lowered, model[2 * r :], 0)
    lanes = iota((1, HEAD_WIDTH), 1)
    for slot in range(tokens):
        held = routes[0].shape[0]
        route = routes[slot // held][slot % held][QUERY_HEADS:].astype(jnp.float32)
        route = route[GATE_ROW - QUERY_HEADS : GATE_ROW - QUERY_HEADS + 1]
        share = jnp.sum(jnp.where(lanes == me[0], route, 0.0), axis=1, keepdims=True)
        line = as_rows(result[slot : slot + 1] * share, QUERY_HEADS)
        parts[slot % outs][slot // outs] = line.astype(jnp.bfloat16)


def add_kernel(*refs, pieces, outs):
    got, parts = refs[:pieces], refs[pieces:]
    for slot in range(got[0].shape[0]):
        total = sum(ref[slot].astype(jnp.float32) for ref in got)
        parts[slot % outs][slot // outs] = total.astype(jnp.bfloat16)


def finish_kernel(hidden, *refs):
    got, out = refs[:-1], refs[-1]
    total = hidden[...] + sum(ref[0].astype(jnp.float32) for ref in got)
    line = jnp.concatenate([total[j : j + 1] for j in range(QUERY_HEADS)], axis=1)
    out[...] = line.astype(jnp.bfloat16)


def split_shapes(count, size, dims):
    return tuple(shape((count // size,) + dims, jnp.bfloat16) for _ in range(size))


def scatter(parts, n, kernel, dims):
    found = stages_of(n)
    for index, (stride, size) in enumerate(found):
        pieces = [parts[0]] + [swap(parts[k], n, k * stride) for k in range(1, size)]
        if index + 1 < len(found):
            outs = found[index + 1][1]
            parts = call(
                functools.partial(kernel, pieces=size, outs=outs),
                split_shapes(pieces[0].shape[0], outs, dims),
                [VMEM] * size,
                *pieces,
            )
    return pieces


def lora_pack_kernel(me, model, inner, *outs):
    ranks = model.shape[1]
    for d, out in enumerate(outs):
        at = me[0] ^ d
        out[:ranks] = model[at]
        out[ranks:, :ranks] = inner[at]
        out[ranks:, ranks:] = jnp.zeros((out.shape[0] - ranks, HEAD_WIDTH - ranks), out.dtype)


def lora_join_kernel(me, *refs):
    got, (model, inner) = refs[:-2], refs[-2:]
    ranks = model.shape[0]
    width = inner.shape[0] // len(got)
    for d, ref in enumerate(got):
        at = me[0] ^ d
        model[:, pl.ds(pl.multiple_of(at * HEAD_WIDTH, HEAD_WIDTH), HEAD_WIDTH)] = ref[:ranks]
        inner[pl.ds(pl.multiple_of(at * width, width), width)] = ref[ranks:]


def lora(adapter_model, adapter_hidden, me, n):
    total, ranks, model_width = adapter_model.shape
    inner_width = adapter_hidden.shape[2]
    inner = jnp.transpose(adapter_hidden, (0, 2, 1))
    if model_width != HEAD_WIDTH or inner_width % 16:
        model = lax.all_to_all(adapter_model, "exp", split_axis=0, concat_axis=2, tiled=True)
        inner = lax.all_to_all(inner, "exp", split_axis=0, concat_axis=1, tiled=True)
        return model[0], inner[0]
    packed = call(
        lora_pack_kernel,
        (shape((ranks + inner_width, HEAD_WIDTH), jnp.bfloat16),) * total,
        [SMEM, VMEM, VMEM],
        me,
        adapter_model,
        inner,
    )
    got = [packed[0]] + [swap(packed[d], n, d) for d in range(1, n)]
    return call(
        lora_join_kernel,
        (
            shape((ranks, n * model_width), jnp.bfloat16),
            shape((n * inner_width, HEAD_WIDTH), jnp.bfloat16),
        ),
        [SMEM] + [VMEM] * n,
        me,
        *got,
    )


def body(
    resid,
    queries,
    incoming_key_value,
    key_value_cache,
    lengths,
    norm_scale_vector,
    expert_choice,
    router_probability,
    gate_weight,
    up_weight,
    down_weight,
    adapter_model,
    adapter_hidden,
):
    n = lax.axis_size("exp")
    me = lax.axis_index("exp").astype(jnp.int32).reshape(1)
    first = stages_of(n)[0][1]

    message = call(
        pack_kernel,
        shape((1,) + MESSAGE, jnp.bfloat16),
        [VMEM] * 4,
        queries,
        incoming_key_value,
        expert_choice,
        router_probability,
    )
    partner = None
    pieces = gather(message, n)
    partner = swap(message, n, 1)
    parts = call(
        functools.partial(attend_kernel, pieces=len(pieces), outs=first),
        split_shapes(n, first, MESSAGE),
        [SMEM, SMEM] + [VMEM] * (len(pieces) + 1),
        lengths,
        me,
        *pieces,
        key_value_cache,
    )
    got = scatter(parts, n, merge_kernel, MESSAGE)
    hidden, normed = call(
        functools.partial(token_kernel, pieces=len(got)),
        (shape(HEADS, jnp.float32), shape((1,) + HEADS, jnp.bfloat16)),
        [SMEM] + [VMEM] * (4 + len(got)),
        me,
        message,
        partner,
        resid,
        norm_scale_vector.reshape(HEADS),
        *got,
    )
    rows = gather(normed, n)
    model, inner = lora(adapter_model, adapter_hidden, me, n)
    outs = call(
        functools.partial(expert_kernel, pieces=len(rows), outs=first),
        split_shapes(n, first, HEADS),
        [SMEM] + [VMEM] * (5 + 2 * len(rows)),
        me,
        gate_weight[0],
        up_weight[0],
        down_weight[0],
        model,
        inner,
        *rows,
        *pieces,
        limit=32,
    )
    return call(
        finish_kernel,
        shape((1, WIDTH), jnp.bfloat16),
        [VMEM] * (1 + len(got)),
        hidden,
        *scatter(outs, n, add_kernel, HEADS),
    )


def solution(mesh):
    return jax.shard_map(
        body,
        mesh=mesh,
        in_specs=(
            P(("grp", "exp"), None),
            P(("grp", "exp"), None),
            P(("grp", "exp"), None),
            P("grp", "exp", None),
            P("grp"),
            P(),
            P(("grp", "exp"), None),
            P(("grp", "exp"), None),
            P("exp", None, None),
            P("exp", None, None),
            P("exp", None, None),
            P(None, None, "exp"),
            P(None, None, "exp"),
        ),
        out_specs=P(("grp", "exp"), None),
        check_vma=False,
    )
```

time: 86.4 us -> 82 us (0.949)
  blocking collectives: 36.3 us -> 0 us
  starting transfers between devices: 12.8 us -> 46 us
  local copies, waits for them, and re-layouts: 9.19 us -> 12.1 us
  other arithmetic: 2.31 us -> 0 us
  Pallas kernels: 8.79 us -> 7.08 us
    ppermute x1 -> x39, starting transfers between devices: 0.29 us -> 46 us  [swap(): return lax.ppermute(value, 'exp', [(t, t ^ distance) for t in range(n)])]
    all_to_all x3 -> x0, blocking collectives: 36.3 us -> none  [exchange(): return lax.all_to_all(parts, 'exp', split_axis=0, concat_axis=0, tiled=True)]
    ppermute x1 -> x39, waiting for transfers between devices: 0.18 us -> 16.3 us  [swap(): return lax.ppermute(value, 'exp', [(t, t ^ distance) for t in range(n)])]
    all_to_all x3 -> x0, waiting for transfers between devices: 16 us -> none  [the longest x1 7.85 us: body(): lax.all_to_all(adapter_model, 'exp', split_axis=0, concat_axis=2, tiled=T...]
    all_to_all x3 -> x0, starting transfers between devices: 12.5 us -> none  [the longest x1 4.22 us: body(): lax.all_to_all(adapter_model, 'exp', split_axis=0, concat_axis=2, tiled=T...]
    unnamed x16 -> x26, local copies, waits for them, and re-layouts: 5.69 us -> 12.1 us
    unnamed x3 -> x0, other arithmetic: 2.31 us -> none
    pallas_call x4 -> x11, Pallas kernels: 8.79 us -> 7.08 us  [call(): pl.pallas_call(kernel, out_shape=shapes, in_specs=specs, out_specs=jax.tr...]
  transfers between devices with their start and end apart: 4 -> 39, of which waited for: 4 -> 12; matrix products, arithmetic and copies ran while one was open for 5% -> 0% of each run, Pallas kernels for 4% -> 4%
where the time goes in v2:
time: 82 us; the launch traced here: 81.7 us
  starting transfers between devices  46 us (56%)
  waiting for transfers between devices  16.3 us (20%)
  local copies, waits for them, and re-layouts  12.1 us (15%)
  Pallas kernels  7.08 us (9%)
    ppermute x39, starting transfers between devices, swap(): return lax.ppermute(value, 'exp', [(t, t ^ distance) for t in range(n)])  46 us
    ppermute x39, waiting for transfers between devices, swap(): return lax.ppermute(value, 'exp', [(t, t ^ distance) for t in range(n)])  16.3 us
    unnamed x26, local copies, waits for them, and re-layouts  12.1 us
    pallas_call x11, Pallas kernels, call(): pl.pallas_call(kernel, out_shape=shapes, in_specs=specs, out_specs=jax.tr...  7.08 us
  transfers between devices with their start and end apart: 39, of which 12 were waited for; matrix products, arithmetic and copies ran while one was open for 0% of the time, Pallas kernels for 4%

profile of v2, /device:TPU:0, one launch (start us, length us, event | category | flops | bytes accessed | tf_op | source)
XLA Modules:
  0.0 81.7 jit_solution(12453311697312290194)
XLA Ops:
  0.0 0.8 %copy-done.6 = bf16[1,2048]{1,0:T(2,128)(2,1)S(1)} copy-done((bf16[1,2048]{1,0:T(2,128)(2,1)S(1)}, bf16[1,2048]{1,0:T(2,128)(2,1)}, u32[]{:S(2)}) %copy-start.6) | copy-done | bytes 4120
  0.9 0.8 copy-done.9
  1.6 0.7 copy-done.11
  2.3 0.7 copy-done.12
  3.7 2.6 %collective-permute-start.1 = (bf16[1,32,128]{2,1,0:T(8,128)(2,1)S(1)}, bf16[1,32,128]{2,1,0:T(8,128)(2,1)S(1)}, u32[]{:S(2)}, u32[]{:S(2)}) collective-permute-start(bf16[1,32,128]{2,1,0:T(8,128)(2,1)S(1)} %shard_map.127.refs_0_.own), channel_id=1, source_target_pairs={{0,2},{1,3},{2,0},{3,1},{4,6},{5,7},{6,4},{7,5},{8,10},{9,11},{10,... | collective-permute-start | bytes 24584 | tf_op jit(solution)/shard_map/ppermute | solution.py:61
  6.3 1.6 %collective-permute-done.1.refs_2_ = bf16[1,32,128]{2,1,0:T(8,128)(2,1)S(1)} collective-permute-done((bf16[1,32,128]{2,1,0:T(8,128)(2,1)S(1)}, bf16[1,32,128]{2,1,0:T(8,128)(2,1)S(1)}, u32[]{:S(2)}, u32[]{:S(2)}) %collective-permute-start.1) | collective-permute-done | bytes 8224 | tf_op jit(solution)/shard_map/ppermute | solution.py:61
  7.9 1.4 %collective-permute-done.2.refs_3_ = bf16[1,32,128]{2,1,0:T(8,128)(2,1)S(1)} collective-permute-done((bf16[1,32,128]{2,1,0:T(8,128)(2,1)S(1)}, bf16[1,32,128]{2,1,0:T(8,128)(2,1)S(1)}, u32[]{:S(2)}, u32[]{:S(2)}) %collective-permute-start.2) | collective-permute-done | bytes 8224 | tf_op jit(solution)/shard_map/ppermute | solution.py:61
  9.3 1.6 %collective-permute-start.3 = (bf16[4,32,128]{2,1,0:T(8,128)(2,1)S(1)}, bf16[4,32,128]{2,1,0:T(8,128)(2,1)S(1)}, u32[]{:S(2)}, u32[]{:S(2)}) collective-permute-start(bf16[4,32,128]{2,1,0:T(8,128)(2,1)S(1)} %shard_map.128.refs_0_.refs_4_), channel_id=1, source_target_pairs={{0,4},{1,5},{2,6},{3,7},{4,0},{5,1},{6,2},{7,3},{8,12},{9,13},{10,... | collective-permute-start | bytes 98312 | tf_op jit(solution)/shard_map/ppermute | solution.py:61
  10.9 2.6 %collective-permute-start.4 = (bf16[4,32,128]{2,1,0:T(8,128)(2,1)S(1)}, bf16[4,32,128]{2,1,0:T(8,128)(2,1)S(1)}, u32[]{:S(2)}, u32[]{:S(2)}) collective-permute-start(bf16[4,32,128]{2,1,0:T(8,128)(2,1)S(1)} %shard_map.128.refs_0_.refs_4_), channel_id=1, source_target_pairs={{0,8},{1,9},{2,10},{3,11},{4,12},{5,13},{6,14},{7,15},{8,0},{9,1},... | collective-permute-start | bytes 98312 | tf_op jit(solution)/shard_map/ppermute | solution.py:61
  13.7 1.0 %copy-done.4 = bf16[16,96,128]{2,1,0:T(8,128)(2,1)S(1)} copy-done((bf16[16,96,128]{2,1,0:T(8,128)(2,1)S(1)}, bf16[16,96,128]{2,1,0:T(8,128)(2,1)}, u32[]{:S(2)}) %copy-start.4) | copy-done | bytes 393240
  14.7 0.9 %copy-done.5 = bf16[16,96,48]{1,2,0:T(8,128)(2,1)S(1)} copy-done((bf16[16,96,48]{1,2,0:T(8,128)(2,1)S(1)}, bf16[16,96,48]{1,2,0:T(8,128)(2,1)}, u32[]{:S(2)}) %copy-start.5) | copy-done | bytes 147480
  15.8 0.6 collective-permute-start.13
  16.5 1.2 %collective-permute-start.14 = (bf16[144,128]{1,0:T(8,128)(2,1)S(1)}, bf16[144,128]{1,0:T(8,128)(2,1)S(1)}, u32[]{:S(2)}, u32[]{:S(2)}) collective-permute-start(bf16[144,128]{1,0:T(8,128)(2,1)S(1)} %get-tuple-element.53), channel_id=1, source_target_pairs={{0,3},{1,2},{2,1},{3,0},{4,7},{5,6},{6,5},{7,4},{8,11},{9,10},{10,... | collective-permute-start | bytes 110600 | tf_op jit(solution)/shard_map/ppermute | solution.py:61
  17.7 0.7 collective-permute-start.15
  18.4 0.9 %collective-permute-done.5.refs_3_.refs_7_ = bf16[4,32,128]{2,1,0:T(8,128)(2,1)S(1)} collective-permute-done((bf16[4,32,128]{2,1,0:T(8,128)(2,1)S(1)}, bf16[4,32,128]{2,1,0:T(8,128)(2,1)S(1)}, u32[]{:S(2)}, u32[]{:S(2)}) %collective-permute-start.5) | collective-permute-done | bytes 32800 | tf_op jit(solution)/shard_map/ppermute | solution.py:61
  19.4 1.4 %copy-done.3 = bf16[8,192,512]{2,1,0:T(8,128)(2,1)S(1)} copy-done((bf16[8,192,512]{2,1,0:T(8,128)(2,1)S(1)}, bf16[8,192,512]{2,1,0:T(8,128)(2,1)}, u32[]{:S(2)}) %copy-start.3) | copy-done | bytes 1572888
  20.8 0.7 copy-done.10
  21.4 2.7 %shard_map.129 = (bf16[4,32,128]{2,1,0:T(8,128)(2,1)S(1)}, bf16[4,32,128]{2,1,0:T(8,128)(2,1)S(1)}, bf16[4,32,128]{2,1,0:T(8,128)(2,1)S(1)}, bf16[4,32,128]{2,1,0:T(8,128)(2,1)S(1)}) custom-call(s32[8]{0:T(128)S(1)} %copy-done.10, s32[1]{0:T(128)} %bitcast.me, bf16[4,32,128]{2,1,0:T(8,128)(2,1)S(1)} %shard_map.128.refs_0_.refs_4_, ...), custom_call_target="tpu_custom_call" | custom-call | tf_op jit(solution)/shard_map/pallas_call | solution.py:32
  25.2 0.9 %collective-permute-start.8 = (bf16[4,32,128]{2,1,0:T(8,128)(2,1)S(1)}, bf16[4,32,128]{2,1,0:T(8,128)(2,1)S(1)}, u32[]{:S(2)}, u32[]{:S(2)}) collective-permute-start(bf16[4,32,128]{2,1,0:T(8,128)(2,1)S(1)} %get-tuple-element.44), channel_id=1, source_target_pairs={{0,3},{1,2},{2,1},{3,0},{4,7},{5,6},{6,5},{7,4},{8,11},{9,10},{10,... | collective-permute-start | bytes 98312 | tf_op jit(solution)/shard_map/ppermute | solution.py:61
  26.1 1.6 %collective-permute-start.17 = (bf16[144,128]{1,0:T(8,128)(2,1)S(1)}, bf16[144,128]{1,0:T(8,128)(2,1)S(1)}, u32[]{:S(2)}, u32[]{:S(2)}) collective-permute-start(bf16[144,128]{1,0:T(8,128)(2,1)S(1)} %get-tuple-element.56), channel_id=1, source_target_pairs={{0,6},{1,7},{2,4},{3,5},{4,2},{5,3},{6,0},{7,1},{8,14},{9,15},{10,... | collective-permute-start | bytes 110600 | tf_op jit(solution)/shard_map/ppermute | solution.py:61
  27.7 1.4 %collective-permute-start.18 = (bf16[144,128]{1,0:T(8,128)(2,1)S(1)}, bf16[144,128]{1,0:T(8,128)(2,1)S(1)}, u32[]{:S(2)}, u32[]{:S(2)}) collective-permute-start(bf16[144,128]{1,0:T(8,128)(2,1)S(1)} %get-tuple-element.57), channel_id=1, source_target_pairs={{0,7},{1,6},{2,5},{3,4},{4,3},{5,2},{6,1},{7,0},{8,15},{9,14},{10,... | collective-permute-start | bytes 110600 | tf_op jit(solution)/shard_map/ppermute | solution.py:61
  29.1 2.2 %collective-permute-start.19 = (bf16[144,128]{1,0:T(8,128)(2,1)S(1)}, bf16[144,128]{1,0:T(8,128)(2,1)S(1)}, u32[]{:S(2)}, u32[]{:S(2)}) collective-permute-start(bf16[144,128]{1,0:T(8,128)(2,1)S(1)} %get-tuple-element.58), channel_id=1, source_target_pairs={{0,8},{1,9},{2,10},{3,11},{4,12},{5,13},{6,14},{7,15},{8,0},{9,1},... | collective-permute-start | bytes 110600 | tf_op jit(solution)/shard_map/ppermute | solution.py:61
  31.4 2.5 %collective-permute-start.21 = (bf16[144,128]{1,0:T(8,128)(2,1)S(1)}, bf16[144,128]{1,0:T(8,128)(2,1)S(1)}, u32[]{:S(2)}, u32[]{:S(2)}) collective-permute-start(bf16[144,128]{1,0:T(8,128)(2,1)S(1)} %get-tuple-element.60), channel_id=1, source_target_pairs={{0,10},{1,11},{2,8},{3,9},{4,14},{5,15},{6,12},{7,13},{8,2},{9,3},... | collective-permute-start | bytes 110600 | tf_op jit(solution)/shard_map/ppermute | solution.py:61
  34.2 0.7 collective-permute-start.10
  35.0 3.5 %collective-permute-start.11 = (bf16[1,32,128]{2,1,0:T(8,128)(2,1)S(1)}, bf16[1,32,128]{2,1,0:T(8,128)(2,1)S(1)}, u32[]{:S(2)}, u32[]{:S(2)}) collective-permute-start(bf16[1,32,128]{2,1,0:T(8,128)(2,1)S(1)} %get-tuple-element.48), channel_id=1, source_target_pairs={{0,12},{1,13},{2,14},{3,15},{4,8},{5,9},{6,10},{7,11},{8,4},{9,5},... | collective-permute-start | bytes 24584 | tf_op jit(solution)/shard_map/ppermute | solution.py:61
  38.8 0.6 collective-permute-start.22
  39.4 1.0 %collective-permute-done.11.refs_3_ = bf16[1,32,128]{2,1,0:T(8,128)(2,1)S(1)} collective-permute-done((bf16[1,32,128]{2,1,0:T(8,128)(2,1)S(1)}, bf16[1,32,128]{2,1,0:T(8,128)(2,1)S(1)}, u32[]{:S(2)}, u32[]{:S(2)}) %collective-permute-start.11) | collective-permute-done | bytes 8224 | tf_op jit(solution)/shard_map/ppermute | solution.py:61
  40.4 3.5 %collective-permute-start.23 = (bf16[144,128]{1,0:T(8,128)(2,1)S(1)}, bf16[144,128]{1,0:T(8,128)(2,1)S(1)}, u32[]{:S(2)}, u32[]{:S(2)}) collective-permute-start(bf16[144,128]{1,0:T(8,128)(2,1)S(1)} %get-tuple-element.62), channel_id=1, source_target_pairs={{0,12},{1,13},{2,14},{3,15},{4,8},{5,9},{6,10},{7,11},{8,4},{9,5},... | collective-permute-start | bytes 110600 | tf_op jit(solution)/shard_map/ppermute | solution.py:61
  43.9 0.7 copy-done.7
  44.6 0.7 copy-done.8
  46.1 1.2 %collective-permute-start.28 = (bf16[1,16,128]{2,1,0:T(8,128)(2,1)S(1)}, bf16[1,16,128]{2,1,0:T(8,128)(2,1)S(1)}, u32[]{:S(2)}, u32[]{:S(2)}) collective-permute-start(bf16[1,16,128]{2,1,0:T(8,128)(2,1)S(1)} %get-tuple-element.68.refs_0_), channel_id=1, source_target_pairs={{0,2},{1,3},{2,0},{3,1},{4,6},{5,7},{6,4},{7,5},{8,10},{9,11},{10,... | collective-permute-start | bytes 12296 | tf_op jit(solution)/shard_map/ppermute | solution.py:61
  47.4 0.8 collective-permute-start.29
  48.1 1.6 %collective-permute-done.28.refs_2_ = bf16[1,16,128]{2,1,0:T(8,128)(2,1)S(1)} collective-permute-done((bf16[1,16,128]{2,1,0:T(8,128)(2,1)S(1)}, bf16[1,16,128]{2,1,0:T(8,128)(2,1)S(1)}, u32[]{:S(2)}, u32[]{:S(2)}) %collective-permute-start.28) | collective-permute-done | bytes 4128 | tf_op jit(solution)/shard_map/ppermute | solution.py:61
  49.7 4.2 %collective-permute-start.25 = (bf16[144,128]{1,0:T(8,128)(2,1)S(1)}, bf16[144,128]{1,0:T(8,128)(2,1)S(1)}, u32[]{:S(2)}, u32[]{:S(2)}) collective-permute-start(bf16[144,128]{1,0:T(8,128)(2,1)S(1)} %get-tuple-element.64), channel_id=1, source_target_pairs={{0,14},{1,15},{2,12},{3,13},{4,10},{5,11},{6,8},{7,9},{8,6},{9,7},... | collective-permute-start | bytes 110600 | tf_op jit(solution)/shard_map/ppermute | solution.py:61
  54.2 2.6 %collective-permute-start.31 = (bf16[4,16,128]{2,1,0:T(8,128)(2,1)S(1)}, bf16[4,16,128]{2,1,0:T(8,128)(2,1)S(1)}, u32[]{:S(2)}, u32[]{:S(2)}) collective-permute-start(bf16[4,16,128]{2,1,0:T(8,128)(2,1)S(1)} %shard_map.134.refs_0_), channel_id=1, source_target_pairs={{0,8},{1,9},{2,10},{3,11},{4,12},{5,13},{6,14},{7,15},{8,0},{9,1},... | collective-permute-start | bytes 49160 | tf_op jit(solution)/shard_map/ppermute | solution.py:61
  56.8 1.8 %collective-permute-start.32 = (bf16[4,16,128]{2,1,0:T(8,128)(2,1)S(1)}, bf16[4,16,128]{2,1,0:T(8,128)(2,1)S(1)}, u32[]{:S(2)}, u32[]{:S(2)}) collective-permute-start(bf16[4,16,128]{2,1,0:T(8,128)(2,1)S(1)} %shard_map.134.refs_0_), channel_id=1, source_target_pairs={{0,12},{1,13},{2,14},{3,15},{4,8},{5,9},{6,10},{7,11},{8,4},{9,5},... | collective-permute-start | bytes 49160 | tf_op jit(solution)/shard_map/ppermute | solution.py:61
  58.6 1.5 %collective-permute-done.26.refs_15_ = bf16[144,128]{1,0:T(8,128)(2,1)S(1)} collective-permute-done((bf16[144,128]{1,0:T(8,128)(2,1)S(1)}, bf16[144,128]{1,0:T(8,128)(2,1)S(1)}, u32[]{:S(2)}, u32[]{:S(2)}) %collective-permute-start.26) | collective-permute-done | bytes 36896 | tf_op jit(solution)/shard_map/ppermute | solution.py:61
  60.2 2.1 %collective-permute-done.32.refs_3_ = bf16[4,16,128]{2,1,0:T(8,128)(2,1)S(1)} collective-permute-done((bf16[4,16,128]{2,1,0:T(8,128)(2,1)S(1)}, bf16[4,16,128]{2,1,0:T(8,128)(2,1)S(1)}, u32[]{:S(2)}, u32[]{:S(2)}) %collective-permute-start.32) | collective-permute-done | bytes 16416 | tf_op jit(solution)/shard_map/ppermute | solution.py:61
  62.3 1.9 %copy-done.1 = bf16[1,2048,768]{2,1,0:T(8,128)(2,1)S(1)} copy-done((bf16[1,2048,768]{2,1,0:T(8,128)(2,1)S(1)}, bf16[1,2048,768]{2,1,0:T(8,128)(2,1)}, u32[]{:S(2)}) %copy-start.1) | copy-done | bytes 3145752
  64.2 1.9 %copy-done.2 = bf16[1,768,2048]{2,1,0:T(8,128)(2,1)S(1)} copy-done((bf16[1,768,2048]{2,1,0:T(8,128)(2,1)S(1)}, bf16[1,768,2048]{2,1,0:T(8,128)(2,1)}, u32[]{:S(2)}) %copy-start.2) | copy-done | bytes 3145752
  66.1 2.8 %shard_map.135 = (bf16[4,16,128]{2,1,0:T(8,128)(2,1)S(1)}, bf16[4,16,128]{2,1,0:T(8,128)(2,1)S(1)}, bf16[4,16,128]{2,1,0:T(8,128)(2,1)S(1)}, bf16[4,16,128]{2,1,0:T(8,128)(2,1)S(1)}) custom-call(s32[1]{0:T(128)} %bitcast.me, bf16[2048,768]{1,0:T(8,128)(2,1)S(1)} %bitcast.6, bf16[2048,768]{1,0:T(8,128)(2,1)S(1)} %bitcast.7, bf16[768,2048]{1,0:T(8,128)(2,1)S(1)} %bitcast.8, ...), custom_call_target="tpu_custom_call" | custom-call | tf_op jit(solution)/shard_map/pallas_call | solution.py:32
  69.1 1.4 %collective-permute-start.34 = (bf16[4,16,128]{2,1,0:T(8,128)(2,1)S(1)}, bf16[4,16,128]{2,1,0:T(8,128)(2,1)S(1)}, u32[]{:S(2)}, u32[]{:S(2)}) collective-permute-start(bf16[4,16,128]{2,1,0:T(8,128)(2,1)S(1)} %get-tuple-element.71), channel_id=1, source_target_pairs={{0,2},{1,3},{2,0},{3,1},{4,6},{5,7},{6,4},{7,5},{8,10},{9,11},{10,... | collective-permute-start | bytes 49160 | tf_op jit(solution)/shard_map/ppermute | solution.py:61
  70.8 2.0 %collective-permute-done.34.refs_2_ = bf16[4,16,128]{2,1,0:T(8,128)(2,1)S(1)} collective-permute-done((bf16[4,16,128]{2,1,0:T(8,128)(2,1)S(1)}, bf16[4,16,128]{2,1,0:T(8,128)(2,1)S(1)}, u32[]{:S(2)}, u32[]{:S(2)}) %collective-permute-start.34) | collective-permute-done | bytes 16416 | tf_op jit(solution)/shard_map/ppermute | solution.py:61
  72.8 0.8 collective-permute-done.35.refs_3_
  73.7 1.9 %collective-permute-start.37 = (bf16[1,16,128]{2,1,0:T(8,128)(2,1)S(1)}, bf16[1,16,128]{2,1,0:T(8,128)(2,1)S(1)}, u32[]{:S(2)}, u32[]{:S(2)}) collective-permute-start(bf16[1,16,128]{2,1,0:T(8,128)(2,1)S(1)} %get-tuple-element.75), channel_id=1, source_target_pairs={{0,8},{1,9},{2,10},{3,11},{4,12},{5,13},{6,14},{7,15},{8,0},{9,1},... | collective-permute-start | bytes 12296 | tf_op jit(solution)/shard_map/ppermute | solution.py:61
  75.6 2.4 %collective-permute-start.38 = (bf16[1,16,128]{2,1,0:T(8,128)(2,1)S(1)}, bf16[1,16,128]{2,1,0:T(8,128)(2,1)S(1)}, u32[]{:S(2)}, u32[]{:S(2)}) collective-permute-start(bf16[1,16,128]{2,1,0:T(8,128)(2,1)S(1)} %get-tuple-element.76), channel_id=1, source_target_pairs={{0,12},{1,13},{2,14},{3,15},{4,8},{5,9},{6,10},{7,11},{8,4},{9,5},... | collective-permute-start | bytes 12296 | tf_op jit(solution)/shard_map/ppermute | solution.py:61
  78.3 2.8 %collective-permute-done.38.refs_3_ = bf16[1,16,128]{2,1,0:T(8,128)(2,1)S(1)} collective-permute-done((bf16[1,16,128]{2,1,0:T(8,128)(2,1)S(1)}, bf16[1,16,128]{2,1,0:T(8,128)(2,1)S(1)}, u32[]{:S(2)}, u32[]{:S(2)}) %collective-permute-start.38) | collective-permute-done | bytes 4128 | tf_op jit(solution)/shard_map/ppermute | solution.py:61
  81.0 0.6 shard_map.137
  (67 shorter events, 5.3 us)
Async XLA Ops:
  0.0 62.3 %copy-start = (bf16[1,2048,768]{2,1,0:T(8,128)(2,1)S(1)}, bf16[1,2048,768]{2,1,0:T(8,128)(2,1)}, u32[]{:S(2)}) copy-start(bf16[1,2048,768]{2,1,0:T(8,128)(2,1)} %param.21) | copy-start | bytes 9437188
  0.0 0.8 %copy-start.6 = (bf16[1,2048]{1,0:T(2,128)(2,1)S(1)}, bf16[1,2048]{1,0:T(2,128)(2,1)}, u32[]{:S(2)}) copy-start(bf16[1,2048]{1,0:T(2,128)(2,1)} %query.1) | copy-start | bytes 12292
  0.8 0.8 copy-start.9
  3.1 3.2 %collective-permute-start = (bf16[1,32,128]{2,1,0:T(8,128)(2,1)S(1)}, bf16[1,32,128]{2,1,0:T(8,128)(2,1)S(1)}, u32[]{:S(2)}, u32[]{:S(2)}) collective-permute-start(bf16[1,32,128]{2,1,0:T(8,128)(2,1)S(1)} %shard_map.127.refs_0_.own), channel_id=1, source_target_pairs={{0,1},{1,0},{2,3},{3,2},{4,5},{5,4},{6,7},{7,6},{8,9},{9,8},{10,11... | collective-permute-start | bytes 24584 | tf_op jit(solution)/shard_map/ppermute | solution.py:61
  3.7 4.2 %collective-permute-start.1 = (bf16[1,32,128]{2,1,0:T(8,128)(2,1)S(1)}, bf16[1,32,128]{2,1,0:T(8,128)(2,1)S(1)}, u32[]{:S(2)}, u32[]{:S(2)}) collective-permute-start(bf16[1,32,128]{2,1,0:T(8,128)(2,1)S(1)} %shard_map.127.refs_0_.own), channel_id=1, source_target_pairs={{0,2},{1,3},{2,0},{3,1},{4,6},{5,7},{6,4},{7,5},{8,10},{9,11},{10,... | collective-permute-start | bytes 24584 | tf_op jit(solution)/shard_map/ppermute | solution.py:61
  6.3 3.1 %collective-permute-start.2 = (bf16[1,32,128]{2,1,0:T(8,128)(2,1)S(1)}, bf16[1,32,128]{2,1,0:T(8,128)(2,1)S(1)}, u32[]{:S(2)}, u32[]{:S(2)}) collective-permute-start(bf16[1,32,128]{2,1,0:T(8,128)(2,1)S(1)} %shard_map.127.refs_0_.own), channel_id=1, source_target_pairs={{0,3},{1,2},{2,1},{3,0},{4,7},{5,6},{6,5},{7,4},{8,11},{9,10},{10,... | collective-permute-start | bytes 24584 | tf_op jit(solution)/shard_map/ppermute | solution.py:61
  9.3 7.1 %collective-permute-start.3 = (bf16[4,32,128]{2,1,0:T(8,128)(2,1)S(1)}, bf16[4,32,128]{2,1,0:T(8,128)(2,1)S(1)}, u32[]{:S(2)}, u32[]{:S(2)}) collective-permute-start(bf16[4,32,128]{2,1,0:T(8,128)(2,1)S(1)} %shard_map.128.refs_0_.refs_4_), channel_id=1, source_target_pairs={{0,4},{1,5},{2,6},{3,7},{4,0},{5,1},{6,2},{7,3},{8,12},{9,13},{10,... | collective-permute-start | bytes 98312 | tf_op jit(solution)/shard_map/ppermute | solution.py:61
  10.9 6.8 %collective-permute-start.4 = (bf16[4,32,128]{2,1,0:T(8,128)(2,1)S(1)}, bf16[4,32,128]{2,1,0:T(8,128)(2,1)S(1)}, u32[]{:S(2)}, u32[]{:S(2)}) collective-permute-start(bf16[4,32,128]{2,1,0:T(8,128)(2,1)S(1)} %shard_map.128.refs_0_.refs_4_), channel_id=1, source_target_pairs={{0,8},{1,9},{2,10},{3,11},{4,12},{5,13},{6,14},{7,15},{8,0},{9,1},... | collective-permute-start | bytes 98312 | tf_op jit(solution)/shard_map/ppermute | solution.py:61
  13.5 5.7 %collective-permute-start.5 = (bf16[4,32,128]{2,1,0:T(8,128)(2,1)S(1)}, bf16[4,32,128]{2,1,0:T(8,128)(2,1)S(1)}, u32[]{:S(2)}, u32[]{:S(2)}) collective-permute-start(bf16[4,32,128]{2,1,0:T(8,128)(2,1)S(1)} %shard_map.128.refs_0_.refs_4_), channel_id=1, source_target_pairs={{0,12},{1,13},{2,14},{3,15},{4,8},{5,9},{6,10},{7,11},{8,4},{9,5},... | collective-permute-start | bytes 98312 | tf_op jit(solution)/shard_map/ppermute | solution.py:61
  13.7 1.0 %copy-start.4 = (bf16[16,96,128]{2,1,0:T(8,128)(2,1)S(1)}, bf16[16,96,128]{2,1,0:T(8,128)(2,1)}, u32[]{:S(2)}) copy-start(bf16[16,96,128]{2,1,0:T(8,128)(2,1)} %model.1) | copy-start | bytes 1179652
  14.7 0.9 %copy-start.5 = (bf16[16,96,48]{1,2,0:T(8,128)(2,1)S(1)}, bf16[16,96,48]{1,2,0:T(8,128)(2,1)}, u32[]{:S(2)}) copy-start(bf16[16,96,48]{1,2,0:T(8,128)(2,1)} %param.25) | copy-start | bytes 442372
  15.7 8.4 %collective-permute-start.12 = (bf16[144,128]{1,0:T(8,128)(2,1)S(1)}, bf16[144,128]{1,0:T(8,128)(2,1)S(1)}, u32[]{:S(2)}, u32[]{:S(2)}) collective-permute-start(bf16[144,128]{1,0:T(8,128)(2,1)S(1)} %get-tuple-element.51), channel_id=1, source_target_pairs={{0,1},{1,0},{2,3},{3,2},{4,5},{5,4},{6,7},{7,6},{8,9},{9,8},{10,11... | collective-permute-start | bytes 110600 | tf_op jit(solution)/shard_map/ppermute | solution.py:61
  15.8 8.8 %collective-permute-start.13 = (bf16[144,128]{1,0:T(8,128)(2,1)S(1)}, bf16[144,128]{1,0:T(8,128)(2,1)S(1)}, u32[]{:S(2)}, u32[]{:S(2)}) collective-permute-start(bf16[144,128]{1,0:T(8,128)(2,1)S(1)} %get-tuple-element.52), channel_id=1, source_target_pairs={{0,2},{1,3},{2,0},{3,1},{4,6},{5,7},{6,4},{7,5},{8,10},{9,11},{10,... | collective-permute-start | bytes 110600 | tf_op jit(solution)/shard_map/ppermute | solution.py:61
  16.5 8.8 %collective-permute-start.14 = (bf16[144,128]{1,0:T(8,128)(2,1)S(1)}, bf16[144,128]{1,0:T(8,128)(2,1)S(1)}, u32[]{:S(2)}, u32[]{:S(2)}) collective-permute-start(bf16[144,128]{1,0:T(8,128)(2,1)S(1)} %get-tuple-element.53), channel_id=1, source_target_pairs={{0,3},{1,2},{2,1},{3,0},{4,7},{5,6},{6,5},{7,4},{8,11},{9,10},{10,... | collective-permute-start | bytes 110600 | tf_op jit(solution)/shard_map/ppermute | solution.py:61
  17.7 8.4 %collective-permute-start.15 = (bf16[144,128]{1,0:T(8,128)(2,1)S(1)}, bf16[144,128]{1,0:T(8,128)(2,1)S(1)}, u32[]{:S(2)}, u32[]{:S(2)}) collective-permute-start(bf16[144,128]{1,0:T(8,128)(2,1)S(1)} %get-tuple-element.54), channel_id=1, source_target_pairs={{0,4},{1,5},{2,6},{3,7},{4,0},{5,1},{6,2},{7,3},{8,12},{9,13},{10,... | collective-permute-start | bytes 110600 | tf_op jit(solution)/shard_map/ppermute | solution.py:61
  19.2 8.5 %collective-permute-start.16 = (bf16[144,128]{1,0:T(8,128)(2,1)S(1)}, bf16[144,128]{1,0:T(8,128)(2,1)S(1)}, u32[]{:S(2)}, u32[]{:S(2)}) collective-permute-start(bf16[144,128]{1,0:T(8,128)(2,1)S(1)} %get-tuple-element.55), channel_id=1, source_target_pairs={{0,5},{1,4},{2,7},{3,6},{4,1},{5,0},{6,3},{7,2},{8,13},{9,12},{10,... | collective-permute-start | bytes 110600 | tf_op jit(solution)/shard_map/ppermute | solution.py:61
  19.4 1.4 %copy-start.3 = (bf16[8,192,512]{2,1,0:T(8,128)(2,1)S(1)}, bf16[8,192,512]{2,1,0:T(8,128)(2,1)}, u32[]{:S(2)}) copy-start(bf16[8,192,512]{2,1,0:T(8,128)(2,1)} %refs_4_.1) | copy-start | bytes 4718596
  24.1 4.9 %collective-permute-start.6 = (bf16[4,32,128]{2,1,0:T(8,128)(2,1)S(1)}, bf16[4,32,128]{2,1,0:T(8,128)(2,1)S(1)}, u32[]{:S(2)}, u32[]{:S(2)}) collective-permute-start(bf16[4,32,128]{2,1,0:T(8,128)(2,1)S(1)} %get-tuple-element.42), channel_id=1, source_target_pairs={{0,1},{1,0},{2,3},{3,2},{4,5},{5,4},{6,7},{7,6},{8,9},{9,8},{10,11... | collective-permute-start | bytes 98312 | tf_op jit(solution)/shard_map/ppermute | solution.py:61
  24.7 6.6 %collective-permute-start.7 = (bf16[4,32,128]{2,1,0:T(8,128)(2,1)S(1)}, bf16[4,32,128]{2,1,0:T(8,128)(2,1)S(1)}, u32[]{:S(2)}, u32[]{:S(2)}) collective-permute-start(bf16[4,32,128]{2,1,0:T(8,128)(2,1)S(1)} %get-tuple-element.43), channel_id=1, source_target_pairs={{0,2},{1,3},{2,0},{3,1},{4,6},{5,7},{6,4},{7,5},{8,10},{9,11},{10,... | collective-permute-start | bytes 98312 | tf_op jit(solution)/shard_map/ppermute | solution.py:61
  25.2 6.2 %collective-permute-start.8 = (bf16[4,32,128]{2,1,0:T(8,128)(2,1)S(1)}, bf16[4,32,128]{2,1,0:T(8,128)(2,1)S(1)}, u32[]{:S(2)}, u32[]{:S(2)}) collective-permute-start(bf16[4,32,128]{2,1,0:T(8,128)(2,1)S(1)} %get-tuple-element.44), channel_id=1, source_target_pairs={{0,3},{1,2},{2,1},{3,0},{4,7},{5,6},{6,5},{7,4},{8,11},{9,10},{10,... | collective-permute-start | bytes 98312 | tf_op jit(solution)/shard_map/ppermute | solution.py:61
  26.1 8.1 %collective-permute-start.17 = (bf16[144,128]{1,0:T(8,128)(2,1)S(1)}, bf16[144,128]{1,0:T(8,128)(2,1)S(1)}, u32[]{:S(2)}, u32[]{:S(2)}) collective-permute-start(bf16[144,128]{1,0:T(8,128)(2,1)S(1)} %get-tuple-element.56), channel_id=1, source_target_pairs={{0,6},{1,7},{2,4},{3,5},{4,2},{5,3},{6,0},{7,1},{8,14},{9,15},{10,... | collective-permute-start | bytes 110600 | tf_op jit(solution)/shard_map/ppermute | solution.py:61
  27.7 7.2 %collective-permute-start.18 = (bf16[144,128]{1,0:T(8,128)(2,1)S(1)}, bf16[144,128]{1,0:T(8,128)(2,1)S(1)}, u32[]{:S(2)}, u32[]{:S(2)}) collective-permute-start(bf16[144,128]{1,0:T(8,128)(2,1)S(1)} %get-tuple-element.57), channel_id=1, source_target_pairs={{0,7},{1,6},{2,5},{3,4},{4,3},{5,2},{6,1},{7,0},{8,15},{9,14},{10,... | collective-permute-start | bytes 110600 | tf_op jit(solution)/shard_map/ppermute | solution.py:61
  29.1 9.3 %collective-permute-start.19 = (bf16[144,128]{1,0:T(8,128)(2,1)S(1)}, bf16[144,128]{1,0:T(8,128)(2,1)S(1)}, u32[]{:S(2)}, u32[]{:S(2)}) collective-permute-start(bf16[144,128]{1,0:T(8,128)(2,1)S(1)} %get-tuple-element.58), channel_id=1, source_target_pairs={{0,8},{1,9},{2,10},{3,11},{4,12},{5,13},{6,14},{7,15},{8,0},{9,1},... | collective-permute-start | bytes 110600 | tf_op jit(solution)/shard_map/ppermute | solution.py:61
  31.3 14.3 %collective-permute-start.20 = (bf16[144,128]{1,0:T(8,128)(2,1)S(1)}, bf16[144,128]{1,0:T(8,128)(2,1)S(1)}, u32[]{:S(2)}, u32[]{:S(2)}) collective-permute-start(bf16[144,128]{1,0:T(8,128)(2,1)S(1)} %get-tuple-element.59), channel_id=1, source_target_pairs={{0,9},{1,8},{2,11},{3,10},{4,13},{5,12},{6,15},{7,14},{8,1},{9,0},... | collective-permute-start | bytes 110600 | tf_op jit(solution)/shard_map/ppermute | solution.py:61
  31.4 14.7 %collective-permute-start.21 = (bf16[144,128]{1,0:T(8,128)(2,1)S(1)}, bf16[144,128]{1,0:T(8,128)(2,1)S(1)}, u32[]{:S(2)}, u32[]{:S(2)}) collective-permute-start(bf16[144,128]{1,0:T(8,128)(2,1)S(1)} %get-tuple-element.60), channel_id=1, source_target_pairs={{0,10},{1,11},{2,8},{3,9},{4,14},{5,15},{6,12},{7,13},{8,2},{9,3},... | collective-permute-start | bytes 110600 | tf_op jit(solution)/shard_map/ppermute | solution.py:61
  34.2 4.6 %collective-permute-start.10 = (bf16[1,32,128]{2,1,0:T(8,128)(2,1)S(1)}, bf16[1,32,128]{2,1,0:T(8,128)(2,1)S(1)}, u32[]{:S(2)}, u32[]{:S(2)}) collective-permute-start(bf16[1,32,128]{2,1,0:T(8,128)(2,1)S(1)} %get-tuple-element.47), channel_id=1, source_target_pairs={{0,8},{1,9},{2,10},{3,11},{4,12},{5,13},{6,14},{7,15},{8,0},{9,1},... | collective-permute-start | bytes 24584 | tf_op jit(solution)/shard_map/ppermute | solution.py:61
  35.0 5.4 %collective-permute-start.11 = (bf16[1,32,128]{2,1,0:T(8,128)(2,1)S(1)}, bf16[1,32,128]{2,1,0:T(8,128)(2,1)S(1)}, u32[]{:S(2)}, u32[]{:S(2)}) collective-permute-start(bf16[1,32,128]{2,1,0:T(8,128)(2,1)S(1)} %get-tuple-element.48), channel_id=1, source_target_pairs={{0,12},{1,13},{2,14},{3,15},{4,8},{5,9},{6,10},{7,11},{8,4},{9,5},... | collective-permute-start | bytes 24584 | tf_op jit(solution)/shard_map/ppermute | solution.py:61
  38.4 5.4 %collective-permute-start.9 = (bf16[1,32,128]{2,1,0:T(8,128)(2,1)S(1)}, bf16[1,32,128]{2,1,0:T(8,128)(2,1)S(1)}, u32[]{:S(2)}, u32[]{:S(2)}) collective-permute-start(bf16[1,32,128]{2,1,0:T(8,128)(2,1)S(1)} %get-tuple-element.46), channel_id=1, source_target_pairs={{0,4},{1,5},{2,6},{3,7},{4,0},{5,1},{6,2},{7,3},{8,12},{9,13},{10,... | collective-permute-start | bytes 24584 | tf_op jit(solution)/shard_map/ppermute | solution.py:61
  38.8 15.3 %collective-permute-start.22 = (bf16[144,128]{1,0:T(8,128)(2,1)S(1)}, bf16[144,128]{1,0:T(8,128)(2,1)S(1)}, u32[]{:S(2)}, u32[]{:S(2)}) collective-permute-start(bf16[144,128]{1,0:T(8,128)(2,1)S(1)} %get-tuple-element.61), channel_id=1, source_target_pairs={{0,11},{1,10},{2,9},{3,8},{4,15},{5,14},{6,13},{7,12},{8,3},{9,2},... | collective-permute-start | bytes 110600 | tf_op jit(solution)/shard_map/ppermute | solution.py:61
  40.4 13.8 %collective-permute-start.23 = (bf16[144,128]{1,0:T(8,128)(2,1)S(1)}, bf16[144,128]{1,0:T(8,128)(2,1)S(1)}, u32[]{:S(2)}, u32[]{:S(2)}) collective-permute-start(bf16[144,128]{1,0:T(8,128)(2,1)S(1)} %get-tuple-element.62), channel_id=1, source_target_pairs={{0,12},{1,13},{2,14},{3,15},{4,8},{5,9},{6,10},{7,11},{8,4},{9,5},... | collective-permute-start | bytes 110600 | tf_op jit(solution)/shard_map/ppermute | solution.py:61
  43.9 12.9 %collective-permute-start.24 = (bf16[144,128]{1,0:T(8,128)(2,1)S(1)}, bf16[144,128]{1,0:T(8,128)(2,1)S(1)}, u32[]{:S(2)}, u32[]{:S(2)}) collective-permute-start(bf16[144,128]{1,0:T(8,128)(2,1)S(1)} %get-tuple-element.63), channel_id=1, source_target_pairs={{0,13},{1,12},{2,15},{3,14},{4,9},{5,8},{6,11},{7,10},{8,5},{9,4},... | collective-permute-start | bytes 110600 | tf_op jit(solution)/shard_map/ppermute | solution.py:61
  43.9 0.7 copy-start.7
  45.6 1.8 %collective-permute-start.27 = (bf16[1,16,128]{2,1,0:T(8,128)(2,1)S(1)}, bf16[1,16,128]{2,1,0:T(8,128)(2,1)S(1)}, u32[]{:S(2)}, u32[]{:S(2)}) collective-permute-start(bf16[1,16,128]{2,1,0:T(8,128)(2,1)S(1)} %get-tuple-element.68.refs_0_), channel_id=1, source_target_pairs={{0,1},{1,0},{2,3},{3,2},{4,5},{5,4},{6,7},{7,6},{8,9},{9,8},{10,11... | collective-permute-start | bytes 12296 | tf_op jit(solution)/shard_map/ppermute | solution.py:61
  46.1 3.6 %collective-permute-start.28 = (bf16[1,16,128]{2,1,0:T(8,128)(2,1)S(1)}, bf16[1,16,128]{2,1,0:T(8,128)(2,1)S(1)}, u32[]{:S(2)}, u32[]{:S(2)}) collective-permute-start(bf16[1,16,128]{2,1,0:T(8,128)(2,1)S(1)} %get-tuple-element.68.refs_0_), channel_id=1, source_target_pairs={{0,2},{1,3},{2,0},{3,1},{4,6},{5,7},{6,4},{7,5},{8,10},{9,11},{10,... | collective-permute-start | bytes 12296 | tf_op jit(solution)/shard_map/ppermute | solution.py:61
  47.4 6.6 %collective-permute-start.29 = (bf16[1,16,128]{2,1,0:T(8,128)(2,1)S(1)}, bf16[1,16,128]{2,1,0:T(8,128)(2,1)S(1)}, u32[]{:S(2)}, u32[]{:S(2)}) collective-permute-start(bf16[1,16,128]{2,1,0:T(8,128)(2,1)S(1)} %get-tuple-element.68.refs_0_), channel_id=1, source_target_pairs={{0,3},{1,2},{2,1},{3,0},{4,7},{5,6},{6,5},{7,4},{8,11},{9,10},{10,... | collective-permute-start | bytes 12296 | tf_op jit(solution)/shard_map/ppermute | solution.py:61
  49.7 8.8 %collective-permute-start.25 = (bf16[144,128]{1,0:T(8,128)(2,1)S(1)}, bf16[144,128]{1,0:T(8,128)(2,1)S(1)}, u32[]{:S(2)}, u32[]{:S(2)}) collective-permute-start(bf16[144,128]{1,0:T(8,128)(2,1)S(1)} %get-tuple-element.64), channel_id=1, source_target_pairs={{0,14},{1,15},{2,12},{3,13},{4,10},{5,11},{6,8},{7,9},{8,6},{9,7},... | collective-permute-start | bytes 110600 | tf_op jit(solution)/shard_map/ppermute | solution.py:61
  54.0 6.1 %collective-permute-start.26 = (bf16[144,128]{1,0:T(8,128)(2,1)S(1)}, bf16[144,128]{1,0:T(8,128)(2,1)S(1)}, u32[]{:S(2)}, u32[]{:S(2)}) collective-permute-start(bf16[144,128]{1,0:T(8,128)(2,1)S(1)} %get-tuple-element.65), channel_id=1, source_target_pairs={{0,15},{1,14},{2,13},{3,12},{4,11},{5,10},{6,9},{7,8},{8,7},{9,6},... | collective-permute-start | bytes 110600 | tf_op jit(solution)/shard_map/ppermute | solution.py:61
  54.2 6.0 %collective-permute-start.30 = (bf16[4,16,128]{2,1,0:T(8,128)(2,1)S(1)}, bf16[4,16,128]{2,1,0:T(8,128)(2,1)S(1)}, u32[]{:S(2)}, u32[]{:S(2)}) collective-permute-start(bf16[4,16,128]{2,1,0:T(8,128)(2,1)S(1)} %shard_map.134.refs_0_), channel_id=1, source_target_pairs={{0,4},{1,5},{2,6},{3,7},{4,0},{5,1},{6,2},{7,3},{8,12},{9,13},{10,... | collective-permute-start | bytes 49160 | tf_op jit(solution)/shard_map/ppermute | solution.py:61
  54.2 6.0 %collective-permute-start.31 = (bf16[4,16,128]{2,1,0:T(8,128)(2,1)S(1)}, bf16[4,16,128]{2,1,0:T(8,128)(2,1)S(1)}, u32[]{:S(2)}, u32[]{:S(2)}) collective-permute-start(bf16[4,16,128]{2,1,0:T(8,128)(2,1)S(1)} %shard_map.134.refs_0_), channel_id=1, source_target_pairs={{0,8},{1,9},{2,10},{3,11},{4,12},{5,13},{6,14},{7,15},{8,0},{9,1},... | collective-permute-start | bytes 49160 | tf_op jit(solution)/shard_map/ppermute | solution.py:61
  56.8 5.5 %collective-permute-start.32 = (bf16[4,16,128]{2,1,0:T(8,128)(2,1)S(1)}, bf16[4,16,128]{2,1,0:T(8,128)(2,1)S(1)}, u32[]{:S(2)}, u32[]{:S(2)}) collective-permute-start(bf16[4,16,128]{2,1,0:T(8,128)(2,1)S(1)} %shard_map.134.refs_0_), channel_id=1, source_target_pairs={{0,12},{1,13},{2,14},{3,15},{4,8},{5,9},{6,10},{7,11},{8,4},{9,5},... | collective-permute-start | bytes 49160 | tf_op jit(solution)/shard_map/ppermute | solution.py:61
  62.3 1.9 %copy-start.1 = (bf16[1,2048,768]{2,1,0:T(8,128)(2,1)S(1)}, bf16[1,2048,768]{2,1,0:T(8,128)(2,1)}, u32[]{:S(2)}) copy-start(bf16[1,2048,768]{2,1,0:T(8,128)(2,1)} %param.22) | copy-start | bytes 9437188
  64.2 1.9 %copy-start.2 = (bf16[1,768,2048]{2,1,0:T(8,128)(2,1)S(1)}, bf16[1,768,2048]{2,1,0:T(8,128)(2,1)}, u32[]{:S(2)}) copy-start(bf16[1,768,2048]{2,1,0:T(8,128)(2,1)} %param.23) | copy-start | bytes 9437188
  68.9 1.9 %collective-permute-start.33 = (bf16[4,16,128]{2,1,0:T(8,128)(2,1)S(1)}, bf16[4,16,128]{2,1,0:T(8,128)(2,1)S(1)}, u32[]{:S(2)}, u32[]{:S(2)}) collective-permute-start(bf16[4,16,128]{2,1,0:T(8,128)(2,1)S(1)} %get-tuple-element.70), channel_id=1, source_target_pairs={{0,1},{1,0},{2,3},{3,2},{4,5},{5,4},{6,7},{7,6},{8,9},{9,8},{10,11... | collective-permute-start | bytes 49160 | tf_op jit(solution)/shard_map/ppermute | solution.py:61
  69.1 3.8 %collective-permute-start.34 = (bf16[4,16,128]{2,1,0:T(8,128)(2,1)S(1)}, bf16[4,16,128]{2,1,0:T(8,128)(2,1)S(1)}, u32[]{:S(2)}, u32[]{:S(2)}) collective-permute-start(bf16[4,16,128]{2,1,0:T(8,128)(2,1)S(1)} %get-tuple-element.71), channel_id=1, source_target_pairs={{0,2},{1,3},{2,0},{3,1},{4,6},{5,7},{6,4},{7,5},{8,10},{9,11},{10,... | collective-permute-start | bytes 49160 | tf_op jit(solution)/shard_map/ppermute | solution.py:61
  70.4 3.2 %collective-permute-start.35 = (bf16[4,16,128]{2,1,0:T(8,128)(2,1)S(1)}, bf16[4,16,128]{2,1,0:T(8,128)(2,1)S(1)}, u32[]{:S(2)}, u32[]{:S(2)}) collective-permute-start(bf16[4,16,128]{2,1,0:T(8,128)(2,1)S(1)} %get-tuple-element.72), channel_id=1, source_target_pairs={{0,3},{1,2},{2,1},{3,0},{4,7},{5,6},{6,5},{7,4},{8,11},{9,10},{10,... | collective-permute-start | bytes 49160 | tf_op jit(solution)/shard_map/ppermute | solution.py:61
  73.6 4.5 %collective-permute-start.36 = (bf16[1,16,128]{2,1,0:T(8,128)(2,1)S(1)}, bf16[1,16,128]{2,1,0:T(8,128)(2,1)S(1)}, u32[]{:S(2)}, u32[]{:S(2)}) collective-permute-start(bf16[1,16,128]{2,1,0:T(8,128)(2,1)S(1)} %get-tuple-element.74), channel_id=1, source_target_pairs={{0,4},{1,5},{2,6},{3,7},{4,0},{5,1},{6,2},{7,3},{8,12},{9,13},{10,... | collective-permute-start | bytes 12296 | tf_op jit(solution)/shard_map/ppermute | solution.py:61
  73.7 4.6 %collective-permute-start.37 = (bf16[1,16,128]{2,1,0:T(8,128)(2,1)S(1)}, bf16[1,16,128]{2,1,0:T(8,128)(2,1)S(1)}, u32[]{:S(2)}, u32[]{:S(2)}) collective-permute-start(bf16[1,16,128]{2,1,0:T(8,128)(2,1)S(1)} %get-tuple-element.75), channel_id=1, source_target_pairs={{0,8},{1,9},{2,10},{3,11},{4,12},{5,13},{6,14},{7,15},{8,0},{9,1},... | collective-permute-start | bytes 12296 | tf_op jit(solution)/shard_map/ppermute | solution.py:61
  75.6 5.4 %collective-permute-start.38 = (bf16[1,16,128]{2,1,0:T(8,128)(2,1)S(1)}, bf16[1,16,128]{2,1,0:T(8,128)(2,1)S(1)}, u32[]{:S(2)}, u32[]{:S(2)}) collective-permute-start(bf16[1,16,128]{2,1,0:T(8,128)(2,1)S(1)} %get-tuple-element.76), channel_id=1, source_target_pairs={{0,12},{1,13},{2,14},{3,15},{4,8},{5,9},{6,10},{7,11},{8,4},{9,5},... | collective-permute-start | bytes 12296 | tf_op jit(solution)/shard_map/ppermute | solution.py:61
  (4 other events, 2.7 us)

commit v3 on v2

v3 whole, which is shorter than its diff:
```python
import functools

import jax
import jax.numpy as jnp
from jax import lax
from jax.experimental import pallas as pl
from jax.experimental.pallas import tpu as pltpu
from jax.sharding import PartitionSpec as P

QUERY_HEADS = 16
KEY_VALUE_HEADS = 2
HEAD_WIDTH = 128
ADAPTER_RANK = 32
GROUPED = QUERY_HEADS // KEY_VALUE_HEADS
KEY_VALUE_WIDTH = KEY_VALUE_HEADS * HEAD_WIDTH
WIDTH = QUERY_HEADS * HEAD_WIDTH
INV_ROOT = HEAD_WIDTH ** (-0.5)
NEAR = 4
HEADS = (QUERY_HEADS, HEAD_WIDTH)
PARTIAL = (2 * QUERY_HEADS, HEAD_WIDTH)
RESID_ROW = QUERY_HEADS
NEW_ROW = 2 * QUERY_HEADS
GATE_ROW = NEW_ROW + 2 * KEY_VALUE_HEADS
MESSAGE = (3 * QUERY_HEADS, HEAD_WIDTH)

floor_score = -1e30
epsilon = 1e-06

VMEM = pl.BlockSpec(memory_space=pltpu.VMEM)
SMEM = pl.BlockSpec(memory_space=pltpu.SMEM)
HBM = pl.BlockSpec(memory_space=pltpu.HBM)
ANY = pl.BlockSpec(memory_space=pl.ANY)
shape = jax.ShapeDtypeStruct


def call(kernel, shapes, specs, *args, limit=8, scratch=()):
    return pl.pallas_call(
        kernel,
        out_shape=shapes,
        in_specs=specs,
        out_specs=jax.tree.map(lambda _: VMEM, shapes),
        scratch_shapes=scratch,
        compiler_params=pltpu.CompilerParams(vmem_limit_bytes=limit * 1024 * 1024),
    )(*args)


def iota(dims, dim):
    return lax.broadcasted_iota(jnp.int32, dims, dim)


def place():
    me = lax.axis_index("exp")
    return me, me % NEAR, me // NEAR


def as_rows(line, rows):
    return jnp.concatenate(
        [line[:, j * HEAD_WIDTH : (j + 1) * HEAD_WIDTH] for j in range(rows)], axis=0
    )


def exchange(value, n, near):
    if near:
        groups = [[z * NEAR + l for l in range(NEAR)] for z in range(n // NEAR)]
    else:
        groups = [[z * NEAR + l for z in range(n // NEAR)] for l in range(NEAR)]
    return lax.all_to_all(
        value, "exp", split_axis=0, concat_axis=0, axis_index_groups=groups, tiled=True
    )


def pack_kernel(query, resid, new, choice, probability, out, q_in, r_in, n_in, c_in, p_in, sems):
    copies = [
        pltpu.make_async_copy(source, target, sems.at[k])
        for k, (source, target) in enumerate(
            ((query, q_in), (resid, r_in), (new, n_in), (choice, c_in), (probability, p_in))
        )
    ]
    for copy in copies:
        copy.start()
    for copy in copies:
        copy.wait()
    q = as_rows(q_in[...].astype(jnp.float32), QUERY_HEADS)
    r = as_rows(r_in[...].astype(jnp.float32), QUERY_HEADS)
    fresh = as_rows(n_in[...].astype(jnp.float32), 2 * KEY_VALUE_HEADS)
    p = p_in[...]
    shares = p / jnp.sum(p, axis=1, keepdims=True)
    lanes = iota((1, HEAD_WIDTH), 1)
    gates = jnp.zeros((1, HEAD_WIDTH), jnp.float32)
    for k in range(p.shape[1]):
        gates = gates + jnp.where(c_in[:, k : k + 1] == lanes, shares[:, k : k + 1], 0.0)
    rest = jnp.zeros((MESSAGE[0] - GATE_ROW - 1, HEAD_WIDTH), jnp.float32)
    message = jnp.concatenate([q, r, fresh, gates, rest], axis=0).astype(jnp.bfloat16)
    for k in range(NEAR):
        out[k] = message


def repeat_kernel(value, out):
    for k in range(out.shape[0]):
        out[k] = value[...]


def encode(top, total, acc):
    lanes = iota(HEADS, 1)
    stats = jnp.zeros(HEADS, jnp.float32)
    for at, value in ((0, top), (3, total)):
        for k in range(3):
            part = value.astype(jnp.bfloat16).astype(jnp.float32)
            stats = jnp.where(lanes == at + k, part, stats)
            value = value - part
    return jnp.concatenate([acc, stats], axis=0).astype(jnp.bfloat16)


def decode(message):
    value = message.astype(jnp.float32)
    acc, stats = value[:QUERY_HEADS], value[QUERY_HEADS:]
    top = stats[:, 0:1] + stats[:, 1:2] + stats[:, 2:3]
    total = stats[:, 3:4] + stats[:, 4:5] + stats[:, 5:6]
    return top, total, acc


def merged(messages, extra=None):
    parts = [decode(message) for message in messages] + ([extra] if extra else [])
    top = functools.reduce(jnp.maximum, [part[0] for part in parts])
    total, acc = 0.0, 0.0
    for peak, amount, value in parts:
        share = jnp.exp(peak - top)
        total = total + share * amount
        acc = acc + share * value
    return top, total, acc


def attend_kernel(lengths, got, cache, parts):
    me, _, _ = place()
    sequences, block, _ = cache.shape
    rows = 2 * QUERY_HEADS
    first_group = (iota((rows, HEAD_WIDTH), 0) % QUERY_HEADS) < GROUPED
    positions = me * block + iota((rows, block), 1)
    for s in range(sequences):
        z, l = 2 * s // NEAR, 2 * s % NEAR
        both = jnp.concatenate([got[z, l, :QUERY_HEADS], got[z, l + 1, :QUERY_HEADS]], axis=0)
        zero = jnp.zeros_like(both)
        wide = jnp.concatenate(
            [jnp.where(first_group, both, zero), jnp.where(first_group, zero, both)], axis=1
        )
        keys = cache[s, :, :KEY_VALUE_WIDTH]
        values = cache[s, :, KEY_VALUE_WIDTH:]
        scores = (
            lax.dot_general(
                wide, keys, (((1,), (1,)), ((), ())), preferred_element_type=jnp.float32
            )
            * INV_ROOT
        )
        valid = positions < lengths[s]
        scores = jnp.where(valid, scores, floor_score)
        top = jnp.max(scores, axis=1, keepdims=True)
        weights = jnp.where(valid, jnp.exp(scores - top), 0.0).astype(jnp.bfloat16)
        total = jnp.sum(weights.astype(jnp.float32), axis=1, keepdims=True)
        acc = jnp.dot(weights, values, preferred_element_type=jnp.float32)
        acc = jnp.where(first_group, acc[:, :HEAD_WIDTH], acc[:, HEAD_WIDTH:])
        for p in range(2):
            cut = slice(p * QUERY_HEADS, (p + 1) * QUERY_HEADS)
            parts[l + p, z] = encode(top[cut], total[cut], acc[cut])


def merge_kernel(got, out):
    for z in range(got.shape[1]):
        value = encode(*merged([got[k, z] for k in range(got.shape[0])]))
        for k in range(out.shape[0]):
            out[k, z] = value


def token_kernel(got, messages, scale, hidden_out, normed_out, hidden_all):
    _, low, high = place()
    first_group = iota(HEADS, 0) < GROUPED
    second = low % 2 == 1

    def by_head(rows, at):
        return jnp.where(first_group, rows[at : at + 1], rows[at + 1 : at + 2])

    for z in range(got.shape[1]):
        message = messages[z, low].astype(jnp.float32)
        q, resid = message[:QUERY_HEADS], message[RESID_ROW:NEW_ROW]
        mine = message[NEW_ROW:GATE_ROW]
        other = messages[z, low ^ 1, NEW_ROW:].astype(jnp.float32)[: GATE_ROW - NEW_ROW]
        own_score = jnp.sum(q * by_head(mine, 0), axis=1, keepdims=True) * INV_ROOT
        other_score = jnp.sum(q * by_head(other, 0), axis=1, keepdims=True) * INV_ROOT
        other_score = jnp.where(second, other_score, floor_score)
        new_max = jnp.maximum(own_score, other_score)
        own_weight = jnp.exp(own_score - new_max).astype(jnp.bfloat16).astype(jnp.float32)
        other_weight = jnp.where(second, jnp.exp(other_score - new_max), 0.0)
        other_weight = other_weight.astype(jnp.bfloat16).astype(jnp.float32)
        new_acc = own_weight * by_head(mine, 2) + other_weight * by_head(other, 2)
        _, total, acc = merged(
            [got[k, z] for k in range(got.shape[0])],
            (new_max, own_weight + other_weight, new_acc),
        )
        hidden = resid + acc / total
        squares = jnp.sum(jnp.sum(hidden * hidden, axis=1, keepdims=True), axis=0, keepdims=True)
        normed = hidden * lax.rsqrt(squares / WIDTH + epsilon) * scale[...]
        hidden_all[z] = hidden
        for k in range(NEAR):
            normed_out[k, z] = normed.astype(jnp.bfloat16)
    hidden_out[...] = hidden_all[high]


def dot_pair(value, factor, contract):
    high = value.astype(jnp.bfloat16)
    low = (value - high.astype(jnp.float32)).astype(jnp.bfloat16)
    both = lax.dot_general(
        jnp.concatenate([high, low], axis=0),
        factor,
        (((1,), (contract,)), ((), ())),
        preferred_element_type=jnp.float32,
    )
    return both[: value.shape[0]] + both[value.shape[0] :]


def expert_kernel(got, messages, gate_w, up_w, down_w, model, inner, parts):
    me, _, _ = place()
    near, far = got.shape[:2]
    tokens = near * far
    x = got[...].astype(jnp.float32).reshape(tokens, WIDTH).astype(jnp.bfloat16)
    r = ADAPTER_RANK
    mixed = lax.dot_general(
        x, model[: 2 * r], (((1,), (1,)), ((), ())), preferred_element_type=jnp.float32
    )
    gate = jnp.dot(x, gate_w[...], preferred_element_type=jnp.float32)
    gate = gate + dot_pair(mixed[:, :r], inner[:, :r], 1)
    up = jnp.dot(x, up_w[...], preferred_element_type=jnp.float32)
    up = up + dot_pair(mixed[:, r:], inner[:, r : 2 * r], 1)
    act = (gate / (1.0 + jnp.exp(-gate)) * up).astype(jnp.bfloat16)
    lowered = jnp.dot(act, inner[:, 2 * r : 3 * r], preferred_element_type=jnp.float32)
    result = jnp.dot(act, down_w[...], preferred_element_type=jnp.float32)
    result = result + dot_pair(lowered, model[2 * r :], 0)
    lanes = iota((1, HEAD_WIDTH), 1)
    for l in range(near):
        for z in range(far):
            slot = l * far + z
            route = messages[z, l, NEW_ROW:].astype(jnp.float32)
            route = route[GATE_ROW - NEW_ROW : GATE_ROW - NEW_ROW + 1]
            share = jnp.sum(jnp.where(lanes == me, route, 0.0), axis=1, keepdims=True)
            line = as_rows(result[slot : slot + 1] * share, QUERY_HEADS)
            parts[l, z] = line.astype(jnp.bfloat16)


def add_kernel(got, out):
    for z in range(got.shape[1]):
        total = sum(got[k, z].astype(jnp.float32) for k in range(got.shape[0]))
        out[z] = total.astype(jnp.bfloat16)


def finish_kernel(hidden, got, out):
    total = hidden[...] + sum(got[k].astype(jnp.float32) for k in range(got.shape[0]))
    line = jnp.concatenate([total[j : j + 1] for j in range(QUERY_HEADS)], axis=1)
    out[...] = line.astype(jnp.bfloat16)


def swap(value, n, distance):
    return lax.ppermute(value, "exp", [(t, t ^ distance) for t in range(n)])


def lora_pack_kernel(after, model, inner, *outs):
    _, low, _ = place()
    ranks = model.shape[1]
    for k, out in enumerate(outs):
        for z in range(out.shape[0]):
            at = z * NEAR + (low ^ k)
            out[z, :ranks] = model[at]
            out[z, ranks:, :ranks] = inner[at]
            out[z, ranks:, ranks:] = jnp.zeros(
                (out.shape[1] - ranks, HEAD_WIDTH - ranks), out.dtype
            )


def lora_turn_kernel(after, *refs):
    _, low, high = place()
    got, outs = refs[:NEAR], refs[NEAR:]
    for j, out in enumerate(outs):
        for k, ref in enumerate(got):
            out[low ^ k] = ref[high ^ j]


def lora_join_kernel(*refs):
    _, _, high = place()
    got, (model, inner) = refs[:-2], refs[-2:]
    ranks = model.shape[0]
    width = inner.shape[0] // (len(got) * NEAR)
    for j, ref in enumerate(got):
        for l in range(NEAR):
            at = (high ^ j) * NEAR + l
            columns = pl.ds(pl.multiple_of(at * HEAD_WIDTH, HEAD_WIDTH), HEAD_WIDTH)
            model[:, columns] = ref[l, :ranks]
            inner[pl.ds(pl.multiple_of(at * width, width), width)] = ref[l, ranks:]


def lora(adapter_model, adapter_hidden, n, after_first, after_second):
    total, ranks, model_width = adapter_model.shape
    inner_width = adapter_hidden.shape[2]
    inner = jnp.transpose(adapter_hidden, (0, 2, 1))
    if model_width != HEAD_WIDTH or inner_width % 16:
        model = lax.all_to_all(adapter_model, "exp", split_axis=0, concat_axis=2, tiled=True)
        inner = lax.all_to_all(inner, "exp", split_axis=0, concat_axis=1, tiled=True)
        return model[0], inner[0]
    far = n // NEAR
    packed = call(
        lora_pack_kernel,
        (shape((far, ranks + inner_width, HEAD_WIDTH), jnp.bfloat16),) * NEAR,
        [ANY, VMEM, VMEM],
        after_first,
        adapter_model,
        inner,
    )
    got = [packed[0]] + [swap(packed[k], n, k) for k in range(1, NEAR)]
    turned = call(
        lora_turn_kernel,
        (shape((NEAR, ranks + inner_width, HEAD_WIDTH), jnp.bfloat16),) * far,
        [ANY] + [VMEM] * NEAR,
        after_second,
        *got,
    )
    got = [turned[0]] + [swap(turned[j], n, j * NEAR) for j in range(1, far)]
    return call(
        lora_join_kernel,
        (
            shape((ranks, n * model_width), jnp.bfloat16),
            shape((n * inner_width, HEAD_WIDTH), jnp.bfloat16),
        ),
        [VMEM] * far,
        *got,
    )


def body(
    resid,
    queries,
    incoming_key_value,
    key_value_cache,
    lengths,
    norm_scale_vector,
    expert_choice,
    router_probability,
    gate_weight,
    up_weight,
    down_weight,
    adapter_model,
    adapter_hidden,
):
    n = lax.axis_size("exp")
    far = n // NEAR
    bf16, f32 = jnp.bfloat16, jnp.float32

    message = call(
        pack_kernel,
        shape((NEAR,) + MESSAGE, bf16),
        [HBM] * 5,
        queries,
        resid,
        incoming_key_value,
        expert_choice,
        router_probability,
        scratch=[
            pltpu.VMEM(queries.shape, bf16),
            pltpu.VMEM(resid.shape, bf16),
            pltpu.VMEM(incoming_key_value.shape, bf16),
            pltpu.VMEM(expert_choice.shape, jnp.int32),
            pltpu.VMEM(router_probability.shape, f32),
            pltpu.SemaphoreType.DMA((5,)),
        ],
    )
    close = exchange(message, n, True)
    close_copies = call(repeat_kernel, shape((far,) + close.shape, bf16), [VMEM], close)
    messages = exchange(close_copies, n, False)
    parts = call(
        attend_kernel,
        shape((NEAR, far) + PARTIAL, bf16),
        [SMEM, VMEM, VMEM],
        lengths,
        messages,
        key_value_cache,
    )
    partial_sums = exchange(parts, n, True)
    merged_copies = call(
        merge_kernel, shape((far, far) + PARTIAL, bf16), [VMEM], partial_sums
    )
    columns = exchange(merged_copies, n, False)
    hidden, normed = call(
        token_kernel,
        (shape(HEADS, f32), shape((NEAR, far) + HEADS, bf16)),
        [VMEM] * 3,
        columns,
        messages,
        norm_scale_vector.reshape(HEADS),
        scratch=[pltpu.VMEM((far,) + HEADS, f32)],
    )
    rows = exchange(normed, n, True)
    model, inner = lora(adapter_model, adapter_hidden, n, close, partial_sums)
    outs = call(
        expert_kernel,
        shape((NEAR, far) + HEADS, bf16),
        [VMEM] * 7,
        rows,
        messages,
        gate_weight[0],
        up_weight[0],
        down_weight[0],
        model,
        inner,
        limit=32,
    )
    sums = call(add_kernel, shape((far,) + HEADS, bf16), [VMEM], exchange(outs, n, True))
    return call(
        finish_kernel,
        shape((1, WIDTH), bf16),
        [VMEM] * 2,
        hidden,
        exchange(sums, n, False),
    )


def solution(mesh):
    return jax.shard_map(
        body,
        mesh=mesh,
        in_specs=(
            P(("grp", "exp"), None),
            P(("grp", "exp"), None),
            P(("grp", "exp"), None),
            P("grp", "exp", None),
            P("grp"),
            P(),
            P(("grp", "exp"), None),
            P(("grp", "exp"), None),
            P("exp", None, None),
            P("exp", None, None),
            P("exp", None, None),
            P(None, None, "exp"),
            P(None, None, "exp"),
        ),
        out_specs=P(("grp", "exp"), None),
        check_vma=False,
    )
```

time: 82 us -> 93.9 us (1.15)
  blocking collectives: 0 us -> 36.8 us
  starting transfers between devices: 46 us -> 17.1 us
  waiting for transfers between devices: 16.3 us -> 5.96 us
  local copies, waits for them, and re-layouts: 12.1 us -> 21.1 us
  Pallas kernels: 7.08 us -> 11.8 us
    ppermute x39 -> x6, starting transfers between devices: 46 us -> 6.54 us  [swap(): return lax.ppermute(value, 'exp', [(t, t ^ distance) for t in range(n)])]
    all_to_all x0 -> x4, blocking collectives: none -> 36.8 us  [exchange(): lax.all_to_all(value, 'exp', split_axis=0, concat_axis=0, axis_index_grou...]
    all_to_all x0 -> x3, starting transfers between devices: none -> 10.6 us  [exchange(): lax.all_to_all(value, 'exp', split_axis=0, concat_axis=0, axis_index_grou...]
    ppermute x39 -> x6, waiting for transfers between devices: 16.3 us -> 5.95 us  [swap(): return lax.ppermute(value, 'exp', [(t, t ^ distance) for t in range(n)])]
    unnamed x26 -> x52, local copies, waits for them, and re-layouts: 12.1 us -> 21.1 us
    pallas_call x11, Pallas kernels: 7.08 us -> 11.8 us  [call(): pl.pallas_call(kernel, out_shape=shapes, in_specs=specs, out_specs=jax.tr...]
  transfers between devices with their start and end apart: 39 -> 9, of which waited for: 12 -> 3; matrix products, arithmetic and copies ran while one was open for 0% -> 0% of each run, Pallas kernels for 4% -> 6%
where the time goes in v3:
time: 93.9 us; the launch traced here: 93 us
  blocking collectives  36.8 us (39%)
  local copies, waits for them, and re-layouts  21.1 us (22%)
  starting transfers between devices  17.1 us (18%)
  Pallas kernels  11.8 us (13%)
  waiting for transfers between devices  5.96 us (6%)
    all_to_all x4, blocking collectives, exchange(): lax.all_to_all(value, 'exp', split_axis=0, concat_axis=0, axis_index_grou...  36.8 us
    unnamed x52, local copies, waits for them, and re-layouts  21.1 us
    pallas_call x11, Pallas kernels, call(): pl.pallas_call(kernel, out_shape=shapes, in_specs=specs, out_specs=jax.tr...  11.8 us
    all_to_all x3, starting transfers between devices, exchange(): lax.all_to_all(value, 'exp', split_axis=0, concat_axis=0, axis_index_grou...  10.6 us
    ppermute x6, starting transfers between devices, swap(): return lax.ppermute(value, 'exp', [(t, t ^ distance) for t in range(n)])  6.54 us
    ppermute x6, waiting for transfers between devices, swap(): return lax.ppermute(value, 'exp', [(t, t ^ distance) for t in range(n)])  5.95 us
  transfers between devices with their start and end apart: 9, of which 3 were waited for; matrix products, arithmetic and copies ran while one was open for 0% of the time, Pallas kernels for 6%

profile of v3, /device:TPU:0, one launch (start us, length us, event | category | flops | bytes accessed | tf_op | source)
XLA Modules:
  0.0 93.0 jit_solution(15306266635240961343)
XLA Ops:
  0.0 0.8 copy-done.17
  0.9 0.8 copy-done.18
  1.7 0.7 copy-done.22
  2.3 0.7 copy-done.23
  3.0 0.7 copy-done.24
  3.7 0.2 shard_map.127
  3.9 8.1 %all_to_all.35.value.after = bf16[4,48,128]{2,1,0:T(8,128)(2,1)S(1)} all-to-all(bf16[4,48,128]{2,1,0:T(8,128)(2,1)S(1)} %shard_map.127), channel_id=1, replica_groups={{0,1,2,3},{4,5,6,7},{8,9,10,11},{12,13,14,15},{16,17,18,19},{20,21,22,2..., dimensions={0} | all-to-all | bytes 98304 | tf_op jit(solution)/shard_map/all_to_all | solution.py:67
  12.0 12.2 %all_to_all.36.got.messages = bf16[4,4,48,128]{3,2,1,0:T(8,128)(2,1)S(1)} all-to-all(bf16[4,4,48,128]{3,2,1,0:T(8,128)(2,1)S(1)} %shard_map.128), channel_id=1, replica_groups={{0,4,8,12},{1,5,9,13},{2,6,10,14},{3,7,11,15},{16,20,24,28},{17,21,25,2..., dimensions={0} | all-to-all | bytes 393216 | tf_op jit(solution)/shard_map/all_to_all | solution.py:67
  24.2 1.4 %copy-done.3 = bf16[8,192,512]{2,1,0:T(8,128)(2,1)S(1)} copy-done((bf16[8,192,512]{2,1,0:T(8,128)(2,1)S(1)}, bf16[8,192,512]{2,1,0:T(8,128)(2,1)}, u32[]{:S(2)}) %copy-start.3) | copy-done | bytes 1572888
  25.6 0.7 copy-done.25
  26.2 2.7 %shard_map.129 = bf16[4,4,32,128]{3,2,1,0:T(8,128)(2,1)S(1)} custom-call(s32[8]{0:T(128)S(1)} %copy-done.25, bf16[4,4,48,128]{3,2,1,0:T(8,128)(2,1)S(1)} %all_to_all.36.got.messages, bf16[8,192,512]{2,1,0:T(8,128)(2,1)S(1)} %copy-done.3), custom_call_target="tpu_custom_call" | custom-call | tf_op jit(solution)/shard_map/pallas_call | solution.py:37
  28.9 0.7 copy-done.4
  29.6 3.3 %all-to-all-start.2 = ((bf16[4,4,32,128]{3,2,1,0:T(8,128)(2,1)}), bf16[4,4,32,128]{3,2,1,0:T(8,128)(2,1)S(1)}, u32[]{:S(2)}, u32[]{:S(2)}) async-start(bf16[4,4,32,128]{3,2,1,0:T(8,128)(2,1)} %copy-done.4), calls=%async_computation.2 | async-start | bytes 262144 | tf_op jit(solution)/shard_map/all_to_all | solution.py:67
  32.9 1.0 %copy-done.8 = bf16[16,96,128]{2,1,0:T(8,128)(2,1)S(1)} copy-done((bf16[16,96,128]{2,1,0:T(8,128)(2,1)S(1)}, bf16[16,96,128]{2,1,0:T(8,128)(2,1)}, u32[]{:S(2)}) %copy-start.8) | copy-done | bytes 393240
  33.9 0.9 copy-done.9
  34.8 0.9 shard_map.132
  35.7 0.6 copy-done.14
  36.3 0.5 collective-permute-start
  36.8 1.7 %collective-permute-start.1 = (bf16[4,144,128]{2,1,0:T(8,128)(2,1)}, bf16[4,144,128]{2,1,0:T(8,128)(2,1)}, u32[]{:S(2)}, u32[]{:S(2)}) collective-permute-start(bf16[4,144,128]{2,1,0:T(8,128)(2,1)} %get-tuple-element.21), channel_id=1, source_target_pairs={{0,2},{1,3},{2,0},{3,1},{4,6},{5,7},{6,4},{7,5},{8,10},{9,11},{10,... | collective-permute-start | bytes 442376 | tf_op jit(solution)/shard_map/ppermute | solution.py:260
  38.5 0.3 shard_map.130
  38.8 0.6 copy-done.5
  39.4 3.9 %all-to-all-start.3 = ((bf16[4,4,32,128]{3,2,1,0:T(8,128)(2,1)}), bf16[4,4,32,128]{3,2,1,0:T(8,128)(2,1)}, u32[]{:S(2)}, u32[]{:S(2)}) async-start(bf16[4,4,32,128]{3,2,1,0:T(8,128)(2,1)} %copy-done.5), calls=%async_computation.3 | async-start | bytes 262144 | tf_op jit(solution)/shard_map/all_to_all | solution.py:67
  43.4 0.4 collective-permute-done.1.refs_2_
  43.8 1.9 %collective-permute-done.2.refs_3_ = bf16[4,144,128]{2,1,0:T(8,128)(2,1)} collective-permute-done((bf16[4,144,128]{2,1,0:T(8,128)(2,1)}, bf16[4,144,128]{2,1,0:T(8,128)(2,1)}, u32[]{:S(2)}, u32[]{:S(2)}) %collective-permute-start.2) | collective-permute-done | bytes 147488 | tf_op jit(solution)/shard_map/ppermute | solution.py:260
  45.7 0.9 copy-done.15
  46.6 1.9 %shard_map.133 = (bf16[4,144,128]{2,1,0:T(8,128)(2,1)S(1)}, bf16[4,144,128]{2,1,0:T(8,128)(2,1)}, bf16[4,144,128]{2,1,0:T(8,128)(2,1)}, bf16[4,144,128]{2,1,0:T(8,128)(2,1)}) custom-call(bf16[4,4,32,128]{3,2,1,0:T(8,128)(2,1)S(1)} %all-to-all-done.2.got.after, bf16[4,144,128]{2,1,0:T(8,128)(2,1)S(1)} %copy-done.15, ...), custom_call_target="tpu_custom_call" | custom-call | tf_op jit(solution)/shard_map/pallas_call | solution.py:37
  48.5 0.6 copy-done.12
  49.1 0.4 collective-permute-start.3
  49.5 1.7 %collective-permute-start.4 = (bf16[4,144,128]{2,1,0:T(8,128)(2,1)}, bf16[4,144,128]{2,1,0:T(8,128)(2,1)}, u32[]{:S(2)}, u32[]{:S(2)}) collective-permute-start(bf16[4,144,128]{2,1,0:T(8,128)(2,1)} %get-tuple-element.25), channel_id=1, source_target_pairs={{0,8},{1,9},{2,10},{3,11},{4,12},{5,13},{6,14},{7,15},{8,0},{9,1},... | collective-permute-start | bytes 442376 | tf_op jit(solution)/shard_map/ppermute | solution.py:260
  51.2 2.3 %collective-permute-start.5 = (bf16[4,144,128]{2,1,0:T(8,128)(2,1)}, bf16[4,144,128]{2,1,0:T(8,128)(2,1)}, u32[]{:S(2)}, u32[]{:S(2)}) collective-permute-start(bf16[4,144,128]{2,1,0:T(8,128)(2,1)} %get-tuple-element.26), channel_id=1, source_target_pairs={{0,12},{1,13},{2,14},{3,15},{4,8},{5,9},{6,10},{7,11},{8,4},{9,5},... | collective-permute-start | bytes 442376 | tf_op jit(solution)/shard_map/ppermute | solution.py:260
  53.5 0.7 copy-done.21
  54.2 1.4 %shard_map.131 = (f32[16,128]{1,0:T(8,128)S(1)}, bf16[4,4,16,128]{3,2,1,0:T(8,128)(2,1)S(1)}) custom-call(bf16[4,4,32,128]{3,2,1,0:T(8,128)(2,1)} %all-to-all-done.3.got, bf16[4,4,48,128]{3,2,1,0:T(8,128)(2,1)S(1)} %all_to_all.36.got.messages, f32[16,128]{1,0:T(8,128)S(1)} %bitcast.9), custom_call_target="tpu_custom_call" | custom-call | tf_op jit(solution)/shard_map/pallas_call | solution.py:37
  55.6 0.6 copy-done.16
  56.2 0.6 copy-done.19
  56.8 3.3 %all-to-all-start.4 = ((bf16[4,4,16,128]{3,2,1,0:T(8,128)(2,1)}), bf16[4,4,16,128]{3,2,1,0:T(8,128)(2,1)S(1)}, u32[]{:S(2)}, u32[]{:S(2)}) async-start(bf16[4,4,16,128]{3,2,1,0:T(8,128)(2,1)} %copy-done.16), calls=%async_computation.4 | async-start | bytes 131072 | tf_op jit(solution)/shard_map/all_to_all | solution.py:67
  60.1 3.7 %collective-permute-done.4.refs_2_ = bf16[4,144,128]{2,1,0:T(8,128)(2,1)} collective-permute-done((bf16[4,144,128]{2,1,0:T(8,128)(2,1)}, bf16[4,144,128]{2,1,0:T(8,128)(2,1)}, u32[]{:S(2)}, u32[]{:S(2)}) %collective-permute-start.4) | collective-permute-done | bytes 147488 | tf_op jit(solution)/shard_map/ppermute | solution.py:260
  63.8 0.9 copy-done.13
  64.7 1.1 %shard_map.134 = (bf16[96,2048]{1,0:T(8,128)(2,1)S(1)}, bf16[768,128]{1,0:T(8,128)(2,1)S(1)}) custom-call(bf16[4,144,128]{2,1,0:T(8,128)(2,1)S(1)} %copy-done.13, bf16[4,144,128]{2,1,0:T(8,128)(2,1)S(1)} %collective-permute-done.3.refs_1_, bf16[4,144,128]{2,1,0:T(8,128)(2,1)} %collective-permute-done.4.refs_2_, ...), custom_call_target="tpu_custom_call" | custom-call | tf_op jit(solution)/shard_map/pallas_call | solution.py:37
  65.8 0.7 copy-done.6
  66.5 0.7 copy-done.10
  67.2 1.9 %copy-done.1 = bf16[1,2048,768]{2,1,0:T(8,128)(2,1)S(1)} copy-done((bf16[1,2048,768]{2,1,0:T(8,128)(2,1)S(1)}, bf16[1,2048,768]{2,1,0:T(8,128)(2,1)}, u32[]{:S(2)}) %copy-start.1) | copy-done | bytes 3145752
  69.1 1.9 %copy-done.2 = bf16[1,768,2048]{2,1,0:T(8,128)(2,1)S(1)} copy-done((bf16[1,768,2048]{2,1,0:T(8,128)(2,1)S(1)}, bf16[1,768,2048]{2,1,0:T(8,128)(2,1)}, u32[]{:S(2)}) %copy-start.2) | copy-done | bytes 3145752
  71.0 1.0 %copy-done.7 = bf16[96,2048]{1,0:T(8,128)(2,1)S(1)} copy-done((bf16[96,2048]{1,0:T(8,128)(2,1)S(1)}, bf16[96,2048]{1,0:T(8,128)(2,1)}, u32[]{:S(2)}) %copy-start.7) | copy-done | bytes 393240
  72.0 0.9 copy-done.11
  72.9 2.8 %shard_map.135 = bf16[4,4,16,128]{3,2,1,0:T(8,128)(2,1)S(1)} custom-call(bf16[4,4,16,128]{3,2,1,0:T(8,128)(2,1)S(1)} %all-to-all-done.4.got, bf16[4,4,48,128]{3,2,1,0:T(8,128)(2,1)S(1)} %all_to_all.36.got.messages, bf16[2048,768]{1,0:T(8,128)(2,1)S(1)} %bitcast.5, bf16[2048,768]{1,0:T(8,128)(2,1)S(1)} %bitcast.6, bf16[768,2048]{1,0:T(8,128)(2,1)S(1)} %bitcast.7, ...), custom_call_target="tpu_custom_call" | custom-call | tf_op jit(solution)/shard_map/pallas_call | solution.py:37
  75.7 7.0 %all_to_all.37.got = bf16[4,4,16,128]{3,2,1,0:T(8,128)(2,1)S(1)} all-to-all(bf16[4,4,16,128]{3,2,1,0:T(8,128)(2,1)S(1)} %shard_map.135), channel_id=1, replica_groups={{0,1,2,3},{4,5,6,7},{8,9,10,11},{12,13,14,15},{16,17,18,19},{20,21,22,2..., dimensions={0} | all-to-all | bytes 131072 | tf_op jit(solution)/shard_map/all_to_all | solution.py:67
  82.7 9.6 %all_to_all.38.got = bf16[4,16,128]{2,1,0:T(8,128)(2,1)S(1)} all-to-all(bf16[4,16,128]{2,1,0:T(8,128)(2,1)S(1)} %shard_map.136), channel_id=1, replica_groups={{0,4,8,12},{1,5,9,13},{2,6,10,14},{3,7,11,15},{16,20,24,28},{17,21,25,2..., dimensions={0} | all-to-all | bytes 32768 | tf_op jit(solution)/shard_map/all_to_all | solution.py:67
  92.3 0.6 shard_map.137
  (37 shorter events, 0.1 us)
Async XLA Ops:
  0.0 67.2 %copy-start = (bf16[1,2048,768]{2,1,0:T(8,128)(2,1)S(1)}, bf16[1,2048,768]{2,1,0:T(8,128)(2,1)}, u32[]{:S(2)}) copy-start(bf16[1,2048,768]{2,1,0:T(8,128)(2,1)} %param.21) | copy-start | bytes 9437188
  0.0 0.8 copy-start.17
  0.8 0.8 copy-start.18
  1.7 0.7 copy-start.22
  2.3 0.7 copy-start.23
  3.0 0.7 copy-start.24
  24.2 1.4 %copy-start.3 = (bf16[8,192,512]{2,1,0:T(8,128)(2,1)S(1)}, bf16[8,192,512]{2,1,0:T(8,128)(2,1)}, u32[]{:S(2)}) copy-start(bf16[8,192,512]{2,1,0:T(8,128)(2,1)} %cache.1) | copy-start | bytes 4718596
  25.6 0.7 copy-start.25
  28.9 0.7 copy-start.4
  29.6 8.9 %all-to-all-start.2 = ((bf16[4,4,32,128]{3,2,1,0:T(8,128)(2,1)}), bf16[4,4,32,128]{3,2,1,0:T(8,128)(2,1)S(1)}, u32[]{:S(2)}, u32[]{:S(2)}) async-start(bf16[4,4,32,128]{3,2,1,0:T(8,128)(2,1)} %copy-done.4), calls=%async_computation.2 | async-start | bytes 262144 | tf_op jit(solution)/shard_map/all_to_all | solution.py:67
  32.9 1.0 %copy-start.8 = (bf16[16,96,128]{2,1,0:T(8,128)(2,1)S(1)}, bf16[16,96,128]{2,1,0:T(8,128)(2,1)}, u32[]{:S(2)}) copy-start(bf16[16,96,128]{2,1,0:T(8,128)(2,1)} %model.1) | copy-start | bytes 1179652
  33.9 0.9 copy-start.9
  35.7 0.7 copy-start.14
  36.3 7.1 %collective-permute-start = (bf16[4,144,128]{2,1,0:T(8,128)(2,1)}, bf16[4,144,128]{2,1,0:T(8,128)(2,1)}, u32[]{:S(2)}, u32[]{:S(2)}) collective-permute-start(bf16[4,144,128]{2,1,0:T(8,128)(2,1)} %get-tuple-element.20), channel_id=1, source_target_pairs={{0,1},{1,0},{2,3},{3,2},{4,5},{5,4},{6,7},{7,6},{8,9},{9,8},{10,11... | collective-permute-start | bytes 442376 | tf_op jit(solution)/shard_map/ppermute | solution.py:260
  36.8 7.0 %collective-permute-start.1 = (bf16[4,144,128]{2,1,0:T(8,128)(2,1)}, bf16[4,144,128]{2,1,0:T(8,128)(2,1)}, u32[]{:S(2)}, u32[]{:S(2)}) collective-permute-start(bf16[4,144,128]{2,1,0:T(8,128)(2,1)} %get-tuple-element.21), channel_id=1, source_target_pairs={{0,2},{1,3},{2,0},{3,1},{4,6},{5,7},{6,4},{7,5},{8,10},{9,11},{10,... | collective-permute-start | bytes 442376 | tf_op jit(solution)/shard_map/ppermute | solution.py:260
  38.5 7.2 %collective-permute-start.2 = (bf16[4,144,128]{2,1,0:T(8,128)(2,1)}, bf16[4,144,128]{2,1,0:T(8,128)(2,1)}, u32[]{:S(2)}, u32[]{:S(2)}) collective-permute-start(bf16[4,144,128]{2,1,0:T(8,128)(2,1)} %get-tuple-element.22), channel_id=1, source_target_pairs={{0,3},{1,2},{2,1},{3,0},{4,7},{5,6},{6,5},{7,4},{8,11},{9,10},{10,... | collective-permute-start | bytes 442376 | tf_op jit(solution)/shard_map/ppermute | solution.py:260
  38.8 0.6 copy-start.5
  39.4 14.1 %all-to-all-start.3 = ((bf16[4,4,32,128]{3,2,1,0:T(8,128)(2,1)}), bf16[4,4,32,128]{3,2,1,0:T(8,128)(2,1)}, u32[]{:S(2)}, u32[]{:S(2)}) async-start(bf16[4,4,32,128]{3,2,1,0:T(8,128)(2,1)} %copy-done.5), calls=%async_computation.3 | async-start | bytes 262144 | tf_op jit(solution)/shard_map/all_to_all | solution.py:67
  45.7 0.9 copy-start.15
  48.5 0.7 copy-start.12
  49.1 11.0 %collective-permute-start.3 = (bf16[4,144,128]{2,1,0:T(8,128)(2,1)}, bf16[4,144,128]{2,1,0:T(8,128)(2,1)S(1)}, u32[]{:S(2)}, u32[]{:S(2)}) collective-permute-start(bf16[4,144,128]{2,1,0:T(8,128)(2,1)} %get-tuple-element.24), channel_id=1, source_target_pairs={{0,4},{1,5},{2,6},{3,7},{4,0},{5,1},{6,2},{7,3},{8,12},{9,13},{10,... | collective-permute-start | bytes 442376 | tf_op jit(solution)/shard_map/ppermute | solution.py:260
  49.5 14.3 %collective-permute-start.4 = (bf16[4,144,128]{2,1,0:T(8,128)(2,1)}, bf16[4,144,128]{2,1,0:T(8,128)(2,1)}, u32[]{:S(2)}, u32[]{:S(2)}) collective-permute-start(bf16[4,144,128]{2,1,0:T(8,128)(2,1)} %get-tuple-element.25), channel_id=1, source_target_pairs={{0,8},{1,9},{2,10},{3,11},{4,12},{5,13},{6,14},{7,15},{8,0},{9,1},... | collective-permute-start | bytes 442376 | tf_op jit(solution)/shard_map/ppermute | solution.py:260
  51.2 12.6 %collective-permute-start.5 = (bf16[4,144,128]{2,1,0:T(8,128)(2,1)}, bf16[4,144,128]{2,1,0:T(8,128)(2,1)}, u32[]{:S(2)}, u32[]{:S(2)}) collective-permute-start(bf16[4,144,128]{2,1,0:T(8,128)(2,1)} %get-tuple-element.26), channel_id=1, source_target_pairs={{0,12},{1,13},{2,14},{3,15},{4,8},{5,9},{6,10},{7,11},{8,4},{9,5},... | collective-permute-start | bytes 442376 | tf_op jit(solution)/shard_map/ppermute | solution.py:260
  53.5 0.7 copy-start.21
  55.6 0.6 copy-start.16
  56.2 0.6 copy-start.19
  56.8 10.4 %all-to-all-start.4 = ((bf16[4,4,16,128]{3,2,1,0:T(8,128)(2,1)}), bf16[4,4,16,128]{3,2,1,0:T(8,128)(2,1)S(1)}, u32[]{:S(2)}, u32[]{:S(2)}) async-start(bf16[4,4,16,128]{3,2,1,0:T(8,128)(2,1)} %copy-done.16), calls=%async_computation.4 | async-start | bytes 131072 | tf_op jit(solution)/shard_map/all_to_all | solution.py:67
  63.8 0.9 copy-start.13
  65.8 0.7 copy-start.6
  66.5 0.7 copy-start.10
  67.2 1.9 %copy-start.1 = (bf16[1,2048,768]{2,1,0:T(8,128)(2,1)S(1)}, bf16[1,2048,768]{2,1,0:T(8,128)(2,1)}, u32[]{:S(2)}) copy-start(bf16[1,2048,768]{2,1,0:T(8,128)(2,1)} %param.22) | copy-start | bytes 9437188
  69.1 1.9 %copy-start.2 = (bf16[1,768,2048]{2,1,0:T(8,128)(2,1)S(1)}, bf16[1,768,2048]{2,1,0:T(8,128)(2,1)}, u32[]{:S(2)}) copy-start(bf16[1,768,2048]{2,1,0:T(8,128)(2,1)} %param.23) | copy-start | bytes 9437188
  71.0 1.0 %copy-start.7 = (bf16[96,2048]{1,0:T(8,128)(2,1)S(1)}, bf16[96,2048]{1,0:T(8,128)(2,1)}, u32[]{:S(2)}) copy-start(bf16[96,2048]{1,0:T(8,128)(2,1)} %copy-done.6) | copy-start | bytes 1179652
  72.0 0.9 copy-start.11
  72.9 19.4 %copy-start.20 = (f32[16,128]{1,0:T(8,128)S(1)}, f32[16,128]{1,0:T(8,128)}, u32[]{:S(2)}) copy-start(f32[16,128]{1,0:T(8,128)} %copy-done.19) | copy-start | bytes 24580

commit v4 on v3

v4 whole, which is shorter than its diff:
```python
import functools

import jax
import jax.numpy as jnp
from jax import lax
from jax.experimental import pallas as pl
from jax.experimental.pallas import tpu as pltpu
from jax.sharding import PartitionSpec as P

QUERY_HEADS = 16
KEY_VALUE_HEADS = 2
HEAD_WIDTH = 128
ADAPTER_RANK = 32
GROUPED = QUERY_HEADS // KEY_VALUE_HEADS
KEY_VALUE_WIDTH = KEY_VALUE_HEADS * HEAD_WIDTH
WIDTH = QUERY_HEADS * HEAD_WIDTH
INV_ROOT = HEAD_WIDTH ** (-0.5)
NEAR = 4
NEW_ROWS = 2 * KEY_VALUE_HEADS
HEADS = (QUERY_HEADS, HEAD_WIDTH)
PARTIAL = (2 * QUERY_HEADS, HEAD_WIDTH)
RESID_ROW = QUERY_HEADS
NEW_ROW = 2 * QUERY_HEADS
GATE_ROW = NEW_ROW + NEW_ROWS
MESSAGE = (3 * QUERY_HEADS, HEAD_WIDTH)

floor_score = -1e30
epsilon = 1e-06

VMEM = pl.BlockSpec(memory_space=pltpu.VMEM)
SMEM = pl.BlockSpec(memory_space=pltpu.SMEM)
HBM = pl.BlockSpec(memory_space=pltpu.HBM)
ANY = pl.BlockSpec(memory_space=pl.ANY)
shape = jax.ShapeDtypeStruct
bf16, f32 = jnp.bfloat16, jnp.float32


def call(kernel, shapes, specs, *args, limit=8, scratch=()):
    return pl.pallas_call(
        kernel,
        out_shape=shapes,
        in_specs=specs,
        out_specs=jax.tree.map(lambda _: VMEM, shapes),
        scratch_shapes=scratch,
        compiler_params=pltpu.CompilerParams(vmem_limit_bytes=limit * 1024 * 1024),
    )(*args)


def iota(dims, dim):
    return lax.broadcasted_iota(jnp.int32, dims, dim)


def as_rows(line, rows):
    return jnp.concatenate(
        [line[:, j * HEAD_WIDTH : (j + 1) * HEAD_WIDTH] for j in range(rows)], axis=0
    )


def swap(value, n, distance):
    return lax.ppermute(value, "exp", [(t, t ^ distance) for t in range(n)])


def distance_of(column, far):
    bits = far.bit_length() - 1
    return sum(NEAR << i for i in range(bits) if column >> (bits - 1 - i) & 1)


def pad16(rows):
    return -(-rows // 16) * 16


def pack_kernel(query, resid, new, choice, probability, out, q_in, r_in, n_in, c_in, p_in, sems):
    copies = [
        pltpu.make_async_copy(source, target, sems.at[k])
        for k, (source, target) in enumerate(
            ((query, q_in), (resid, r_in), (new, n_in), (choice, c_in), (probability, p_in))
        )
    ]
    for copy in copies:
        copy.start()
    for copy in copies:
        copy.wait()
    q = as_rows(q_in[...].astype(f32), QUERY_HEADS)
    r = as_rows(r_in[...].astype(f32), QUERY_HEADS)
    fresh = as_rows(n_in[...].astype(f32), NEW_ROWS)
    p = p_in[...]
    shares = p / jnp.sum(p, axis=1, keepdims=True)
    lanes = iota((1, HEAD_WIDTH), 1)
    gates = jnp.zeros((1, HEAD_WIDTH), f32)
    for k in range(p.shape[1]):
        gates = gates + jnp.where(c_in[:, k : k + 1] == lanes, shares[:, k : k + 1], 0.0)
    rest = jnp.zeros((MESSAGE[0] - GATE_ROW - 1, HEAD_WIDTH), f32)
    out[0] = jnp.concatenate([q, r, fresh, gates, rest], axis=0).astype(bf16)


def join_kernel(mine, theirs, out):
    half = mine.shape[0]
    out[:half] = mine[...]
    out[half:] = theirs[...]


def narrow_kernel(mine, theirs, column, out):
    half = mine.shape[0]
    far = 2 * half
    column[:half] = mine[...]
    column[half:] = theirs[...]
    tails = []
    for w in range(far):
        source, at = (mine, w) if w < half else (theirs, w - half)
        out[w * QUERY_HEADS : (w + 1) * QUERY_HEADS] = source[at, :QUERY_HEADS]
        tails.append(source[at, NEW_ROW:].astype(f32))
    fresh = jnp.concatenate([tail[:NEW_ROWS] for tail in tails], axis=0)
    gates = jnp.concatenate([tail[NEW_ROWS : NEW_ROWS + 1] for tail in tails], axis=0)
    for rows, at in ((gates, far * QUERY_HEADS), (fresh, far * QUERY_HEADS + pad16(far))):
        extra = pad16(rows.shape[0]) - rows.shape[0]
        if extra:
            rows = jnp.concatenate([rows, jnp.zeros((extra, HEAD_WIDTH), f32)], axis=0)
        out[at : at + rows.shape[0]] = rows.astype(bf16)


def encode(top, total, acc):
    lanes = iota(HEADS, 1)
    stats = jnp.zeros(HEADS, f32)
    for at, value in ((0, top), (3, total)):
        for k in range(3):
            part = value.astype(bf16).astype(f32)
            stats = jnp.where(lanes == at + k, part, stats)
            value = value - part
    return jnp.concatenate([acc, stats], axis=0).astype(bf16)


def decode(message):
    value = message.astype(f32)
    acc, stats = value[:QUERY_HEADS], value[QUERY_HEADS:]
    top = stats[:, 0:1] + stats[:, 1:2] + stats[:, 2:3]
    total = stats[:, 3:4] + stats[:, 4:5] + stats[:, 5:6]
    return top, total, acc


def merged(parts):
    top = functools.reduce(jnp.maximum, [part[0] for part in parts])
    total, acc = 0.0, 0.0
    for peak, amount, value in parts:
        share = jnp.exp(peak - top)
        total = total + share * amount
        acc = acc + share * value
    return top, total, acc


def attend_kernel(lengths, mine, theirs, cache, keep, send, *, far):
    me = lax.axis_index("exp")
    sequences, block, _ = cache.shape
    rows = 2 * QUERY_HEADS
    first_group = (iota((rows, HEAD_WIDTH), 0) % QUERY_HEADS) < GROUPED
    positions = me * block + iota((rows, block), 1)
    for y in range(2):
        for w in range(far):
            s = lax.shift_right_logical(me, 1) ^ ((distance_of(w, far) >> 1) | y)
            cut = slice(w * QUERY_HEADS, (w + 1) * QUERY_HEADS)
            both = jnp.concatenate([mine[y, cut], theirs[y, cut]], axis=0)
            zero = jnp.zeros_like(both)
            wide = jnp.concatenate(
                [jnp.where(first_group, both, zero), jnp.where(first_group, zero, both)], axis=1
            )
            keys = cache[s, :, :KEY_VALUE_WIDTH]
            values = cache[s, :, KEY_VALUE_WIDTH:]
            scores = (
                lax.dot_general(
                    wide, keys, (((1,), (1,)), ((), ())), preferred_element_type=f32
                )
                * INV_ROOT
            )
            valid = positions < lengths[s]
            scores = jnp.where(valid, scores, floor_score)
            top = jnp.max(scores, axis=1, keepdims=True)
            weights = jnp.where(valid, jnp.exp(scores - top), 0.0).astype(bf16)
            total = jnp.sum(weights.astype(f32), axis=1, keepdims=True)
            acc = jnp.dot(weights, values, preferred_element_type=f32)
            acc = jnp.where(first_group, acc[:, :HEAD_WIDTH], acc[:, HEAD_WIDTH:])
            for part, cut in (
                (keep, slice(0, QUERY_HEADS)),
                (send, slice(QUERY_HEADS, 2 * QUERY_HEADS)),
            ):
                part[y * far + w] = encode(top[cut], total[cut], acc[cut])


def merge_kernel(mine, theirs, *outs, flip):
    count = mine.shape[0] // len(outs)
    for slot in range(mine.shape[0]):
        parts = [decode(mine[slot]), decode(theirs[slot ^ flip])]
        outs[slot // count][slot % count] = encode(*merged(parts))


def token_kernel(mine, theirs, column, near, scale, hidden_out, normed_out):
    second = lax.axis_index("exp") % 2 == 1
    first_group = iota(HEADS, 0) < GROUPED
    far = column.shape[0]
    near_at = far * QUERY_HEADS + pad16(far)
    others = near[0, near_at:].astype(f32)

    def by_head(rows, at):
        return jnp.where(first_group, rows[at : at + 1], rows[at + 1 : at + 2])

    for w in range(far):
        message = column[w].astype(f32)
        q, resid, new = message[:QUERY_HEADS], message[RESID_ROW:NEW_ROW], message[NEW_ROW:GATE_ROW]
        other = others[w * NEW_ROWS : (w + 1) * NEW_ROWS]
        own_score = jnp.sum(q * by_head(new, 0), axis=1, keepdims=True) * INV_ROOT
        other_score = jnp.sum(q * by_head(other, 0), axis=1, keepdims=True) * INV_ROOT
        other_score = jnp.where(second, other_score, floor_score)
        new_max = jnp.maximum(own_score, other_score)
        own_weight = jnp.exp(own_score - new_max).astype(bf16).astype(f32)
        other_weight = jnp.where(second, jnp.exp(other_score - new_max), 0.0)
        other_weight = other_weight.astype(bf16).astype(f32)
        fresh = own_weight * by_head(new, 2) + other_weight * by_head(other, 2)
        _, total, acc = merged(
            [
                decode(mine[w]),
                decode(theirs[w ^ 1]),
                (new_max, own_weight + other_weight, fresh),
            ]
        )
        hidden = resid + acc / total
        squares = jnp.sum(jnp.sum(hidden * hidden, axis=1, keepdims=True), axis=0, keepdims=True)
        normed = hidden * lax.rsqrt(squares / WIDTH + epsilon) * scale[...]
        if w == 0:
            hidden_out[...] = hidden
        normed_out[w] = normed.astype(bf16)


def dot_pair(value, factor, contract):
    high = value.astype(bf16)
    low = (value - high.astype(f32)).astype(bf16)
    both = lax.dot_general(
        jnp.concatenate([high, low], axis=0),
        factor,
        (((1,), (contract,)), ((), ())),
        preferred_element_type=f32,
    )
    return both[: value.shape[0]] + both[value.shape[0] :]


def expert_kernel(
    mine, theirs, near, next_near, gate_w, up_w, down_w, model, inner, keep, send, *, far
):
    me = lax.axis_index("exp")
    half = mine.shape[0]
    x = jnp.concatenate([mine[...].astype(f32), theirs[...].astype(f32)], axis=0)
    x = x.reshape(2 * half, WIDTH).astype(bf16)
    r = ADAPTER_RANK
    mixed = lax.dot_general(
        x, model[: 2 * r], (((1,), (1,)), ((), ())), preferred_element_type=f32
    )
    gate = jnp.dot(x, gate_w[...], preferred_element_type=f32)
    gate = gate + dot_pair(mixed[:, :r], inner[:, :r], 1)
    up = jnp.dot(x, up_w[...], preferred_element_type=f32)
    up = up + dot_pair(mixed[:, r:], inner[:, r : 2 * r], 1)
    act = (gate / (1.0 + jnp.exp(-gate)) * up).astype(bf16)
    lowered = jnp.dot(act, inner[:, 2 * r : 3 * r], preferred_element_type=f32)
    result = jnp.dot(act, down_w[...], preferred_element_type=f32)
    result = result + dot_pair(lowered, model[2 * r :], 0)
    lanes = iota((pad16(far), HEAD_WIDTH), 1)
    gate_at = far * QUERY_HEADS
    for c, (routes, part) in enumerate(((near, keep), (next_near, send))):
        for y in range(2):
            route = routes[y, gate_at : gate_at + pad16(far)].astype(f32)
            share = jnp.sum(jnp.where(lanes == me, route, 0.0), axis=1, keepdims=True)
            for w in range(far):
                slot = y * far + w
                line = result[c * half + slot : c * half + slot + 1] * share[w : w + 1]
                part[slot] = as_rows(line, QUERY_HEADS).astype(bf16)


def add_kernel(mine, theirs, keep, send):
    half = keep.shape[0]
    for out, at in ((keep, 0), (send, half)):
        total = mine[at : at + half].astype(f32) + theirs[at : at + half].astype(f32)
        out[...] = total.astype(bf16)


def finish_kernel(hidden, mine, theirs, out):
    total = hidden[...] + mine[0].astype(f32) + theirs[0].astype(f32)
    line = jnp.concatenate([total[j : j + 1] for j in range(QUERY_HEADS)], axis=1)
    out[...] = line.astype(bf16)


def lora_pack_kernel(after, model, inner, *outs):
    low = lax.axis_index("exp") % NEAR
    ranks = model.shape[1]
    for k, out in enumerate(outs):
        for z in range(out.shape[0]):
            at = z * NEAR + (low ^ k)
            out[z, :ranks] = model[at]
            out[z, ranks:, :ranks] = inner[at]
            out[z, ranks:, ranks:] = jnp.zeros(
                (out.shape[1] - ranks, HEAD_WIDTH - ranks), out.dtype
            )


def lora_turn_kernel(after, *refs):
    me = lax.axis_index("exp")
    low, high = me % NEAR, me // NEAR
    got, outs = refs[:NEAR], refs[NEAR:]
    for j, out in enumerate(outs):
        for k, ref in enumerate(got):
            out[low ^ k] = ref[high ^ j]


def lora_join_kernel(*refs):
    high = lax.axis_index("exp") // NEAR
    got, (model, inner) = refs[:-2], refs[-2:]
    ranks = model.shape[0]
    width = inner.shape[0] // (len(got) * NEAR)
    for j, ref in enumerate(got):
        for l in range(NEAR):
            at = (high ^ j) * NEAR + l
            columns = pl.ds(pl.multiple_of(at * HEAD_WIDTH, HEAD_WIDTH), HEAD_WIDTH)
            model[:, columns] = ref[l, :ranks]
            inner[pl.ds(pl.multiple_of(at * width, width), width)] = ref[l, ranks:]


def lora(adapter_model, adapter_hidden, n, after_first, after_second):
    total, ranks, model_width = adapter_model.shape
    inner_width = adapter_hidden.shape[2]
    inner = jnp.transpose(adapter_hidden, (0, 2, 1))
    if model_width != HEAD_WIDTH or inner_width % 16:
        model = lax.all_to_all(adapter_model, "exp", split_axis=0, concat_axis=2, tiled=True)
        inner = lax.all_to_all(inner, "exp", split_axis=0, concat_axis=1, tiled=True)
        return model[0], inner[0]
    far = n // NEAR
    packed = call(
        lora_pack_kernel,
        (shape((far, ranks + inner_width, HEAD_WIDTH), bf16),) * NEAR,
        [ANY, VMEM, VMEM],
        after_first,
        adapter_model,
        inner,
    )
    got = [packed[0]] + [swap(packed[k], n, k) for k in range(1, NEAR)]
    turned = call(
        lora_turn_kernel,
        (shape((NEAR, ranks + inner_width, HEAD_WIDTH), bf16),) * far,
        [ANY] + [VMEM] * NEAR,
        after_second,
        *got,
    )
    got = [turned[0]] + [swap(turned[j], n, j * NEAR) for j in range(1, far)]
    return call(
        lora_join_kernel,
        (
            shape((ranks, n * model_width), bf16),
            shape((n * inner_width, HEAD_WIDTH), bf16),
        ),
        [VMEM] * far,
        *got,
    )


def body(
    resid,
    queries,
    incoming_key_value,
    key_value_cache,
    lengths,
    norm_scale_vector,
    expert_choice,
    router_probability,
    gate_weight,
    up_weight,
    down_weight,
    adapter_model,
    adapter_hidden,
):
    n = lax.axis_size("exp")
    far = n // NEAR

    first_inputs = (queries, resid, incoming_key_value, expert_choice, router_probability)
    message = call(
        pack_kernel,
        shape((1,) + MESSAGE, bf16),
        [HBM] * 5,
        *[pltpu.with_memory_space_constraint(x, pltpu.HBM) for x in first_inputs],
        scratch=[pltpu.VMEM(x.shape, x.dtype) for x in first_inputs]
        + [pltpu.SemaphoreType.DMA((5,))],
    )
    distance, first_join = n // 2, message
    while distance > NEAR:
        message = call(
            join_kernel,
            shape((2 * message.shape[0],) + MESSAGE, bf16),
            [VMEM] * 2,
            message,
            swap(message, n, distance),
        )
        distance //= 2
    near_rows = far * QUERY_HEADS + pad16(far) + pad16(NEW_ROWS * far)
    column, narrow = call(
        narrow_kernel,
        (shape((far,) + MESSAGE, bf16), shape((near_rows, HEAD_WIDTH), bf16)),
        [VMEM] * 2,
        message,
        swap(message, n, NEAR),
    )
    narrow = narrow[None]
    near = call(
        join_kernel,
        shape((2, near_rows, HEAD_WIDTH), bf16),
        [VMEM] * 2,
        narrow,
        swap(narrow, n, 2),
    )
    next_near = swap(near, n, 1)
    keep, send = call(
        functools.partial(attend_kernel, far=far),
        (shape((2 * far,) + PARTIAL, bf16),) * 2,
        [SMEM] + [VMEM] * 3,
        lengths,
        near,
        next_near,
        key_value_cache,
    )
    first_part = keep
    keep, send = call(
        functools.partial(merge_kernel, flip=0),
        (shape((far,) + PARTIAL, bf16),) * 2,
        [VMEM] * 2,
        keep,
        swap(send, n, 1),
    )
    theirs, distance, flip = swap(send, n, 2), NEAR, 0
    while distance < n:
        keep = call(
            functools.partial(merge_kernel, flip=flip),
            shape((far,) + PARTIAL, bf16),
            [VMEM] * 2,
            keep,
            theirs,
        )
        theirs = swap(keep, n, distance)
        flip = far * NEAR // (2 * distance)
        distance *= 2
    hidden, normed = call(
        token_kernel,
        (shape(HEADS, f32), shape((far,) + HEADS, bf16)),
        [VMEM] * 5,
        keep,
        theirs,
        column,
        next_near,
        norm_scale_vector.reshape(HEADS),
    )
    rows = call(
        join_kernel, shape((2 * far,) + HEADS, bf16), [VMEM] * 2, normed, swap(normed, n, 2)
    )
    next_rows = swap(rows, n, 1)
    model, inner = lora(adapter_model, adapter_hidden, n, near, first_part)
    keep, send = call(
        functools.partial(expert_kernel, far=far),
        (shape((2 * far,) + HEADS, bf16),) * 2,
        [VMEM] * 9,
        rows,
        next_rows,
        near,
        next_near,
        gate_weight[0],
        up_weight[0],
        down_weight[0],
        model,
        inner,
        limit=32,
    )
    distance = 1
    while distance < n // 2:
        keep, send = call(
            add_kernel,
            (shape((keep.shape[0] // 2,) + HEADS, bf16),) * 2,
            [VMEM] * 2,
            keep,
            swap(send, n, distance),
        )
        distance *= 2
    return call(
        finish_kernel,
        shape((1, WIDTH), bf16),
        [VMEM] * 3,
        hidden,
        keep,
        swap(send, n, distance),
    )


def solution(mesh):
    return jax.shard_map(
        body,
        mesh=mesh,
        in_specs=(
            P(("grp", "exp"), None),
            P(("grp", "exp"), None),
            P(("grp", "exp"), None),
            P("grp", "exp", None),
            P("grp"),
            P(),
            P(("grp", "exp"), None),
            P(("grp", "exp"), None),
            P("exp", None, None),
            P("exp", None, None),
            P("exp", None, None),
            P(None, None, "exp"),
            P(None, None, "exp"),
        ),
        out_specs=P(("grp", "exp"), None),
        check_vma=False,
    )
```

time: 93.9 us -> 73.8 us (0.79)
  blocking collectives: 36.8 us -> 0 us
  waiting for transfers between devices: 5.96 us -> 30.7 us
  local copies, waits for them, and re-layouts: 21.1 us -> 8.46 us
  starting transfers between devices: 17.1 us -> 25.4 us
  Pallas kernels: 11.8 us -> 8.76 us
    all_to_all x4 -> x0, blocking collectives: 36.8 us -> none  [exchange(): lax.all_to_all(value, 'exp', split_axis=0, concat_axis=0, axis_index_grou...]
    ppermute x6 -> x20, waiting for transfers between devices: 5.95 us -> 30.7 us  [swap(): return lax.ppermute(value, 'exp', [(t, t ^ distance) for t in range(n)])]
    ppermute x6 -> x20, starting transfers between devices: 6.54 us -> 25.4 us  [swap(): return lax.ppermute(value, 'exp', [(t, t ^ distance) for t in range(n)])]
    unnamed x52 -> x16, local copies, waits for them, and re-layouts: 21.1 us -> 8.46 us
    all_to_all x3 -> x0, starting transfers between devices: 10.6 us -> none  [exchange(): lax.all_to_all(value, 'exp', split_axis=0, concat_axis=0, axis_index_grou...]
    pallas_call x11 -> x18, Pallas kernels: 11.8 us -> 8.76 us  [call(): pl.pallas_call(kernel, out_shape=shapes, in_specs=specs, out_specs=jax.tr...]
  transfers between devices with their start and end apart: 9 -> 20, of which waited for: 3 -> 13; matrix products, arithmetic and copies ran while one was open for 0% -> 0% of each run, Pallas kernels for 6% -> 6%
where the time goes in v4:
time: 73.8 us; the launch traced here: 73.5 us
  waiting for transfers between devices  30.7 us (42%)
  starting transfers between devices  25.4 us (34%)
  Pallas kernels  8.76 us (12%)
  local copies, waits for them, and re-layouts  8.46 us (11%)
    ppermute x20, waiting for transfers between devices, swap(): return lax.ppermute(value, 'exp', [(t, t ^ distance) for t in range(n)])  30.7 us
    ppermute x20, starting transfers between devices, swap(): return lax.ppermute(value, 'exp', [(t, t ^ distance) for t in range(n)])  25.4 us
    pallas_call x18, Pallas kernels, call(): pl.pallas_call(kernel, out_shape=shapes, in_specs=specs, out_specs=jax.tr...  8.76 us
    unnamed x16, local copies, waits for them, and re-layouts  8.46 us
  transfers between devices with their start and end apart: 20, of which 13 were waited for; matrix products, arithmetic and copies ran while one was open for 0% of the time, Pallas kernels for 6%

profile of v4, /device:TPU:0, one launch (start us, length us, event | category | flops | bytes accessed | tf_op | source)
XLA Modules:
  0.0 73.5 jit_solution(16107400644418831914)
XLA Ops:
  0.0 1.1 %shard_map.127.mine = bf16[1,48,128]{2,1,0:T(8,128)(2,1)S(1)} custom-call(bf16[1,2048]{1,0:T(2,128)(2,1)} %query.1, bf16[1,2048]{1,0:T(2,128)(2,1)} %resid.1, bf16[1,512]{1,0:T(2,128)(2,1)} %new.1, s32[1,8]{1,0:T(1,128)} %choice.1, f32[1,8]{1,0:T(1,128)} %probability.1), custom_call_target="tpu_custom_call" | custom-call | tf_op jit(solution)/shard_map/pallas_call | solution.py:39
  1.1 4.1 %collective-permute-start = (bf16[1,48,128]{2,1,0:T(8,128)(2,1)S(1)}, bf16[1,48,128]{2,1,0:T(8,128)(2,1)S(1)}, u32[]{:S(2)}, u32[]{:S(2)}) collective-permute-start(bf16[1,48,128]{2,1,0:T(8,128)(2,1)S(1)} %shard_map.127.mine), channel_id=1, source_target_pairs={{0,8},{1,9},{2,10},{3,11},{4,12},{5,13},{6,14},{7,15},{8,0},{9,1},... | collective-permute-start | bytes 36872 | tf_op jit(solution)/shard_map/ppermute | solution.py:60
  5.2 1.7 %collective-permute-done.theirs = bf16[1,48,128]{2,1,0:T(8,128)(2,1)S(1)} collective-permute-done((bf16[1,48,128]{2,1,0:T(8,128)(2,1)S(1)}, bf16[1,48,128]{2,1,0:T(8,128)(2,1)S(1)}, u32[]{:S(2)}, u32[]{:S(2)}) %collective-permute-start) | collective-permute-done | bytes 12320 | tf_op jit(solution)/shard_map/ppermute | solution.py:60
  6.9 1.9 %collective-permute-start.1 = (bf16[2,48,128]{2,1,0:T(8,128)(2,1)S(1)}, bf16[2,48,128]{2,1,0:T(8,128)(2,1)S(1)}, u32[]{:S(2)}, u32[]{:S(2)}) collective-permute-start(bf16[2,48,128]{2,1,0:T(8,128)(2,1)S(1)} %shard_map.128.mine), channel_id=1, source_target_pairs={{0,4},{1,5},{2,6},{3,7},{4,0},{5,1},{6,2},{7,3},{8,12},{9,13},{10,... | collective-permute-start | bytes 73736 | tf_op jit(solution)/shard_map/ppermute | solution.py:60
  8.8 1.9 %collective-permute-done.1.theirs = bf16[2,48,128]{2,1,0:T(8,128)(2,1)S(1)} collective-permute-done((bf16[2,48,128]{2,1,0:T(8,128)(2,1)S(1)}, bf16[2,48,128]{2,1,0:T(8,128)(2,1)S(1)}, u32[]{:S(2)}, u32[]{:S(2)}) %collective-permute-start.1) | collective-permute-done | bytes 24608 | tf_op jit(solution)/shard_map/ppermute | solution.py:60
  10.7 1.9 %collective-permute-start.2 = (bf16[1,96,128]{2,1,0:T(8,128)(2,1)S(1)}, bf16[1,96,128]{2,1,0:T(8,128)(2,1)S(1)}, u32[]{:S(2)}, u32[]{:S(2)}) collective-permute-start(bf16[1,96,128]{2,1,0:T(8,128)(2,1)S(1)} %bitcast.10), channel_id=1, source_target_pairs={{0,2},{1,3},{2,0},{3,1},{4,6},{5,7},{6,4},{7,5},{8,10},{9,11},{10,... | collective-permute-start | bytes 73736 | tf_op jit(solution)/shard_map/ppermute | solution.py:60
  12.7 2.0 %collective-permute-done.2.theirs = bf16[1,96,128]{2,1,0:T(8,128)(2,1)S(1)} collective-permute-done((bf16[1,96,128]{2,1,0:T(8,128)(2,1)S(1)}, bf16[1,96,128]{2,1,0:T(8,128)(2,1)S(1)}, u32[]{:S(2)}, u32[]{:S(2)}) %collective-permute-start.2) | collective-permute-done | bytes 24608 | tf_op jit(solution)/shard_map/ppermute | solution.py:60
  14.6 1.0 %copy-done.4 = bf16[16,96,128]{2,1,0:T(8,128)(2,1)S(1)} copy-done((bf16[16,96,128]{2,1,0:T(8,128)(2,1)S(1)}, bf16[16,96,128]{2,1,0:T(8,128)(2,1)}, u32[]{:S(2)}) %copy-start.4) | copy-done | bytes 393240
  15.6 0.9 %copy-done.5 = bf16[16,96,48]{1,2,0:T(8,128)(2,1)S(1)} copy-done((bf16[16,96,48]{1,2,0:T(8,128)(2,1)S(1)}, bf16[16,96,48]{1,2,0:T(8,128)(2,1)}, u32[]{:S(2)}) %copy-start.5) | copy-done | bytes 147480
  16.6 0.1 shard_map.137
  16.6 0.1 collective-permute-start.10
  16.7 1.9 %collective-permute-start.11 = (bf16[4,144,128]{2,1,0:T(8,128)(2,1)S(1)}, bf16[4,144,128]{2,1,0:T(8,128)(2,1)S(1)}, u32[]{:S(2)}, u32[]{:S(2)}) collective-permute-start(bf16[4,144,128]{2,1,0:T(8,128)(2,1)S(1)} %get-tuple-element.41), channel_id=1, source_target_pairs={{0,2},{1,3},{2,0},{3,1},{4,6},{5,7},{6,4},{7,5},{8,10},{9,11},{10,... | collective-permute-start | bytes 442376 | tf_op jit(solution)/shard_map/ppermute | solution.py:60
  18.7 0.2 collective-permute-start.3
  18.9 1.0 %collective-permute-done.3.theirs.near.next_near = bf16[2,96,128]{2,1,0:T(8,128)(2,1)S(1)} collective-permute-done((bf16[2,96,128]{2,1,0:T(8,128)(2,1)S(1)}, bf16[2,96,128]{2,1,0:T(8,128)(2,1)S(1)}, u32[]{:S(2)}, u32[]{:S(2)}) %collective-permute-start.3) | collective-permute-done | bytes 49184 | tf_op jit(solution)/shard_map/ppermute | solution.py:60
  19.9 1.4 %copy-done.3 = bf16[8,192,512]{2,1,0:T(8,128)(2,1)S(1)} copy-done((bf16[8,192,512]{2,1,0:T(8,128)(2,1)S(1)}, bf16[8,192,512]{2,1,0:T(8,128)(2,1)}, u32[]{:S(2)}) %copy-start.3) | copy-done | bytes 1572888
  21.3 0.7 copy-done.7
  22.0 2.7 %shard_map.131 = (bf16[8,32,128]{2,1,0:T(8,128)(2,1)S(1)}, bf16[8,32,128]{2,1,0:T(8,128)(2,1)S(1)}) custom-call(s32[8]{0:T(128)S(1)} %copy-done.7, bf16[2,96,128]{2,1,0:T(8,128)(2,1)S(1)} %shard_map.130.mine.after.near, bf16[2,96,128]{2,1,0:T(8,128)(2,1)S(1)} %collective-permute-done.3.theirs.near.next_near, bf16[8,192,512]{2,1,0:T(8,128)(2,1)S(1)} %copy-done.3), custom_call_target="tpu_custom_call" | custom-call | tf_op jit(solution)/shard_map/pallas_call | solution.py:39
  24.7 0.3 collective-permute-start.4
  25.0 1.0 %collective-permute-done.4.theirs = bf16[8,32,128]{2,1,0:T(8,128)(2,1)S(1)} collective-permute-done((bf16[8,32,128]{2,1,0:T(8,128)(2,1)S(1)}, bf16[8,32,128]{2,1,0:T(8,128)(2,1)S(1)}, u32[]{:S(2)}, u32[]{:S(2)}) %collective-permute-start.4) | collective-permute-done | bytes 65568 | tf_op jit(solution)/shard_map/ppermute | solution.py:60
  26.0 0.5 shard_map.132
  26.5 1.8 %collective-permute-start.5 = (bf16[4,32,128]{2,1,0:T(8,128)(2,1)S(1)}, bf16[4,32,128]{2,1,0:T(8,128)(2,1)S(1)}, u32[]{:S(2)}, u32[]{:S(2)}) collective-permute-start(bf16[4,32,128]{2,1,0:T(8,128)(2,1)S(1)} %get-tuple-element.35), channel_id=1, source_target_pairs={{0,2},{1,3},{2,0},{3,1},{4,6},{5,7},{6,4},{7,5},{8,10},{9,11},{10,... | collective-permute-start | bytes 98312 | tf_op jit(solution)/shard_map/ppermute | solution.py:60
  28.4 1.6 %collective-permute-start.13 = (bf16[4,144,128]{2,1,0:T(8,128)(2,1)S(1)}, bf16[4,144,128]{2,1,0:T(8,128)(2,1)S(1)}, u32[]{:S(2)}, u32[]{:S(2)}) collective-permute-start(bf16[4,144,128]{2,1,0:T(8,128)(2,1)S(1)} %get-tuple-element.44), channel_id=1, source_target_pairs={{0,4},{1,5},{2,6},{3,7},{4,0},{5,1},{6,2},{7,3},{8,12},{9,13},{10,... | collective-permute-start | bytes 442376 | tf_op jit(solution)/shard_map/ppermute | solution.py:60
  30.0 2.6 %collective-permute-start.14 = (bf16[4,144,128]{2,1,0:T(8,128)(2,1)S(1)}, bf16[4,144,128]{2,1,0:T(8,128)(2,1)S(1)}, u32[]{:S(2)}, u32[]{:S(2)}) collective-permute-start(bf16[4,144,128]{2,1,0:T(8,128)(2,1)S(1)} %get-tuple-element.45), channel_id=1, source_target_pairs={{0,8},{1,9},{2,10},{3,11},{4,12},{5,13},{6,14},{7,15},{8,0},{9,1},... | collective-permute-start | bytes 442376 | tf_op jit(solution)/shard_map/ppermute | solution.py:60
  32.6 0.2 collective-permute-start.15
  32.8 0.2 shard_map.133.mine
  33.1 0.7 collective-permute-start.6
  33.8 6.6 %collective-permute-done.6.theirs = bf16[4,32,128]{2,1,0:T(8,128)(2,1)S(1)} collective-permute-done((bf16[4,32,128]{2,1,0:T(8,128)(2,1)S(1)}, bf16[4,32,128]{2,1,0:T(8,128)(2,1)S(1)}, u32[]{:S(2)}, u32[]{:S(2)}) %collective-permute-start.6) | collective-permute-done | bytes 32800 | tf_op jit(solution)/shard_map/ppermute | solution.py:60
  40.4 0.2 shard_map.134.mine
  40.6 3.6 %collective-permute-start.7 = (bf16[4,32,128]{2,1,0:T(8,128)(2,1)S(1)}, bf16[4,32,128]{2,1,0:T(8,128)(2,1)S(1)}, u32[]{:S(2)}, u32[]{:S(2)}) collective-permute-start(bf16[4,32,128]{2,1,0:T(8,128)(2,1)S(1)} %shard_map.134.mine), channel_id=1, source_target_pairs={{0,8},{1,9},{2,10},{3,11},{4,12},{5,13},{6,14},{7,15},{8,0},{9,1},... | collective-permute-start | bytes 98312 | tf_op jit(solution)/shard_map/ppermute | solution.py:60
  44.2 2.8 %collective-permute-done.7.theirs = bf16[4,32,128]{2,1,0:T(8,128)(2,1)S(1)} collective-permute-done((bf16[4,32,128]{2,1,0:T(8,128)(2,1)S(1)}, bf16[4,32,128]{2,1,0:T(8,128)(2,1)S(1)}, u32[]{:S(2)}, u32[]{:S(2)}) %collective-permute-start.7) | collective-permute-done | bytes 32800 | tf_op jit(solution)/shard_map/ppermute | solution.py:60
  47.0 0.7 copy-done.6
  47.7 0.4 shard_map.135
  48.1 0.6 collective-permute-start.8
  48.6 3.2 %collective-permute-done.8.theirs = bf16[4,16,128]{2,1,0:T(8,128)(2,1)S(1)} collective-permute-done((bf16[4,16,128]{2,1,0:T(8,128)(2,1)S(1)}, bf16[4,16,128]{2,1,0:T(8,128)(2,1)S(1)}, u32[]{:S(2)}, u32[]{:S(2)}) %collective-permute-start.8) | collective-permute-done | bytes 16416 | tf_op jit(solution)/shard_map/ppermute | solution.py:60
  51.9 0.1 shard_map.139
  52.0 1.1 %collective-permute-done.9.theirs = bf16[8,16,128]{2,1,0:T(8,128)(2,1)S(1)} collective-permute-done((bf16[8,16,128]{2,1,0:T(8,128)(2,1)S(1)}, bf16[8,16,128]{2,1,0:T(8,128)(2,1)S(1)}, u32[]{:S(2)}, u32[]{:S(2)}) %collective-permute-start.9) | collective-permute-done | bytes 32800 | tf_op jit(solution)/shard_map/ppermute | solution.py:60
  53.1 1.9 %copy-done.1 = bf16[1,2048,768]{2,1,0:T(8,128)(2,1)S(1)} copy-done((bf16[1,2048,768]{2,1,0:T(8,128)(2,1)S(1)}, bf16[1,2048,768]{2,1,0:T(8,128)(2,1)}, u32[]{:S(2)}) %copy-start.1) | copy-done | bytes 3145752
  55.0 1.9 %copy-done.2 = bf16[1,768,2048]{2,1,0:T(8,128)(2,1)S(1)} copy-done((bf16[1,768,2048]{2,1,0:T(8,128)(2,1)S(1)}, bf16[1,768,2048]{2,1,0:T(8,128)(2,1)}, u32[]{:S(2)}) %copy-start.2) | copy-done | bytes 3145752
  56.9 2.8 %shard_map.140 = (bf16[8,16,128]{2,1,0:T(8,128)(2,1)S(1)}, bf16[8,16,128]{2,1,0:T(8,128)(2,1)S(1)}) custom-call(bf16[8,16,128]{2,1,0:T(8,128)(2,1)S(1)} %shard_map.136.mine, bf16[8,16,128]{2,1,0:T(8,128)(2,1)S(1)} %collective-permute-done.9.theirs, bf16[2,96,128]{2,1,0:T(8,128)(2,1)S(1)} %shard_map.130.mine.after.near, ...), custom_call_target="tpu_custom_call" | custom-call | tf_op jit(solution)/shard_map/pallas_call | solution.py:39
  59.6 0.2 collective-permute-start.16
  59.9 1.0 %collective-permute-done.16.theirs = bf16[8,16,128]{2,1,0:T(8,128)(2,1)S(1)} collective-permute-done((bf16[8,16,128]{2,1,0:T(8,128)(2,1)S(1)}, bf16[8,16,128]{2,1,0:T(8,128)(2,1)S(1)}, u32[]{:S(2)}, u32[]{:S(2)}) %collective-permute-start.16) | collective-permute-done | bytes 32800 | tf_op jit(solution)/shard_map/ppermute | solution.py:60
  60.9 0.6 collective-permute-start.17
  61.5 3.2 %collective-permute-done.17.theirs = bf16[4,16,128]{2,1,0:T(8,128)(2,1)S(1)} collective-permute-done((bf16[4,16,128]{2,1,0:T(8,128)(2,1)S(1)}, bf16[4,16,128]{2,1,0:T(8,128)(2,1)S(1)}, u32[]{:S(2)}, u32[]{:S(2)}) %collective-permute-start.17) | collective-permute-done | bytes 16416 | tf_op jit(solution)/shard_map/ppermute | solution.py:60
  64.7 1.0 %collective-permute-start.18 = (bf16[2,16,128]{2,1,0:T(8,128)(2,1)S(1)}, bf16[2,16,128]{2,1,0:T(8,128)(2,1)S(1)}, u32[]{:S(2)}, u32[]{:S(2)}) collective-permute-start(bf16[2,16,128]{2,1,0:T(8,128)(2,1)S(1)} %get-tuple-element.54), channel_id=1, source_target_pairs={{0,4},{1,5},{2,6},{3,7},{4,0},{5,1},{6,2},{7,3},{8,12},{9,13},{10,... | collective-permute-start | bytes 24584 | tf_op jit(solution)/shard_map/ppermute | solution.py:60
  65.7 2.7 %collective-permute-done.18.theirs = bf16[2,16,128]{2,1,0:T(8,128)(2,1)S(1)} collective-permute-done((bf16[2,16,128]{2,1,0:T(8,128)(2,1)S(1)}, bf16[2,16,128]{2,1,0:T(8,128)(2,1)S(1)}, u32[]{:S(2)}, u32[]{:S(2)}) %collective-permute-start.18) | collective-permute-done | bytes 8224 | tf_op jit(solution)/shard_map/ppermute | solution.py:60
  68.4 2.0 %collective-permute-start.19 = (bf16[1,16,128]{2,1,0:T(8,128)(2,1)S(1)}, bf16[1,16,128]{2,1,0:T(8,128)(2,1)S(1)}, u32[]{:S(2)}, u32[]{:S(2)}) collective-permute-start(bf16[1,16,128]{2,1,0:T(8,128)(2,1)S(1)} %get-tuple-element.56), channel_id=1, source_target_pairs={{0,8},{1,9},{2,10},{3,11},{4,12},{5,13},{6,14},{7,15},{8,0},{9,1},... | collective-permute-start | bytes 12296 | tf_op jit(solution)/shard_map/ppermute | solution.py:60
  70.4 2.5 %collective-permute-done.19.theirs = bf16[1,16,128]{2,1,0:T(8,128)(2,1)S(1)} collective-permute-done((bf16[1,16,128]{2,1,0:T(8,128)(2,1)S(1)}, bf16[1,16,128]{2,1,0:T(8,128)(2,1)S(1)}, u32[]{:S(2)}, u32[]{:S(2)}) %collective-permute-start.19) | collective-permute-done | bytes 4128 | tf_op jit(solution)/shard_map/ppermute | solution.py:60
  72.9 0.6 shard_map.144
  (26 shorter events, 0.2 us)
Async XLA Ops:
  0.0 53.1 %copy-start = (bf16[1,2048,768]{2,1,0:T(8,128)(2,1)S(1)}, bf16[1,2048,768]{2,1,0:T(8,128)(2,1)}, u32[]{:S(2)}) copy-start(bf16[1,2048,768]{2,1,0:T(8,128)(2,1)} %param.21) | copy-start | bytes 9437188
  1.1 5.8 %collective-permute-start = (bf16[1,48,128]{2,1,0:T(8,128)(2,1)S(1)}, bf16[1,48,128]{2,1,0:T(8,128)(2,1)S(1)}, u32[]{:S(2)}, u32[]{:S(2)}) collective-permute-start(bf16[1,48,128]{2,1,0:T(8,128)(2,1)S(1)} %shard_map.127.mine), channel_id=1, source_target_pairs={{0,8},{1,9},{2,10},{3,11},{4,12},{5,13},{6,14},{7,15},{8,0},{9,1},... | collective-permute-start | bytes 36872 | tf_op jit(solution)/shard_map/ppermute | solution.py:60
  6.9 3.8 %collective-permute-start.1 = (bf16[2,48,128]{2,1,0:T(8,128)(2,1)S(1)}, bf16[2,48,128]{2,1,0:T(8,128)(2,1)S(1)}, u32[]{:S(2)}, u32[]{:S(2)}) collective-permute-start(bf16[2,48,128]{2,1,0:T(8,128)(2,1)S(1)} %shard_map.128.mine), channel_id=1, source_target_pairs={{0,4},{1,5},{2,6},{3,7},{4,0},{5,1},{6,2},{7,3},{8,12},{9,13},{10,... | collective-permute-start | bytes 73736 | tf_op jit(solution)/shard_map/ppermute | solution.py:60
  10.7 3.9 %collective-permute-start.2 = (bf16[1,96,128]{2,1,0:T(8,128)(2,1)S(1)}, bf16[1,96,128]{2,1,0:T(8,128)(2,1)S(1)}, u32[]{:S(2)}, u32[]{:S(2)}) collective-permute-start(bf16[1,96,128]{2,1,0:T(8,128)(2,1)S(1)} %bitcast.10), channel_id=1, source_target_pairs={{0,2},{1,3},{2,0},{3,1},{4,6},{5,7},{6,4},{7,5},{8,10},{9,11},{10,... | collective-permute-start | bytes 73736 | tf_op jit(solution)/shard_map/ppermute | solution.py:60
  14.6 1.0 %copy-start.4 = (bf16[16,96,128]{2,1,0:T(8,128)(2,1)S(1)}, bf16[16,96,128]{2,1,0:T(8,128)(2,1)}, u32[]{:S(2)}) copy-start(bf16[16,96,128]{2,1,0:T(8,128)(2,1)} %model.1) | copy-start | bytes 1179652
  15.6 0.9 %copy-start.5 = (bf16[16,96,48]{1,2,0:T(8,128)(2,1)S(1)}, bf16[16,96,48]{1,2,0:T(8,128)(2,1)}, u32[]{:S(2)}) copy-start(bf16[16,96,48]{1,2,0:T(8,128)(2,1)} %param.25) | copy-start | bytes 442372
  16.6 11.6 %collective-permute-start.10 = (bf16[4,144,128]{2,1,0:T(8,128)(2,1)S(1)}, bf16[4,144,128]{2,1,0:T(8,128)(2,1)S(1)}, u32[]{:S(2)}, u32[]{:S(2)}) collective-permute-start(bf16[4,144,128]{2,1,0:T(8,128)(2,1)S(1)} %get-tuple-element.40), channel_id=1, source_target_pairs={{0,1},{1,0},{2,3},{3,2},{4,5},{5,4},{6,7},{7,6},{8,9},{9,8},{10,11... | collective-permute-start | bytes 442376 | tf_op jit(solution)/shard_map/ppermute | solution.py:60
  16.7 11.6 %collective-permute-start.11 = (bf16[4,144,128]{2,1,0:T(8,128)(2,1)S(1)}, bf16[4,144,128]{2,1,0:T(8,128)(2,1)S(1)}, u32[]{:S(2)}, u32[]{:S(2)}) collective-permute-start(bf16[4,144,128]{2,1,0:T(8,128)(2,1)S(1)} %get-tuple-element.41), channel_id=1, source_target_pairs={{0,2},{1,3},{2,0},{3,1},{4,6},{5,7},{6,4},{7,5},{8,10},{9,11},{10,... | collective-permute-start | bytes 442376 | tf_op jit(solution)/shard_map/ppermute | solution.py:60
  18.6 9.6 %collective-permute-start.12 = (bf16[4,144,128]{2,1,0:T(8,128)(2,1)S(1)}, bf16[4,144,128]{2,1,0:T(8,128)(2,1)S(1)}, u32[]{:S(2)}, u32[]{:S(2)}) collective-permute-start(bf16[4,144,128]{2,1,0:T(8,128)(2,1)S(1)} %get-tuple-element.42), channel_id=1, source_target_pairs={{0,3},{1,2},{2,1},{3,0},{4,7},{5,6},{6,5},{7,4},{8,11},{9,10},{10,... | collective-permute-start | bytes 442376 | tf_op jit(solution)/shard_map/ppermute | solution.py:60
  18.7 1.2 %collective-permute-start.3 = (bf16[2,96,128]{2,1,0:T(8,128)(2,1)S(1)}, bf16[2,96,128]{2,1,0:T(8,128)(2,1)S(1)}, u32[]{:S(2)}, u32[]{:S(2)}) collective-permute-start(bf16[2,96,128]{2,1,0:T(8,128)(2,1)S(1)} %shard_map.130.mine.after.near), channel_id=1, source_target_pairs={{0,1},{1,0},{2,3},{3,2},{4,5},{5,4},{6,7},{7,6},{8,9},{9,8},{10,11... | collective-permute-start | bytes 147464 | tf_op jit(solution)/shard_map/ppermute | solution.py:60
  19.9 1.4 %copy-start.3 = (bf16[8,192,512]{2,1,0:T(8,128)(2,1)S(1)}, bf16[8,192,512]{2,1,0:T(8,128)(2,1)}, u32[]{:S(2)}) copy-start(bf16[8,192,512]{2,1,0:T(8,128)(2,1)} %cache.1) | copy-start | bytes 4718596
  21.3 0.7 copy-start.7
  24.7 1.3 %collective-permute-start.4 = (bf16[8,32,128]{2,1,0:T(8,128)(2,1)S(1)}, bf16[8,32,128]{2,1,0:T(8,128)(2,1)S(1)}, u32[]{:S(2)}, u32[]{:S(2)}) collective-permute-start(bf16[8,32,128]{2,1,0:T(8,128)(2,1)S(1)} %get-tuple-element.33), channel_id=1, source_target_pairs={{0,1},{1,0},{2,3},{3,2},{4,5},{5,4},{6,7},{7,6},{8,9},{9,8},{10,11... | collective-permute-start | bytes 196616 | tf_op jit(solution)/shard_map/ppermute | solution.py:60
  26.5 6.3 %collective-permute-start.5 = (bf16[4,32,128]{2,1,0:T(8,128)(2,1)S(1)}, bf16[4,32,128]{2,1,0:T(8,128)(2,1)S(1)}, u32[]{:S(2)}, u32[]{:S(2)}) collective-permute-start(bf16[4,32,128]{2,1,0:T(8,128)(2,1)S(1)} %get-tuple-element.35), channel_id=1, source_target_pairs={{0,2},{1,3},{2,0},{3,1},{4,6},{5,7},{6,4},{7,5},{8,10},{9,11},{10,... | collective-permute-start | bytes 98312 | tf_op jit(solution)/shard_map/ppermute | solution.py:60
  28.4 23.5 %collective-permute-start.13 = (bf16[4,144,128]{2,1,0:T(8,128)(2,1)S(1)}, bf16[4,144,128]{2,1,0:T(8,128)(2,1)S(1)}, u32[]{:S(2)}, u32[]{:S(2)}) collective-permute-start(bf16[4,144,128]{2,1,0:T(8,128)(2,1)S(1)} %get-tuple-element.44), channel_id=1, source_target_pairs={{0,4},{1,5},{2,6},{3,7},{4,0},{5,1},{6,2},{7,3},{8,12},{9,13},{10,... | collective-permute-start | bytes 442376 | tf_op jit(solution)/shard_map/ppermute | solution.py:60
  30.0 21.9 %collective-permute-start.14 = (bf16[4,144,128]{2,1,0:T(8,128)(2,1)S(1)}, bf16[4,144,128]{2,1,0:T(8,128)(2,1)S(1)}, u32[]{:S(2)}, u32[]{:S(2)}) collective-permute-start(bf16[4,144,128]{2,1,0:T(8,128)(2,1)S(1)} %get-tuple-element.45), channel_id=1, source_target_pairs={{0,8},{1,9},{2,10},{3,11},{4,12},{5,13},{6,14},{7,15},{8,0},{9,1},... | collective-permute-start | bytes 442376 | tf_op jit(solution)/shard_map/ppermute | solution.py:60
  32.6 19.3 %collective-permute-start.15 = (bf16[4,144,128]{2,1,0:T(8,128)(2,1)S(1)}, bf16[4,144,128]{2,1,0:T(8,128)(2,1)S(1)}, u32[]{:S(2)}, u32[]{:S(2)}) collective-permute-start(bf16[4,144,128]{2,1,0:T(8,128)(2,1)S(1)} %get-tuple-element.46), channel_id=1, source_target_pairs={{0,12},{1,13},{2,14},{3,15},{4,8},{5,9},{6,10},{7,11},{8,4},{9,5},... | collective-permute-start | bytes 442376 | tf_op jit(solution)/shard_map/ppermute | solution.py:60
  33.1 7.3 %collective-permute-start.6 = (bf16[4,32,128]{2,1,0:T(8,128)(2,1)S(1)}, bf16[4,32,128]{2,1,0:T(8,128)(2,1)S(1)}, u32[]{:S(2)}, u32[]{:S(2)}) collective-permute-start(bf16[4,32,128]{2,1,0:T(8,128)(2,1)S(1)} %shard_map.133.mine), channel_id=1, source_target_pairs={{0,4},{1,5},{2,6},{3,7},{4,0},{5,1},{6,2},{7,3},{8,12},{9,13},{10,... | collective-permute-start | bytes 98312 | tf_op jit(solution)/shard_map/ppermute | solution.py:60
  40.6 6.4 %collective-permute-start.7 = (bf16[4,32,128]{2,1,0:T(8,128)(2,1)S(1)}, bf16[4,32,128]{2,1,0:T(8,128)(2,1)S(1)}, u32[]{:S(2)}, u32[]{:S(2)}) collective-permute-start(bf16[4,32,128]{2,1,0:T(8,128)(2,1)S(1)} %shard_map.134.mine), channel_id=1, source_target_pairs={{0,8},{1,9},{2,10},{3,11},{4,12},{5,13},{6,14},{7,15},{8,0},{9,1},... | collective-permute-start | bytes 98312 | tf_op jit(solution)/shard_map/ppermute | solution.py:60
  47.0 0.7 copy-start.6
  48.1 3.8 %collective-permute-start.8 = (bf16[4,16,128]{2,1,0:T(8,128)(2,1)S(1)}, bf16[4,16,128]{2,1,0:T(8,128)(2,1)S(1)}, u32[]{:S(2)}, u32[]{:S(2)}) collective-permute-start(bf16[4,16,128]{2,1,0:T(8,128)(2,1)S(1)} %get-tuple-element.38.mine), channel_id=1, source_target_pairs={{0,2},{1,3},{2,0},{3,1},{4,6},{5,7},{6,4},{7,5},{8,10},{9,11},{10,... | collective-permute-start | bytes 49160 | tf_op jit(solution)/shard_map/ppermute | solution.py:60
  51.9 1.2 %collective-permute-start.9 = (bf16[8,16,128]{2,1,0:T(8,128)(2,1)S(1)}, bf16[8,16,128]{2,1,0:T(8,128)(2,1)S(1)}, u32[]{:S(2)}, u32[]{:S(2)}) collective-permute-start(bf16[8,16,128]{2,1,0:T(8,128)(2,1)S(1)} %shard_map.136.mine), channel_id=1, source_target_pairs={{0,1},{1,0},{2,3},{3,2},{4,5},{5,4},{6,7},{7,6},{8,9},{9,8},{10,11... | collective-permute-start | bytes 98312 | tf_op jit(solution)/shard_map/ppermute | solution.py:60
  53.1 1.9 %copy-start.1 = (bf16[1,2048,768]{2,1,0:T(8,128)(2,1)S(1)}, bf16[1,2048,768]{2,1,0:T(8,128)(2,1)}, u32[]{:S(2)}) copy-start(bf16[1,2048,768]{2,1,0:T(8,128)(2,1)} %param.22) | copy-start | bytes 9437188
  55.0 1.9 %copy-start.2 = (bf16[1,768,2048]{2,1,0:T(8,128)(2,1)S(1)}, bf16[1,768,2048]{2,1,0:T(8,128)(2,1)}, u32[]{:S(2)}) copy-start(bf16[1,768,2048]{2,1,0:T(8,128)(2,1)} %param.23) | copy-start | bytes 9437188
  59.6 1.3 %collective-permute-start.16 = (bf16[8,16,128]{2,1,0:T(8,128)(2,1)S(1)}, bf16[8,16,128]{2,1,0:T(8,128)(2,1)S(1)}, u32[]{:S(2)}, u32[]{:S(2)}) collective-permute-start(bf16[8,16,128]{2,1,0:T(8,128)(2,1)S(1)} %get-tuple-element.50), channel_id=1, source_target_pairs={{0,1},{1,0},{2,3},{3,2},{4,5},{5,4},{6,7},{7,6},{8,9},{9,8},{10,11... | collective-permute-start | bytes 98312 | tf_op jit(solution)/shard_map/ppermute | solution.py:60
  60.9 3.8 %collective-permute-start.17 = (bf16[4,16,128]{2,1,0:T(8,128)(2,1)S(1)}, bf16[4,16,128]{2,1,0:T(8,128)(2,1)S(1)}, u32[]{:S(2)}, u32[]{:S(2)}) collective-permute-start(bf16[4,16,128]{2,1,0:T(8,128)(2,1)S(1)} %get-tuple-element.52), channel_id=1, source_target_pairs={{0,2},{1,3},{2,0},{3,1},{4,6},{5,7},{6,4},{7,5},{8,10},{9,11},{10,... | collective-permute-start | bytes 49160 | tf_op jit(solution)/shard_map/ppermute | solution.py:60
  64.7 3.7 %collective-permute-start.18 = (bf16[2,16,128]{2,1,0:T(8,128)(2,1)S(1)}, bf16[2,16,128]{2,1,0:T(8,128)(2,1)S(1)}, u32[]{:S(2)}, u32[]{:S(2)}) collective-permute-start(bf16[2,16,128]{2,1,0:T(8,128)(2,1)S(1)} %get-tuple-element.54), channel_id=1, source_target_pairs={{0,4},{1,5},{2,6},{3,7},{4,0},{5,1},{6,2},{7,3},{8,12},{9,13},{10,... | collective-permute-start | bytes 24584 | tf_op jit(solution)/shard_map/ppermute | solution.py:60
  68.4 4.5 %collective-permute-start.19 = (bf16[1,16,128]{2,1,0:T(8,128)(2,1)S(1)}, bf16[1,16,128]{2,1,0:T(8,128)(2,1)S(1)}, u32[]{:S(2)}, u32[]{:S(2)}) collective-permute-start(bf16[1,16,128]{2,1,0:T(8,128)(2,1)S(1)} %get-tuple-element.56), channel_id=1, source_target_pairs={{0,8},{1,9},{2,10},{3,11},{4,12},{5,13},{6,14},{7,15},{8,0},{9,1},... | collective-permute-start | bytes 12296 | tf_op jit(solution)/shard_map/ppermute | solution.py:60

commit v5 on v4

--- a/solution.py
+++ b/solution.py
@@ -35,15 +35,32 @@
 bf16, f32 = jnp.bfloat16, jnp.float32
 
 
-def call(kernel, shapes, specs, *args, limit=8, scratch=()):
+def call(kernel, shapes, specs, *args, limit=8, scratch=(), nanos=50):
     return pl.pallas_call(
         kernel,
         out_shape=shapes,
         in_specs=specs,
         out_specs=jax.tree.map(lambda _: VMEM, shapes),
         scratch_shapes=scratch,
+        cost_estimate=pl.CostEstimate(
+            flops=nanos * 1000000, transcendentals=0, bytes_accessed=0
+        ),
         compiler_params=pltpu.CompilerParams(vmem_limit_bytes=limit * 1024 * 1024),
     )(*args)
+
+
+def hold_kernel(value, after, out):
+    pass
+
+
+def hold(value, after):
+    return pl.pallas_call(
+        hold_kernel,
+        out_shape=shape(value.shape, value.dtype),
+        in_specs=[ANY, ANY],
+        out_specs=ANY,
+        input_output_aliases={0: 0},
+    )(value, after)
 
 
 def iota(dims, dim):
@@ -147,7 +164,7 @@
     return top, total, acc
 
 
-def attend_kernel(lengths, mine, theirs, cache, keep, send, *, far):
+def attend_kernel(after, lengths, mine, theirs, cache, keep, send, *, far):
     me = lax.axis_index("exp")
     sequences, block, _ = cache.shape
     rows = 2 * QUERY_HEADS
@@ -319,38 +336,46 @@
             inner[pl.ds(pl.multiple_of(at * width, width), width)] = ref[l, ranks:]
 
 
-def lora(adapter_model, adapter_hidden, n, after_first, after_second):
+def lora_near(adapter_model, adapter_hidden, n, marks):
     total, ranks, model_width = adapter_model.shape
     inner_width = adapter_hidden.shape[2]
     inner = jnp.transpose(adapter_hidden, (0, 2, 1))
     if model_width != HEAD_WIDTH or inner_width % 16:
         model = lax.all_to_all(adapter_model, "exp", split_axis=0, concat_axis=2, tiled=True)
         inner = lax.all_to_all(inner, "exp", split_axis=0, concat_axis=1, tiled=True)
-        return model[0], inner[0]
+        return [model[0], inner[0]], True
     far = n // NEAR
     packed = call(
         lora_pack_kernel,
         (shape((far, ranks + inner_width, HEAD_WIDTH), bf16),) * NEAR,
         [ANY, VMEM, VMEM],
-        after_first,
+        marks[0],
         adapter_model,
         inner,
     )
-    got = [packed[0]] + [swap(packed[k], n, k) for k in range(1, NEAR)]
+    got = [packed[0]]
+    for k in range(1, NEAR):
+        got.append(swap(hold(packed[k], marks[1 + k // 3]), n, k))
     turned = call(
         lora_turn_kernel,
         (shape((NEAR, ranks + inner_width, HEAD_WIDTH), bf16),) * far,
         [ANY] + [VMEM] * NEAR,
-        after_second,
+        marks[3],
         *got,
     )
-    got = [turned[0]] + [swap(turned[j], n, j * NEAR) for j in range(1, far)]
+    return turned, False
+
+
+def lora_far(turned, n, marks):
+    far = len(turned)
+    rows = turned[0].shape[1]
+    ranks = 3 * ADAPTER_RANK
+    got = [turned[0]]
+    for j in range(1, far):
+        got.append(swap(hold(turned[j], marks[min(j - 1, len(marks) - 1)]), n, j * NEAR))
     return call(
         lora_join_kernel,
-        (
-            shape((ranks, n * model_width), bf16),
-            shape((n * inner_width, HEAD_WIDTH), bf16),
-        ),
+        (shape((ranks, n * HEAD_WIDTH), bf16), shape((n * (rows - ranks), HEAD_WIDTH), bf16)),
         [VMEM] * far,
         *got,
     )
@@ -382,8 +407,9 @@
         *[pltpu.with_memory_space_constraint(x, pltpu.HBM) for x in first_inputs],
         scratch=[pltpu.VMEM(x.shape, x.dtype) for x in first_inputs]
         + [pltpu.SemaphoreType.DMA((5,))],
-    )
-    distance, first_join = n // 2, message
+        nanos=4000,
+    )
+    marks, distance = [message], n // 2
     while distance > NEAR:
         message = call(
             join_kernel,
@@ -401,6 +427,7 @@
         message,
         swap(message, n, NEAR),
     )
+    marks += [message, column]
     narrow = narrow[None]
     near = call(
         join_kernel,
@@ -409,17 +436,21 @@
         narrow,
         swap(narrow, n, 2),
     )
+    marks.append(near)
+    turned, whole = lora_near(adapter_model, adapter_hidden, n, marks)
     next_near = swap(near, n, 1)
     keep, send = call(
         functools.partial(attend_kernel, far=far),
         (shape((2 * far,) + PARTIAL, bf16),) * 2,
-        [SMEM] + [VMEM] * 3,
+        [ANY, SMEM] + [VMEM] * 3,
+        turned[0],
         lengths,
         near,
         next_near,
         key_value_cache,
-    )
-    first_part = keep
+        nanos=8000,
+    )
+    marks = [keep]
     keep, send = call(
         functools.partial(merge_kernel, flip=0),
         (shape((far,) + PARTIAL, bf16),) * 2,
@@ -427,6 +458,7 @@
         keep,
         swap(send, n, 1),
     )
+    marks.append(keep)
     theirs, distance, flip = swap(send, n, 2), NEAR, 0
     while distance < n:
         keep = call(
@@ -436,6 +468,7 @@
             keep,
             theirs,
         )
+        marks.append(keep)
         theirs = swap(keep, n, distance)
         flip = far * NEAR // (2 * distance)
         distance *= 2
@@ -453,7 +486,7 @@
         join_kernel, shape((2 * far,) + HEADS, bf16), [VMEM] * 2, normed, swap(normed, n, 2)
     )
     next_rows = swap(rows, n, 1)
-    model, inner = lora(adapter_model, adapter_hidden, n, near, first_part)
+    model, inner = turned if whole else lora_far(turned, n, marks)
     keep, send = call(
         functools.partial(expert_kernel, far=far),
         (shape((2 * far,) + HEADS, bf16),) * 2,

time: 73.8 us -> 78.6 us (1.065)
  local copies, waits for them, and re-layouts: 8.46 us -> 14 us
  starting transfers between devices: 25.4 us -> 22.5 us
  Pallas kernels: 8.76 us -> 10.9 us
    unnamed x16 -> x46, local copies, waits for them, and re-layouts: 8.46 us -> 14 us
    ppermute x20, starting transfers between devices: 25.4 us -> 22.5 us  [swap(): return lax.ppermute(value, 'exp', [(t, t ^ distance) for t in range(n)])]
    pallas_call x18, Pallas kernels: 8.76 us -> 10.9 us  [call(): pl.pallas_call(kernel, out_shape=shapes, in_specs=specs, out_specs=jax.tr...]
  transfers between devices with their start and end apart: 20 -> 20, of which waited for: 13 -> 12; matrix products, arithmetic and copies ran while one was open for 0% -> 0% of each run, Pallas kernels for 6% -> 4%
where the time goes in v5:
time: 78.6 us; the launch traced here: 78.1 us
  waiting for transfers between devices  30.4 us (39%)
  starting transfers between devices  22.5 us (29%)
  local copies, waits for them, and re-layouts  14 us (18%)
  Pallas kernels  10.9 us (14%)
    ppermute x20, waiting for transfers between devices, swap(): return lax.ppermute(value, 'exp', [(t, t ^ distance) for t in range(n)])  30.4 us
    ppermute x20, starting transfers between devices, swap(): return lax.ppermute(value, 'exp', [(t, t ^ distance) for t in range(n)])  22.5 us
    unnamed x46, local copies, waits for them, and re-layouts  14 us
    pallas_call x18, Pallas kernels, call(): pl.pallas_call(kernel, out_shape=shapes, in_specs=specs, out_specs=jax.tr...  10.9 us
  transfers between devices with their start and end apart: 20, of which 12 were waited for; matrix products, arithmetic and copies ran while one was open for 0% of the time, Pallas kernels for 4%

profile of v5, /device:TPU:0, one launch (start us, length us, event | category | flops | bytes accessed | tf_op | source)
XLA Modules:
  0.0 78.1 jit_solution(3994008445892385705)
XLA Ops:
  0.0 1.0 %shard_map.127.mine.after = bf16[1,48,128]{2,1,0:T(8,128)(2,1)S(1)} custom-call(bf16[1,2048]{1,0:T(2,128)(2,1)} %query.1, bf16[1,2048]{1,0:T(2,128)(2,1)} %resid.1, bf16[1,512]{1,0:T(2,128)(2,1)} %new.1, s32[1,8]{1,0:T(1,128)} %choice.1, f32[1,8]{1,0:T(1,128)} %probability.1), custom_call_target="tpu_custom_call" | custom-call | flops 4000000000 | tf_op jit(solution)/shard_map/pallas_call | solution.py:39
  1.0 4.1 %collective-permute-start = (bf16[1,48,128]{2,1,0:T(8,128)(2,1)S(1)}, bf16[1,48,128]{2,1,0:T(8,128)(2,1)S(1)}, u32[]{:S(2)}, u32[]{:S(2)}) collective-permute-start(bf16[1,48,128]{2,1,0:T(8,128)(2,1)S(1)} %shard_map.127.mine.after), channel_id=1, source_target_pairs={{0,8},{1,9},{2,10},{3,11},{4,12},{5,13},{6,14},{7,15},{8,0},{9,1},... | collective-permute-start | bytes 36872 | tf_op jit(solution)/shard_map/ppermute | solution.py:77
  5.1 1.7 %collective-permute-done.theirs = bf16[1,48,128]{2,1,0:T(8,128)(2,1)S(1)} collective-permute-done((bf16[1,48,128]{2,1,0:T(8,128)(2,1)S(1)}, bf16[1,48,128]{2,1,0:T(8,128)(2,1)S(1)}, u32[]{:S(2)}, u32[]{:S(2)}) %collective-permute-start) | collective-permute-done | bytes 12320 | tf_op jit(solution)/shard_map/ppermute | solution.py:77
  6.8 1.9 %collective-permute-start.1 = (bf16[2,48,128]{2,1,0:T(8,128)(2,1)S(1)}, bf16[2,48,128]{2,1,0:T(8,128)(2,1)S(1)}, u32[]{:S(2)}, u32[]{:S(2)}) collective-permute-start(bf16[2,48,128]{2,1,0:T(8,128)(2,1)S(1)} %shard_map.128.mine.after), channel_id=1, source_target_pairs={{0,4},{1,5},{2,6},{3,7},{4,0},{5,1},{6,2},{7,3},{8,12},{9,13},{10,... | collective-permute-start | bytes 73736 | tf_op jit(solution)/shard_map/ppermute | solution.py:77
  8.8 0.6 copy-done.5
  9.5 0.7 copy-done.6
  10.1 0.7 copy-done.10
  10.8 1.5 %collective-permute-start.4 = (bf16[4,144,128]{2,1,0:T(8,128)(2,1)}, bf16[4,144,128]{2,1,0:T(8,128)(2,1)S(1)}, u32[]{:S(2)}, u32[]{:S(2)}) collective-permute-start(bf16[4,144,128]{2,1,0:T(8,128)(2,1)} %shard_map.133), channel_id=1, source_target_pairs={{0,2},{1,3},{2,0},{3,1},{4,6},{5,7},{6,4},{7,5},{8,10},{9,11},{10,... | collective-permute-start | bytes 442376 | tf_op jit(solution)/shard_map/ppermute | solution.py:77
  12.3 0.7 copy-done.12
  13.1 0.6 copy-done.14
  13.7 0.6 collective-permute-start.5
  14.3 1.5 %collective-permute-start.2 = (bf16[1,96,128]{2,1,0:T(8,128)(2,1)S(1)}, bf16[1,96,128]{2,1,0:T(8,128)(2,1)S(1)}, u32[]{:S(2)}, u32[]{:S(2)}) collective-permute-start(bf16[1,96,128]{2,1,0:T(8,128)(2,1)S(1)} %bitcast.10), channel_id=1, source_target_pairs={{0,2},{1,3},{2,0},{3,1},{4,6},{5,7},{6,4},{7,5},{8,10},{9,11},{10,... | collective-permute-start | bytes 73736 | tf_op jit(solution)/shard_map/ppermute | solution.py:77
  15.8 4.7 %collective-permute-done.2.theirs = bf16[1,96,128]{2,1,0:T(8,128)(2,1)S(1)} collective-permute-done((bf16[1,96,128]{2,1,0:T(8,128)(2,1)S(1)}, bf16[1,96,128]{2,1,0:T(8,128)(2,1)S(1)}, u32[]{:S(2)}, u32[]{:S(2)}) %collective-permute-start.2) | collective-permute-done | bytes 24608 | tf_op jit(solution)/shard_map/ppermute | solution.py:77
  20.7 0.7 copy-done.7
  21.3 0.7 copy-done.8
  22.0 0.7 copy-done.9
  22.7 1.4 %copy-done.20 = bf16[8,192,512]{2,1,0:T(8,128)(2,1)S(1)} copy-done((bf16[8,192,512]{2,1,0:T(8,128)(2,1)S(1)}, bf16[8,192,512]{2,1,0:T(8,128)(2,1)}, u32[]{:S(2)}) %copy-start.20) | copy-done | bytes 1572888
  24.1 2.7 %shard_map.136 = (bf16[8,32,128]{2,1,0:T(8,128)(2,1)S(1)}, bf16[8,32,128]{2,1,0:T(8,128)(2,1)S(1)}) custom-call(bf16[4,144,128]{2,1,0:T(8,128)(2,1)S(1)} %get-tuple-element.37.after.refs_0_, s32[8]{0:T(128)S(1)} %copy-done.22, bf16[2,96,128]{2,1,0:T(8,128)(2,1)S(1)} %shard_map.130.after.mine.near, ...), custom_call_target="tpu_custom_call" | custom-call | flops 8000000000 | tf_op jit(solution)/shard_map/pallas_call | solution.py:39
  26.8 0.6 collective-permute-start.7
  27.3 0.9 %collective-permute-done.7.theirs = bf16[8,32,128]{2,1,0:T(8,128)(2,1)S(1)} collective-permute-done((bf16[8,32,128]{2,1,0:T(8,128)(2,1)S(1)}, bf16[8,32,128]{2,1,0:T(8,128)(2,1)S(1)}, u32[]{:S(2)}, u32[]{:S(2)}) %collective-permute-start.7) | collective-permute-done | bytes 65568 | tf_op jit(solution)/shard_map/ppermute | solution.py:77
  28.2 1.1 %shard_map.137 = (bf16[4,32,128]{2,1,0:T(8,128)(2,1)S(1)}, bf16[4,32,128]{2,1,0:T(8,128)(2,1)}) custom-call(bf16[8,32,128]{2,1,0:T(8,128)(2,1)S(1)} %get-tuple-element.38.mine.after, bf16[8,32,128]{2,1,0:T(8,128)(2,1)S(1)} %collective-permute-done.7.theirs), custom_call_target="tpu_custom_call" | custom-call | flops 50000000 | tf_op jit(solution)/shard_map/pallas_call | solution.py:39
  29.3 0.6 copy-done.16
  29.9 0.8 collective-permute-start.8
  30.9 3.1 %collective-permute-start.14 = (bf16[4,144,128]{2,1,0:T(8,128)(2,1)}, bf16[4,144,128]{2,1,0:T(8,128)(2,1)}, u32[]{:S(2)}, u32[]{:S(2)}) collective-permute-start(bf16[4,144,128]{2,1,0:T(8,128)(2,1)} %shard_map.143), channel_id=1, source_target_pairs={{0,8},{1,9},{2,10},{3,11},{4,12},{5,13},{6,14},{7,15},{8,0},{9,1},... | collective-permute-start | bytes 442376 | tf_op jit(solution)/shard_map/ppermute | solution.py:77
  34.2 0.8 copy-done.17
  34.9 1.0 %shard_map.138.mine.after = bf16[4,32,128]{2,1,0:T(8,128)(2,1)S(1)} custom-call(bf16[4,32,128]{2,1,0:T(8,128)(2,1)S(1)} %copy-done.17, bf16[4,32,128]{2,1,0:T(8,128)(2,1)} %collective-permute-done.8.theirs), custom_call_target="tpu_custom_call" | custom-call | flops 50000000 | tf_op jit(solution)/shard_map/pallas_call | solution.py:39
  35.9 0.6 copy-done.18
  36.5 2.5 %collective-permute-start.15 = (bf16[4,144,128]{2,1,0:T(8,128)(2,1)}, bf16[4,144,128]{2,1,0:T(8,128)(2,1)S(1)}, u32[]{:S(2)}, u32[]{:S(2)}) collective-permute-start(bf16[4,144,128]{2,1,0:T(8,128)(2,1)} %shard_map.144), channel_id=1, source_target_pairs={{0,12},{1,13},{2,14},{3,15},{4,8},{5,9},{6,10},{7,11},{8,4},{9,5},... | collective-permute-start | bytes 442376 | tf_op jit(solution)/shard_map/ppermute | solution.py:77
  39.0 0.7 collective-permute-start.9
  39.7 5.2 %collective-permute-done.9.theirs = bf16[4,32,128]{2,1,0:T(8,128)(2,1)S(1)} collective-permute-done((bf16[4,32,128]{2,1,0:T(8,128)(2,1)}, bf16[4,32,128]{2,1,0:T(8,128)(2,1)S(1)}, u32[]{:S(2)}, u32[]{:S(2)}) %collective-permute-start.9) | collective-permute-done | bytes 32800 | tf_op jit(solution)/shard_map/ppermute | solution.py:77
  44.9 0.8 copy-done.19
  45.9 1.6 %collective-permute-start.10 = (bf16[4,32,128]{2,1,0:T(8,128)(2,1)S(1)}, bf16[4,32,128]{2,1,0:T(8,128)(2,1)S(1)}, u32[]{:S(2)}, u32[]{:S(2)}) collective-permute-start(bf16[4,32,128]{2,1,0:T(8,128)(2,1)S(1)} %shard_map.139.mine), channel_id=1, source_target_pairs={{0,8},{1,9},{2,10},{3,11},{4,12},{5,13},{6,14},{7,15},{8,0},{9,1},... | collective-permute-start | bytes 98312 | tf_op jit(solution)/shard_map/ppermute | solution.py:77
  47.5 3.9 %collective-permute-done.10.theirs = bf16[4,32,128]{2,1,0:T(8,128)(2,1)S(1)} collective-permute-done((bf16[4,32,128]{2,1,0:T(8,128)(2,1)S(1)}, bf16[4,32,128]{2,1,0:T(8,128)(2,1)S(1)}, u32[]{:S(2)}, u32[]{:S(2)}) %collective-permute-start.10) | collective-permute-done | bytes 32800 | tf_op jit(solution)/shard_map/ppermute | solution.py:77
  51.4 0.8 %copy-done.15 = bf16[4,48,128]{2,1,0:T(8,128)(2,1)S(1)} copy-done((bf16[4,48,128]{2,1,0:T(8,128)(2,1)S(1)}, bf16[4,48,128]{2,1,0:T(8,128)(2,1)}, u32[]{:S(2)}) %copy-start.15) | copy-done | bytes 49176
  52.6 0.5 collective-permute-start.11
  53.1 3.3 %collective-permute-done.11.theirs = bf16[4,16,128]{2,1,0:T(8,128)(2,1)S(1)} collective-permute-done((bf16[4,16,128]{2,1,0:T(8,128)(2,1)S(1)}, bf16[4,16,128]{2,1,0:T(8,128)(2,1)S(1)}, u32[]{:S(2)}, u32[]{:S(2)}) %collective-permute-start.11) | collective-permute-done | bytes 16416 | tf_op jit(solution)/shard_map/ppermute | solution.py:77
  56.4 1.0 %shard_map.145 = (bf16[96,2048]{1,0:T(8,128)(2,1)S(1)}, bf16[768,128]{1,0:T(8,128)(2,1)S(1)}) custom-call(bf16[4,144,128]{2,1,0:T(8,128)(2,1)S(1)} %get-tuple-element.37.after.refs_0_, bf16[4,144,128]{2,1,0:T(8,128)(2,1)S(1)} %collective-permute-done.13.refs_1_, bf16[4,144,128]{2,1,0:T(8,128)(2,1)} %collective-permute-done.14.refs_2_, ...), custom_call_target="tpu_custom_call" | custom-call | flops 50000000 | tf_op jit(solution)/shard_map/pallas_call | solution.py:39
  57.6 1.9 %copy-done.1 = bf16[1,2048,768]{2,1,0:T(8,128)(2,1)S(1)} copy-done((bf16[1,2048,768]{2,1,0:T(8,128)(2,1)S(1)}, bf16[1,2048,768]{2,1,0:T(8,128)(2,1)}, u32[]{:S(2)}) %copy-start.1) | copy-done | bytes 3145752
  59.5 1.9 %copy-done.2 = bf16[1,768,2048]{2,1,0:T(8,128)(2,1)S(1)} copy-done((bf16[1,768,2048]{2,1,0:T(8,128)(2,1)S(1)}, bf16[1,768,2048]{2,1,0:T(8,128)(2,1)}, u32[]{:S(2)}) %copy-start.2) | copy-done | bytes 3145752
  61.4 2.8 %shard_map.146 = (bf16[8,16,128]{2,1,0:T(8,128)(2,1)S(1)}, bf16[8,16,128]{2,1,0:T(8,128)(2,1)S(1)}) custom-call(bf16[8,16,128]{2,1,0:T(8,128)(2,1)S(1)} %shard_map.141.mine, bf16[8,16,128]{2,1,0:T(8,128)(2,1)S(1)} %collective-permute-done.12.theirs, bf16[2,96,128]{2,1,0:T(8,128)(2,1)S(1)} %shard_map.130.after.mine.near, ...), custom_call_target="tpu_custom_call" | custom-call | flops 50000000 | tf_op jit(solution)/shard_map/pallas_call | solution.py:39
  64.6 0.9 %collective-permute-done.16.theirs = bf16[8,16,128]{2,1,0:T(8,128)(2,1)S(1)} collective-permute-done((bf16[8,16,128]{2,1,0:T(8,128)(2,1)S(1)}, bf16[8,16,128]{2,1,0:T(8,128)(2,1)S(1)}, u32[]{:S(2)}, u32[]{:S(2)}) %collective-permute-start.16) | collective-permute-done | bytes 32800 | tf_op jit(solution)/shard_map/ppermute | solution.py:77
  65.5 0.5 collective-permute-start.17
  66.0 3.3 %collective-permute-done.17.theirs = bf16[4,16,128]{2,1,0:T(8,128)(2,1)S(1)} collective-permute-done((bf16[4,16,128]{2,1,0:T(8,128)(2,1)S(1)}, bf16[4,16,128]{2,1,0:T(8,128)(2,1)S(1)}, u32[]{:S(2)}, u32[]{:S(2)}) %collective-permute-start.17) | collective-permute-done | bytes 16416 | tf_op jit(solution)/shard_map/ppermute | solution.py:77
  69.3 0.5 collective-permute-start.18
  69.8 3.1 %collective-permute-done.18.theirs = bf16[2,16,128]{2,1,0:T(8,128)(2,1)S(1)} collective-permute-done((bf16[2,16,128]{2,1,0:T(8,128)(2,1)S(1)}, bf16[2,16,128]{2,1,0:T(8,128)(2,1)S(1)}, u32[]{:S(2)}, u32[]{:S(2)}) %collective-permute-start.18) | collective-permute-done | bytes 8224 | tf_op jit(solution)/shard_map/ppermute | solution.py:77
  72.9 1.4 %collective-permute-start.19 = (bf16[1,16,128]{2,1,0:T(8,128)(2,1)S(1)}, bf16[1,16,128]{2,1,0:T(8,128)(2,1)S(1)}, u32[]{:S(2)}, u32[]{:S(2)}) collective-permute-start(bf16[1,16,128]{2,1,0:T(8,128)(2,1)S(1)} %get-tuple-element.56), channel_id=1, source_target_pairs={{0,8},{1,9},{2,10},{3,11},{4,12},{5,13},{6,14},{7,15},{8,0},{9,1},... | collective-permute-start | bytes 12296 | tf_op jit(solution)/shard_map/ppermute | solution.py:77
  74.3 3.1 %collective-permute-done.19.theirs = bf16[1,16,128]{2,1,0:T(8,128)(2,1)S(1)} collective-permute-done((bf16[1,16,128]{2,1,0:T(8,128)(2,1)S(1)}, bf16[1,16,128]{2,1,0:T(8,128)(2,1)S(1)}, u32[]{:S(2)}, u32[]{:S(2)}) %collective-permute-start.19) | collective-permute-done | bytes 4128 | tf_op jit(solution)/shard_map/ppermute | solution.py:77
  77.4 0.6 shard_map.150
  (62 shorter events, 1.8 us)
Async XLA Ops:
  0.0 8.7 %copy-start.4 = (bf16[16,96,48]{1,2,0:T(8,128)(2,1)S(1)}, bf16[16,96,48]{1,2,0:T(8,128)(2,1)}, u32[]{:S(2)}) copy-start(bf16[16,96,48]{1,2,0:T(8,128)(2,1)} %param.25) | copy-start | bytes 442372
  0.0 8.7 %copy-start.3 = (bf16[16,96,128]{2,1,0:T(8,128)(2,1)S(1)}, bf16[16,96,128]{2,1,0:T(8,128)(2,1)}, u32[]{:S(2)}) copy-start(bf16[16,96,128]{2,1,0:T(8,128)(2,1)} %model.1) | copy-start | bytes 1179652
  0.0 22.7 %copy-start.22 = (s32[8]{0:T(128)S(1)}, s32[8]{0:T(128)}, u32[]{:S(2)}) copy-start(s32[8]{0:T(128)} %lengths.1) | copy-start | bytes 100
  1.0 5.8 %collective-permute-start = (bf16[1,48,128]{2,1,0:T(8,128)(2,1)S(1)}, bf16[1,48,128]{2,1,0:T(8,128)(2,1)S(1)}, u32[]{:S(2)}, u32[]{:S(2)}) collective-permute-start(bf16[1,48,128]{2,1,0:T(8,128)(2,1)S(1)} %shard_map.127.mine.after), channel_id=1, source_target_pairs={{0,8},{1,9},{2,10},{3,11},{4,12},{5,13},{6,14},{7,15},{8,0},{9,1},... | collective-permute-start | bytes 36872 | tf_op jit(solution)/shard_map/ppermute | solution.py:77
  6.8 4.0 %copy-start.11 = (bf16[2,48,128]{2,1,0:T(8,128)(2,1)}, bf16[2,48,128]{2,1,0:T(8,128)(2,1)S(1)}, u32[]{:S(2)}) copy-start(bf16[2,48,128]{2,1,0:T(8,128)(2,1)S(1)} %shard_map.128.mine.after) | copy-start | bytes 73732
  6.8 5.5 %collective-permute-start.1 = (bf16[2,48,128]{2,1,0:T(8,128)(2,1)S(1)}, bf16[2,48,128]{2,1,0:T(8,128)(2,1)S(1)}, u32[]{:S(2)}, u32[]{:S(2)}) collective-permute-start(bf16[2,48,128]{2,1,0:T(8,128)(2,1)S(1)} %shard_map.128.mine.after), channel_id=1, source_target_pairs={{0,4},{1,5},{2,6},{3,7},{4,0},{5,1},{6,2},{7,3},{8,12},{9,13},{10,... | collective-permute-start | bytes 73736 | tf_op jit(solution)/shard_map/ppermute | solution.py:77
  8.8 0.6 copy-start.5
  9.5 0.7 copy-start.6
  10.1 0.7 copy-start.10
  10.8 9.8 %collective-permute-start.4 = (bf16[4,144,128]{2,1,0:T(8,128)(2,1)}, bf16[4,144,128]{2,1,0:T(8,128)(2,1)S(1)}, u32[]{:S(2)}, u32[]{:S(2)}) collective-permute-start(bf16[4,144,128]{2,1,0:T(8,128)(2,1)} %shard_map.133), channel_id=1, source_target_pairs={{0,2},{1,3},{2,0},{3,1},{4,6},{5,7},{6,4},{7,5},{8,10},{9,11},{10,... | collective-permute-start | bytes 442376 | tf_op jit(solution)/shard_map/ppermute | solution.py:77
  12.3 8.3 %collective-permute-start.3 = (bf16[4,144,128]{2,1,0:T(8,128)(2,1)}, bf16[4,144,128]{2,1,0:T(8,128)(2,1)S(1)}, u32[]{:S(2)}, u32[]{:S(2)}) collective-permute-start(bf16[4,144,128]{2,1,0:T(8,128)(2,1)} %shard_map.132), channel_id=1, source_target_pairs={{0,1},{1,0},{2,3},{3,2},{4,5},{5,4},{6,7},{7,6},{8,9},{9,8},{10,11... | collective-permute-start | bytes 442376 | tf_op jit(solution)/shard_map/ppermute | solution.py:77
  12.3 0.7 copy-start.12
  13.1 0.6 copy-start.14
  13.7 6.9 %collective-permute-start.5 = (bf16[4,144,128]{2,1,0:T(8,128)(2,1)}, bf16[4,144,128]{2,1,0:T(8,128)(2,1)S(1)}, u32[]{:S(2)}, u32[]{:S(2)}) collective-permute-start(bf16[4,144,128]{2,1,0:T(8,128)(2,1)} %shard_map.134), channel_id=1, source_target_pairs={{0,3},{1,2},{2,1},{3,0},{4,7},{5,6},{6,5},{7,4},{8,11},{9,10},{10,... | collective-permute-start | bytes 442376 | tf_op jit(solution)/shard_map/ppermute | solution.py:77
  14.3 6.3 %collective-permute-start.2 = (bf16[1,96,128]{2,1,0:T(8,128)(2,1)S(1)}, bf16[1,96,128]{2,1,0:T(8,128)(2,1)S(1)}, u32[]{:S(2)}, u32[]{:S(2)}) collective-permute-start(bf16[1,96,128]{2,1,0:T(8,128)(2,1)S(1)} %bitcast.10), channel_id=1, source_target_pairs={{0,2},{1,3},{2,0},{3,1},{4,6},{5,7},{6,4},{7,5},{8,10},{9,11},{10,... | collective-permute-start | bytes 73736 | tf_op jit(solution)/shard_map/ppermute | solution.py:77
  20.6 2.1 %collective-permute-start.6 = (bf16[2,96,128]{2,1,0:T(8,128)(2,1)S(1)}, bf16[2,96,128]{2,1,0:T(8,128)(2,1)S(1)}, u32[]{:S(2)}, u32[]{:S(2)}) collective-permute-start(bf16[2,96,128]{2,1,0:T(8,128)(2,1)S(1)} %shard_map.130.after.mine.near), channel_id=1, source_target_pairs={{0,1},{1,0},{2,3},{3,2},{4,5},{5,4},{6,7},{7,6},{8,9},{9,8},{10,11... | collective-permute-start | bytes 147464 | tf_op jit(solution)/shard_map/ppermute | solution.py:77
  20.7 0.7 copy-start.7
  21.3 0.7 copy-start.8
  22.0 0.7 copy-start.9
  22.7 1.4 %copy-start.20 = (bf16[8,192,512]{2,1,0:T(8,128)(2,1)S(1)}, bf16[8,192,512]{2,1,0:T(8,128)(2,1)}, u32[]{:S(2)}) copy-start(bf16[8,192,512]{2,1,0:T(8,128)(2,1)} %cache.1) | copy-start | bytes 4718596
  24.1 27.3 %copy-start.21 = (f32[2048]{0:T(1024)S(1)}, f32[2048]{0:T(1024)}, u32[]{:S(2)}) copy-start(f32[2048]{0:T(1024)} %param.18) | copy-start | bytes 24580
  24.1 33.5 %copy-start = (bf16[1,2048,768]{2,1,0:T(8,128)(2,1)S(1)}, bf16[1,2048,768]{2,1,0:T(8,128)(2,1)}, u32[]{:S(2)}) copy-start(bf16[1,2048,768]{2,1,0:T(8,128)(2,1)} %param.21) | copy-start | bytes 9437188
  26.8 3.9 %copy-start.13 = (bf16[8,32,128]{2,1,0:T(8,128)(2,1)}, bf16[8,32,128]{2,1,0:T(8,128)(2,1)S(1)}, u32[]{:S(2)}) copy-start(bf16[8,32,128]{2,1,0:T(8,128)(2,1)S(1)} %get-tuple-element.38.mine.after) | copy-start | bytes 196612
  26.8 1.5 %collective-permute-start.7 = (bf16[8,32,128]{2,1,0:T(8,128)(2,1)S(1)}, bf16[8,32,128]{2,1,0:T(8,128)(2,1)S(1)}, u32[]{:S(2)}, u32[]{:S(2)}) collective-permute-start(bf16[8,32,128]{2,1,0:T(8,128)(2,1)S(1)} %get-tuple-element.39), channel_id=1, source_target_pairs={{0,1},{1,0},{2,3},{3,2},{4,5},{5,4},{6,7},{7,6},{8,9},{9,8},{10,11... | collective-permute-start | bytes 196616 | tf_op jit(solution)/shard_map/ppermute | solution.py:77
  29.3 0.6 copy-start.16
  29.9 4.2 %collective-permute-start.8 = (bf16[4,32,128]{2,1,0:T(8,128)(2,1)}, bf16[4,32,128]{2,1,0:T(8,128)(2,1)}, u32[]{:S(2)}, u32[]{:S(2)}) collective-permute-start(bf16[4,32,128]{2,1,0:T(8,128)(2,1)} %get-tuple-element.41), channel_id=1, source_target_pairs={{0,2},{1,3},{2,0},{3,1},{4,6},{5,7},{6,4},{7,5},{8,10},{9,11},{10,... | collective-permute-start | bytes 98312 | tf_op jit(solution)/shard_map/ppermute | solution.py:77
  30.7 25.7 %collective-permute-start.13 = (bf16[4,144,128]{2,1,0:T(8,128)(2,1)}, bf16[4,144,128]{2,1,0:T(8,128)(2,1)S(1)}, u32[]{:S(2)}, u32[]{:S(2)}) collective-permute-start(bf16[4,144,128]{2,1,0:T(8,128)(2,1)} %shard_map.142), channel_id=1, source_target_pairs={{0,4},{1,5},{2,6},{3,7},{4,0},{5,1},{6,2},{7,3},{8,12},{9,13},{10,... | collective-permute-start | bytes 442376 | tf_op jit(solution)/shard_map/ppermute | solution.py:77
  30.9 25.5 %collective-permute-start.14 = (bf16[4,144,128]{2,1,0:T(8,128)(2,1)}, bf16[4,144,128]{2,1,0:T(8,128)(2,1)}, u32[]{:S(2)}, u32[]{:S(2)}) collective-permute-start(bf16[4,144,128]{2,1,0:T(8,128)(2,1)} %shard_map.143), channel_id=1, source_target_pairs={{0,8},{1,9},{2,10},{3,11},{4,12},{5,13},{6,14},{7,15},{8,0},{9,1},... | collective-permute-start | bytes 442376 | tf_op jit(solution)/shard_map/ppermute | solution.py:77
  34.1 0.8 copy-start.17
  35.9 0.6 copy-start.18
  36.5 19.9 %collective-permute-start.15 = (bf16[4,144,128]{2,1,0:T(8,128)(2,1)}, bf16[4,144,128]{2,1,0:T(8,128)(2,1)S(1)}, u32[]{:S(2)}, u32[]{:S(2)}) collective-permute-start(bf16[4,144,128]{2,1,0:T(8,128)(2,1)} %shard_map.144), channel_id=1, source_target_pairs={{0,12},{1,13},{2,14},{3,15},{4,8},{5,9},{6,10},{7,11},{8,4},{9,5},... | collective-permute-start | bytes 442376 | tf_op jit(solution)/shard_map/ppermute | solution.py:77
  39.0 5.9 %collective-permute-start.9 = (bf16[4,32,128]{2,1,0:T(8,128)(2,1)}, bf16[4,32,128]{2,1,0:T(8,128)(2,1)S(1)}, u32[]{:S(2)}, u32[]{:S(2)}) collective-permute-start(bf16[4,32,128]{2,1,0:T(8,128)(2,1)} %copy-done.18), channel_id=1, source_target_pairs={{0,4},{1,5},{2,6},{3,7},{4,0},{5,1},{6,2},{7,3},{8,12},{9,13},{10,... | collective-permute-start | bytes 98312 | tf_op jit(solution)/shard_map/ppermute | solution.py:77
  44.9 0.8 copy-start.19
  45.9 5.5 %collective-permute-start.10 = (bf16[4,32,128]{2,1,0:T(8,128)(2,1)S(1)}, bf16[4,32,128]{2,1,0:T(8,128)(2,1)S(1)}, u32[]{:S(2)}, u32[]{:S(2)}) collective-permute-start(bf16[4,32,128]{2,1,0:T(8,128)(2,1)S(1)} %shard_map.139.mine), channel_id=1, source_target_pairs={{0,8},{1,9},{2,10},{3,11},{4,12},{5,13},{6,14},{7,15},{8,0},{9,1},... | collective-permute-start | bytes 98312 | tf_op jit(solution)/shard_map/ppermute | solution.py:77
  51.4 0.8 %copy-start.15 = (bf16[4,48,128]{2,1,0:T(8,128)(2,1)S(1)}, bf16[4,48,128]{2,1,0:T(8,128)(2,1)}, u32[]{:S(2)}) copy-start(bf16[4,48,128]{2,1,0:T(8,128)(2,1)} %copy-done.14) | copy-start | bytes 147460
  52.6 3.8 %collective-permute-start.11 = (bf16[4,16,128]{2,1,0:T(8,128)(2,1)S(1)}, bf16[4,16,128]{2,1,0:T(8,128)(2,1)S(1)}, u32[]{:S(2)}, u32[]{:S(2)}) collective-permute-start(bf16[4,16,128]{2,1,0:T(8,128)(2,1)S(1)} %get-tuple-element.43.mine), channel_id=1, source_target_pairs={{0,2},{1,3},{2,0},{3,1},{4,6},{5,7},{6,4},{7,5},{8,10},{9,11},{10,... | collective-permute-start | bytes 49160 | tf_op jit(solution)/shard_map/ppermute | solution.py:77
  56.4 1.2 %collective-permute-start.12 = (bf16[8,16,128]{2,1,0:T(8,128)(2,1)S(1)}, bf16[8,16,128]{2,1,0:T(8,128)(2,1)S(1)}, u32[]{:S(2)}, u32[]{:S(2)}) collective-permute-start(bf16[8,16,128]{2,1,0:T(8,128)(2,1)S(1)} %shard_map.141.mine), channel_id=1, source_target_pairs={{0,1},{1,0},{2,3},{3,2},{4,5},{5,4},{6,7},{7,6},{8,9},{9,8},{10,11... | collective-permute-start | bytes 98312 | tf_op jit(solution)/shard_map/ppermute | solution.py:77
  57.6 1.9 %copy-start.1 = (bf16[1,2048,768]{2,1,0:T(8,128)(2,1)S(1)}, bf16[1,2048,768]{2,1,0:T(8,128)(2,1)}, u32[]{:S(2)}) copy-start(bf16[1,2048,768]{2,1,0:T(8,128)(2,1)} %param.22) | copy-start | bytes 9437188
  59.5 1.9 %copy-start.2 = (bf16[1,768,2048]{2,1,0:T(8,128)(2,1)S(1)}, bf16[1,768,2048]{2,1,0:T(8,128)(2,1)}, u32[]{:S(2)}) copy-start(bf16[1,768,2048]{2,1,0:T(8,128)(2,1)} %param.23) | copy-start | bytes 9437188
  64.2 1.3 %collective-permute-start.16 = (bf16[8,16,128]{2,1,0:T(8,128)(2,1)S(1)}, bf16[8,16,128]{2,1,0:T(8,128)(2,1)S(1)}, u32[]{:S(2)}, u32[]{:S(2)}) collective-permute-start(bf16[8,16,128]{2,1,0:T(8,128)(2,1)S(1)} %get-tuple-element.50), channel_id=1, source_target_pairs={{0,1},{1,0},{2,3},{3,2},{4,5},{5,4},{6,7},{7,6},{8,9},{9,8},{10,11... | collective-permute-start | bytes 98312 | tf_op jit(solution)/shard_map/ppermute | solution.py:77
  65.5 3.8 %collective-permute-start.17 = (bf16[4,16,128]{2,1,0:T(8,128)(2,1)S(1)}, bf16[4,16,128]{2,1,0:T(8,128)(2,1)S(1)}, u32[]{:S(2)}, u32[]{:S(2)}) collective-permute-start(bf16[4,16,128]{2,1,0:T(8,128)(2,1)S(1)} %get-tuple-element.52), channel_id=1, source_target_pairs={{0,2},{1,3},{2,0},{3,1},{4,6},{5,7},{6,4},{7,5},{8,10},{9,11},{10,... | collective-permute-start | bytes 49160 | tf_op jit(solution)/shard_map/ppermute | solution.py:77
  69.3 3.7 %collective-permute-start.18 = (bf16[2,16,128]{2,1,0:T(8,128)(2,1)S(1)}, bf16[2,16,128]{2,1,0:T(8,128)(2,1)S(1)}, u32[]{:S(2)}, u32[]{:S(2)}) collective-permute-start(bf16[2,16,128]{2,1,0:T(8,128)(2,1)S(1)} %get-tuple-element.54), channel_id=1, source_target_pairs={{0,4},{1,5},{2,6},{3,7},{4,0},{5,1},{6,2},{7,3},{8,12},{9,13},{10,... | collective-permute-start | bytes 24584 | tf_op jit(solution)/shard_map/ppermute | solution.py:77
  72.9 4.5 %collective-permute-start.19 = (bf16[1,16,128]{2,1,0:T(8,128)(2,1)S(1)}, bf16[1,16,128]{2,1,0:T(8,128)(2,1)S(1)}, u32[]{:S(2)}, u32[]{:S(2)}) collective-permute-start(bf16[1,16,128]{2,1,0:T(8,128)(2,1)S(1)} %get-tuple-element.56), channel_id=1, source_target_pairs={{0,8},{1,9},{2,10},{3,11},{4,12},{5,13},{6,14},{7,15},{8,0},{9,1},... | collective-permute-start | bytes 12296 | tf_op jit(solution)/shard_map/ppermute | solution.py:77

commit v6 on v5

--- a/solution.py
+++ b/solution.py
@@ -26,16 +26,16 @@
 
 floor_score = -1e30
 epsilon = 1e-06
+FILL = 4000
 
 VMEM = pl.BlockSpec(memory_space=pltpu.VMEM)
 SMEM = pl.BlockSpec(memory_space=pltpu.SMEM)
 HBM = pl.BlockSpec(memory_space=pltpu.HBM)
-ANY = pl.BlockSpec(memory_space=pl.ANY)
 shape = jax.ShapeDtypeStruct
 bf16, f32 = jnp.bfloat16, jnp.float32
 
 
-def call(kernel, shapes, specs, *args, limit=8, scratch=(), nanos=50):
+def call(kernel, shapes, specs, *args, limit=8, scratch=(), nanos=400):
     return pl.pallas_call(
         kernel,
         out_shape=shapes,
@@ -50,17 +50,13 @@
 
 
 def hold_kernel(value, after, out):
-    pass
+    out[...] = value[...]
 
 
 def hold(value, after):
-    return pl.pallas_call(
-        hold_kernel,
-        out_shape=shape(value.shape, value.dtype),
-        in_specs=[ANY, ANY],
-        out_specs=ANY,
-        input_output_aliases={0: 0},
-    )(value, after)
+    return call(
+        hold_kernel, shape(value.shape, value.dtype), [VMEM] * 2, value, after, nanos=FILL
+    )
 
 
 def iota(dims, dim):
@@ -208,7 +204,7 @@
         outs[slot // count][slot % count] = encode(*merged(parts))
 
 
-def token_kernel(mine, theirs, column, near, scale, hidden_out, normed_out):
+def token_kernel(after, mine, theirs, column, near, scale, hidden_out, normed_out):
     second = lax.axis_index("exp") % 2 == 1
     first_group = iota(HEADS, 0) < GROUPED
     far = column.shape[0]
@@ -302,16 +298,19 @@
 
 
 def lora_pack_kernel(after, model, inner, *outs):
-    low = lax.axis_index("exp") % NEAR
-    ranks = model.shape[1]
+    low, first = lax.axis_index("exp") % NEAR, lax.axis_index("grp") == 0
+    ranks, split, most = model.shape[1], model.shape[1] // 2, outs[0].shape[1] - model.shape[1] // 2
+    rest = inner.shape[1] - most
     for k, out in enumerate(outs):
+        out[:, split:, ranks:] = jnp.zeros((out.shape[0], most, HEAD_WIDTH - ranks), out.dtype)
         for z in range(out.shape[0]):
             at = z * NEAR + (low ^ k)
-            out[z, :ranks] = model[at]
-            out[z, ranks:, :ranks] = inner[at]
-            out[z, ranks:, ranks:] = jnp.zeros(
-                (out.shape[1] - ranks, HEAD_WIDTH - ranks), out.dtype
-            )
+            out[z, :split] = jnp.where(first, model[at, :split], model[at, split:])
+            lower = inner[at, most:]
+            if rest < most:
+                pad = jnp.zeros((most - rest, ranks), out.dtype)
+                lower = jnp.concatenate([lower, pad], axis=0)
+            out[z, split:, :ranks] = jnp.where(first, inner[at, :most], lower)
 
 
 def lora_turn_kernel(after, *refs):
@@ -323,45 +322,56 @@
             out[low ^ k] = ref[high ^ j]
 
 
-def lora_join_kernel(*refs):
+def lora_order_kernel(after, *refs):
     high = lax.axis_index("exp") // NEAR
-    got, (model, inner) = refs[:-2], refs[-2:]
-    ranks = model.shape[0]
-    width = inner.shape[0] // (len(got) * NEAR)
+    got, out = refs[:-1], refs[-1]
     for j, ref in enumerate(got):
-        for l in range(NEAR):
-            at = (high ^ j) * NEAR + l
-            columns = pl.ds(pl.multiple_of(at * HEAD_WIDTH, HEAD_WIDTH), HEAD_WIDTH)
-            model[:, columns] = ref[l, :ranks]
-            inner[pl.ds(pl.multiple_of(at * width, width), width)] = ref[l, ranks:]
+        out[pl.ds((high ^ j) * NEAR, NEAR)] = ref[...]
+
+
+def lora_join_kernel(mine, theirs, model, inner):
+    first = lax.axis_index("grp") == 0
+    split = model.shape[0] // 2
+    most, width = mine.shape[1] - split, inner.shape[0] // mine.shape[0]
+    for at in range(mine.shape[0]):
+        own, other = mine[at], theirs[at]
+        halves = jnp.where(first, own, other), jnp.where(first, other, own)
+        columns = slice(at * HEAD_WIDTH, (at + 1) * HEAD_WIDTH)
+        model[:split, columns] = halves[0][:split]
+        model[split:, columns] = halves[1][:split]
+        inner[at * width : at * width + most] = halves[0][split:]
+        inner[at * width + most : (at + 1) * width] = halves[1][split : split + width - most]
 
 
 def lora_near(adapter_model, adapter_hidden, n, marks):
     total, ranks, model_width = adapter_model.shape
     inner_width = adapter_hidden.shape[2]
     inner = jnp.transpose(adapter_hidden, (0, 2, 1))
-    if model_width != HEAD_WIDTH or inner_width % 16:
+    if model_width != HEAD_WIDTH or inner_width % 16 or lax.axis_size("grp") != 2:
         model = lax.all_to_all(adapter_model, "exp", split_axis=0, concat_axis=2, tiled=True)
         inner = lax.all_to_all(inner, "exp", split_axis=0, concat_axis=1, tiled=True)
         return [model[0], inner[0]], True
     far = n // NEAR
+    block = (ranks // 2 + pad16(inner_width // 2), HEAD_WIDTH)
     packed = call(
         lora_pack_kernel,
-        (shape((far, ranks + inner_width, HEAD_WIDTH), bf16),) * NEAR,
-        [ANY, VMEM, VMEM],
+        (shape((far,) + block, bf16),) * NEAR,
+        [VMEM] * 3,
         marks[0],
         adapter_model,
         inner,
-    )
-    got = [packed[0]]
-    for k in range(1, NEAR):
-        got.append(swap(hold(packed[k], marks[1 + k // 3]), n, k))
+        nanos=FILL,
+    )
     turned = call(
         lora_turn_kernel,
-        (shape((NEAR, ranks + inner_width, HEAD_WIDTH), bf16),) * far,
-        [ANY] + [VMEM] * NEAR,
+        (shape((NEAR,) + block, bf16),) * far,
+        [VMEM] * (1 + NEAR),
         marks[3],
-        *got,
+        packed[0],
+        swap(hold(packed[1], marks[1]), n, 1),
+        swap(packed[2], n, 2),
+        swap(hold(packed[3], marks[1]), n, 3),
+        nanos=FILL,
     )
     return turned, False
 
@@ -369,15 +379,30 @@
 def lora_far(turned, n, marks):
     far = len(turned)
     rows = turned[0].shape[1]
-    ranks = 3 * ADAPTER_RANK
-    got = [turned[0]]
-    for j in range(1, far):
-        got.append(swap(hold(turned[j], marks[min(j - 1, len(marks) - 1)]), n, j * NEAR))
+    got = [turned[0], swap(turned[1], n, NEAR)]
+    for j in range(2, far):
+        got.append(swap(hold(turned[j], marks[j - 2]), n, j * NEAR))
+    return call(
+        lora_order_kernel,
+        shape((n, rows, HEAD_WIDTH), bf16),
+        [VMEM] * (1 + far),
+        marks[far - 2],
+        *got,
+        nanos=FILL,
+    )
+
+
+def lora_join(ordered, inner_width):
+    n = ordered.shape[0]
     return call(
         lora_join_kernel,
-        (shape((ranks, n * HEAD_WIDTH), bf16), shape((n * (rows - ranks), HEAD_WIDTH), bf16)),
-        [VMEM] * far,
-        *got,
+        (
+            shape((3 * ADAPTER_RANK, n * HEAD_WIDTH), bf16),
+            shape((n * inner_width, HEAD_WIDTH), bf16),
+        ),
+        [VMEM] * 2,
+        ordered,
+        lax.ppermute(ordered, "grp", [(0, 1), (1, 0)]),
     )
 
 
@@ -442,7 +467,7 @@
     keep, send = call(
         functools.partial(attend_kernel, far=far),
         (shape((2 * far,) + PARTIAL, bf16),) * 2,
-        [ANY, SMEM] + [VMEM] * 3,
+        [VMEM, SMEM] + [VMEM] * 3,
         turned[0],
         lengths,
         near,
@@ -468,25 +493,29 @@
             keep,
             theirs,
         )
-        marks.append(keep)
+        if distance == NEAR:
+            marks.append(keep)
+            ordered = turned[0] if whole else lora_far(turned, n, marks)
         theirs = swap(keep, n, distance)
         flip = far * NEAR // (2 * distance)
         distance *= 2
     hidden, normed = call(
         token_kernel,
         (shape(HEADS, f32), shape((far,) + HEADS, bf16)),
-        [VMEM] * 5,
+        [VMEM] * 6,
+        ordered,
         keep,
         theirs,
         column,
         next_near,
         norm_scale_vector.reshape(HEADS),
+        nanos=4000,
     )
     rows = call(
         join_kernel, shape((2 * far,) + HEADS, bf16), [VMEM] * 2, normed, swap(normed, n, 2)
     )
     next_rows = swap(rows, n, 1)
-    model, inner = turned if whole else lora_far(turned, n, marks)
+    model, inner = turned if whole else lora_join(ordered, adapter_hidden.shape[2])
     keep, send = call(
         functools.partial(expert_kernel, far=far),
         (shape((2 * far,) + HEADS, bf16),) * 2,

time: 78.6 us -> 58.4 us (0.74)
  local copies, waits for them, and re-layouts: 14 us -> 0.04 us
  waiting for transfers between devices: 30.4 us -> 20.1 us
  starting transfers between devices: 22.5 us -> 29.2 us
  Pallas kernels: 10.9 us -> 8.76 us
    unnamed x46 -> x16, local copies, waits for them, and re-layouts: 14 us -> 0.04 us
    ppermute x20, waiting for transfers between devices: 30.4 us -> 20 us  [swap(): return lax.ppermute(value, 'exp', [(t, t ^ distance) for t in range(n)])]
    ppermute x20, starting transfers between devices: 22.5 us -> 27.6 us  [swap(): return lax.ppermute(value, 'exp', [(t, t ^ distance) for t in range(n)])]
    pallas_call x18 -> x23, Pallas kernels: 10.9 us -> 8.76 us  [call(): pl.pallas_call(kernel, out_shape=shapes, in_specs=specs, out_specs=jax.tr...]
    ppermute x0 -> x1, starting transfers between devices: none -> 1.56 us  [lora_join(): lax.ppermute(ordered, 'grp', [(0, 1), (1, 0)])]
  transfers between devices with their start and end apart: 20 -> 21, of which waited for: 12 -> 11; matrix products, arithmetic and copies ran while one was open for 0% -> 0% of each run, Pallas kernels for 4% -> 7%
where the time goes in v6:
time: 58.4 us; the launch traced here: 58.2 us
  starting transfers between devices  29.2 us (50%)
  waiting for transfers between devices  20.1 us (34%)
  Pallas kernels  8.76 us (15%)
    ppermute x20, starting transfers between devices, swap(): return lax.ppermute(value, 'exp', [(t, t ^ distance) for t in range(n)])  27.6 us
    ppermute x20, waiting for transfers between devices, swap(): return lax.ppermute(value, 'exp', [(t, t ^ distance) for t in range(n)])  20 us
    pallas_call x23, Pallas kernels, call(): pl.pallas_call(kernel, out_shape=shapes, in_specs=specs, out_specs=jax.tr...  8.76 us
    ppermute x1, starting transfers between devices, lora_join(): lax.ppermute(ordered, 'grp', [(0, 1), (1, 0)])  1.56 us
  transfers between devices with their start and end apart: 21, of which 11 were waited for; matrix products, arithmetic and copies ran while one was open for 0% of the time, Pallas kernels for 7%

profile of v6, /device:TPU:0, one launch (start us, length us, event | category | flops | bytes accessed | tf_op | source)
XLA Modules:
  0.0 58.2 jit_solution(10064072589921125868)
XLA Ops:
  0.0 1.0 %shard_map.127.mine.after = bf16[1,48,128]{2,1,0:T(8,128)(2,1)S(1)} custom-call(bf16[1,2048]{1,0:T(2,128)(2,1)} %query.1, bf16[1,2048]{1,0:T(2,128)(2,1)} %resid.1, bf16[1,512]{1,0:T(2,128)(2,1)} %new.1, s32[1,8]{1,0:T(1,128)} %choice.1, f32[1,8]{1,0:T(1,128)} %probability.1), custom_call_target="tpu_custom_call" | custom-call | flops 4000000000 | tf_op jit(solution)/shard_map/pallas_call | solution.py:39
  1.0 4.1 %collective-permute-start = (bf16[1,48,128]{2,1,0:T(8,128)(2,1)S(1)}, bf16[1,48,128]{2,1,0:T(8,128)(2,1)S(1)}, u32[]{:S(2)}, u32[]{:S(2)}) collective-permute-start(bf16[1,48,128]{2,1,0:T(8,128)(2,1)S(1)} %shard_map.127.mine.after), channel_id=1, source_target_pairs={{0,8},{1,9},{2,10},{3,11},{4,12},{5,13},{6,14},{7,15},{8,0},{9,1},... | collective-permute-start | bytes 36872 | tf_op jit(solution)/shard_map/ppermute | solution.py:73
  5.1 0.1 shard_map.131
  5.2 1.6 %collective-permute-start.4 = (bf16[4,80,128]{2,1,0:T(8,128)(2,1)S(1)}, bf16[4,80,128]{2,1,0:T(8,128)(2,1)S(1)}, u32[]{:S(2)}, u32[]{:S(2)}) collective-permute-start(bf16[4,80,128]{2,1,0:T(8,128)(2,1)S(1)} %get-tuple-element.34), channel_id=1, source_target_pairs={{0,2},{1,3},{2,0},{3,1},{4,6},{5,7},{6,4},{7,5},{8,10},{9,11},{10,... | collective-permute-start | bytes 245768 | tf_op jit(solution)/shard_map/ppermute | solution.py:73
  6.8 1.9 %collective-permute-start.1 = (bf16[2,48,128]{2,1,0:T(8,128)(2,1)S(1)}, bf16[2,48,128]{2,1,0:T(8,128)(2,1)S(1)}, u32[]{:S(2)}, u32[]{:S(2)}) collective-permute-start(bf16[2,48,128]{2,1,0:T(8,128)(2,1)S(1)} %shard_map.128.mine.after), channel_id=1, source_target_pairs={{0,4},{1,5},{2,6},{3,7},{4,0},{5,1},{6,2},{7,3},{8,12},{9,13},{10,... | collective-permute-start | bytes 73736 | tf_op jit(solution)/shard_map/ppermute | solution.py:73
  8.7 0.1 collective-permute-start.5
  8.8 1.6 %collective-permute-start.3 = (bf16[4,80,128]{2,1,0:T(8,128)(2,1)S(1)}, bf16[4,80,128]{2,1,0:T(8,128)(2,1)S(1)}, u32[]{:S(2)}, u32[]{:S(2)}) collective-permute-start(bf16[4,80,128]{2,1,0:T(8,128)(2,1)S(1)} %shard_map.132), channel_id=1, source_target_pairs={{0,1},{1,0},{2,3},{3,2},{4,5},{5,4},{6,7},{7,6},{8,9},{9,8},{10,11... | collective-permute-start | bytes 245768 | tf_op jit(solution)/shard_map/ppermute | solution.py:73
  10.4 0.2 collective-permute-done.1.theirs
  10.7 1.9 %collective-permute-start.2 = (bf16[1,96,128]{2,1,0:T(8,128)(2,1)S(1)}, bf16[1,96,128]{2,1,0:T(8,128)(2,1)S(1)}, u32[]{:S(2)}, u32[]{:S(2)}) collective-permute-start(bf16[1,96,128]{2,1,0:T(8,128)(2,1)S(1)} %bitcast.10), channel_id=1, source_target_pairs={{0,2},{1,3},{2,0},{3,1},{4,6},{5,7},{6,4},{7,5},{8,10},{9,11},{10,... | collective-permute-start | bytes 73736 | tf_op jit(solution)/shard_map/ppermute | solution.py:73
  12.6 2.0 %collective-permute-done.2.theirs = bf16[1,96,128]{2,1,0:T(8,128)(2,1)S(1)} collective-permute-done((bf16[1,96,128]{2,1,0:T(8,128)(2,1)S(1)}, bf16[1,96,128]{2,1,0:T(8,128)(2,1)S(1)}, u32[]{:S(2)}, u32[]{:S(2)}) %collective-permute-start.2) | collective-permute-done | bytes 24608 | tf_op jit(solution)/shard_map/ppermute | solution.py:73
  14.6 0.0 collective-permute-start.6
  14.6 0.0 collective-permute-done.5.refs_3_
  14.6 0.0 copy-start.3
  14.6 0.0 copy-start.7
  14.7 2.0 %collective-permute-start.9 = (bf16[4,80,128]{2,1,0:T(8,128)(2,1)S(1)}, bf16[4,80,128]{2,1,0:T(8,128)(2,1)S(1)}, u32[]{:S(2)}, u32[]{:S(2)}) collective-permute-start(bf16[4,80,128]{2,1,0:T(8,128)(2,1)S(1)} %get-tuple-element.41), channel_id=1, source_target_pairs={{0,4},{1,5},{2,6},{3,7},{4,0},{5,1},{6,2},{7,3},{8,12},{9,13},{10,... | collective-permute-start | bytes 245768 | tf_op jit(solution)/shard_map/ppermute | solution.py:73
  16.6 2.7 %shard_map.135 = (bf16[8,32,128]{2,1,0:T(8,128)(2,1)S(1)}, bf16[8,32,128]{2,1,0:T(8,128)(2,1)S(1)}) custom-call(bf16[4,80,128]{2,1,0:T(8,128)(2,1)S(1)} %get-tuple-element.36.after.refs_0_, s32[8]{0:T(128)S(1)} %copy-done.7, bf16[2,96,128]{2,1,0:T(8,128)(2,1)S(1)} %shard_map.130.after.mine.near, ...), custom_call_target="tpu_custom_call" | custom-call | flops 8000000000 | tf_op jit(solution)/shard_map/pallas_call | solution.py:39
  19.3 0.3 collective-permute-start.7
  19.6 2.6 %collective-permute-start.10 = (bf16[4,80,128]{2,1,0:T(8,128)(2,1)S(1)}, bf16[4,80,128]{2,1,0:T(8,128)(2,1)S(1)}, u32[]{:S(2)}, u32[]{:S(2)}) collective-permute-start(bf16[4,80,128]{2,1,0:T(8,128)(2,1)S(1)} %shard_map.138), channel_id=1, source_target_pairs={{0,8},{1,9},{2,10},{3,11},{4,12},{5,13},{6,14},{7,15},{8,0},{9,1},... | collective-permute-start | bytes 245768 | tf_op jit(solution)/shard_map/ppermute | solution.py:73
  22.2 0.0 collective-permute-done.7.theirs
  22.2 0.5 shard_map.136
  22.7 1.6 %collective-permute-start.8 = (bf16[4,32,128]{2,1,0:T(8,128)(2,1)S(1)}, bf16[4,32,128]{2,1,0:T(8,128)(2,1)S(1)}, u32[]{:S(2)}, u32[]{:S(2)}) collective-permute-start(bf16[4,32,128]{2,1,0:T(8,128)(2,1)S(1)} %get-tuple-element.40), channel_id=1, source_target_pairs={{0,2},{1,3},{2,0},{3,1},{4,6},{5,7},{6,4},{7,5},{8,10},{9,11},{10,... | collective-permute-start | bytes 98312 | tf_op jit(solution)/shard_map/ppermute | solution.py:73
  24.3 1.9 %collective-permute-start.11 = (bf16[4,80,128]{2,1,0:T(8,128)(2,1)S(1)}, bf16[4,80,128]{2,1,0:T(8,128)(2,1)S(1)}, u32[]{:S(2)}, u32[]{:S(2)}) collective-permute-start(bf16[4,80,128]{2,1,0:T(8,128)(2,1)S(1)} %shard_map.139), channel_id=1, source_target_pairs={{0,12},{1,13},{2,14},{3,15},{4,8},{5,9},{6,10},{7,11},{8,4},{9,5},... | collective-permute-start | bytes 245768 | tf_op jit(solution)/shard_map/ppermute | solution.py:73
  26.1 0.5 collective-permute-done.8.theirs
  26.7 0.2 shard_map.137.after.mine
  26.9 1.6 %collective-permute-start.12 = (bf16[4,32,128]{2,1,0:T(8,128)(2,1)S(1)}, bf16[4,32,128]{2,1,0:T(8,128)(2,1)S(1)}, u32[]{:S(2)}, u32[]{:S(2)}) collective-permute-start(bf16[4,32,128]{2,1,0:T(8,128)(2,1)S(1)} %shard_map.137.after.mine), channel_id=1, source_target_pairs={{0,4},{1,5},{2,6},{3,7},{4,0},{5,1},{6,2},{7,3},{8,12},{9,13},{10,... | collective-permute-start | bytes 98312 | tf_op jit(solution)/shard_map/ppermute | solution.py:73
  28.5 2.5 %collective-permute-done.12.theirs = bf16[4,32,128]{2,1,0:T(8,128)(2,1)S(1)} collective-permute-done((bf16[4,32,128]{2,1,0:T(8,128)(2,1)S(1)}, bf16[4,32,128]{2,1,0:T(8,128)(2,1)S(1)}, u32[]{:S(2)}, u32[]{:S(2)}) %collective-permute-start.12) | collective-permute-done | bytes 32800 | tf_op jit(solution)/shard_map/ppermute | solution.py:73
  31.0 0.2 shard_map.141.mine
  31.3 0.0 copy-start.6
  31.3 1.0 %collective-permute-start.13 = (bf16[4,32,128]{2,1,0:T(8,128)(2,1)S(1)}, bf16[4,32,128]{2,1,0:T(8,128)(2,1)S(1)}, u32[]{:S(2)}, u32[]{:S(2)}) collective-permute-start(bf16[4,32,128]{2,1,0:T(8,128)(2,1)S(1)} %shard_map.141.mine), channel_id=1, source_target_pairs={{0,8},{1,9},{2,10},{3,11},{4,12},{5,13},{6,14},{7,15},{8,0},{9,1},... | collective-permute-start | bytes 98312 | tf_op jit(solution)/shard_map/ppermute | solution.py:73
  32.3 0.0 collective-permute-done.10.refs_2_
  32.3 0.0 collective-permute-done.11.refs_3_
  32.3 1.6 %collective-permute-start.16 = (bf16[16,80,128]{2,1,0:T(8,128)(2,1)S(1)}, bf16[16,80,128]{2,1,0:T(8,128)(2,1)S(1)}, u32[]{:S(2)}, u32[]{:S(2)}) collective-permute-start(bf16[16,80,128]{2,1,0:T(8,128)(2,1)S(1)} %shard_map.140.after.mine), channel_id=1, source_target_pairs={{0,16},{16,0},{1,17},{17,1},{2,18},{18,2},{3,19},{19,3},{4,20},{20... | collective-permute-start | bytes 983048 | tf_op jit(solution)/shard_map/ppermute | solution.py:405
  33.9 2.3 %collective-permute-done.13.theirs = bf16[4,32,128]{2,1,0:T(8,128)(2,1)S(1)} collective-permute-done((bf16[4,32,128]{2,1,0:T(8,128)(2,1)S(1)}, bf16[4,32,128]{2,1,0:T(8,128)(2,1)S(1)}, u32[]{:S(2)}, u32[]{:S(2)}) %collective-permute-start.13) | collective-permute-done | bytes 32800 | tf_op jit(solution)/shard_map/ppermute | solution.py:73
  36.2 0.4 shard_map.142
  36.5 1.4 %collective-permute-start.14 = (bf16[4,16,128]{2,1,0:T(8,128)(2,1)S(1)}, bf16[4,16,128]{2,1,0:T(8,128)(2,1)S(1)}, u32[]{:S(2)}, u32[]{:S(2)}) collective-permute-start(bf16[4,16,128]{2,1,0:T(8,128)(2,1)S(1)} %get-tuple-element.46.mine), channel_id=1, source_target_pairs={{0,2},{1,3},{2,0},{3,1},{4,6},{5,7},{6,4},{7,5},{8,10},{9,11},{10,... | collective-permute-start | bytes 49160 | tf_op jit(solution)/shard_map/ppermute | solution.py:73
  38.0 2.4 %collective-permute-done.14.theirs = bf16[4,16,128]{2,1,0:T(8,128)(2,1)S(1)} collective-permute-done((bf16[4,16,128]{2,1,0:T(8,128)(2,1)S(1)}, bf16[4,16,128]{2,1,0:T(8,128)(2,1)S(1)}, u32[]{:S(2)}, u32[]{:S(2)}) %collective-permute-start.14) | collective-permute-done | bytes 16416 | tf_op jit(solution)/shard_map/ppermute | solution.py:73
  40.4 0.1 shard_map.144
  40.5 1.1 %collective-permute-done.15.theirs = bf16[8,16,128]{2,1,0:T(8,128)(2,1)S(1)} collective-permute-done((bf16[8,16,128]{2,1,0:T(8,128)(2,1)S(1)}, bf16[8,16,128]{2,1,0:T(8,128)(2,1)S(1)}, u32[]{:S(2)}, u32[]{:S(2)}) %collective-permute-start.15) | collective-permute-done | bytes 32800 | tf_op jit(solution)/shard_map/ppermute | solution.py:73
  41.6 2.8 %shard_map.145 = (bf16[8,16,128]{2,1,0:T(8,128)(2,1)S(1)}, bf16[8,16,128]{2,1,0:T(8,128)(2,1)S(1)}) custom-call(bf16[8,16,128]{2,1,0:T(8,128)(2,1)S(1)} %shard_map.143.mine, bf16[8,16,128]{2,1,0:T(8,128)(2,1)S(1)} %collective-permute-done.15.theirs, bf16[2,96,128]{2,1,0:T(8,128)(2,1)S(1)} %shard_map.130.after.mine.near, ...), custom_call_target="tpu_custom_call" | custom-call | flops 400000000 | tf_op jit(solution)/shard_map/pallas_call | solution.py:39
  44.3 0.2 collective-permute-start.17
  44.6 1.0 %collective-permute-done.17.theirs = bf16[8,16,128]{2,1,0:T(8,128)(2,1)S(1)} collective-permute-done((bf16[8,16,128]{2,1,0:T(8,128)(2,1)S(1)}, bf16[8,16,128]{2,1,0:T(8,128)(2,1)S(1)}, u32[]{:S(2)}, u32[]{:S(2)}) %collective-permute-start.17) | collective-permute-done | bytes 32800 | tf_op jit(solution)/shard_map/ppermute | solution.py:73
  45.6 1.4 %collective-permute-start.18 = (bf16[4,16,128]{2,1,0:T(8,128)(2,1)S(1)}, bf16[4,16,128]{2,1,0:T(8,128)(2,1)S(1)}, u32[]{:S(2)}, u32[]{:S(2)}) collective-permute-start(bf16[4,16,128]{2,1,0:T(8,128)(2,1)S(1)} %get-tuple-element.52), channel_id=1, source_target_pairs={{0,2},{1,3},{2,0},{3,1},{4,6},{5,7},{6,4},{7,5},{8,10},{9,11},{10,... | collective-permute-start | bytes 49160 | tf_op jit(solution)/shard_map/ppermute | solution.py:73
  47.1 2.4 %collective-permute-done.18.theirs = bf16[4,16,128]{2,1,0:T(8,128)(2,1)S(1)} collective-permute-done((bf16[4,16,128]{2,1,0:T(8,128)(2,1)S(1)}, bf16[4,16,128]{2,1,0:T(8,128)(2,1)S(1)}, u32[]{:S(2)}, u32[]{:S(2)}) %collective-permute-start.18) | collective-permute-done | bytes 16416 | tf_op jit(solution)/shard_map/ppermute | solution.py:73
  49.4 1.4 %collective-permute-start.19 = (bf16[2,16,128]{2,1,0:T(8,128)(2,1)S(1)}, bf16[2,16,128]{2,1,0:T(8,128)(2,1)S(1)}, u32[]{:S(2)}, u32[]{:S(2)}) collective-permute-start(bf16[2,16,128]{2,1,0:T(8,128)(2,1)S(1)} %get-tuple-element.54), channel_id=1, source_target_pairs={{0,4},{1,5},{2,6},{3,7},{4,0},{5,1},{6,2},{7,3},{8,12},{9,13},{10,... | collective-permute-start | bytes 24584 | tf_op jit(solution)/shard_map/ppermute | solution.py:73
  50.8 2.2 %collective-permute-done.19.theirs = bf16[2,16,128]{2,1,0:T(8,128)(2,1)S(1)} collective-permute-done((bf16[2,16,128]{2,1,0:T(8,128)(2,1)S(1)}, bf16[2,16,128]{2,1,0:T(8,128)(2,1)S(1)}, u32[]{:S(2)}, u32[]{:S(2)}) %collective-permute-start.19) | collective-permute-done | bytes 8224 | tf_op jit(solution)/shard_map/ppermute | solution.py:73
  53.1 1.1 %collective-permute-start.20 = (bf16[1,16,128]{2,1,0:T(8,128)(2,1)S(1)}, bf16[1,16,128]{2,1,0:T(8,128)(2,1)S(1)}, u32[]{:S(2)}, u32[]{:S(2)}) collective-permute-start(bf16[1,16,128]{2,1,0:T(8,128)(2,1)S(1)} %get-tuple-element.56), channel_id=1, source_target_pairs={{0,8},{1,9},{2,10},{3,11},{4,12},{5,13},{6,14},{7,15},{8,0},{9,1},... | collective-permute-start | bytes 12296 | tf_op jit(solution)/shard_map/ppermute | solution.py:73
  54.2 3.4 %collective-permute-done.20.theirs = bf16[1,16,128]{2,1,0:T(8,128)(2,1)S(1)} collective-permute-done((bf16[1,16,128]{2,1,0:T(8,128)(2,1)S(1)}, bf16[1,16,128]{2,1,0:T(8,128)(2,1)S(1)}, u32[]{:S(2)}, u32[]{:S(2)}) %collective-permute-start.20) | collective-permute-done | bytes 4128 | tf_op jit(solution)/shard_map/ppermute | solution.py:73
  57.6 0.6 %shard_map.149 = bf16[1,2048]{1,0:T(2,128)(2,1)} custom-call(f32[16,128]{1,0:T(8,128)S(1)} %get-tuple-element.45.hidden, bf16[1,16,128]{2,1,0:T(8,128)(2,1)S(1)} %get-tuple-element.55.mine, bf16[1,16,128]{2,1,0:T(8,128)(2,1)S(1)} %collective-permute-done.20.theirs), custom_call_target="tpu_custom_call" | custom-call | flops 400000000 | tf_op jit(solution)/shard_map/pallas_call | solution.py:39
  (33 shorter events, 0.2 us)
Async XLA Ops:
  0.0 5.1 %copy-start.5 = (bf16[16,96,48]{1,2,0:T(8,128)(2,1)S(1)}, bf16[16,96,48]{1,2,0:T(8,128)(2,1)}, u32[]{:S(2)}) copy-start(bf16[16,96,48]{1,2,0:T(8,128)(2,1)} %param.25) | copy-start | bytes 442372
  0.0 5.1 %copy-start.4 = (bf16[16,96,128]{2,1,0:T(8,128)(2,1)S(1)}, bf16[16,96,128]{2,1,0:T(8,128)(2,1)}, u32[]{:S(2)}) copy-start(bf16[16,96,128]{2,1,0:T(8,128)(2,1)} %model.1) | copy-start | bytes 1179652
  1.0 5.8 %collective-permute-start = (bf16[1,48,128]{2,1,0:T(8,128)(2,1)S(1)}, bf16[1,48,128]{2,1,0:T(8,128)(2,1)S(1)}, u32[]{:S(2)}, u32[]{:S(2)}) collective-permute-start(bf16[1,48,128]{2,1,0:T(8,128)(2,1)S(1)} %shard_map.127.mine.after), channel_id=1, source_target_pairs={{0,8},{1,9},{2,10},{3,11},{4,12},{5,13},{6,14},{7,15},{8,0},{9,1},... | collective-permute-start | bytes 36872 | tf_op jit(solution)/shard_map/ppermute | solution.py:73
  5.2 9.3 %collective-permute-start.4 = (bf16[4,80,128]{2,1,0:T(8,128)(2,1)S(1)}, bf16[4,80,128]{2,1,0:T(8,128)(2,1)S(1)}, u32[]{:S(2)}, u32[]{:S(2)}) collective-permute-start(bf16[4,80,128]{2,1,0:T(8,128)(2,1)S(1)} %get-tuple-element.34), channel_id=1, source_target_pairs={{0,2},{1,3},{2,0},{3,1},{4,6},{5,7},{6,4},{7,5},{8,10},{9,11},{10,... | collective-permute-start | bytes 245768 | tf_op jit(solution)/shard_map/ppermute | solution.py:73
  6.8 3.8 %collective-permute-start.1 = (bf16[2,48,128]{2,1,0:T(8,128)(2,1)S(1)}, bf16[2,48,128]{2,1,0:T(8,128)(2,1)S(1)}, u32[]{:S(2)}, u32[]{:S(2)}) collective-permute-start(bf16[2,48,128]{2,1,0:T(8,128)(2,1)S(1)} %shard_map.128.mine.after), channel_id=1, source_target_pairs={{0,4},{1,5},{2,6},{3,7},{4,0},{5,1},{6,2},{7,3},{8,12},{9,13},{10,... | collective-permute-start | bytes 73736 | tf_op jit(solution)/shard_map/ppermute | solution.py:73
  8.7 5.9 %collective-permute-start.5 = (bf16[4,80,128]{2,1,0:T(8,128)(2,1)S(1)}, bf16[4,80,128]{2,1,0:T(8,128)(2,1)S(1)}, u32[]{:S(2)}, u32[]{:S(2)}) collective-permute-start(bf16[4,80,128]{2,1,0:T(8,128)(2,1)S(1)} %shard_map.133), channel_id=1, source_target_pairs={{0,3},{1,2},{2,1},{3,0},{4,7},{5,6},{6,5},{7,4},{8,11},{9,10},{10,... | collective-permute-start | bytes 245768 | tf_op jit(solution)/shard_map/ppermute | solution.py:73
  8.8 5.8 %collective-permute-start.3 = (bf16[4,80,128]{2,1,0:T(8,128)(2,1)S(1)}, bf16[4,80,128]{2,1,0:T(8,128)(2,1)S(1)}, u32[]{:S(2)}, u32[]{:S(2)}) collective-permute-start(bf16[4,80,128]{2,1,0:T(8,128)(2,1)S(1)} %shard_map.132), channel_id=1, source_target_pairs={{0,1},{1,0},{2,3},{3,2},{4,5},{5,4},{6,7},{7,6},{8,9},{9,8},{10,11... | collective-permute-start | bytes 245768 | tf_op jit(solution)/shard_map/ppermute | solution.py:73
  10.7 3.9 %collective-permute-start.2 = (bf16[1,96,128]{2,1,0:T(8,128)(2,1)S(1)}, bf16[1,96,128]{2,1,0:T(8,128)(2,1)S(1)}, u32[]{:S(2)}, u32[]{:S(2)}) collective-permute-start(bf16[1,96,128]{2,1,0:T(8,128)(2,1)S(1)} %bitcast.10), channel_id=1, source_target_pairs={{0,2},{1,3},{2,0},{3,1},{4,6},{5,7},{6,4},{7,5},{8,10},{9,11},{10,... | collective-permute-start | bytes 73736 | tf_op jit(solution)/shard_map/ppermute | solution.py:73
  14.6 2.1 %collective-permute-start.6 = (bf16[2,96,128]{2,1,0:T(8,128)(2,1)S(1)}, bf16[2,96,128]{2,1,0:T(8,128)(2,1)S(1)}, u32[]{:S(2)}, u32[]{:S(2)}) collective-permute-start(bf16[2,96,128]{2,1,0:T(8,128)(2,1)S(1)} %shard_map.130.after.mine.near), channel_id=1, source_target_pairs={{0,1},{1,0},{2,3},{3,2},{4,5},{5,4},{6,7},{7,6},{8,9},{9,8},{10,11... | collective-permute-start | bytes 147464 | tf_op jit(solution)/shard_map/ppermute | solution.py:73
  14.6 2.0 %copy-start.3 = (bf16[8,192,512]{2,1,0:T(8,128)(2,1)S(1)}, bf16[8,192,512]{2,1,0:T(8,128)(2,1)}, u32[]{:S(2)}) copy-start(bf16[8,192,512]{2,1,0:T(8,128)(2,1)} %cache.1) | copy-start | bytes 4718596
  14.6 2.0 %copy-start.7 = (s32[8]{0:T(128)S(1)}, s32[8]{0:T(128)}, u32[]{:S(2)}) copy-start(s32[8]{0:T(128)} %lengths.1) | copy-start | bytes 100
  14.7 17.6 %collective-permute-start.9 = (bf16[4,80,128]{2,1,0:T(8,128)(2,1)S(1)}, bf16[4,80,128]{2,1,0:T(8,128)(2,1)S(1)}, u32[]{:S(2)}, u32[]{:S(2)}) collective-permute-start(bf16[4,80,128]{2,1,0:T(8,128)(2,1)S(1)} %get-tuple-element.41), channel_id=1, source_target_pairs={{0,4},{1,5},{2,6},{3,7},{4,0},{5,1},{6,2},{7,3},{8,12},{9,13},{10,... | collective-permute-start | bytes 245768 | tf_op jit(solution)/shard_map/ppermute | solution.py:73
  19.3 2.9 %collective-permute-start.7 = (bf16[8,32,128]{2,1,0:T(8,128)(2,1)S(1)}, bf16[8,32,128]{2,1,0:T(8,128)(2,1)S(1)}, u32[]{:S(2)}, u32[]{:S(2)}) collective-permute-start(bf16[8,32,128]{2,1,0:T(8,128)(2,1)S(1)} %get-tuple-element.38), channel_id=1, source_target_pairs={{0,1},{1,0},{2,3},{3,2},{4,5},{5,4},{6,7},{7,6},{8,9},{9,8},{10,11... | collective-permute-start | bytes 196616 | tf_op jit(solution)/shard_map/ppermute | solution.py:73
  19.6 12.7 %collective-permute-start.10 = (bf16[4,80,128]{2,1,0:T(8,128)(2,1)S(1)}, bf16[4,80,128]{2,1,0:T(8,128)(2,1)S(1)}, u32[]{:S(2)}, u32[]{:S(2)}) collective-permute-start(bf16[4,80,128]{2,1,0:T(8,128)(2,1)S(1)} %shard_map.138), channel_id=1, source_target_pairs={{0,8},{1,9},{2,10},{3,11},{4,12},{5,13},{6,14},{7,15},{8,0},{9,1},... | collective-permute-start | bytes 245768 | tf_op jit(solution)/shard_map/ppermute | solution.py:73
  22.7 4.0 %collective-permute-start.8 = (bf16[4,32,128]{2,1,0:T(8,128)(2,1)S(1)}, bf16[4,32,128]{2,1,0:T(8,128)(2,1)S(1)}, u32[]{:S(2)}, u32[]{:S(2)}) collective-permute-start(bf16[4,32,128]{2,1,0:T(8,128)(2,1)S(1)} %get-tuple-element.40), channel_id=1, source_target_pairs={{0,2},{1,3},{2,0},{3,1},{4,6},{5,7},{6,4},{7,5},{8,10},{9,11},{10,... | collective-permute-start | bytes 98312 | tf_op jit(solution)/shard_map/ppermute | solution.py:73
  24.3 8.0 %collective-permute-start.11 = (bf16[4,80,128]{2,1,0:T(8,128)(2,1)S(1)}, bf16[4,80,128]{2,1,0:T(8,128)(2,1)S(1)}, u32[]{:S(2)}, u32[]{:S(2)}) collective-permute-start(bf16[4,80,128]{2,1,0:T(8,128)(2,1)S(1)} %shard_map.139), channel_id=1, source_target_pairs={{0,12},{1,13},{2,14},{3,15},{4,8},{5,9},{6,10},{7,11},{8,4},{9,5},... | collective-permute-start | bytes 245768 | tf_op jit(solution)/shard_map/ppermute | solution.py:73
  26.9 4.1 %collective-permute-start.12 = (bf16[4,32,128]{2,1,0:T(8,128)(2,1)S(1)}, bf16[4,32,128]{2,1,0:T(8,128)(2,1)S(1)}, u32[]{:S(2)}, u32[]{:S(2)}) collective-permute-start(bf16[4,32,128]{2,1,0:T(8,128)(2,1)S(1)} %shard_map.137.after.mine), channel_id=1, source_target_pairs={{0,4},{1,5},{2,6},{3,7},{4,0},{5,1},{6,2},{7,3},{8,12},{9,13},{10,... | collective-permute-start | bytes 98312 | tf_op jit(solution)/shard_map/ppermute | solution.py:73
  31.3 4.9 %copy-start.6 = (f32[2048]{0:T(1024)S(1)}, f32[2048]{0:T(1024)}, u32[]{:S(2)}) copy-start(f32[2048]{0:T(1024)} %param.18) | copy-start | bytes 24580
  31.3 4.9 %collective-permute-start.13 = (bf16[4,32,128]{2,1,0:T(8,128)(2,1)S(1)}, bf16[4,32,128]{2,1,0:T(8,128)(2,1)S(1)}, u32[]{:S(2)}, u32[]{:S(2)}) collective-permute-start(bf16[4,32,128]{2,1,0:T(8,128)(2,1)S(1)} %shard_map.141.mine), channel_id=1, source_target_pairs={{0,8},{1,9},{2,10},{3,11},{4,12},{5,13},{6,14},{7,15},{8,0},{9,1},... | collective-permute-start | bytes 98312 | tf_op jit(solution)/shard_map/ppermute | solution.py:73
  32.3 8.0 %collective-permute-start.16 = (bf16[16,80,128]{2,1,0:T(8,128)(2,1)S(1)}, bf16[16,80,128]{2,1,0:T(8,128)(2,1)S(1)}, u32[]{:S(2)}, u32[]{:S(2)}) collective-permute-start(bf16[16,80,128]{2,1,0:T(8,128)(2,1)S(1)} %shard_map.140.after.mine), channel_id=1, source_target_pairs={{0,16},{16,0},{1,17},{17,1},{2,18},{18,2},{3,19},{19,3},{4,20},{20... | collective-permute-start | bytes 983048 | tf_op jit(solution)/shard_map/ppermute | solution.py:405
  36.2 5.4 %copy-start = (bf16[1,2048,768]{2,1,0:T(8,128)(2,1)S(1)}, bf16[1,2048,768]{2,1,0:T(8,128)(2,1)}, u32[]{:S(2)}) copy-start(bf16[1,2048,768]{2,1,0:T(8,128)(2,1)} %param.21) | copy-start | bytes 9437188
  36.2 5.4 %copy-start.1 = (bf16[1,2048,768]{2,1,0:T(8,128)(2,1)S(1)}, bf16[1,2048,768]{2,1,0:T(8,128)(2,1)}, u32[]{:S(2)}) copy-start(bf16[1,2048,768]{2,1,0:T(8,128)(2,1)} %param.22) | copy-start | bytes 9437188
  36.2 5.4 %copy-start.2 = (bf16[1,768,2048]{2,1,0:T(8,128)(2,1)S(1)}, bf16[1,768,2048]{2,1,0:T(8,128)(2,1)}, u32[]{:S(2)}) copy-start(bf16[1,768,2048]{2,1,0:T(8,128)(2,1)} %param.23) | copy-start | bytes 9437188
  36.5 3.8 %collective-permute-start.14 = (bf16[4,16,128]{2,1,0:T(8,128)(2,1)S(1)}, bf16[4,16,128]{2,1,0:T(8,128)(2,1)S(1)}, u32[]{:S(2)}, u32[]{:S(2)}) collective-permute-start(bf16[4,16,128]{2,1,0:T(8,128)(2,1)S(1)} %get-tuple-element.46.mine), channel_id=1, source_target_pairs={{0,2},{1,3},{2,0},{3,1},{4,6},{5,7},{6,4},{7,5},{8,10},{9,11},{10,... | collective-permute-start | bytes 49160 | tf_op jit(solution)/shard_map/ppermute | solution.py:73
  40.4 1.2 %collective-permute-start.15 = (bf16[8,16,128]{2,1,0:T(8,128)(2,1)S(1)}, bf16[8,16,128]{2,1,0:T(8,128)(2,1)S(1)}, u32[]{:S(2)}, u32[]{:S(2)}) collective-permute-start(bf16[8,16,128]{2,1,0:T(8,128)(2,1)S(1)} %shard_map.143.mine), channel_id=1, source_target_pairs={{0,1},{1,0},{2,3},{3,2},{4,5},{5,4},{6,7},{7,6},{8,9},{9,8},{10,11... | collective-permute-start | bytes 98312 | tf_op jit(solution)/shard_map/ppermute | solution.py:73
  44.3 1.3 %collective-permute-start.17 = (bf16[8,16,128]{2,1,0:T(8,128)(2,1)S(1)}, bf16[8,16,128]{2,1,0:T(8,128)(2,1)S(1)}, u32[]{:S(2)}, u32[]{:S(2)}) collective-permute-start(bf16[8,16,128]{2,1,0:T(8,128)(2,1)S(1)} %get-tuple-element.50), channel_id=1, source_target_pairs={{0,1},{1,0},{2,3},{3,2},{4,5},{5,4},{6,7},{7,6},{8,9},{9,8},{10,11... | collective-permute-start | bytes 98312 | tf_op jit(solution)/shard_map/ppermute | solution.py:73
  45.6 3.8 %collective-permute-start.18 = (bf16[4,16,128]{2,1,0:T(8,128)(2,1)S(1)}, bf16[4,16,128]{2,1,0:T(8,128)(2,1)S(1)}, u32[]{:S(2)}, u32[]{:S(2)}) collective-permute-start(bf16[4,16,128]{2,1,0:T(8,128)(2,1)S(1)} %get-tuple-element.52), channel_id=1, source_target_pairs={{0,2},{1,3},{2,0},{3,1},{4,6},{5,7},{6,4},{7,5},{8,10},{9,11},{10,... | collective-permute-start | bytes 49160 | tf_op jit(solution)/shard_map/ppermute | solution.py:73
  49.4 3.7 %collective-permute-start.19 = (bf16[2,16,128]{2,1,0:T(8,128)(2,1)S(1)}, bf16[2,16,128]{2,1,0:T(8,128)(2,1)S(1)}, u32[]{:S(2)}, u32[]{:S(2)}) collective-permute-start(bf16[2,16,128]{2,1,0:T(8,128)(2,1)S(1)} %get-tuple-element.54), channel_id=1, source_target_pairs={{0,4},{1,5},{2,6},{3,7},{4,0},{5,1},{6,2},{7,3},{8,12},{9,13},{10,... | collective-permute-start | bytes 24584 | tf_op jit(solution)/shard_map/ppermute | solution.py:73
  53.1 4.5 %collective-permute-start.20 = (bf16[1,16,128]{2,1,0:T(8,128)(2,1)S(1)}, bf16[1,16,128]{2,1,0:T(8,128)(2,1)S(1)}, u32[]{:S(2)}, u32[]{:S(2)}) collective-permute-start(bf16[1,16,128]{2,1,0:T(8,128)(2,1)S(1)} %get-tuple-element.56), channel_id=1, source_target_pairs={{0,8},{1,9},{2,10},{3,11},{4,12},{5,13},{6,14},{7,15},{8,0},{9,1},... | collective-permute-start | bytes 12296 | tf_op jit(solution)/shard_map/ppermute | solution.py:73

commit v7 on v6

--- a/solution.py
+++ b/solution.py
@@ -27,6 +27,7 @@
 floor_score = -1e30
 epsilon = 1e-06
 FILL = 4000
+MERGE = 1600
 
 VMEM = pl.BlockSpec(memory_space=pltpu.VMEM)
 SMEM = pl.BlockSpec(memory_space=pltpu.SMEM)
@@ -47,16 +48,6 @@
         ),
         compiler_params=pltpu.CompilerParams(vmem_limit_bytes=limit * 1024 * 1024),
     )(*args)
-
-
-def hold_kernel(value, after, out):
-    out[...] = value[...]
-
-
-def hold(value, after):
-    return call(
-        hold_kernel, shape(value.shape, value.dtype), [VMEM] * 2, value, after, nanos=FILL
-    )
 
 
 def iota(dims, dim):
@@ -297,36 +288,37 @@
     out[...] = line.astype(bf16)
 
 
-def lora_pack_kernel(after, model, inner, *outs):
-    low, first = lax.axis_index("exp") % NEAR, lax.axis_index("grp") == 0
-    ranks, split, most = model.shape[1], model.shape[1] // 2, outs[0].shape[1] - model.shape[1] // 2
+def without(index, bit):
+    return (index // (2 * bit)) * bit + index % bit
+
+
+def lora_pack_kernel(after, model, inner, keep, send, *, bit):
+    me, first = lax.axis_index("exp"), lax.axis_index("grp") == 0
+    ranks, split = model.shape[1], model.shape[1] // 2
+    most = keep.shape[1] - split
     rest = inner.shape[1] - most
-    for k, out in enumerate(outs):
+    for out in (keep, send):
         out[:, split:, ranks:] = jnp.zeros((out.shape[0], most, HEAD_WIDTH - ranks), out.dtype)
-        for z in range(out.shape[0]):
-            at = z * NEAR + (low ^ k)
-            out[z, :split] = jnp.where(first, model[at, :split], model[at, split:])
-            lower = inner[at, most:]
-            if rest < most:
-                pad = jnp.zeros((most - rest, ranks), out.dtype)
-                lower = jnp.concatenate([lower, pad], axis=0)
-            out[z, split:, :ranks] = jnp.where(first, inner[at, :most], lower)
-
-
-def lora_turn_kernel(after, *refs):
+    for d in range(model.shape[0]):
+        out, at, source = (send if d & bit else keep), without(d, bit), me ^ d
+        out[at, :split] = jnp.where(first, model[source, :split], model[source, split:])
+        lower = inner[source, most:]
+        if rest < most:
+            pad = jnp.zeros((most - rest, ranks), out.dtype)
+            lower = jnp.concatenate([lower, pad], axis=0)
+        out[at, split:, :ranks] = jnp.where(first, inner[source, :most], lower)
+
+
+def lora_turn_kernel(after, kept, got, *outs, bit, following):
+    for d in range(2 * kept.shape[0]):
+        value = (got if d & bit else kept)[without(d, bit)]
+        outs[1 if d & following else 0][without(d, following)] = value
+
+
+def lora_order_kernel(after, kept, got, out, *, bit):
     me = lax.axis_index("exp")
-    low, high = me % NEAR, me // NEAR
-    got, outs = refs[:NEAR], refs[NEAR:]
-    for j, out in enumerate(outs):
-        for k, ref in enumerate(got):
-            out[low ^ k] = ref[high ^ j]
-
-
-def lora_order_kernel(after, *refs):
-    high = lax.axis_index("exp") // NEAR
-    got, out = refs[:-1], refs[-1]
-    for j, ref in enumerate(got):
-        out[pl.ds((high ^ j) * NEAR, NEAR)] = ref[...]
+    for d in range(2 * kept.shape[0]):
+        out[me ^ d] = (got if d & bit else kept)[without(d, bit)]
 
 
 def lora_join_kernel(mine, theirs, model, inner):
@@ -343,7 +335,7 @@
         inner[at * width + most : (at + 1) * width] = halves[1][split : split + width - most]
 
 
-def lora_near(adapter_model, adapter_hidden, n, marks):
+def lora_start(adapter_model, adapter_hidden, n, after):
     total, ranks, model_width = adapter_model.shape
     inner_width = adapter_hidden.shape[2]
     inner = jnp.transpose(adapter_hidden, (0, 2, 1))
@@ -351,43 +343,41 @@
         model = lax.all_to_all(adapter_model, "exp", split_axis=0, concat_axis=2, tiled=True)
         inner = lax.all_to_all(inner, "exp", split_axis=0, concat_axis=1, tiled=True)
         return [model[0], inner[0]], True
-    far = n // NEAR
     block = (ranks // 2 + pad16(inner_width // 2), HEAD_WIDTH)
     packed = call(
-        lora_pack_kernel,
-        (shape((far,) + block, bf16),) * NEAR,
+        functools.partial(lora_pack_kernel, bit=n // 2),
+        (shape((n // 2,) + block, bf16),) * 2,
         [VMEM] * 3,
-        marks[0],
+        after,
         adapter_model,
         inner,
         nanos=FILL,
     )
-    turned = call(
-        lora_turn_kernel,
-        (shape((NEAR,) + block, bf16),) * far,
-        [VMEM] * (1 + NEAR),
-        marks[3],
-        packed[0],
-        swap(hold(packed[1], marks[1]), n, 1),
-        swap(packed[2], n, 2),
-        swap(hold(packed[3], marks[1]), n, 3),
+    return packed, False
+
+
+def lora_turn(state, n, bit, following, after):
+    keep, send = state
+    return call(
+        functools.partial(lora_turn_kernel, bit=bit, following=following),
+        (shape(keep.shape, bf16),) * 2,
+        [VMEM] * 3,
+        after,
+        keep,
+        swap(send, n, bit),
         nanos=FILL,
     )
-    return turned, False
-
-
-def lora_far(turned, n, marks):
-    far = len(turned)
-    rows = turned[0].shape[1]
-    got = [turned[0], swap(turned[1], n, NEAR)]
-    for j in range(2, far):
-        got.append(swap(hold(turned[j], marks[j - 2]), n, j * NEAR))
+
+
+def lora_order(state, n, bit, after):
+    keep, send = state
     return call(
-        lora_order_kernel,
-        shape((n, rows, HEAD_WIDTH), bf16),
-        [VMEM] * (1 + far),
-        marks[far - 2],
-        *got,
+        functools.partial(lora_order_kernel, bit=bit),
+        shape((n,) + keep.shape[1:], bf16),
+        [VMEM] * 3,
+        after,
+        keep,
+        swap(send, n, bit),
         nanos=FILL,
     )
 
@@ -434,7 +424,8 @@
         + [pltpu.SemaphoreType.DMA((5,))],
         nanos=4000,
     )
-    marks, distance = [message], n // 2
+    state, whole = lora_start(adapter_model, adapter_hidden, n, message)
+    distance = n // 2
     while distance > NEAR:
         message = call(
             join_kernel,
@@ -452,7 +443,8 @@
         message,
         swap(message, n, NEAR),
     )
-    marks += [message, column]
+    if not whole:
+        state = lora_turn(state, n, n // 2, NEAR, column)
     narrow = narrow[None]
     near = call(
         join_kernel,
@@ -461,29 +453,28 @@
         narrow,
         swap(narrow, n, 2),
     )
-    marks.append(near)
-    turned, whole = lora_near(adapter_model, adapter_hidden, n, marks)
     next_near = swap(near, n, 1)
     keep, send = call(
         functools.partial(attend_kernel, far=far),
         (shape((2 * far,) + PARTIAL, bf16),) * 2,
         [VMEM, SMEM] + [VMEM] * 3,
-        turned[0],
+        state[0],
         lengths,
         near,
         next_near,
         key_value_cache,
         nanos=8000,
     )
-    marks = [keep]
     keep, send = call(
         functools.partial(merge_kernel, flip=0),
         (shape((far,) + PARTIAL, bf16),) * 2,
         [VMEM] * 2,
         keep,
         swap(send, n, 1),
-    )
-    marks.append(keep)
+        nanos=MERGE,
+    )
+    if not whole:
+        state = lora_turn(state, n, NEAR, 2, keep)
     theirs, distance, flip = swap(send, n, 2), NEAR, 0
     while distance < n:
         keep = call(
@@ -492,13 +483,16 @@
             [VMEM] * 2,
             keep,
             theirs,
+            nanos=MERGE,
         )
-        if distance == NEAR:
-            marks.append(keep)
-            ordered = turned[0] if whole else lora_far(turned, n, marks)
+        if distance == NEAR and not whole:
+            state = lora_turn(state, n, 2, 1, keep)
+        elif not whole:
+            ordered = lora_order(state, n, 1, keep)
         theirs = swap(keep, n, distance)
         flip = far * NEAR // (2 * distance)
         distance *= 2
+    ordered = state[0] if whole else ordered
     hidden, normed = call(
         token_kernel,
         (shape(HEADS, f32), shape((far,) + HEADS, bf16)),
@@ -515,7 +509,7 @@
         join_kernel, shape((2 * far,) + HEADS, bf16), [VMEM] * 2, normed, swap(normed, n, 2)
     )
     next_rows = swap(rows, n, 1)
-    model, inner = turned if whole else lora_join(ordered, adapter_hidden.shape[2])
+    model, inner = state if whole else lora_join(ordered, adapter_hidden.shape[2])
     keep, send = call(
         functools.partial(expert_kernel, far=far),
         (shape((2 * far,) + HEADS, bf16),) * 2,

time: 58.4 us -> 63.9 us (1.094)
  waiting for transfers between devices: 20.1 us -> 27.8 us
  starting transfers between devices: 29.2 us -> 26 us
  local copies, waits for them, and re-layouts: 0.04 us -> 1.03 us
    ppermute x20 -> x18, waiting for transfers between devices: 20 us -> 24.1 us  [swap(): return lax.ppermute(value, 'exp', [(t, t ^ distance) for t in range(n)])]
    ppermute x1, waiting for transfers between devices: 0.01 us -> 3.7 us  [lora_join(): lax.ppermute(ordered, 'grp', [(0, 1), (1, 0)])]
    ppermute x20 -> x18, starting transfers between devices: 27.6 us -> 24.4 us  [swap(): return lax.ppermute(value, 'exp', [(t, t ^ distance) for t in range(n)])]
    unnamed x16, local copies, waits for them, and re-layouts: 0.04 us -> 1.03 us
    pallas_call x23 -> x21, Pallas kernels: 8.76 us -> 8.75 us  [call(): pl.pallas_call(kernel, out_shape=shapes, in_specs=specs, out_specs=jax.tr...]
  transfers between devices with their start and end apart: 21 -> 19, of which waited for: 11 -> 14; matrix products, arithmetic and copies ran while one was open for 0% -> 0% of each run, Pallas kernels for 7% -> 3%
where the time goes in v7:
time: 63.9 us; the launch traced here: 63.7 us
  waiting for transfers between devices  27.8 us (44%)
  starting transfers between devices  26 us (41%)
  Pallas kernels  8.75 us (14%)
  local copies, waits for them, and re-layouts  1.03 us (2%)
    ppermute x18, starting transfers between devices, swap(): return lax.ppermute(value, 'exp', [(t, t ^ distance) for t in range(n)])  24.4 us
    ppermute x18, waiting for transfers between devices, swap(): return lax.ppermute(value, 'exp', [(t, t ^ distance) for t in range(n)])  24.1 us
    pallas_call x21, Pallas kernels, call(): pl.pallas_call(kernel, out_shape=shapes, in_specs=specs, out_specs=jax.tr...  8.75 us
    ppermute x1, waiting for transfers between devices, lora_join(): lax.ppermute(ordered, 'grp', [(0, 1), (1, 0)])  3.7 us
    ppermute x1, starting transfers between devices, lora_join(): lax.ppermute(ordered, 'grp', [(0, 1), (1, 0)])  1.56 us
  transfers between devices with their start and end apart: 19, of which 14 were waited for; matrix products, arithmetic and copies ran while one was open for 0% of the time, Pallas kernels for 3%

profile of v7, /device:TPU:0, one launch (start us, length us, event | category | flops | bytes accessed | tf_op | source)
XLA Modules:
  0.0 63.7 jit_solution(9790711890526511775)
XLA Ops:
  0.0 1.0 %shard_map.127.mine.after = bf16[1,48,128]{2,1,0:T(8,128)(2,1)S(1)} custom-call(bf16[1,2048]{1,0:T(2,128)(2,1)} %query.1, bf16[1,2048]{1,0:T(2,128)(2,1)} %resid.1, bf16[1,512]{1,0:T(2,128)(2,1)} %new.1, s32[1,8]{1,0:T(1,128)} %choice.1, f32[1,8]{1,0:T(1,128)} %probability.1), custom_call_target="tpu_custom_call" | custom-call | flops 4000000000 | tf_op jit(solution)/shard_map/pallas_call | solution.py:40
  1.0 4.1 %collective-permute-start = (bf16[1,48,128]{2,1,0:T(8,128)(2,1)S(1)}, bf16[1,48,128]{2,1,0:T(8,128)(2,1)S(1)}, u32[]{:S(2)}, u32[]{:S(2)}) collective-permute-start(bf16[1,48,128]{2,1,0:T(8,128)(2,1)S(1)} %shard_map.127.mine.after), channel_id=1, source_target_pairs={{0,8},{1,9},{2,10},{3,11},{4,12},{5,13},{6,14},{7,15},{8,0},{9,1},... | collective-permute-start | bytes 36872 | tf_op jit(solution)/shard_map/ppermute | solution.py:64
  5.1 0.1 shard_map.130
  5.2 0.2 collective-permute-start.2
  5.4 1.4 %collective-permute-done.theirs = bf16[1,48,128]{2,1,0:T(8,128)(2,1)S(1)} collective-permute-done((bf16[1,48,128]{2,1,0:T(8,128)(2,1)S(1)}, bf16[1,48,128]{2,1,0:T(8,128)(2,1)S(1)}, u32[]{:S(2)}, u32[]{:S(2)}) %collective-permute-start) | collective-permute-done | bytes 12320 | tf_op jit(solution)/shard_map/ppermute | solution.py:64
  6.8 1.9 %collective-permute-start.1 = (bf16[2,48,128]{2,1,0:T(8,128)(2,1)S(1)}, bf16[2,48,128]{2,1,0:T(8,128)(2,1)S(1)}, u32[]{:S(2)}, u32[]{:S(2)}) collective-permute-start(bf16[2,48,128]{2,1,0:T(8,128)(2,1)S(1)} %shard_map.128.mine), channel_id=1, source_target_pairs={{0,4},{1,5},{2,6},{3,7},{4,0},{5,1},{6,2},{7,3},{8,12},{9,13},{10,... | collective-permute-start | bytes 73736 | tf_op jit(solution)/shard_map/ppermute | solution.py:64
  8.7 1.9 %collective-permute-done.1.theirs = bf16[2,48,128]{2,1,0:T(8,128)(2,1)S(1)} collective-permute-done((bf16[2,48,128]{2,1,0:T(8,128)(2,1)S(1)}, bf16[2,48,128]{2,1,0:T(8,128)(2,1)S(1)}, u32[]{:S(2)}, u32[]{:S(2)}) %collective-permute-start.1) | collective-permute-done | bytes 24608 | tf_op jit(solution)/shard_map/ppermute | solution.py:64
  10.6 1.9 %collective-permute-start.3 = (bf16[1,96,128]{2,1,0:T(8,128)(2,1)S(1)}, bf16[1,96,128]{2,1,0:T(8,128)(2,1)S(1)}, u32[]{:S(2)}, u32[]{:S(2)}) collective-permute-start(bf16[1,96,128]{2,1,0:T(8,128)(2,1)S(1)} %bitcast.10), channel_id=1, source_target_pairs={{0,2},{1,3},{2,0},{3,1},{4,6},{5,7},{6,4},{7,5},{8,10},{9,11},{10,... | collective-permute-start | bytes 73736 | tf_op jit(solution)/shard_map/ppermute | solution.py:64
  12.6 2.0 %collective-permute-done.3.theirs = bf16[1,96,128]{2,1,0:T(8,128)(2,1)S(1)} collective-permute-done((bf16[1,96,128]{2,1,0:T(8,128)(2,1)S(1)}, bf16[1,96,128]{2,1,0:T(8,128)(2,1)S(1)}, u32[]{:S(2)}, u32[]{:S(2)}) %collective-permute-start.3) | collective-permute-done | bytes 24608 | tf_op jit(solution)/shard_map/ppermute | solution.py:64
  14.5 0.0 collective-permute-start.4
  14.5 0.8 %collective-permute-done.2.got = bf16[8,80,128]{2,1,0:T(8,128)(2,1)S(1)} collective-permute-done((bf16[8,80,128]{2,1,0:T(8,128)(2,1)S(1)}, bf16[8,80,128]{2,1,0:T(8,128)(2,1)S(1)}, u32[]{:S(2)}, u32[]{:S(2)}) %collective-permute-start.2) | collective-permute-done | bytes 163872 | tf_op jit(solution)/shard_map/ppermute | solution.py:64
  15.4 0.4 collective-permute-done.4.theirs.near.next_near
  15.8 1.0 %copy-done.3 = bf16[8,192,512]{2,1,0:T(8,128)(2,1)S(1)} copy-done((bf16[8,192,512]{2,1,0:T(8,128)(2,1)S(1)}, bf16[8,192,512]{2,1,0:T(8,128)(2,1)}, u32[]{:S(2)}) %copy-start.3) | copy-done | bytes 1572888
  16.8 2.7 %shard_map.133 = (bf16[8,32,128]{2,1,0:T(8,128)(2,1)S(1)}, bf16[8,32,128]{2,1,0:T(8,128)(2,1)S(1)}) custom-call(bf16[8,80,128]{2,1,0:T(8,128)(2,1)S(1)} %get-tuple-element.34.after.kept, s32[8]{0:T(128)S(1)} %copy-done.7, bf16[2,96,128]{2,1,0:T(8,128)(2,1)S(1)} %shard_map.132.mine.near, bf16[2,96,128]{2,1,0:T(8,128)(2,1)S(1)} %collective-permute-done.4.theirs.near.next_near, ...), custom_call_target="tpu_custom_call" | custom-call | flops 8000000000 | tf_op jit(solution)/shard_map/pallas_call | solution.py:40
  19.5 0.1 collective-permute-start.5
  19.5 1.6 %collective-permute-start.8 = (bf16[8,80,128]{2,1,0:T(8,128)(2,1)S(1)}, bf16[8,80,128]{2,1,0:T(8,128)(2,1)S(1)}, u32[]{:S(2)}, u32[]{:S(2)}) collective-permute-start(bf16[8,80,128]{2,1,0:T(8,128)(2,1)S(1)} %get-tuple-element.40), channel_id=1, source_target_pairs={{0,4},{1,5},{2,6},{3,7},{4,0},{5,1},{6,2},{7,3},{8,12},{9,13},{10,... | collective-permute-start | bytes 491528 | tf_op jit(solution)/shard_map/ppermute | solution.py:64
  21.1 0.0 collective-permute-done.5.theirs
  21.1 0.5 shard_map.134
  21.6 1.6 %collective-permute-start.6 = (bf16[4,32,128]{2,1,0:T(8,128)(2,1)S(1)}, bf16[4,32,128]{2,1,0:T(8,128)(2,1)S(1)}, u32[]{:S(2)}, u32[]{:S(2)}) collective-permute-start(bf16[4,32,128]{2,1,0:T(8,128)(2,1)S(1)} %get-tuple-element.39), channel_id=1, source_target_pairs={{0,2},{1,3},{2,0},{3,1},{4,6},{5,7},{6,4},{7,5},{8,10},{9,11},{10,... | collective-permute-start | bytes 98312 | tf_op jit(solution)/shard_map/ppermute | solution.py:64
  23.2 3.0 %collective-permute-done.8.got = bf16[8,80,128]{2,1,0:T(8,128)(2,1)S(1)} collective-permute-done((bf16[8,80,128]{2,1,0:T(8,128)(2,1)S(1)}, bf16[8,80,128]{2,1,0:T(8,128)(2,1)S(1)}, u32[]{:S(2)}, u32[]{:S(2)}) %collective-permute-start.8) | collective-permute-done | bytes 163872 | tf_op jit(solution)/shard_map/ppermute | solution.py:64
  26.2 1.6 %collective-permute-start.9 = (bf16[8,80,128]{2,1,0:T(8,128)(2,1)S(1)}, bf16[8,80,128]{2,1,0:T(8,128)(2,1)S(1)}, u32[]{:S(2)}, u32[]{:S(2)}) collective-permute-start(bf16[8,80,128]{2,1,0:T(8,128)(2,1)S(1)} %get-tuple-element.42), channel_id=1, source_target_pairs={{0,2},{1,3},{2,0},{3,1},{4,6},{5,7},{6,4},{7,5},{8,10},{9,11},{10,... | collective-permute-start | bytes 491528 | tf_op jit(solution)/shard_map/ppermute | solution.py:64
  27.8 0.0 collective-permute-done.6.theirs
  27.8 0.2 shard_map.135.mine.after
  28.0 1.2 %collective-permute-start.7 = (bf16[4,32,128]{2,1,0:T(8,128)(2,1)S(1)}, bf16[4,32,128]{2,1,0:T(8,128)(2,1)S(1)}, u32[]{:S(2)}, u32[]{:S(2)}) collective-permute-start(bf16[4,32,128]{2,1,0:T(8,128)(2,1)S(1)} %shard_map.135.mine.after), channel_id=1, source_target_pairs={{0,4},{1,5},{2,6},{3,7},{4,0},{5,1},{6,2},{7,3},{8,12},{9,13},{10,... | collective-permute-start | bytes 98312 | tf_op jit(solution)/shard_map/ppermute | solution.py:64
  29.2 2.8 %collective-permute-done.9.got = bf16[8,80,128]{2,1,0:T(8,128)(2,1)S(1)} collective-permute-done((bf16[8,80,128]{2,1,0:T(8,128)(2,1)S(1)}, bf16[8,80,128]{2,1,0:T(8,128)(2,1)S(1)}, u32[]{:S(2)}, u32[]{:S(2)}) %collective-permute-start.9) | collective-permute-done | bytes 163872 | tf_op jit(solution)/shard_map/ppermute | solution.py:64
  32.0 0.1 collective-permute-start.10
  32.1 0.0 collective-permute-done.7.theirs
  32.1 0.2 shard_map.136.after.mine
  32.4 4.6 %collective-permute-start.11 = (bf16[4,32,128]{2,1,0:T(8,128)(2,1)S(1)}, bf16[4,32,128]{2,1,0:T(8,128)(2,1)S(1)}, u32[]{:S(2)}, u32[]{:S(2)}) collective-permute-start(bf16[4,32,128]{2,1,0:T(8,128)(2,1)S(1)} %shard_map.136.after.mine), channel_id=1, source_target_pairs={{0,8},{1,9},{2,10},{3,11},{4,12},{5,13},{6,14},{7,15},{8,0},{9,1},... | collective-permute-start | bytes 98312 | tf_op jit(solution)/shard_map/ppermute | solution.py:64
  36.9 0.0 collective-permute-done.10.got
  37.0 1.6 %collective-permute-start.14 = (bf16[16,80,128]{2,1,0:T(8,128)(2,1)S(1)}, bf16[16,80,128]{2,1,0:T(8,128)(2,1)S(1)}, u32[]{:S(2)}, u32[]{:S(2)}) collective-permute-start(bf16[16,80,128]{2,1,0:T(8,128)(2,1)S(1)} %shard_map.139.after.mine), channel_id=1, source_target_pairs={{0,16},{16,0},{1,17},{17,1},{2,18},{18,2},{3,19},{19,3},{4,20},{20... | collective-permute-start | bytes 983048 | tf_op jit(solution)/shard_map/ppermute | solution.py:395
  38.6 0.4 collective-permute-done.11.theirs
  39.0 0.4 shard_map.140
  39.4 1.6 %collective-permute-start.12 = (bf16[4,16,128]{2,1,0:T(8,128)(2,1)S(1)}, bf16[4,16,128]{2,1,0:T(8,128)(2,1)S(1)}, u32[]{:S(2)}, u32[]{:S(2)}) collective-permute-start(bf16[4,16,128]{2,1,0:T(8,128)(2,1)S(1)} %get-tuple-element.46.mine), channel_id=1, source_target_pairs={{0,2},{1,3},{2,0},{3,1},{4,6},{5,7},{6,4},{7,5},{8,10},{9,11},{10,... | collective-permute-start | bytes 49160 | tf_op jit(solution)/shard_map/ppermute | solution.py:64
  41.0 2.2 %collective-permute-done.12.theirs = bf16[4,16,128]{2,1,0:T(8,128)(2,1)S(1)} collective-permute-done((bf16[4,16,128]{2,1,0:T(8,128)(2,1)S(1)}, bf16[4,16,128]{2,1,0:T(8,128)(2,1)S(1)}, u32[]{:S(2)}, u32[]{:S(2)}) %collective-permute-start.12) | collective-permute-done | bytes 16416 | tf_op jit(solution)/shard_map/ppermute | solution.py:64
  43.2 0.0 collective-permute-start.13
  43.2 3.7 %collective-permute-done.14.theirs = bf16[16,80,128]{2,1,0:T(8,128)(2,1)S(1)} collective-permute-done((bf16[16,80,128]{2,1,0:T(8,128)(2,1)S(1)}, bf16[16,80,128]{2,1,0:T(8,128)(2,1)S(1)}, u32[]{:S(2)}, u32[]{:S(2)}) %collective-permute-start.14) | collective-permute-done | bytes 327712 | tf_op jit(solution)/shard_map/ppermute | solution.py:395
  46.9 0.1 shard_map.142
  47.1 2.8 %shard_map.143 = (bf16[8,16,128]{2,1,0:T(8,128)(2,1)S(1)}, bf16[8,16,128]{2,1,0:T(8,128)(2,1)S(1)}) custom-call(bf16[8,16,128]{2,1,0:T(8,128)(2,1)S(1)} %shard_map.141.mine, bf16[8,16,128]{2,1,0:T(8,128)(2,1)S(1)} %collective-permute-done.13.theirs, bf16[2,96,128]{2,1,0:T(8,128)(2,1)S(1)} %shard_map.132.mine.near, ...), custom_call_target="tpu_custom_call" | custom-call | flops 400000000 | tf_op jit(solution)/shard_map/pallas_call | solution.py:40
  49.8 0.1 collective-permute-start.15
  49.9 1.2 %collective-permute-done.15.theirs = bf16[8,16,128]{2,1,0:T(8,128)(2,1)S(1)} collective-permute-done((bf16[8,16,128]{2,1,0:T(8,128)(2,1)S(1)}, bf16[8,16,128]{2,1,0:T(8,128)(2,1)S(1)}, u32[]{:S(2)}, u32[]{:S(2)}) %collective-permute-start.15) | collective-permute-done | bytes 32800 | tf_op jit(solution)/shard_map/ppermute | solution.py:64
  51.1 1.6 %collective-permute-start.16 = (bf16[4,16,128]{2,1,0:T(8,128)(2,1)S(1)}, bf16[4,16,128]{2,1,0:T(8,128)(2,1)S(1)}, u32[]{:S(2)}, u32[]{:S(2)}) collective-permute-start(bf16[4,16,128]{2,1,0:T(8,128)(2,1)S(1)} %get-tuple-element.52), channel_id=1, source_target_pairs={{0,2},{1,3},{2,0},{3,1},{4,6},{5,7},{6,4},{7,5},{8,10},{9,11},{10,... | collective-permute-start | bytes 49160 | tf_op jit(solution)/shard_map/ppermute | solution.py:64
  52.7 2.2 %collective-permute-done.16.theirs = bf16[4,16,128]{2,1,0:T(8,128)(2,1)S(1)} collective-permute-done((bf16[4,16,128]{2,1,0:T(8,128)(2,1)S(1)}, bf16[4,16,128]{2,1,0:T(8,128)(2,1)S(1)}, u32[]{:S(2)}, u32[]{:S(2)}) %collective-permute-start.16) | collective-permute-done | bytes 16416 | tf_op jit(solution)/shard_map/ppermute | solution.py:64
  54.9 1.4 %collective-permute-start.17 = (bf16[2,16,128]{2,1,0:T(8,128)(2,1)S(1)}, bf16[2,16,128]{2,1,0:T(8,128)(2,1)S(1)}, u32[]{:S(2)}, u32[]{:S(2)}) collective-permute-start(bf16[2,16,128]{2,1,0:T(8,128)(2,1)S(1)} %get-tuple-element.54), channel_id=1, source_target_pairs={{0,4},{1,5},{2,6},{3,7},{4,0},{5,1},{6,2},{7,3},{8,12},{9,13},{10,... | collective-permute-start | bytes 24584 | tf_op jit(solution)/shard_map/ppermute | solution.py:64
  56.3 2.2 %collective-permute-done.17.theirs = bf16[2,16,128]{2,1,0:T(8,128)(2,1)S(1)} collective-permute-done((bf16[2,16,128]{2,1,0:T(8,128)(2,1)S(1)}, bf16[2,16,128]{2,1,0:T(8,128)(2,1)S(1)}, u32[]{:S(2)}, u32[]{:S(2)}) %collective-permute-start.17) | collective-permute-done | bytes 8224 | tf_op jit(solution)/shard_map/ppermute | solution.py:64
  58.6 1.0 %collective-permute-start.18 = (bf16[1,16,128]{2,1,0:T(8,128)(2,1)S(1)}, bf16[1,16,128]{2,1,0:T(8,128)(2,1)S(1)}, u32[]{:S(2)}, u32[]{:S(2)}) collective-permute-start(bf16[1,16,128]{2,1,0:T(8,128)(2,1)S(1)} %get-tuple-element.56), channel_id=1, source_target_pairs={{0,8},{1,9},{2,10},{3,11},{4,12},{5,13},{6,14},{7,15},{8,0},{9,1},... | collective-permute-start | bytes 12296 | tf_op jit(solution)/shard_map/ppermute | solution.py:64
  59.6 3.5 %collective-permute-done.18.theirs = bf16[1,16,128]{2,1,0:T(8,128)(2,1)S(1)} collective-permute-done((bf16[1,16,128]{2,1,0:T(8,128)(2,1)S(1)}, bf16[1,16,128]{2,1,0:T(8,128)(2,1)S(1)}, u32[]{:S(2)}, u32[]{:S(2)}) %collective-permute-start.18) | collective-permute-done | bytes 4128 | tf_op jit(solution)/shard_map/ppermute | solution.py:64
  63.1 0.6 shard_map.147
  (27 shorter events, 0.2 us)
Async XLA Ops:
  0.0 5.1 %copy-start.5 = (bf16[16,96,48]{1,2,0:T(8,128)(2,1)S(1)}, bf16[16,96,48]{1,2,0:T(8,128)(2,1)}, u32[]{:S(2)}) copy-start(bf16[16,96,48]{1,2,0:T(8,128)(2,1)} %param.25) | copy-start | bytes 442372
  0.0 5.1 %copy-start.4 = (bf16[16,96,128]{2,1,0:T(8,128)(2,1)S(1)}, bf16[16,96,128]{2,1,0:T(8,128)(2,1)}, u32[]{:S(2)}) copy-start(bf16[16,96,128]{2,1,0:T(8,128)(2,1)} %model.1) | copy-start | bytes 1179652
  1.0 5.8 %collective-permute-start = (bf16[1,48,128]{2,1,0:T(8,128)(2,1)S(1)}, bf16[1,48,128]{2,1,0:T(8,128)(2,1)S(1)}, u32[]{:S(2)}, u32[]{:S(2)}) collective-permute-start(bf16[1,48,128]{2,1,0:T(8,128)(2,1)S(1)} %shard_map.127.mine.after), channel_id=1, source_target_pairs={{0,8},{1,9},{2,10},{3,11},{4,12},{5,13},{6,14},{7,15},{8,0},{9,1},... | collective-permute-start | bytes 36872 | tf_op jit(solution)/shard_map/ppermute | solution.py:64
  5.2 10.1 %collective-permute-start.2 = (bf16[8,80,128]{2,1,0:T(8,128)(2,1)S(1)}, bf16[8,80,128]{2,1,0:T(8,128)(2,1)S(1)}, u32[]{:S(2)}, u32[]{:S(2)}) collective-permute-start(bf16[8,80,128]{2,1,0:T(8,128)(2,1)S(1)} %get-tuple-element.33), channel_id=1, source_target_pairs={{0,8},{1,9},{2,10},{3,11},{4,12},{5,13},{6,14},{7,15},{8,0},{9,1},... | collective-permute-start | bytes 491528 | tf_op jit(solution)/shard_map/ppermute | solution.py:64
  6.8 3.8 %collective-permute-start.1 = (bf16[2,48,128]{2,1,0:T(8,128)(2,1)S(1)}, bf16[2,48,128]{2,1,0:T(8,128)(2,1)S(1)}, u32[]{:S(2)}, u32[]{:S(2)}) collective-permute-start(bf16[2,48,128]{2,1,0:T(8,128)(2,1)S(1)} %shard_map.128.mine), channel_id=1, source_target_pairs={{0,4},{1,5},{2,6},{3,7},{4,0},{5,1},{6,2},{7,3},{8,12},{9,13},{10,... | collective-permute-start | bytes 73736 | tf_op jit(solution)/shard_map/ppermute | solution.py:64
  10.6 3.9 %collective-permute-start.3 = (bf16[1,96,128]{2,1,0:T(8,128)(2,1)S(1)}, bf16[1,96,128]{2,1,0:T(8,128)(2,1)S(1)}, u32[]{:S(2)}, u32[]{:S(2)}) collective-permute-start(bf16[1,96,128]{2,1,0:T(8,128)(2,1)S(1)} %bitcast.10), channel_id=1, source_target_pairs={{0,2},{1,3},{2,0},{3,1},{4,6},{5,7},{6,4},{7,5},{8,10},{9,11},{10,... | collective-permute-start | bytes 73736 | tf_op jit(solution)/shard_map/ppermute | solution.py:64
  14.5 1.2 %collective-permute-start.4 = (bf16[2,96,128]{2,1,0:T(8,128)(2,1)S(1)}, bf16[2,96,128]{2,1,0:T(8,128)(2,1)S(1)}, u32[]{:S(2)}, u32[]{:S(2)}) collective-permute-start(bf16[2,96,128]{2,1,0:T(8,128)(2,1)S(1)} %shard_map.132.mine.near), channel_id=1, source_target_pairs={{0,1},{1,0},{2,3},{3,2},{4,5},{5,4},{6,7},{7,6},{8,9},{9,8},{10,11... | collective-permute-start | bytes 147464 | tf_op jit(solution)/shard_map/ppermute | solution.py:64
  15.4 1.4 %copy-start.3 = (bf16[8,192,512]{2,1,0:T(8,128)(2,1)S(1)}, bf16[8,192,512]{2,1,0:T(8,128)(2,1)}, u32[]{:S(2)}) copy-start(bf16[8,192,512]{2,1,0:T(8,128)(2,1)} %cache.1) | copy-start | bytes 4718596
  15.4 1.4 %copy-start.7 = (s32[8]{0:T(128)S(1)}, s32[8]{0:T(128)}, u32[]{:S(2)}) copy-start(s32[8]{0:T(128)} %lengths.1) | copy-start | bytes 100
  19.5 1.7 %collective-permute-start.5 = (bf16[8,32,128]{2,1,0:T(8,128)(2,1)S(1)}, bf16[8,32,128]{2,1,0:T(8,128)(2,1)S(1)}, u32[]{:S(2)}, u32[]{:S(2)}) collective-permute-start(bf16[8,32,128]{2,1,0:T(8,128)(2,1)S(1)} %get-tuple-element.37), channel_id=1, source_target_pairs={{0,1},{1,0},{2,3},{3,2},{4,5},{5,4},{6,7},{7,6},{8,9},{9,8},{10,11... | collective-permute-start | bytes 196616 | tf_op jit(solution)/shard_map/ppermute | solution.py:64
  19.5 6.6 %collective-permute-start.8 = (bf16[8,80,128]{2,1,0:T(8,128)(2,1)S(1)}, bf16[8,80,128]{2,1,0:T(8,128)(2,1)S(1)}, u32[]{:S(2)}, u32[]{:S(2)}) collective-permute-start(bf16[8,80,128]{2,1,0:T(8,128)(2,1)S(1)} %get-tuple-element.40), channel_id=1, source_target_pairs={{0,4},{1,5},{2,6},{3,7},{4,0},{5,1},{6,2},{7,3},{8,12},{9,13},{10,... | collective-permute-start | bytes 491528 | tf_op jit(solution)/shard_map/ppermute | solution.py:64
  21.6 6.2 %collective-permute-start.6 = (bf16[4,32,128]{2,1,0:T(8,128)(2,1)S(1)}, bf16[4,32,128]{2,1,0:T(8,128)(2,1)S(1)}, u32[]{:S(2)}, u32[]{:S(2)}) collective-permute-start(bf16[4,32,128]{2,1,0:T(8,128)(2,1)S(1)} %get-tuple-element.39), channel_id=1, source_target_pairs={{0,2},{1,3},{2,0},{3,1},{4,6},{5,7},{6,4},{7,5},{8,10},{9,11},{10,... | collective-permute-start | bytes 98312 | tf_op jit(solution)/shard_map/ppermute | solution.py:64
  26.2 5.8 %collective-permute-start.9 = (bf16[8,80,128]{2,1,0:T(8,128)(2,1)S(1)}, bf16[8,80,128]{2,1,0:T(8,128)(2,1)S(1)}, u32[]{:S(2)}, u32[]{:S(2)}) collective-permute-start(bf16[8,80,128]{2,1,0:T(8,128)(2,1)S(1)} %get-tuple-element.42), channel_id=1, source_target_pairs={{0,2},{1,3},{2,0},{3,1},{4,6},{5,7},{6,4},{7,5},{8,10},{9,11},{10,... | collective-permute-start | bytes 491528 | tf_op jit(solution)/shard_map/ppermute | solution.py:64
  28.0 4.1 %collective-permute-start.7 = (bf16[4,32,128]{2,1,0:T(8,128)(2,1)S(1)}, bf16[4,32,128]{2,1,0:T(8,128)(2,1)S(1)}, u32[]{:S(2)}, u32[]{:S(2)}) collective-permute-start(bf16[4,32,128]{2,1,0:T(8,128)(2,1)S(1)} %shard_map.135.mine.after), channel_id=1, source_target_pairs={{0,4},{1,5},{2,6},{3,7},{4,0},{5,1},{6,2},{7,3},{8,12},{9,13},{10,... | collective-permute-start | bytes 98312 | tf_op jit(solution)/shard_map/ppermute | solution.py:64
  32.0 4.9 %collective-permute-start.10 = (bf16[8,80,128]{2,1,0:T(8,128)(2,1)S(1)}, bf16[8,80,128]{2,1,0:T(8,128)(2,1)S(1)}, u32[]{:S(2)}, u32[]{:S(2)}) collective-permute-start(bf16[8,80,128]{2,1,0:T(8,128)(2,1)S(1)} %get-tuple-element.44), channel_id=1, source_target_pairs={{0,1},{1,0},{2,3},{3,2},{4,5},{5,4},{6,7},{7,6},{8,9},{9,8},{10,11... | collective-permute-start | bytes 491528 | tf_op jit(solution)/shard_map/ppermute | solution.py:64
  32.4 6.6 %collective-permute-start.11 = (bf16[4,32,128]{2,1,0:T(8,128)(2,1)S(1)}, bf16[4,32,128]{2,1,0:T(8,128)(2,1)S(1)}, u32[]{:S(2)}, u32[]{:S(2)}) collective-permute-start(bf16[4,32,128]{2,1,0:T(8,128)(2,1)S(1)} %shard_map.136.after.mine), channel_id=1, source_target_pairs={{0,8},{1,9},{2,10},{3,11},{4,12},{5,13},{6,14},{7,15},{8,0},{9,1},... | collective-permute-start | bytes 98312 | tf_op jit(solution)/shard_map/ppermute | solution.py:64
  37.0 2.0 %copy-start.6 = (f32[2048]{0:T(1024)S(1)}, f32[2048]{0:T(1024)}, u32[]{:S(2)}) copy-start(f32[2048]{0:T(1024)} %param.18) | copy-start | bytes 24580
  37.0 9.9 %collective-permute-start.14 = (bf16[16,80,128]{2,1,0:T(8,128)(2,1)S(1)}, bf16[16,80,128]{2,1,0:T(8,128)(2,1)S(1)}, u32[]{:S(2)}, u32[]{:S(2)}) collective-permute-start(bf16[16,80,128]{2,1,0:T(8,128)(2,1)S(1)} %shard_map.139.after.mine), channel_id=1, source_target_pairs={{0,16},{16,0},{1,17},{17,1},{2,18},{18,2},{3,19},{19,3},{4,20},{20... | collective-permute-start | bytes 983048 | tf_op jit(solution)/shard_map/ppermute | solution.py:395
  39.0 8.0 %copy-start = (bf16[1,2048,768]{2,1,0:T(8,128)(2,1)S(1)}, bf16[1,2048,768]{2,1,0:T(8,128)(2,1)}, u32[]{:S(2)}) copy-start(bf16[1,2048,768]{2,1,0:T(8,128)(2,1)} %param.21) | copy-start | bytes 9437188
  39.0 8.0 %copy-start.1 = (bf16[1,2048,768]{2,1,0:T(8,128)(2,1)S(1)}, bf16[1,2048,768]{2,1,0:T(8,128)(2,1)}, u32[]{:S(2)}) copy-start(bf16[1,2048,768]{2,1,0:T(8,128)(2,1)} %param.22) | copy-start | bytes 9437188
  39.0 8.1 %copy-start.2 = (bf16[1,768,2048]{2,1,0:T(8,128)(2,1)S(1)}, bf16[1,768,2048]{2,1,0:T(8,128)(2,1)}, u32[]{:S(2)}) copy-start(bf16[1,768,2048]{2,1,0:T(8,128)(2,1)} %param.23) | copy-start | bytes 9437188
  39.4 3.8 %collective-permute-start.12 = (bf16[4,16,128]{2,1,0:T(8,128)(2,1)S(1)}, bf16[4,16,128]{2,1,0:T(8,128)(2,1)S(1)}, u32[]{:S(2)}, u32[]{:S(2)}) collective-permute-start(bf16[4,16,128]{2,1,0:T(8,128)(2,1)S(1)} %get-tuple-element.46.mine), channel_id=1, source_target_pairs={{0,2},{1,3},{2,0},{3,1},{4,6},{5,7},{6,4},{7,5},{8,10},{9,11},{10,... | collective-permute-start | bytes 49160 | tf_op jit(solution)/shard_map/ppermute | solution.py:64
  43.2 3.8 %collective-permute-start.13 = (bf16[8,16,128]{2,1,0:T(8,128)(2,1)S(1)}, bf16[8,16,128]{2,1,0:T(8,128)(2,1)S(1)}, u32[]{:S(2)}, u32[]{:S(2)}) collective-permute-start(bf16[8,16,128]{2,1,0:T(8,128)(2,1)S(1)} %shard_map.141.mine), channel_id=1, source_target_pairs={{0,1},{1,0},{2,3},{3,2},{4,5},{5,4},{6,7},{7,6},{8,9},{9,8},{10,11... | collective-permute-start | bytes 98312 | tf_op jit(solution)/shard_map/ppermute | solution.py:64
  49.8 1.3 %collective-permute-start.15 = (bf16[8,16,128]{2,1,0:T(8,128)(2,1)S(1)}, bf16[8,16,128]{2,1,0:T(8,128)(2,1)S(1)}, u32[]{:S(2)}, u32[]{:S(2)}) collective-permute-start(bf16[8,16,128]{2,1,0:T(8,128)(2,1)S(1)} %get-tuple-element.50), channel_id=1, source_target_pairs={{0,1},{1,0},{2,3},{3,2},{4,5},{5,4},{6,7},{7,6},{8,9},{9,8},{10,11... | collective-permute-start | bytes 98312 | tf_op jit(solution)/shard_map/ppermute | solution.py:64
  51.1 3.8 %collective-permute-start.16 = (bf16[4,16,128]{2,1,0:T(8,128)(2,1)S(1)}, bf16[4,16,128]{2,1,0:T(8,128)(2,1)S(1)}, u32[]{:S(2)}, u32[]{:S(2)}) collective-permute-start(bf16[4,16,128]{2,1,0:T(8,128)(2,1)S(1)} %get-tuple-element.52), channel_id=1, source_target_pairs={{0,2},{1,3},{2,0},{3,1},{4,6},{5,7},{6,4},{7,5},{8,10},{9,11},{10,... | collective-permute-start | bytes 49160 | tf_op jit(solution)/shard_map/ppermute | solution.py:64
  54.9 3.7 %collective-permute-start.17 = (bf16[2,16,128]{2,1,0:T(8,128)(2,1)S(1)}, bf16[2,16,128]{2,1,0:T(8,128)(2,1)S(1)}, u32[]{:S(2)}, u32[]{:S(2)}) collective-permute-start(bf16[2,16,128]{2,1,0:T(8,128)(2,1)S(1)} %get-tuple-element.54), channel_id=1, source_target_pairs={{0,4},{1,5},{2,6},{3,7},{4,0},{5,1},{6,2},{7,3},{8,12},{9,13},{10,... | collective-permute-start | bytes 24584 | tf_op jit(solution)/shard_map/ppermute | solution.py:64
  58.6 4.5 %collective-permute-start.18 = (bf16[1,16,128]{2,1,0:T(8,128)(2,1)S(1)}, bf16[1,16,128]{2,1,0:T(8,128)(2,1)S(1)}, u32[]{:S(2)}, u32[]{:S(2)}) collective-permute-start(bf16[1,16,128]{2,1,0:T(8,128)(2,1)S(1)} %get-tuple-element.56), channel_id=1, source_target_pairs={{0,8},{1,9},{2,10},{3,11},{4,12},{5,13},{6,14},{7,15},{8,0},{9,1},... | collective-permute-start | bytes 12296 | tf_op jit(solution)/shard_map/ppermute | solution.py:64

commit v8 on v6

v8 whole, which is shorter than its diff:
```python
import functools

import jax
import jax.numpy as jnp
from jax import lax
from jax.experimental import pallas as pl
from jax.experimental.pallas import tpu as pltpu
from jax.sharding import PartitionSpec as P

QUERY_HEADS = 16
KEY_VALUE_HEADS = 2
HEAD_WIDTH = 128
ADAPTER_RANK = 32
GROUPED = QUERY_HEADS // KEY_VALUE_HEADS
KEY_VALUE_WIDTH = KEY_VALUE_HEADS * HEAD_WIDTH
WIDTH = QUERY_HEADS * HEAD_WIDTH
INV_ROOT = HEAD_WIDTH ** (-0.5)
NEAR = 4
NEW_ROWS = 2 * KEY_VALUE_HEADS
HEADS = (QUERY_HEADS, HEAD_WIDTH)
MESSAGE = (2 * QUERY_HEADS, HEAD_WIDTH)

floor_score = -1e30
epsilon = 1e-06
FILL = 4000

VMEM = pl.BlockSpec(memory_space=pltpu.VMEM)
SMEM = pl.BlockSpec(memory_space=pltpu.SMEM)
HBM = pl.BlockSpec(memory_space=pltpu.HBM)
shape = jax.ShapeDtypeStruct
bf16, f32 = jnp.bfloat16, jnp.float32


def call(kernel, shapes, specs, *args, limit=8, scratch=(), nanos=400):
    return pl.pallas_call(
        kernel,
        out_shape=shapes,
        in_specs=specs,
        out_specs=jax.tree.map(lambda _: VMEM, shapes),
        scratch_shapes=scratch,
        cost_estimate=pl.CostEstimate(
            flops=nanos * 1000000, transcendentals=0, bytes_accessed=0
        ),
        compiler_params=pltpu.CompilerParams(vmem_limit_bytes=limit * 1024 * 1024),
    )(*args)


def hold_kernel(value, after, out):
    out[...] = value[...]


def hold(value, after):
    return call(
        hold_kernel, shape(value.shape, value.dtype), [VMEM] * 2, value, after, nanos=FILL
    )


def iota(dims, dim):
    return lax.broadcasted_iota(jnp.int32, dims, dim)


def as_rows(line, rows):
    return jnp.concatenate(
        [line[:, j * HEAD_WIDTH : (j + 1) * HEAD_WIDTH] for j in range(rows)], axis=0
    )


def swap(value, n, distance):
    return lax.ppermute(value, "exp", [(t, t ^ distance) for t in range(n)])


def distance_of(column, far):
    bits = far.bit_length() - 1
    return sum(NEAR << i for i in range(bits) if column >> (bits - 1 - i) & 1)


def pad16(rows):
    return -(-rows // 16) * 16


def stat_tiles(slots):
    return 1 if 6 * slots <= HEAD_WIDTH else 3


def pack_kernel(query, resid, out, q_in, r_in, sems):
    copies = [
        pltpu.make_async_copy(source, target, sems.at[k])
        for k, (source, target) in enumerate(((query, q_in), (resid, r_in)))
    ]
    for copy in copies:
        copy.start()
    for copy in copies:
        copy.wait()
    q = as_rows(q_in[...].astype(f32), QUERY_HEADS)
    r = as_rows(r_in[...].astype(f32), QUERY_HEADS)
    out[0] = jnp.concatenate([q, r], axis=0).astype(bf16)


def join_kernel(mine, theirs, out):
    half = mine.shape[0]
    out[:half] = mine[...]
    out[half:] = theirs[...]


def narrow_kernel(mine, theirs, new, residuals, out):
    half = mine.shape[0]
    for k, source in enumerate((mine, theirs)):
        for w in range(half):
            slot = k * half + w
            out[slot] = source[w, :QUERY_HEADS]
            residuals[slot] = source[w, QUERY_HEADS:]
    fresh = as_rows(new[...].astype(f32), NEW_ROWS)
    rest = jnp.zeros((QUERY_HEADS - NEW_ROWS, HEAD_WIDTH), f32)
    out[2 * half] = jnp.concatenate([fresh, rest], axis=0).astype(bf16)


def write_stats(stats, out, slots):
    parts = []
    for _ in range(3):
        part = stats.astype(bf16).astype(f32)
        parts.append(part)
        stats = stats - part
    if stat_tiles(slots) == 1:
        tile = parts[0]
        for k in (1, 2):
            tile = tile + pltpu.roll(parts[k], 2 * slots * k, 1)
        out[slots] = tile.astype(bf16)
    else:
        for k in range(3):
            out[slots + k] = parts[k].astype(bf16)


def read_stats(message, slots):
    if stat_tiles(slots) == 1:
        tile = message[slots].astype(f32)
        lanes = iota(HEADS, 1)
        stats = tile
        for k in (1, 2):
            stats = stats + pltpu.roll(tile, HEAD_WIDTH - 2 * slots * k, 1)
        stats = jnp.where(lanes < 2 * slots, stats, 0.0)
    else:
        stats = sum(message[slots + k].astype(f32) for k in range(3))
    return stats, pltpu.roll(stats, HEAD_WIDTH - slots, 1)


def flipped(value, flip):
    if not flip:
        return value
    ahead = pltpu.roll(value, HEAD_WIDTH - flip, 1)
    behind = pltpu.roll(value, flip, 1)
    return jnp.where((iota(HEADS, 1) & flip) == 0, ahead, behind)


def merged(mine, theirs, slots, flip):
    top, total = read_stats(mine, slots)
    other_top, other_total = (flipped(x, flip) for x in read_stats(theirs, slots))
    peak = jnp.maximum(top, other_top)
    share, other_share = jnp.exp(top - peak), jnp.exp(other_top - peak)
    total = share * total + other_share * other_total

    def acc(slot):
        return share[:, slot : slot + 1] * mine[slot].astype(f32) + other_share[
            :, slot : slot + 1
        ] * theirs[slot ^ flip].astype(f32)

    return peak, total, acc


def merge_kernel(mine, theirs, out, *, slots, flip):
    peak, total, acc = merged(mine, theirs, slots, flip)
    lanes = iota(HEADS, 1)
    stats = jnp.where(lanes < slots, peak, 0.0)
    stats = stats + pltpu.roll(jnp.where(lanes < slots, total, 0.0), slots, 1)
    write_stats(stats, out, slots)
    for slot in range(slots):
        out[slot] = acc(slot).astype(bf16)


def fresh_block(mine, theirs, me):
    slots = mine.shape[0] - 1
    second = me % 2 == 1
    first_group = iota(HEADS, 0) < GROUPED

    def by_head(rows, at):
        return jnp.where(first_group, rows[at : at + 1], rows[at + 1 : at + 2])

    q = mine[0].astype(f32)
    own, other = mine[slots].astype(f32), theirs[slots].astype(f32)
    own_score = jnp.sum(q * by_head(own, 0), axis=1, keepdims=True) * INV_ROOT
    other_score = jnp.sum(q * by_head(other, 0), axis=1, keepdims=True) * INV_ROOT
    other_score = jnp.where(second, other_score, floor_score)
    top = jnp.maximum(own_score, other_score)
    own_weight = jnp.exp(own_score - top).astype(bf16).astype(f32)
    other_weight = jnp.where(second, jnp.exp(other_score - top), 0.0).astype(bf16).astype(f32)
    acc = own_weight * by_head(own, 2) + other_weight * by_head(other, 2)
    return top, own_weight + other_weight, acc


def attend_kernel(after, lengths, mine, theirs, cache, keep, send, *, far):
    me = lax.axis_index("exp")
    sequences, block, _ = cache.shape
    rows = 2 * QUERY_HEADS
    first_group = (iota((rows, HEAD_WIDTH), 0) % QUERY_HEADS) < GROUPED
    positions = me * block + iota((rows, block), 1)
    lanes = iota(HEADS, 1)
    fresh = fresh_block(mine, theirs, me)
    stats = [jnp.zeros(HEADS, f32), jnp.zeros(HEADS, f32)]
    batch = 8 if sequences % 8 == 0 else 1
    for base in range(0, sequences, batch):
        slots = range(base, base + batch)
        where = [
            lax.shift_right_logical(me, 1)
            ^ ((distance_of(slot % far, far) >> 1) | (slot // far))
            for slot in slots
        ]
        scores, valid = [], []
        for slot, s in zip(slots, where):
            both = jnp.concatenate([mine[slot], theirs[slot]], axis=0)
            zero = jnp.zeros_like(both)
            wide = jnp.concatenate(
                [jnp.where(first_group, both, zero), jnp.where(first_group, zero, both)], axis=1
            )
            product = lax.dot_general(
                wide,
                cache[s, :, :KEY_VALUE_WIDTH],
                (((1,), (1,)), ((), ())),
                preferred_element_type=f32,
            )
            valid.append(positions < lengths[s])
            scores.append(jnp.where(valid[-1], product * INV_ROOT, floor_score))
        tops = [jnp.max(score, axis=1, keepdims=True) for score in scores]
        weights = [
            jnp.where(ok, jnp.exp(score - top), 0.0).astype(bf16)
            for ok, score, top in zip(valid, scores, tops)
        ]
        totals = [jnp.sum(weight.astype(f32), axis=1, keepdims=True) for weight in weights]
        accs = [
            jnp.dot(weight, cache[s, :, KEY_VALUE_WIDTH:], preferred_element_type=f32)
            for weight, s in zip(weights, where)
        ]
        for slot, top, total, acc in zip(slots, tops, totals, accs):
            acc = jnp.where(first_group, acc[:, :HEAD_WIDTH], acc[:, HEAD_WIDTH:])
            for k, part in enumerate((keep, send)):
                cut = slice(k * QUERY_HEADS, (k + 1) * QUERY_HEADS)
                t, z, a = top[cut], total[cut], acc[cut]
                if slot == 0 and k == 0:
                    peak = jnp.maximum(t, fresh[0])
                    old, young = jnp.exp(t - peak), jnp.exp(fresh[0] - peak)
                    t, z, a = peak, old * z + young * fresh[1], old * a + young * fresh[2]
                part[slot] = a.astype(bf16)
                stats[k] = jnp.where(lanes == slot, t, stats[k])
                stats[k] = jnp.where(lanes == sequences + slot, z, stats[k])
    for k, part in enumerate((keep, send)):
        write_stats(stats[k], part, sequences)


def token_kernel(after, mine, theirs, residuals, scale, hidden_out, normed_out):
    slots = residuals.shape[0]
    _, total, acc = merged(mine, theirs, slots, 1)
    inverse = 1.0 / jnp.where(iota(HEADS, 1) < slots, total, 1.0)
    for slot in range(slots):
        hidden = residuals[slot].astype(f32) + acc(slot) * inverse[:, slot : slot + 1]
        squares = jnp.sum(jnp.sum(hidden * hidden, axis=1, keepdims=True), axis=0, keepdims=True)
        normed = hidden * lax.rsqrt(squares / WIDTH + epsilon) * scale[...]
        if slot == 0:
            hidden_out[...] = hidden
        normed_out[slot] = normed.astype(bf16)


def dot_pair(value, factor, contract):
    high = value.astype(bf16)
    low = (value - high.astype(f32)).astype(bf16)
    both = lax.dot_general(
        jnp.concatenate([high, low], axis=0),
        factor,
        (((1,), (contract,)), ((), ())),
        preferred_element_type=f32,
    )
    return both[: value.shape[0]] + both[value.shape[0] :]


def expert_kernel(mine, theirs, gate_w, up_w, down_w, model, inner, out, *, far):
    me = lax.axis_index("exp")
    half = mine.shape[0]
    x = jnp.concatenate([mine[...].astype(f32), theirs[...].astype(f32)], axis=0)
    x = x.reshape(2 * half, WIDTH).astype(bf16)
    r = ADAPTER_RANK
    mixed = lax.dot_general(
        x, model[: 2 * r], (((1,), (1,)), ((), ())), preferred_element_type=f32
    )
    gate = jnp.dot(x, gate_w[...], preferred_element_type=f32)
    gate = gate + dot_pair(mixed[:, :r], inner[:, :r], 1)
    up = jnp.dot(x, up_w[...], preferred_element_type=f32)
    up = up + dot_pair(mixed[:, r:], inner[:, r : 2 * r], 1)
    act = (gate / (1.0 + jnp.exp(-gate)) * up).astype(bf16)
    lowered = jnp.dot(act, inner[:, 2 * r : 3 * r], preferred_element_type=f32)
    result = jnp.dot(act, down_w[...], preferred_element_type=f32)
    result = result + dot_pair(lowered, model[2 * r :], 0)
    for c in range(2):
        for y in range(2):
            for w in range(far):
                slot = (c * 2 + y) * far + w
                line = as_rows(result[slot : slot + 1], QUERY_HEADS)
                out[me ^ (distance_of(w, far) | 2 * y | c)] = line.astype(bf16)


def finish_kernel(hidden, got, choice, probability, out):
    p = probability[...]
    shares = p / jnp.sum(p, axis=1, keepdims=True)
    lanes = iota((1, HEAD_WIDTH), 1)
    gates = jnp.zeros((1, HEAD_WIDTH), f32)
    for k in range(p.shape[1]):
        gates = gates + jnp.where(choice[:, k : k + 1] == lanes, shares[:, k : k + 1], 0.0)
    gates = gates.astype(bf16).astype(f32)
    total = hidden[...]
    for e in range(got.shape[0]):
        total = total + gates[:, e : e + 1] * got[e].astype(f32)
    line = jnp.concatenate([total[j : j + 1] for j in range(QUERY_HEADS)], axis=1)
    out[...] = line.astype(bf16)


def lora_pack_kernel(after, model, inner, *outs):
    low, first = lax.axis_index("exp") % NEAR, lax.axis_index("grp") == 0
    ranks, split, most = model.shape[1], model.shape[1] // 2, outs[0].shape[1] - model.shape[1] // 2
    rest = inner.shape[1] - most
    for k, out in enumerate(outs):
        out[:, split:, ranks:] = jnp.zeros((out.shape[0], most, HEAD_WIDTH - ranks), out.dtype)
        for z in range(out.shape[0]):
            at = z * NEAR + (low ^ k)
            out[z, :split] = jnp.where(first, model[at, :split], model[at, split:])
            lower = inner[at, most:]
            if rest < most:
                pad = jnp.zeros((most - rest, ranks), out.dtype)
                lower = jnp.concatenate([lower, pad], axis=0)
            out[z, split:, :ranks] = jnp.where(first, inner[at, :most], lower)


def lora_turn_kernel(after, *refs):
    me = lax.axis_index("exp")
    low, high = me % NEAR, me // NEAR
    got, outs = refs[:NEAR], refs[NEAR:]
    for j, out in enumerate(outs):
        for k, ref in enumerate(got):
            out[low ^ k] = ref[high ^ j]


def lora_order_kernel(after, *refs):
    high = lax.axis_index("exp") // NEAR
    got, out = refs[:-1], refs[-1]
    for j, ref in enumerate(got):
        out[pl.ds((high ^ j) * NEAR, NEAR)] = ref[...]


def lora_join_kernel(mine, theirs, model, inner):
    first = lax.axis_index("grp") == 0
    split = model.shape[0] // 2
    most, width = mine.shape[1] - split, inner.shape[0] // mine.shape[0]
    for at in range(mine.shape[0]):
        own, other = mine[at], theirs[at]
        halves = jnp.where(first, own, other), jnp.where(first, other, own)
        columns = slice(at * HEAD_WIDTH, (at + 1) * HEAD_WIDTH)
        model[:split, columns] = halves[0][:split]
        model[split:, columns] = halves[1][:split]
        inner[at * width : at * width + most] = halves[0][split:]
        inner[at * width + most : (at + 1) * width] = halves[1][split : split + width - most]


def lora_near(adapter_model, adapter_hidden, n, marks):
    total, ranks, model_width = adapter_model.shape
    inner_width = adapter_hidden.shape[2]
    inner = jnp.transpose(adapter_hidden, (0, 2, 1))
    if model_width != HEAD_WIDTH or inner_width % 16 or lax.axis_size("grp") != 2:
        model = lax.all_to_all(adapter_model, "exp", split_axis=0, concat_axis=2, tiled=True)
        inner = lax.all_to_all(inner, "exp", split_axis=0, concat_axis=1, tiled=True)
        return [model[0], inner[0]], True
    far = n // NEAR
    block = (ranks // 2 + pad16(inner_width // 2), HEAD_WIDTH)
    packed = call(
        lora_pack_kernel,
        (shape((far,) + block, bf16),) * NEAR,
        [VMEM] * 3,
        marks[0],
        adapter_model,
        inner,
        nanos=FILL,
    )
    turned = call(
        lora_turn_kernel,
        (shape((NEAR,) + block, bf16),) * far,
        [VMEM] * (1 + NEAR),
        marks[3],
        packed[0],
        swap(hold(packed[1], marks[1]), n, 1),
        swap(packed[2], n, 2),
        swap(hold(packed[3], marks[1]), n, 3),
        nanos=FILL,
    )
    return turned, False


def lora_far(turned, n, marks):
    far = len(turned)
    rows = turned[0].shape[1]
    got = [turned[0], swap(turned[1], n, NEAR)]
    for j in range(2, far):
        got.append(swap(hold(turned[j], marks[j - 2]), n, j * NEAR))
    return call(
        lora_order_kernel,
        shape((n, rows, HEAD_WIDTH), bf16),
        [VMEM] * (1 + far),
        marks[far - 2],
        *got,
        nanos=FILL,
    )


def lora_join(ordered, inner_width):
    n = ordered.shape[0]
    return call(
        lora_join_kernel,
        (
            shape((3 * ADAPTER_RANK, n * HEAD_WIDTH), bf16),
            shape((n * inner_width, HEAD_WIDTH), bf16),
        ),
        [VMEM] * 2,
        ordered,
        lax.ppermute(ordered, "grp", [(0, 1), (1, 0)]),
    )


def body(
    resid,
    queries,
    incoming_key_value,
    key_value_cache,
    lengths,
    norm_scale_vector,
    expert_choice,
    router_probability,
    gate_weight,
    up_weight,
    down_weight,
    adapter_model,
    adapter_hidden,
):
    n = lax.axis_size("exp")
    far = n // NEAR

    slots = 2 * far
    first_inputs = (queries, resid)
    message = call(
        pack_kernel,
        shape((1,) + MESSAGE, bf16),
        [HBM] * 2,
        *[pltpu.with_memory_space_constraint(x, pltpu.HBM) for x in first_inputs],
        scratch=[pltpu.VMEM(x.shape, x.dtype) for x in first_inputs]
        + [pltpu.SemaphoreType.DMA((2,))],
        nanos=4000,
    )
    marks, distance = [message], n // 2
    while distance > 2:
        message = call(
            join_kernel,
            shape((2 * message.shape[0],) + MESSAGE, bf16),
            [VMEM] * 2,
            message,
            swap(message, n, distance),
        )
        marks.append(message)
        distance //= 2
    residuals, near = call(
        narrow_kernel,
        (shape((slots,) + HEADS, bf16), shape((slots + 1,) + HEADS, bf16)),
        [VMEM] * 3,
        message,
        swap(message, n, 2),
        incoming_key_value,
    )
    marks = marks[:3] + [near]
    turned, whole = lora_near(adapter_model, adapter_hidden, n, marks)
    next_near = swap(near, n, 1)
    partial = shape((slots + stat_tiles(slots),) + HEADS, bf16)
    keep, send = call(
        functools.partial(attend_kernel, far=far),
        (partial,) * 2,
        [VMEM, SMEM] + [VMEM] * 3,
        turned[0],
        lengths,
        near,
        next_near,
        key_value_cache,
        nanos=8000,
    )
    marks = [keep]
    theirs, flip, distance = swap(send, n, 1), 0, 2
    while distance < n:
        keep = call(
            functools.partial(merge_kernel, slots=slots, flip=flip),
            partial,
            [VMEM] * 2,
            keep,
            theirs,
        )
        marks.append(keep)
        if distance == n // 2:
            ordered = turned[0] if whole else lora_far(turned, n, marks)
        theirs = swap(keep, n, distance)
        flip = slots // distance
        distance *= 2
    hidden, normed = call(
        token_kernel,
        (shape(HEADS, f32), shape((slots,) + HEADS, bf16)),
        [VMEM] * 5,
        ordered,
        keep,
        theirs,
        residuals,
        norm_scale_vector.reshape(HEADS),
        nanos=4000,
    )
    model, inner = turned if whole else lora_join(ordered, adapter_hidden.shape[2])
    out = call(
        functools.partial(expert_kernel, far=far),
        shape((n,) + HEADS, bf16),
        [VMEM] * 7,
        normed,
        swap(normed, n, 1),
        gate_weight[0],
        up_weight[0],
        down_weight[0],
        model,
        inner,
        limit=32,
    )
    return call(
        finish_kernel,
        shape((1, WIDTH), bf16),
        [VMEM] * 4,
        hidden,
        lax.all_to_all(out, "exp", split_axis=0, concat_axis=0, tiled=True),
        expert_choice,
        router_probability,
    )


def solution(mesh):
    return jax.shard_map(
        body,
        mesh=mesh,
        in_specs=(
            P(("grp", "exp"), None),
            P(("grp", "exp"), None),
            P(("grp", "exp"), None),
            P("grp", "exp", None),
            P("grp"),
            P(),
            P(("grp", "exp"), None),
            P(("grp", "exp"), None),
            P("exp", None, None),
            P("exp", None, None),
            P("exp", None, None),
            P(None, None, "exp"),
            P(None, None, "exp"),
        ),
        out_specs=P(("grp", "exp"), None),
        check_vma=False,
    )
```

time: 58.4 us -> 54.4 us (0.932)
  blocking collectives: 0 us -> 11.7 us
  waiting for transfers between devices: 20.1 us -> 11.5 us
  starting transfers between devices: 29.2 us -> 23.3 us
  Pallas kernels: 8.76 us -> 7.39 us
    ppermute x20 -> x15, waiting for transfers between devices: 20 us -> 7.87 us  [swap(): return lax.ppermute(value, 'exp', [(t, t ^ distance) for t in range(n)])]
    all_to_all x0 -> x1, blocking collectives: none -> 11.7 us  [body(): lax.all_to_all(out, 'exp', split_axis=0, concat_axis=0, tiled=True)]
    ppermute x20 -> x15, starting transfers between devices: 27.6 us -> 21.8 us  [swap(): return lax.ppermute(value, 'exp', [(t, t ^ distance) for t in range(n)])]
    ppermute x1, waiting for transfers between devices: 0.01 us -> 3.6 us  [lora_join(): lax.ppermute(ordered, 'grp', [(0, 1), (1, 0)])]
    pallas_call x23 -> x19, Pallas kernels: 8.76 us -> 7.39 us  [call(): pl.pallas_call(kernel, out_shape=shapes, in_specs=specs, out_specs=jax.tr...]
  transfers between devices with their start and end apart: 21 -> 16, of which waited for: 11 -> 6; matrix products, arithmetic and copies ran while one was open for 0% -> 0% of each run, Pallas kernels for 7% -> 5%
where the time goes in v8:
time: 54.4 us; the launch traced here: 54.2 us
  starting transfers between devices  23.3 us (43%)
  blocking collectives  11.7 us (22%)
  waiting for transfers between devices  11.5 us (21%)
  Pallas kernels  7.39 us (14%)
    ppermute x15, starting transfers between devices, swap(): return lax.ppermute(value, 'exp', [(t, t ^ distance) for t in range(n)])  21.8 us
    all_to_all x1, blocking collectives, body(): lax.all_to_all(out, 'exp', split_axis=0, concat_axis=0, tiled=True)  11.7 us
    ppermute x15, waiting for transfers between devices, swap(): return lax.ppermute(value, 'exp', [(t, t ^ distance) for t in range(n)])  7.87 us
    pallas_call x19, Pallas kernels, call(): pl.pallas_call(kernel, out_shape=shapes, in_specs=specs, out_specs=jax.tr...  7.39 us
    ppermute x1, waiting for transfers between devices, lora_join(): lax.ppermute(ordered, 'grp', [(0, 1), (1, 0)])  3.6 us
    ppermute x1, starting transfers between devices, lora_join(): lax.ppermute(ordered, 'grp', [(0, 1), (1, 0)])  1.56 us
  transfers between devices with their start and end apart: 16, of which 6 were waited for; matrix products, arithmetic and copies ran while one was open for 0% of the time, Pallas kernels for 5%

profile of v8, /device:TPU:0, one launch (start us, length us, event | category | flops | bytes accessed | tf_op | source)
XLA Modules:
  0.0 54.2 jit_solution(13438351154661563858)
XLA Ops:
  0.0 0.8 %shard_map.127.mine.after = bf16[1,32,128]{2,1,0:T(8,128)(2,1)S(1)} custom-call(bf16[1,2048]{1,0:T(2,128)(2,1)} %query.1, bf16[1,2048]{1,0:T(2,128)(2,1)} %resid.1), custom_call_target="tpu_custom_call" | custom-call | flops 4000000000 | tf_op jit(solution)/shard_map/pallas_call | solution.py:35
  0.8 4.1 %collective-permute-start = (bf16[1,32,128]{2,1,0:T(8,128)(2,1)S(1)}, bf16[1,32,128]{2,1,0:T(8,128)(2,1)S(1)}, u32[]{:S(2)}, u32[]{:S(2)}) collective-permute-start(bf16[1,32,128]{2,1,0:T(8,128)(2,1)S(1)} %shard_map.127.mine.after), channel_id=1, source_target_pairs={{0,8},{1,9},{2,10},{3,11},{4,12},{5,13},{6,14},{7,15},{8,0},{9,1},... | collective-permute-start | bytes 24584 | tf_op jit(solution)/shard_map/ppermute | solution.py:69
  4.9 0.1 shard_map.131
  5.0 1.6 %collective-permute-start.4 = (bf16[4,80,128]{2,1,0:T(8,128)(2,1)S(1)}, bf16[4,80,128]{2,1,0:T(8,128)(2,1)S(1)}, u32[]{:S(2)}, u32[]{:S(2)}) collective-permute-start(bf16[4,80,128]{2,1,0:T(8,128)(2,1)S(1)} %get-tuple-element.24), channel_id=1, source_target_pairs={{0,2},{1,3},{2,0},{3,1},{4,6},{5,7},{6,4},{7,5},{8,10},{9,11},{10,... | collective-permute-start | bytes 245768 | tf_op jit(solution)/shard_map/ppermute | solution.py:69
  6.6 0.0 collective-permute-done.theirs
  6.6 1.8 %collective-permute-start.1 = (bf16[2,32,128]{2,1,0:T(8,128)(2,1)S(1)}, bf16[2,32,128]{2,1,0:T(8,128)(2,1)S(1)}, u32[]{:S(2)}, u32[]{:S(2)}) collective-permute-start(bf16[2,32,128]{2,1,0:T(8,128)(2,1)S(1)} %shard_map.128.mine.after), channel_id=1, source_target_pairs={{0,4},{1,5},{2,6},{3,7},{4,0},{5,1},{6,2},{7,3},{8,12},{9,13},{10,... | collective-permute-start | bytes 49160 | tf_op jit(solution)/shard_map/ppermute | solution.py:69
  8.5 0.0 collective-permute-start.3
  8.5 0.0 copy-start.7
  8.5 1.7 %collective-permute-start.5 = (bf16[4,80,128]{2,1,0:T(8,128)(2,1)S(1)}, bf16[4,80,128]{2,1,0:T(8,128)(2,1)S(1)}, u32[]{:S(2)}, u32[]{:S(2)}) collective-permute-start(bf16[4,80,128]{2,1,0:T(8,128)(2,1)S(1)} %shard_map.133), channel_id=1, source_target_pairs={{0,3},{1,2},{2,1},{3,0},{4,7},{5,6},{6,5},{7,4},{8,11},{9,10},{10,... | collective-permute-start | bytes 245768 | tf_op jit(solution)/shard_map/ppermute | solution.py:69
  10.2 0.2 collective-permute-done.1.theirs
  10.4 1.8 %collective-permute-start.2 = (bf16[4,32,128]{2,1,0:T(8,128)(2,1)S(1)}, bf16[4,32,128]{2,1,0:T(8,128)(2,1)S(1)}, u32[]{:S(2)}, u32[]{:S(2)}) collective-permute-start(bf16[4,32,128]{2,1,0:T(8,128)(2,1)S(1)} %shard_map.129.mine), channel_id=1, source_target_pairs={{0,2},{1,3},{2,0},{3,1},{4,6},{5,7},{6,4},{7,5},{8,10},{9,11},{10,... | collective-permute-start | bytes 98312 | tf_op jit(solution)/shard_map/ppermute | solution.py:69
  12.1 2.1 %collective-permute-done.2.theirs = bf16[4,32,128]{2,1,0:T(8,128)(2,1)S(1)} collective-permute-done((bf16[4,32,128]{2,1,0:T(8,128)(2,1)S(1)}, bf16[4,32,128]{2,1,0:T(8,128)(2,1)S(1)}, u32[]{:S(2)}, u32[]{:S(2)}) %collective-permute-start.2) | collective-permute-done | bytes 32800 | tf_op jit(solution)/shard_map/ppermute | solution.py:69
  14.3 0.1 collective-permute-start.6
  14.4 0.0 collective-permute-done.4.refs_2_
  14.4 0.0 collective-permute-done.3.refs_1_
  14.4 0.0 collective-permute-done.5.refs_3_
  14.4 0.0 copy-start.3
  14.4 0.0 copy-start.8
  14.5 1.9 %collective-permute-start.9 = (bf16[4,80,128]{2,1,0:T(8,128)(2,1)S(1)}, bf16[4,80,128]{2,1,0:T(8,128)(2,1)S(1)}, u32[]{:S(2)}, u32[]{:S(2)}) collective-permute-start(bf16[4,80,128]{2,1,0:T(8,128)(2,1)S(1)} %get-tuple-element.29), channel_id=1, source_target_pairs={{0,4},{1,5},{2,6},{3,7},{4,0},{5,1},{6,2},{7,3},{8,12},{9,13},{10,... | collective-permute-start | bytes 245768 | tf_op jit(solution)/shard_map/ppermute | solution.py:69
  16.4 0.0 collective-permute-done.6.theirs
  16.4 1.2 %shard_map.135 = (bf16[9,16,128]{2,1,0:T(8,128)(2,1)S(1)}, bf16[9,16,128]{2,1,0:T(8,128)(2,1)S(1)}) custom-call(bf16[4,80,128]{2,1,0:T(8,128)(2,1)S(1)} %get-tuple-element.26.after.refs_0_, s32[8]{0:T(128)S(1)} %copy-done.8, bf16[9,16,128]{2,1,0:T(8,128)(2,1)S(1)} %get-tuple-element.21.after.mine, bf16[9,16,128]{2,1,0:T(8,128)(2,1)S(1)} %collective-permute-done.6.theirs, ...), custom_call_target="tpu_custom_call" | custom-call | flops 8000000000 | tf_op jit(solution)/shard_map/pallas_call | solution.py:35
  17.6 0.2 collective-permute-start.7
  17.8 2.6 %collective-permute-start.10 = (bf16[4,80,128]{2,1,0:T(8,128)(2,1)S(1)}, bf16[4,80,128]{2,1,0:T(8,128)(2,1)S(1)}, u32[]{:S(2)}, u32[]{:S(2)}) collective-permute-start(bf16[4,80,128]{2,1,0:T(8,128)(2,1)S(1)} %shard_map.138), channel_id=1, source_target_pairs={{0,8},{1,9},{2,10},{3,11},{4,12},{5,13},{6,14},{7,15},{8,0},{9,1},... | collective-permute-start | bytes 245768 | tf_op jit(solution)/shard_map/ppermute | solution.py:69
  20.4 0.0 collective-permute-done.7.theirs
  20.4 0.3 shard_map.136.mine.after
  20.7 1.6 %collective-permute-start.8 = (bf16[9,16,128]{2,1,0:T(8,128)(2,1)S(1)}, bf16[9,16,128]{2,1,0:T(8,128)(2,1)S(1)}, u32[]{:S(2)}, u32[]{:S(2)}) collective-permute-start(bf16[9,16,128]{2,1,0:T(8,128)(2,1)S(1)} %shard_map.136.mine.after), channel_id=1, source_target_pairs={{0,2},{1,3},{2,0},{3,1},{4,6},{5,7},{6,4},{7,5},{8,10},{9,11},{10,... | collective-permute-start | bytes 110600 | tf_op jit(solution)/shard_map/ppermute | solution.py:69
  22.3 1.8 %collective-permute-start.11 = (bf16[4,80,128]{2,1,0:T(8,128)(2,1)S(1)}, bf16[4,80,128]{2,1,0:T(8,128)(2,1)S(1)}, u32[]{:S(2)}, u32[]{:S(2)}) collective-permute-start(bf16[4,80,128]{2,1,0:T(8,128)(2,1)S(1)} %shard_map.139), channel_id=1, source_target_pairs={{0,12},{1,13},{2,14},{3,15},{4,8},{5,9},{6,10},{7,11},{8,4},{9,5},... | collective-permute-start | bytes 245768 | tf_op jit(solution)/shard_map/ppermute | solution.py:69
  24.1 0.6 %collective-permute-done.8.theirs = bf16[9,16,128]{2,1,0:T(8,128)(2,1)S(1)} collective-permute-done((bf16[9,16,128]{2,1,0:T(8,128)(2,1)S(1)}, bf16[9,16,128]{2,1,0:T(8,128)(2,1)S(1)}, u32[]{:S(2)}, u32[]{:S(2)}) %collective-permute-start.8) | collective-permute-done | bytes 36896 | tf_op jit(solution)/shard_map/ppermute | solution.py:69
  24.7 0.4 shard_map.137.after.mine
  25.1 1.6 %collective-permute-start.12 = (bf16[9,16,128]{2,1,0:T(8,128)(2,1)S(1)}, bf16[9,16,128]{2,1,0:T(8,128)(2,1)S(1)}, u32[]{:S(2)}, u32[]{:S(2)}) collective-permute-start(bf16[9,16,128]{2,1,0:T(8,128)(2,1)S(1)} %shard_map.137.after.mine), channel_id=1, source_target_pairs={{0,4},{1,5},{2,6},{3,7},{4,0},{5,1},{6,2},{7,3},{8,12},{9,13},{10,... | collective-permute-start | bytes 110600 | tf_op jit(solution)/shard_map/ppermute | solution.py:69
  26.6 2.6 %collective-permute-done.12.theirs = bf16[9,16,128]{2,1,0:T(8,128)(2,1)S(1)} collective-permute-done((bf16[9,16,128]{2,1,0:T(8,128)(2,1)S(1)}, bf16[9,16,128]{2,1,0:T(8,128)(2,1)S(1)}, u32[]{:S(2)}, u32[]{:S(2)}) %collective-permute-start.12) | collective-permute-done | bytes 36896 | tf_op jit(solution)/shard_map/ppermute | solution.py:69
  29.2 0.4 shard_map.141.mine
  29.6 0.9 %collective-permute-start.13 = (bf16[9,16,128]{2,1,0:T(8,128)(2,1)S(1)}, bf16[9,16,128]{2,1,0:T(8,128)(2,1)S(1)}, u32[]{:S(2)}, u32[]{:S(2)}) collective-permute-start(bf16[9,16,128]{2,1,0:T(8,128)(2,1)S(1)} %shard_map.141.mine), channel_id=1, source_target_pairs={{0,8},{1,9},{2,10},{3,11},{4,12},{5,13},{6,14},{7,15},{8,0},{9,1},... | collective-permute-start | bytes 110600 | tf_op jit(solution)/shard_map/ppermute | solution.py:69
  30.5 0.0 collective-permute-done.9.refs_1_
  30.5 0.0 collective-permute-done.10.refs_2_
  30.5 0.0 collective-permute-done.11.refs_3_
  30.5 1.6 %collective-permute-start.15 = (bf16[16,80,128]{2,1,0:T(8,128)(2,1)S(1)}, bf16[16,80,128]{2,1,0:T(8,128)(2,1)S(1)}, u32[]{:S(2)}, u32[]{:S(2)}) collective-permute-start(bf16[16,80,128]{2,1,0:T(8,128)(2,1)S(1)} %shard_map.140.after.mine), channel_id=1, source_target_pairs={{0,16},{16,0},{1,17},{17,1},{2,18},{18,2},{3,19},{19,3},{4,20},{20... | collective-permute-start | bytes 983048 | tf_op jit(solution)/shard_map/ppermute | solution.py:427
  32.1 2.4 %collective-permute-done.13.theirs = bf16[9,16,128]{2,1,0:T(8,128)(2,1)S(1)} collective-permute-done((bf16[9,16,128]{2,1,0:T(8,128)(2,1)S(1)}, bf16[9,16,128]{2,1,0:T(8,128)(2,1)S(1)}, u32[]{:S(2)}, u32[]{:S(2)}) %collective-permute-start.13) | collective-permute-done | bytes 36896 | tf_op jit(solution)/shard_map/ppermute | solution.py:69
  34.5 0.4 shard_map.142
  34.9 0.1 collective-permute-start.14
  35.0 3.6 %collective-permute-done.15.theirs = bf16[16,80,128]{2,1,0:T(8,128)(2,1)S(1)} collective-permute-done((bf16[16,80,128]{2,1,0:T(8,128)(2,1)S(1)}, bf16[16,80,128]{2,1,0:T(8,128)(2,1)S(1)}, u32[]{:S(2)}, u32[]{:S(2)}) %collective-permute-start.15) | collective-permute-done | bytes 327712 | tf_op jit(solution)/shard_map/ppermute | solution.py:427
  38.6 0.1 shard_map.143
  38.7 0.0 collective-permute-done.14.theirs
  38.8 0.0 copy-start.9
  38.8 0.0 copy-start.10
  38.8 2.8 %shard_map.144 = bf16[16,16,128]{2,1,0:T(8,128)(2,1)S(1)} custom-call(bf16[8,16,128]{2,1,0:T(8,128)(2,1)S(1)} %get-tuple-element.34.mine, bf16[8,16,128]{2,1,0:T(8,128)(2,1)S(1)} %collective-permute-done.14.theirs, bf16[2048,768]{1,0:T(8,128)(2,1)S(1)} %bitcast.5, bf16[2048,768]{1,0:T(8,128)(2,1)S(1)} %bitcast.6, bf16[768,2048]{1,0:T(8,128)(2,1)S(1)} %bitcast.7, ...), custom_call_target="tpu_custom_call" | custom-call | flops 400000000 | tf_op jit(solution)/shard_map/pallas_call | solution.py:35
  41.5 11.7 %all_to_all.5.got = bf16[16,16,128]{2,1,0:T(8,128)(2,1)S(1)} all-to-all(bf16[16,16,128]{2,1,0:T(8,128)(2,1)S(1)} %shard_map.144), channel_id=1, replica_groups=mesh['grp'=2,'exp'=16] {'exp'}, dimensions={0} | all-to-all | bytes 131072 | tf_op jit(solution)/shard_map/all_to_all | solution.py:540
  53.3 0.9 %shard_map.145 = bf16[1,2048]{1,0:T(2,128)(2,1)} custom-call(f32[16,128]{1,0:T(8,128)S(1)} %get-tuple-element.33.hidden, bf16[16,16,128]{2,1,0:T(8,128)(2,1)S(1)} %all_to_all.5.got, s32[1,8]{1,0:T(1,128)S(1)} %copy-done.9, f32[1,8]{1,0:T(1,128)S(1)} %copy-done.10), custom_call_target="tpu_custom_call" | custom-call | flops 400000000 | tf_op jit(solution)/shard_map/pallas_call | solution.py:35
  (26 shorter events, 0.2 us)
Async XLA Ops:
  0.0 4.9 %copy-start.5 = (bf16[16,96,48]{1,2,0:T(8,128)(2,1)S(1)}, bf16[16,96,48]{1,2,0:T(8,128)(2,1)}, u32[]{:S(2)}) copy-start(bf16[16,96,48]{1,2,0:T(8,128)(2,1)} %param.25) | copy-start | bytes 442372
  0.0 4.9 %copy-start.4 = (bf16[16,96,128]{2,1,0:T(8,128)(2,1)S(1)}, bf16[16,96,128]{2,1,0:T(8,128)(2,1)}, u32[]{:S(2)}) copy-start(bf16[16,96,128]{2,1,0:T(8,128)(2,1)} %model.1) | copy-start | bytes 1179652
  0.8 5.8 %collective-permute-start = (bf16[1,32,128]{2,1,0:T(8,128)(2,1)S(1)}, bf16[1,32,128]{2,1,0:T(8,128)(2,1)S(1)}, u32[]{:S(2)}, u32[]{:S(2)}) collective-permute-start(bf16[1,32,128]{2,1,0:T(8,128)(2,1)S(1)} %shard_map.127.mine.after), channel_id=1, source_target_pairs={{0,8},{1,9},{2,10},{3,11},{4,12},{5,13},{6,14},{7,15},{8,0},{9,1},... | collective-permute-start | bytes 24584 | tf_op jit(solution)/shard_map/ppermute | solution.py:69
  5.0 9.3 %collective-permute-start.4 = (bf16[4,80,128]{2,1,0:T(8,128)(2,1)S(1)}, bf16[4,80,128]{2,1,0:T(8,128)(2,1)S(1)}, u32[]{:S(2)}, u32[]{:S(2)}) collective-permute-start(bf16[4,80,128]{2,1,0:T(8,128)(2,1)S(1)} %get-tuple-element.24), channel_id=1, source_target_pairs={{0,2},{1,3},{2,0},{3,1},{4,6},{5,7},{6,4},{7,5},{8,10},{9,11},{10,... | collective-permute-start | bytes 245768 | tf_op jit(solution)/shard_map/ppermute | solution.py:69
  6.6 3.7 %collective-permute-start.1 = (bf16[2,32,128]{2,1,0:T(8,128)(2,1)S(1)}, bf16[2,32,128]{2,1,0:T(8,128)(2,1)S(1)}, u32[]{:S(2)}, u32[]{:S(2)}) collective-permute-start(bf16[2,32,128]{2,1,0:T(8,128)(2,1)S(1)} %shard_map.128.mine.after), channel_id=1, source_target_pairs={{0,4},{1,5},{2,6},{3,7},{4,0},{5,1},{6,2},{7,3},{8,12},{9,13},{10,... | collective-permute-start | bytes 49160 | tf_op jit(solution)/shard_map/ppermute | solution.py:69
  8.5 5.9 %collective-permute-start.3 = (bf16[4,80,128]{2,1,0:T(8,128)(2,1)S(1)}, bf16[4,80,128]{2,1,0:T(8,128)(2,1)S(1)}, u32[]{:S(2)}, u32[]{:S(2)}) collective-permute-start(bf16[4,80,128]{2,1,0:T(8,128)(2,1)S(1)} %shard_map.132), channel_id=1, source_target_pairs={{0,1},{1,0},{2,3},{3,2},{4,5},{5,4},{6,7},{7,6},{8,9},{9,8},{10,11... | collective-permute-start | bytes 245768 | tf_op jit(solution)/shard_map/ppermute | solution.py:69
  8.5 5.8 %copy-start.7 = (bf16[1,512]{1,0:T(2,128)(2,1)S(1)}, bf16[1,512]{1,0:T(2,128)(2,1)}, u32[]{:S(2)}) copy-start(bf16[1,512]{1,0:T(2,128)(2,1)} %new.1) | copy-start | bytes 3076
  8.5 5.9 %collective-permute-start.5 = (bf16[4,80,128]{2,1,0:T(8,128)(2,1)S(1)}, bf16[4,80,128]{2,1,0:T(8,128)(2,1)S(1)}, u32[]{:S(2)}, u32[]{:S(2)}) collective-permute-start(bf16[4,80,128]{2,1,0:T(8,128)(2,1)S(1)} %shard_map.133), channel_id=1, source_target_pairs={{0,3},{1,2},{2,1},{3,0},{4,7},{5,6},{6,5},{7,4},{8,11},{9,10},{10,... | collective-permute-start | bytes 245768 | tf_op jit(solution)/shard_map/ppermute | solution.py:69
  10.4 3.9 %collective-permute-start.2 = (bf16[4,32,128]{2,1,0:T(8,128)(2,1)S(1)}, bf16[4,32,128]{2,1,0:T(8,128)(2,1)S(1)}, u32[]{:S(2)}, u32[]{:S(2)}) collective-permute-start(bf16[4,32,128]{2,1,0:T(8,128)(2,1)S(1)} %shard_map.129.mine), channel_id=1, source_target_pairs={{0,2},{1,3},{2,0},{3,1},{4,6},{5,7},{6,4},{7,5},{8,10},{9,11},{10,... | collective-permute-start | bytes 98312 | tf_op jit(solution)/shard_map/ppermute | solution.py:69
  14.3 2.1 %collective-permute-start.6 = (bf16[9,16,128]{2,1,0:T(8,128)(2,1)S(1)}, bf16[9,16,128]{2,1,0:T(8,128)(2,1)S(1)}, u32[]{:S(2)}, u32[]{:S(2)}) collective-permute-start(bf16[9,16,128]{2,1,0:T(8,128)(2,1)S(1)} %get-tuple-element.21.after.mine), channel_id=1, source_target_pairs={{0,1},{1,0},{2,3},{3,2},{4,5},{5,4},{6,7},{7,6},{8,9},{9,8},{10,11... | collective-permute-start | bytes 110600 | tf_op jit(solution)/shard_map/ppermute | solution.py:69
  14.4 2.0 %copy-start.3 = (bf16[8,192,512]{2,1,0:T(8,128)(2,1)S(1)}, bf16[8,192,512]{2,1,0:T(8,128)(2,1)}, u32[]{:S(2)}) copy-start(bf16[8,192,512]{2,1,0:T(8,128)(2,1)} %cache.1) | copy-start | bytes 4718596
  14.4 2.0 %copy-start.8 = (s32[8]{0:T(128)S(1)}, s32[8]{0:T(128)}, u32[]{:S(2)}) copy-start(s32[8]{0:T(128)} %lengths.1) | copy-start | bytes 100
  14.5 16.0 %collective-permute-start.9 = (bf16[4,80,128]{2,1,0:T(8,128)(2,1)S(1)}, bf16[4,80,128]{2,1,0:T(8,128)(2,1)S(1)}, u32[]{:S(2)}, u32[]{:S(2)}) collective-permute-start(bf16[4,80,128]{2,1,0:T(8,128)(2,1)S(1)} %get-tuple-element.29), channel_id=1, source_target_pairs={{0,4},{1,5},{2,6},{3,7},{4,0},{5,1},{6,2},{7,3},{8,12},{9,13},{10,... | collective-permute-start | bytes 245768 | tf_op jit(solution)/shard_map/ppermute | solution.py:69
  17.6 2.8 %collective-permute-start.7 = (bf16[9,16,128]{2,1,0:T(8,128)(2,1)S(1)}, bf16[9,16,128]{2,1,0:T(8,128)(2,1)S(1)}, u32[]{:S(2)}, u32[]{:S(2)}) collective-permute-start(bf16[9,16,128]{2,1,0:T(8,128)(2,1)S(1)} %get-tuple-element.28), channel_id=1, source_target_pairs={{0,1},{1,0},{2,3},{3,2},{4,5},{5,4},{6,7},{7,6},{8,9},{9,8},{10,11... | collective-permute-start | bytes 110600 | tf_op jit(solution)/shard_map/ppermute | solution.py:69
  17.8 12.7 %collective-permute-start.10 = (bf16[4,80,128]{2,1,0:T(8,128)(2,1)S(1)}, bf16[4,80,128]{2,1,0:T(8,128)(2,1)S(1)}, u32[]{:S(2)}, u32[]{:S(2)}) collective-permute-start(bf16[4,80,128]{2,1,0:T(8,128)(2,1)S(1)} %shard_map.138), channel_id=1, source_target_pairs={{0,8},{1,9},{2,10},{3,11},{4,12},{5,13},{6,14},{7,15},{8,0},{9,1},... | collective-permute-start | bytes 245768 | tf_op jit(solution)/shard_map/ppermute | solution.py:69
  20.7 4.0 %collective-permute-start.8 = (bf16[9,16,128]{2,1,0:T(8,128)(2,1)S(1)}, bf16[9,16,128]{2,1,0:T(8,128)(2,1)S(1)}, u32[]{:S(2)}, u32[]{:S(2)}) collective-permute-start(bf16[9,16,128]{2,1,0:T(8,128)(2,1)S(1)} %shard_map.136.mine.after), channel_id=1, source_target_pairs={{0,2},{1,3},{2,0},{3,1},{4,6},{5,7},{6,4},{7,5},{8,10},{9,11},{10,... | collective-permute-start | bytes 110600 | tf_op jit(solution)/shard_map/ppermute | solution.py:69
  22.3 8.2 %collective-permute-start.11 = (bf16[4,80,128]{2,1,0:T(8,128)(2,1)S(1)}, bf16[4,80,128]{2,1,0:T(8,128)(2,1)S(1)}, u32[]{:S(2)}, u32[]{:S(2)}) collective-permute-start(bf16[4,80,128]{2,1,0:T(8,128)(2,1)S(1)} %shard_map.139), channel_id=1, source_target_pairs={{0,12},{1,13},{2,14},{3,15},{4,8},{5,9},{6,10},{7,11},{8,4},{9,5},... | collective-permute-start | bytes 245768 | tf_op jit(solution)/shard_map/ppermute | solution.py:69
  25.1 4.1 %collective-permute-start.12 = (bf16[9,16,128]{2,1,0:T(8,128)(2,1)S(1)}, bf16[9,16,128]{2,1,0:T(8,128)(2,1)S(1)}, u32[]{:S(2)}, u32[]{:S(2)}) collective-permute-start(bf16[9,16,128]{2,1,0:T(8,128)(2,1)S(1)} %shard_map.137.after.mine), channel_id=1, source_target_pairs={{0,4},{1,5},{2,6},{3,7},{4,0},{5,1},{6,2},{7,3},{8,12},{9,13},{10,... | collective-permute-start | bytes 110600 | tf_op jit(solution)/shard_map/ppermute | solution.py:69
  29.6 4.9 %copy-start.6 = (f32[2048]{0:T(1024)S(1)}, f32[2048]{0:T(1024)}, u32[]{:S(2)}) copy-start(f32[2048]{0:T(1024)} %param.18) | copy-start | bytes 24580
  29.6 4.9 %collective-permute-start.13 = (bf16[9,16,128]{2,1,0:T(8,128)(2,1)S(1)}, bf16[9,16,128]{2,1,0:T(8,128)(2,1)S(1)}, u32[]{:S(2)}, u32[]{:S(2)}) collective-permute-start(bf16[9,16,128]{2,1,0:T(8,128)(2,1)S(1)} %shard_map.141.mine), channel_id=1, source_target_pairs={{0,8},{1,9},{2,10},{3,11},{4,12},{5,13},{6,14},{7,15},{8,0},{9,1},... | collective-permute-start | bytes 110600 | tf_op jit(solution)/shard_map/ppermute | solution.py:69
  30.5 8.0 %collective-permute-start.15 = (bf16[16,80,128]{2,1,0:T(8,128)(2,1)S(1)}, bf16[16,80,128]{2,1,0:T(8,128)(2,1)S(1)}, u32[]{:S(2)}, u32[]{:S(2)}) collective-permute-start(bf16[16,80,128]{2,1,0:T(8,128)(2,1)S(1)} %shard_map.140.after.mine), channel_id=1, source_target_pairs={{0,16},{16,0},{1,17},{17,1},{2,18},{18,2},{3,19},{19,3},{4,20},{20... | collective-permute-start | bytes 983048 | tf_op jit(solution)/shard_map/ppermute | solution.py:427
  34.5 4.3 %copy-start = (bf16[1,2048,768]{2,1,0:T(8,128)(2,1)S(1)}, bf16[1,2048,768]{2,1,0:T(8,128)(2,1)}, u32[]{:S(2)}) copy-start(bf16[1,2048,768]{2,1,0:T(8,128)(2,1)} %param.21) | copy-start | bytes 9437188
  34.5 4.3 %copy-start.1 = (bf16[1,2048,768]{2,1,0:T(8,128)(2,1)S(1)}, bf16[1,2048,768]{2,1,0:T(8,128)(2,1)}, u32[]{:S(2)}) copy-start(bf16[1,2048,768]{2,1,0:T(8,128)(2,1)} %param.22) | copy-start | bytes 9437188
  34.5 4.3 %copy-start.2 = (bf16[1,768,2048]{2,1,0:T(8,128)(2,1)S(1)}, bf16[1,768,2048]{2,1,0:T(8,128)(2,1)}, u32[]{:S(2)}) copy-start(bf16[1,768,2048]{2,1,0:T(8,128)(2,1)} %param.23) | copy-start | bytes 9437188
  34.9 3.8 %collective-permute-start.14 = (bf16[8,16,128]{2,1,0:T(8,128)(2,1)S(1)}, bf16[8,16,128]{2,1,0:T(8,128)(2,1)S(1)}, u32[]{:S(2)}, u32[]{:S(2)}) collective-permute-start(bf16[8,16,128]{2,1,0:T(8,128)(2,1)S(1)} %get-tuple-element.34.mine), channel_id=1, source_target_pairs={{0,1},{1,0},{2,3},{3,2},{4,5},{5,4},{6,7},{7,6},{8,9},{9,8},{10,11... | collective-permute-start | bytes 98312 | tf_op jit(solution)/shard_map/ppermute | solution.py:69
  38.8 14.5 %copy-start.9 = (s32[1,8]{1,0:T(1,128)S(1)}, s32[1,8]{1,0:T(1,128)}, u32[]{:S(2)}) copy-start(s32[1,8]{1,0:T(1,128)} %choice.1) | copy-start | bytes 100
  38.8 14.5 %copy-start.10 = (f32[1,8]{1,0:T(1,128)S(1)}, f32[1,8]{1,0:T(1,128)}, u32[]{:S(2)}) copy-start(f32[1,8]{1,0:T(1,128)} %probability.1) | copy-start | bytes 100

commit v9 on v8

--- a/solution.py
+++ b/solution.py
@@ -22,7 +22,10 @@
 
 floor_score = -1e30
 epsilon = 1e-06
-FILL = 4000
+FILL = 1000
+TOKEN = 1500
+MERGE = 1600
+JOIN = 800
 
 VMEM = pl.BlockSpec(memory_space=pltpu.VMEM)
 SMEM = pl.BlockSpec(memory_space=pltpu.SMEM)
@@ -31,7 +34,7 @@
 bf16, f32 = jnp.bfloat16, jnp.float32
 
 
-def call(kernel, shapes, specs, *args, limit=8, scratch=(), nanos=400):
+def call(kernel, shapes, specs, *args, limit=8, scratch=(), nanos=JOIN):
     return pl.pallas_call(
         kernel,
         out_shape=shapes,
@@ -102,7 +105,7 @@
     out[half:] = theirs[...]
 
 
-def narrow_kernel(mine, theirs, new, residuals, out):
+def narrow_kernel(after, mine, theirs, new, residuals, out):
     half = mine.shape[0]
     for k, source in enumerate((mine, theirs)):
         for w in range(half):
@@ -166,7 +169,7 @@
     return peak, total, acc
 
 
-def merge_kernel(mine, theirs, out, *, slots, flip):
+def merge_kernel(after, mine, theirs, out, *, slots, flip):
     peak, total, acc = merged(mine, theirs, slots, flip)
     lanes = iota(HEADS, 1)
     stats = jnp.where(lanes < slots, peak, 0.0)
@@ -196,7 +199,7 @@
     return top, own_weight + other_weight, acc
 
 
-def attend_kernel(after, lengths, mine, theirs, cache, keep, send, *, far):
+def attend_kernel(lengths, mine, theirs, cache, keep, send, *, far):
     me = lax.axis_index("exp")
     sequences, block, _ = cache.shape
     rows = 2 * QUERY_HEADS
@@ -254,7 +257,7 @@
         write_stats(stats[k], part, sequences)
 
 
-def token_kernel(after, mine, theirs, residuals, scale, hidden_out, normed_out):
+def token_kernel(mine, theirs, residuals, scale, hidden_out, normed_out):
     slots = residuals.shape[0]
     _, total, acc = merged(mine, theirs, slots, 1)
     inverse = 1.0 / jnp.where(iota(HEADS, 1) < slots, total, 1.0)
@@ -304,14 +307,17 @@
                 out[me ^ (distance_of(w, far) | 2 * y | c)] = line.astype(bf16)
 
 
-def finish_kernel(hidden, got, choice, probability, out):
+def gate_kernel(after, choice, probability, out):
     p = probability[...]
     shares = p / jnp.sum(p, axis=1, keepdims=True)
     lanes = iota((1, HEAD_WIDTH), 1)
     gates = jnp.zeros((1, HEAD_WIDTH), f32)
     for k in range(p.shape[1]):
         gates = gates + jnp.where(choice[:, k : k + 1] == lanes, shares[:, k : k + 1], 0.0)
-    gates = gates.astype(bf16).astype(f32)
+    out[...] = gates.astype(bf16).astype(f32)
+
+
+def finish_kernel(hidden, got, gates, out):
     total = hidden[...]
     for e in range(got.shape[0]):
         total = total + gates[:, e : e + 1] * got[e].astype(f32)
@@ -388,7 +394,7 @@
         lora_turn_kernel,
         (shape((NEAR,) + block, bf16),) * far,
         [VMEM] * (1 + NEAR),
-        marks[3],
+        marks[2],
         packed[0],
         swap(hold(packed[1], marks[1]), n, 1),
         swap(packed[2], n, 2),
@@ -398,18 +404,20 @@
     return turned, False
 
 
-def lora_far(turned, n, marks):
-    far = len(turned)
-    rows = turned[0].shape[1]
-    got = [turned[0], swap(turned[1], n, NEAR)]
-    for j in range(2, far):
-        got.append(swap(hold(turned[j], marks[j - 2]), n, j * NEAR))
+def lora_far_start(turned, n, after):
+    arrived = [turned[0], swap(turned[1], n, NEAR)]
+    for j in range(2, len(turned) - 1):
+        arrived.append(swap(hold(turned[j], after), n, j * NEAR))
+    return arrived
+
+
+def lora_order(arrived, n, after):
     return call(
         lora_order_kernel,
-        shape((n, rows, HEAD_WIDTH), bf16),
-        [VMEM] * (1 + far),
-        marks[far - 2],
-        *got,
+        shape((n,) + arrived[0].shape[1:], bf16),
+        [VMEM] * (1 + len(arrived)),
+        after,
+        *arrived,
         nanos=FILL,
     )
 
@@ -468,55 +476,67 @@
         )
         marks.append(message)
         distance //= 2
+    turned, whole = lora_near(adapter_model, adapter_hidden, n, marks)
     residuals, near = call(
         narrow_kernel,
         (shape((slots,) + HEADS, bf16), shape((slots + 1,) + HEADS, bf16)),
-        [VMEM] * 3,
+        [VMEM] * 4,
+        turned[0],
         message,
         swap(message, n, 2),
         incoming_key_value,
     )
-    marks = marks[:3] + [near]
-    turned, whole = lora_near(adapter_model, adapter_hidden, n, marks)
+    if not whole:
+        arrived = lora_far_start(turned, n, near)
     next_near = swap(near, n, 1)
     partial = shape((slots + stat_tiles(slots),) + HEADS, bf16)
     keep, send = call(
         functools.partial(attend_kernel, far=far),
         (partial,) * 2,
-        [VMEM, SMEM] + [VMEM] * 3,
-        turned[0],
+        [SMEM] + [VMEM] * 3,
         lengths,
         near,
         next_near,
         key_value_cache,
         nanos=8000,
     )
-    marks = [keep]
-    theirs, flip, distance = swap(send, n, 1), 0, 2
+    gates = call(
+        gate_kernel,
+        shape((1, HEAD_WIDTH), f32),
+        [VMEM] * 3,
+        keep,
+        expert_choice,
+        router_probability,
+    )
+    theirs, flip, distance, after = swap(send, n, 1), 0, 2, gates
     while distance < n:
         keep = call(
             functools.partial(merge_kernel, slots=slots, flip=flip),
             partial,
-            [VMEM] * 2,
+            [VMEM] * 3,
+            after,
             keep,
             theirs,
+            nanos=MERGE,
         )
-        marks.append(keep)
-        if distance == n // 2:
-            ordered = turned[0] if whole else lora_far(turned, n, marks)
+        if distance == 2 and not whole:
+            last = hold(turned[-1], keep)
+            arrived.append(swap(last, n, n - NEAR))
+        if distance == n // 4:
+            after = turned[0] if whole else lora_order(arrived, n, keep)
         theirs = swap(keep, n, distance)
         flip = slots // distance
         distance *= 2
+    ordered = after
     hidden, normed = call(
         token_kernel,
         (shape(HEADS, f32), shape((slots,) + HEADS, bf16)),
-        [VMEM] * 5,
-        ordered,
+        [VMEM] * 4,
         keep,
         theirs,
         residuals,
         norm_scale_vector.reshape(HEADS),
-        nanos=4000,
+        nanos=TOKEN,
     )
     model, inner = turned if whole else lora_join(ordered, adapter_hidden.shape[2])
     out = call(
@@ -535,11 +555,10 @@
     return call(
         finish_kernel,
         shape((1, WIDTH), bf16),
-        [VMEM] * 4,
+        [VMEM] * 3,
         hidden,
         lax.all_to_all(out, "exp", split_axis=0, concat_axis=0, tiled=True),
-        expert_choice,
-        router_probability,
+        gates,
     )
 
 

time: 54.4 us -> 52.6 us (0.967)
  starting transfers between devices: 23.3 us -> 20 us
  waiting for transfers between devices: 11.5 us -> 14.1 us
  blocking collectives: 11.7 us -> 9.48 us
  local copies, waits for them, and re-layouts: 0.05 us -> 1.19 us
    ppermute x15, waiting for transfers between devices: 7.87 us -> 13.1 us  [swap(): return lax.ppermute(value, 'exp', [(t, t ^ distance) for t in range(n)])]
    ppermute x15, starting transfers between devices: 21.8 us -> 18.5 us  [swap(): return lax.ppermute(value, 'exp', [(t, t ^ distance) for t in range(n)])]
    ppermute x1, waiting for transfers between devices: 3.6 us -> 0.98 us  [lora_join(): lax.ppermute(ordered, 'grp', [(0, 1), (1, 0)])]
    all_to_all x1, blocking collectives: 11.7 us -> 9.48 us  [body(): lax.all_to_all(out, 'exp', split_axis=0, concat_axis=0, tiled=True)]
    unnamed x22, local copies, waits for them, and re-layouts: 0.05 us -> 1.19 us
    pallas_call x19 -> x20, Pallas kernels: 7.39 us -> 7.37 us  [call(): pl.pallas_call(kernel, out_shape=shapes, in_specs=specs, out_specs=jax.tr...]
  transfers between devices with their start and end apart: 16 -> 16, of which waited for: 6 -> 9; matrix products, arithmetic and copies ran while one was open for 0% -> 0% of each run, Pallas kernels for 5% -> 6%
where the time goes in v9:
time: 52.6 us; the launch traced here: 52.3 us
  starting transfers between devices  20 us (38%)
  waiting for transfers between devices  14.1 us (27%)
  blocking collectives  9.48 us (18%)
  Pallas kernels  7.37 us (14%)
  local copies, waits for them, and re-layouts  1.19 us (2%)
    ppermute x15, starting transfers between devices, swap(): return lax.ppermute(value, 'exp', [(t, t ^ distance) for t in range(n)])  18.5 us
    ppermute x15, waiting for transfers between devices, swap(): return lax.ppermute(value, 'exp', [(t, t ^ distance) for t in range(n)])  13.1 us
    all_to_all x1, blocking collectives, body(): lax.all_to_all(out, 'exp', split_axis=0, concat_axis=0, tiled=True)  9.48 us
    pallas_call x20, Pallas kernels, call(): pl.pallas_call(kernel, out_shape=shapes, in_specs=specs, out_specs=jax.tr...  7.37 us
    ppermute x1, starting transfers between devices, lora_join(): lax.ppermute(ordered, 'grp', [(0, 1), (1, 0)])  1.56 us
    unnamed x22, local copies, waits for them, and re-layouts  1.19 us
  transfers between devices with their start and end apart: 16, of which 9 were waited for; matrix products, arithmetic and copies ran while one was open for 0% of the time, Pallas kernels for 6%

profile of v9, /device:TPU:0, one launch (start us, length us, event | category | flops | bytes accessed | tf_op | source)
XLA Modules:
  0.0 52.3 jit_solution(16186731706151509227)
XLA Ops:
  0.0 0.8 %shard_map.127.mine.after = bf16[1,32,128]{2,1,0:T(8,128)(2,1)S(1)} custom-call(bf16[1,2048]{1,0:T(2,128)(2,1)} %query.1, bf16[1,2048]{1,0:T(2,128)(2,1)} %resid.1), custom_call_target="tpu_custom_call" | custom-call | flops 4000000000 | tf_op jit(solution)/shard_map/pallas_call | solution.py:38
  0.8 4.1 %collective-permute-start = (bf16[1,32,128]{2,1,0:T(8,128)(2,1)S(1)}, bf16[1,32,128]{2,1,0:T(8,128)(2,1)S(1)}, u32[]{:S(2)}, u32[]{:S(2)}) collective-permute-start(bf16[1,32,128]{2,1,0:T(8,128)(2,1)S(1)} %shard_map.127.mine.after), channel_id=1, source_target_pairs={{0,8},{1,9},{2,10},{3,11},{4,12},{5,13},{6,14},{7,15},{8,0},{9,1},... | collective-permute-start | bytes 24584 | tf_op jit(solution)/shard_map/ppermute | solution.py:72
  4.9 0.1 shard_map.130
  5.0 1.6 %collective-permute-start.3 = (bf16[4,80,128]{2,1,0:T(8,128)(2,1)S(1)}, bf16[4,80,128]{2,1,0:T(8,128)(2,1)S(1)}, u32[]{:S(2)}, u32[]{:S(2)}) collective-permute-start(bf16[4,80,128]{2,1,0:T(8,128)(2,1)S(1)} %get-tuple-element.23), channel_id=1, source_target_pairs={{0,2},{1,3},{2,0},{3,1},{4,6},{5,7},{6,4},{7,5},{8,10},{9,11},{10,... | collective-permute-start | bytes 245768 | tf_op jit(solution)/shard_map/ppermute | solution.py:72
  6.6 0.0 collective-permute-done.theirs
  6.6 1.8 %collective-permute-start.1 = (bf16[2,32,128]{2,1,0:T(8,128)(2,1)S(1)}, bf16[2,32,128]{2,1,0:T(8,128)(2,1)S(1)}, u32[]{:S(2)}, u32[]{:S(2)}) collective-permute-start(bf16[2,32,128]{2,1,0:T(8,128)(2,1)S(1)} %shard_map.128.mine.after), channel_id=1, source_target_pairs={{0,4},{1,5},{2,6},{3,7},{4,0},{5,1},{6,2},{7,3},{8,12},{9,13},{10,... | collective-permute-start | bytes 49160 | tf_op jit(solution)/shard_map/ppermute | solution.py:72
  8.5 0.0 collective-permute-start.2
  8.5 0.0 copy-start.7
  8.5 1.7 %collective-permute-start.4 = (bf16[4,80,128]{2,1,0:T(8,128)(2,1)S(1)}, bf16[4,80,128]{2,1,0:T(8,128)(2,1)S(1)}, u32[]{:S(2)}, u32[]{:S(2)}) collective-permute-start(bf16[4,80,128]{2,1,0:T(8,128)(2,1)S(1)} %shard_map.132), channel_id=1, source_target_pairs={{0,3},{1,2},{2,1},{3,0},{4,7},{5,6},{6,5},{7,4},{8,11},{9,10},{10,... | collective-permute-start | bytes 245768 | tf_op jit(solution)/shard_map/ppermute | solution.py:72
  10.2 0.2 collective-permute-done.1.theirs
  10.4 1.8 %collective-permute-start.5 = (bf16[4,32,128]{2,1,0:T(8,128)(2,1)S(1)}, bf16[4,32,128]{2,1,0:T(8,128)(2,1)S(1)}, u32[]{:S(2)}, u32[]{:S(2)}) collective-permute-start(bf16[4,32,128]{2,1,0:T(8,128)(2,1)S(1)} %shard_map.129.after.mine), channel_id=1, source_target_pairs={{0,2},{1,3},{2,0},{3,1},{4,6},{5,7},{6,4},{7,5},{8,10},{9,11},{10,... | collective-permute-start | bytes 98312 | tf_op jit(solution)/shard_map/ppermute | solution.py:72
  12.1 0.0 collective-permute-done.3.refs_2_
  12.1 0.0 collective-permute-done.2.refs_1_
  12.2 0.6 %collective-permute-done.4.refs_3_ = bf16[4,80,128]{2,1,0:T(8,128)(2,1)S(1)} collective-permute-done((bf16[4,80,128]{2,1,0:T(8,128)(2,1)S(1)}, bf16[4,80,128]{2,1,0:T(8,128)(2,1)S(1)}, u32[]{:S(2)}, u32[]{:S(2)}) %collective-permute-start.4) | collective-permute-done | bytes 81952 | tf_op jit(solution)/shard_map/ppermute | solution.py:72
  12.7 1.5 %collective-permute-done.5.theirs = bf16[4,32,128]{2,1,0:T(8,128)(2,1)S(1)} collective-permute-done((bf16[4,32,128]{2,1,0:T(8,128)(2,1)S(1)}, bf16[4,32,128]{2,1,0:T(8,128)(2,1)S(1)}, u32[]{:S(2)}, u32[]{:S(2)}) %collective-permute-start.5) | collective-permute-done | bytes 32800 | tf_op jit(solution)/shard_map/ppermute | solution.py:72
  14.3 0.1 collective-permute-start.6
  14.4 2.9 %collective-permute-start.10 = (bf16[4,80,128]{2,1,0:T(8,128)(2,1)S(1)}, bf16[4,80,128]{2,1,0:T(8,128)(2,1)S(1)}, u32[]{:S(2)}, u32[]{:S(2)}) collective-permute-start(bf16[4,80,128]{2,1,0:T(8,128)(2,1)S(1)} %shard_map.139), channel_id=1, source_target_pairs={{0,8},{1,9},{2,10},{3,11},{4,12},{5,13},{6,14},{7,15},{8,0},{9,1},... | collective-permute-start | bytes 245768 | tf_op jit(solution)/shard_map/ppermute | solution.py:72
  17.3 1.6 %collective-permute-start.9 = (bf16[4,80,128]{2,1,0:T(8,128)(2,1)S(1)}, bf16[4,80,128]{2,1,0:T(8,128)(2,1)S(1)}, u32[]{:S(2)}, u32[]{:S(2)}) collective-permute-start(bf16[4,80,128]{2,1,0:T(8,128)(2,1)S(1)} %get-tuple-element.29), channel_id=1, source_target_pairs={{0,4},{1,5},{2,6},{3,7},{4,0},{5,1},{6,2},{7,3},{8,12},{9,13},{10,... | collective-permute-start | bytes 245768 | tf_op jit(solution)/shard_map/ppermute | solution.py:72
  18.9 0.0 collective-permute-done.6.theirs
  18.9 1.2 %shard_map.135 = (bf16[9,16,128]{2,1,0:T(8,128)(2,1)S(1)}, bf16[9,16,128]{2,1,0:T(8,128)(2,1)S(1)}) custom-call(s32[8]{0:T(128)S(1)} %copy-done.8, bf16[9,16,128]{2,1,0:T(8,128)(2,1)S(1)} %get-tuple-element.26.mine.after, bf16[9,16,128]{2,1,0:T(8,128)(2,1)S(1)} %collective-permute-done.6.theirs, bf16[8,192,512]{2,1,0:T(8,128)(2,1)S(1)} %copy-done.3), custom_call_target="tpu_custom_call" | custom-call | flops 8000000000 | tf_op jit(solution)/shard_map/pallas_call | solution.py:38
  20.1 0.0 collective-permute-start.7
  20.1 0.2 shard_map.136.after.gates
  20.3 1.0 %collective-permute-done.7.theirs = bf16[9,16,128]{2,1,0:T(8,128)(2,1)S(1)} collective-permute-done((bf16[9,16,128]{2,1,0:T(8,128)(2,1)S(1)}, bf16[9,16,128]{2,1,0:T(8,128)(2,1)S(1)}, u32[]{:S(2)}, u32[]{:S(2)}) %collective-permute-start.7) | collective-permute-done | bytes 36896 | tf_op jit(solution)/shard_map/ppermute | solution.py:72
  21.3 0.3 shard_map.137.mine.after
  21.6 1.6 %collective-permute-start.8 = (bf16[9,16,128]{2,1,0:T(8,128)(2,1)S(1)}, bf16[9,16,128]{2,1,0:T(8,128)(2,1)S(1)}, u32[]{:S(2)}, u32[]{:S(2)}) collective-permute-start(bf16[9,16,128]{2,1,0:T(8,128)(2,1)S(1)} %shard_map.137.mine.after), channel_id=1, source_target_pairs={{0,2},{1,3},{2,0},{3,1},{4,6},{5,7},{6,4},{7,5},{8,10},{9,11},{10,... | collective-permute-start | bytes 110600 | tf_op jit(solution)/shard_map/ppermute | solution.py:72
  23.2 0.7 %collective-permute-start.11 = (bf16[4,80,128]{2,1,0:T(8,128)(2,1)S(1)}, bf16[4,80,128]{2,1,0:T(8,128)(2,1)S(1)}, u32[]{:S(2)}, u32[]{:S(2)}) collective-permute-start(bf16[4,80,128]{2,1,0:T(8,128)(2,1)S(1)} %shard_map.140), channel_id=1, source_target_pairs={{0,12},{1,13},{2,14},{3,15},{4,8},{5,9},{6,10},{7,11},{8,4},{9,5},... | collective-permute-start | bytes 245768 | tf_op jit(solution)/shard_map/ppermute | solution.py:72
  23.8 1.8 %collective-permute-done.8.theirs = bf16[9,16,128]{2,1,0:T(8,128)(2,1)S(1)} collective-permute-done((bf16[9,16,128]{2,1,0:T(8,128)(2,1)S(1)}, bf16[9,16,128]{2,1,0:T(8,128)(2,1)S(1)}, u32[]{:S(2)}, u32[]{:S(2)}) %collective-permute-start.8) | collective-permute-done | bytes 36896 | tf_op jit(solution)/shard_map/ppermute | solution.py:72
  25.6 0.4 shard_map.138.after.mine
  26.0 0.5 collective-permute-start.12
  26.5 0.0 collective-permute-done.10.refs_2_
  26.5 0.0 collective-permute-done.9.refs_1_
  26.5 3.2 %collective-permute-done.11.refs_3_ = bf16[4,80,128]{2,1,0:T(8,128)(2,1)S(1)} collective-permute-done((bf16[4,80,128]{2,1,0:T(8,128)(2,1)S(1)}, bf16[4,80,128]{2,1,0:T(8,128)(2,1)S(1)}, u32[]{:S(2)}, u32[]{:S(2)}) %collective-permute-start.11) | collective-permute-done | bytes 81952 | tf_op jit(solution)/shard_map/ppermute | solution.py:72
  29.7 0.0 copy-start.6
  29.7 1.6 %collective-permute-start.15 = (bf16[16,80,128]{2,1,0:T(8,128)(2,1)S(1)}, bf16[16,80,128]{2,1,0:T(8,128)(2,1)S(1)}, u32[]{:S(2)}, u32[]{:S(2)}) collective-permute-start(bf16[16,80,128]{2,1,0:T(8,128)(2,1)S(1)} %shard_map.141.after.mine), channel_id=1, source_target_pairs={{0,16},{16,0},{1,17},{17,1},{2,18},{18,2},{3,19},{19,3},{4,20},{20... | collective-permute-start | bytes 983048 | tf_op jit(solution)/shard_map/ppermute | solution.py:435
  31.3 0.0 collective-permute-done.12.theirs
  31.3 0.4 shard_map.142.mine
  31.6 0.1 collective-permute-start.13
  31.7 4.8 %collective-permute-done.13.theirs = bf16[9,16,128]{2,1,0:T(8,128)(2,1)S(1)} collective-permute-done((bf16[9,16,128]{2,1,0:T(8,128)(2,1)S(1)}, bf16[9,16,128]{2,1,0:T(8,128)(2,1)S(1)}, u32[]{:S(2)}, u32[]{:S(2)}) %collective-permute-start.13) | collective-permute-done | bytes 36896 | tf_op jit(solution)/shard_map/ppermute | solution.py:72
  36.5 0.4 shard_map.143
  37.0 0.1 collective-permute-start.14
  37.0 1.0 %collective-permute-done.15.theirs = bf16[16,80,128]{2,1,0:T(8,128)(2,1)S(1)} collective-permute-done((bf16[16,80,128]{2,1,0:T(8,128)(2,1)S(1)}, bf16[16,80,128]{2,1,0:T(8,128)(2,1)S(1)}, u32[]{:S(2)}, u32[]{:S(2)}) %collective-permute-start.15) | collective-permute-done | bytes 327712 | tf_op jit(solution)/shard_map/ppermute | solution.py:435
  38.0 0.1 shard_map.144
  38.2 0.1 collective-permute-done.14.theirs
  38.2 0.2 copy-done
  38.4 1.0 %copy-done.1 = bf16[1,2048,768]{2,1,0:T(8,128)(2,1)S(1)} copy-done((bf16[1,2048,768]{2,1,0:T(8,128)(2,1)S(1)}, bf16[1,2048,768]{2,1,0:T(8,128)(2,1)}, u32[]{:S(2)}) %copy-start.1) | copy-done | bytes 3145752
  39.4 2.8 %shard_map.145 = bf16[16,16,128]{2,1,0:T(8,128)(2,1)S(1)} custom-call(bf16[8,16,128]{2,1,0:T(8,128)(2,1)S(1)} %get-tuple-element.34.mine, bf16[8,16,128]{2,1,0:T(8,128)(2,1)S(1)} %collective-permute-done.14.theirs, bf16[2048,768]{1,0:T(8,128)(2,1)S(1)} %bitcast.5, bf16[2048,768]{1,0:T(8,128)(2,1)S(1)} %bitcast.6, bf16[768,2048]{1,0:T(8,128)(2,1)S(1)} %bitcast.7, ...), custom_call_target="tpu_custom_call" | custom-call | flops 800000000 | tf_op jit(solution)/shard_map/pallas_call | solution.py:38
  42.1 9.5 %all_to_all.5.got = bf16[16,16,128]{2,1,0:T(8,128)(2,1)S(1)} all-to-all(bf16[16,16,128]{2,1,0:T(8,128)(2,1)S(1)} %shard_map.145), channel_id=1, replica_groups=mesh['grp'=2,'exp'=16] {'exp'}, dimensions={0} | all-to-all | bytes 131072 | tf_op jit(solution)/shard_map/all_to_all | solution.py:560
  51.6 0.7 %shard_map.146 = bf16[1,2048]{1,0:T(2,128)(2,1)} custom-call(f32[16,128]{1,0:T(8,128)S(1)} %get-tuple-element.33.hidden, bf16[16,16,128]{2,1,0:T(8,128)(2,1)S(1)} %all_to_all.5.got, f32[1,128]{1,0:T(1,128)S(1)} %shard_map.136.after.gates), custom_call_target="tpu_custom_call" | custom-call | flops 800000000 | tf_op jit(solution)/shard_map/pallas_call | solution.py:38
  (27 shorter events, 0.1 us)
Async XLA Ops:
  0.0 4.9 %copy-start.5 = (bf16[16,96,48]{1,2,0:T(8,128)(2,1)S(1)}, bf16[16,96,48]{1,2,0:T(8,128)(2,1)}, u32[]{:S(2)}) copy-start(bf16[16,96,48]{1,2,0:T(8,128)(2,1)} %param.25) | copy-start | bytes 442372
  0.0 4.9 %copy-start.4 = (bf16[16,96,128]{2,1,0:T(8,128)(2,1)S(1)}, bf16[16,96,128]{2,1,0:T(8,128)(2,1)}, u32[]{:S(2)}) copy-start(bf16[16,96,128]{2,1,0:T(8,128)(2,1)} %model.1) | copy-start | bytes 1179652
  0.8 5.8 %collective-permute-start = (bf16[1,32,128]{2,1,0:T(8,128)(2,1)S(1)}, bf16[1,32,128]{2,1,0:T(8,128)(2,1)S(1)}, u32[]{:S(2)}, u32[]{:S(2)}) collective-permute-start(bf16[1,32,128]{2,1,0:T(8,128)(2,1)S(1)} %shard_map.127.mine.after), channel_id=1, source_target_pairs={{0,8},{1,9},{2,10},{3,11},{4,12},{5,13},{6,14},{7,15},{8,0},{9,1},... | collective-permute-start | bytes 24584 | tf_op jit(solution)/shard_map/ppermute | solution.py:72
  5.0 7.1 %collective-permute-start.3 = (bf16[4,80,128]{2,1,0:T(8,128)(2,1)S(1)}, bf16[4,80,128]{2,1,0:T(8,128)(2,1)S(1)}, u32[]{:S(2)}, u32[]{:S(2)}) collective-permute-start(bf16[4,80,128]{2,1,0:T(8,128)(2,1)S(1)} %get-tuple-element.23), channel_id=1, source_target_pairs={{0,2},{1,3},{2,0},{3,1},{4,6},{5,7},{6,4},{7,5},{8,10},{9,11},{10,... | collective-permute-start | bytes 245768 | tf_op jit(solution)/shard_map/ppermute | solution.py:72
  6.6 3.7 %collective-permute-start.1 = (bf16[2,32,128]{2,1,0:T(8,128)(2,1)S(1)}, bf16[2,32,128]{2,1,0:T(8,128)(2,1)S(1)}, u32[]{:S(2)}, u32[]{:S(2)}) collective-permute-start(bf16[2,32,128]{2,1,0:T(8,128)(2,1)S(1)} %shard_map.128.mine.after), channel_id=1, source_target_pairs={{0,4},{1,5},{2,6},{3,7},{4,0},{5,1},{6,2},{7,3},{8,12},{9,13},{10,... | collective-permute-start | bytes 49160 | tf_op jit(solution)/shard_map/ppermute | solution.py:72
  8.5 3.7 %collective-permute-start.2 = (bf16[4,80,128]{2,1,0:T(8,128)(2,1)S(1)}, bf16[4,80,128]{2,1,0:T(8,128)(2,1)S(1)}, u32[]{:S(2)}, u32[]{:S(2)}) collective-permute-start(bf16[4,80,128]{2,1,0:T(8,128)(2,1)S(1)} %shard_map.131), channel_id=1, source_target_pairs={{0,1},{1,0},{2,3},{3,2},{4,5},{5,4},{6,7},{7,6},{8,9},{9,8},{10,11... | collective-permute-start | bytes 245768 | tf_op jit(solution)/shard_map/ppermute | solution.py:72
  8.5 5.8 %copy-start.7 = (bf16[1,512]{1,0:T(2,128)(2,1)S(1)}, bf16[1,512]{1,0:T(2,128)(2,1)}, u32[]{:S(2)}) copy-start(bf16[1,512]{1,0:T(2,128)(2,1)} %new.1) | copy-start | bytes 3076
  8.5 4.2 %collective-permute-start.4 = (bf16[4,80,128]{2,1,0:T(8,128)(2,1)S(1)}, bf16[4,80,128]{2,1,0:T(8,128)(2,1)S(1)}, u32[]{:S(2)}, u32[]{:S(2)}) collective-permute-start(bf16[4,80,128]{2,1,0:T(8,128)(2,1)S(1)} %shard_map.132), channel_id=1, source_target_pairs={{0,3},{1,2},{2,1},{3,0},{4,7},{5,6},{6,5},{7,4},{8,11},{9,10},{10,... | collective-permute-start | bytes 245768 | tf_op jit(solution)/shard_map/ppermute | solution.py:72
  10.4 3.9 %collective-permute-start.5 = (bf16[4,32,128]{2,1,0:T(8,128)(2,1)S(1)}, bf16[4,32,128]{2,1,0:T(8,128)(2,1)S(1)}, u32[]{:S(2)}, u32[]{:S(2)}) collective-permute-start(bf16[4,32,128]{2,1,0:T(8,128)(2,1)S(1)} %shard_map.129.after.mine), channel_id=1, source_target_pairs={{0,2},{1,3},{2,0},{3,1},{4,6},{5,7},{6,4},{7,5},{8,10},{9,11},{10,... | collective-permute-start | bytes 98312 | tf_op jit(solution)/shard_map/ppermute | solution.py:72
  14.3 4.6 %copy-start.3 = (bf16[8,192,512]{2,1,0:T(8,128)(2,1)S(1)}, bf16[8,192,512]{2,1,0:T(8,128)(2,1)}, u32[]{:S(2)}) copy-start(bf16[8,192,512]{2,1,0:T(8,128)(2,1)} %cache.1) | copy-start | bytes 4718596
  14.3 4.6 %copy-start.8 = (s32[8]{0:T(128)S(1)}, s32[8]{0:T(128)}, u32[]{:S(2)}) copy-start(s32[8]{0:T(128)} %lengths.1) | copy-start | bytes 100
  14.3 4.6 %collective-permute-start.6 = (bf16[9,16,128]{2,1,0:T(8,128)(2,1)S(1)}, bf16[9,16,128]{2,1,0:T(8,128)(2,1)S(1)}, u32[]{:S(2)}, u32[]{:S(2)}) collective-permute-start(bf16[9,16,128]{2,1,0:T(8,128)(2,1)S(1)} %get-tuple-element.26.mine.after), channel_id=1, source_target_pairs={{0,1},{1,0},{2,3},{3,2},{4,5},{5,4},{6,7},{7,6},{8,9},{9,8},{10,11... | collective-permute-start | bytes 110600 | tf_op jit(solution)/shard_map/ppermute | solution.py:72
  14.4 12.1 %collective-permute-start.10 = (bf16[4,80,128]{2,1,0:T(8,128)(2,1)S(1)}, bf16[4,80,128]{2,1,0:T(8,128)(2,1)S(1)}, u32[]{:S(2)}, u32[]{:S(2)}) collective-permute-start(bf16[4,80,128]{2,1,0:T(8,128)(2,1)S(1)} %shard_map.139), channel_id=1, source_target_pairs={{0,8},{1,9},{2,10},{3,11},{4,12},{5,13},{6,14},{7,15},{8,0},{9,1},... | collective-permute-start | bytes 245768 | tf_op jit(solution)/shard_map/ppermute | solution.py:72
  17.3 2.8 %copy-start.9 = (s32[1,8]{1,0:T(1,128)S(1)}, s32[1,8]{1,0:T(1,128)}, u32[]{:S(2)}) copy-start(s32[1,8]{1,0:T(1,128)} %choice.1) | copy-start | bytes 100
  17.3 2.8 %copy-start.10 = (f32[1,8]{1,0:T(1,128)S(1)}, f32[1,8]{1,0:T(1,128)}, u32[]{:S(2)}) copy-start(f32[1,8]{1,0:T(1,128)} %probability.1) | copy-start | bytes 100
  17.3 9.2 %collective-permute-start.9 = (bf16[4,80,128]{2,1,0:T(8,128)(2,1)S(1)}, bf16[4,80,128]{2,1,0:T(8,128)(2,1)S(1)}, u32[]{:S(2)}, u32[]{:S(2)}) collective-permute-start(bf16[4,80,128]{2,1,0:T(8,128)(2,1)S(1)} %get-tuple-element.29), channel_id=1, source_target_pairs={{0,4},{1,5},{2,6},{3,7},{4,0},{5,1},{6,2},{7,3},{8,12},{9,13},{10,... | collective-permute-start | bytes 245768 | tf_op jit(solution)/shard_map/ppermute | solution.py:72
  20.1 1.3 %collective-permute-start.7 = (bf16[9,16,128]{2,1,0:T(8,128)(2,1)S(1)}, bf16[9,16,128]{2,1,0:T(8,128)(2,1)S(1)}, u32[]{:S(2)}, u32[]{:S(2)}) collective-permute-start(bf16[9,16,128]{2,1,0:T(8,128)(2,1)S(1)} %get-tuple-element.28), channel_id=1, source_target_pairs={{0,1},{1,0},{2,3},{3,2},{4,5},{5,4},{6,7},{7,6},{8,9},{9,8},{10,11... | collective-permute-start | bytes 110600 | tf_op jit(solution)/shard_map/ppermute | solution.py:72
  21.6 4.0 %collective-permute-start.8 = (bf16[9,16,128]{2,1,0:T(8,128)(2,1)S(1)}, bf16[9,16,128]{2,1,0:T(8,128)(2,1)S(1)}, u32[]{:S(2)}, u32[]{:S(2)}) collective-permute-start(bf16[9,16,128]{2,1,0:T(8,128)(2,1)S(1)} %shard_map.137.mine.after), channel_id=1, source_target_pairs={{0,2},{1,3},{2,0},{3,1},{4,6},{5,7},{6,4},{7,5},{8,10},{9,11},{10,... | collective-permute-start | bytes 110600 | tf_op jit(solution)/shard_map/ppermute | solution.py:72
  23.2 6.5 %collective-permute-start.11 = (bf16[4,80,128]{2,1,0:T(8,128)(2,1)S(1)}, bf16[4,80,128]{2,1,0:T(8,128)(2,1)S(1)}, u32[]{:S(2)}, u32[]{:S(2)}) collective-permute-start(bf16[4,80,128]{2,1,0:T(8,128)(2,1)S(1)} %shard_map.140), channel_id=1, source_target_pairs={{0,12},{1,13},{2,14},{3,15},{4,8},{5,9},{6,10},{7,11},{8,4},{9,5},... | collective-permute-start | bytes 245768 | tf_op jit(solution)/shard_map/ppermute | solution.py:72
  26.0 5.3 %collective-permute-start.12 = (bf16[9,16,128]{2,1,0:T(8,128)(2,1)S(1)}, bf16[9,16,128]{2,1,0:T(8,128)(2,1)S(1)}, u32[]{:S(2)}, u32[]{:S(2)}) collective-permute-start(bf16[9,16,128]{2,1,0:T(8,128)(2,1)S(1)} %shard_map.138.after.mine), channel_id=1, source_target_pairs={{0,4},{1,5},{2,6},{3,7},{4,0},{5,1},{6,2},{7,3},{8,12},{9,13},{10,... | collective-permute-start | bytes 110600 | tf_op jit(solution)/shard_map/ppermute | solution.py:72
  29.7 6.8 %copy-start.6 = (f32[2048]{0:T(1024)S(1)}, f32[2048]{0:T(1024)}, u32[]{:S(2)}) copy-start(f32[2048]{0:T(1024)} %param.18) | copy-start | bytes 24580
  29.7 8.3 %collective-permute-start.15 = (bf16[16,80,128]{2,1,0:T(8,128)(2,1)S(1)}, bf16[16,80,128]{2,1,0:T(8,128)(2,1)S(1)}, u32[]{:S(2)}, u32[]{:S(2)}) collective-permute-start(bf16[16,80,128]{2,1,0:T(8,128)(2,1)S(1)} %shard_map.141.after.mine), channel_id=1, source_target_pairs={{0,16},{16,0},{1,17},{17,1},{2,18},{18,2},{3,19},{19,3},{4,20},{20... | collective-permute-start | bytes 983048 | tf_op jit(solution)/shard_map/ppermute | solution.py:435
  31.3 7.0 %copy-start.2 = (bf16[1,768,2048]{2,1,0:T(8,128)(2,1)S(1)}, bf16[1,768,2048]{2,1,0:T(8,128)(2,1)}, u32[]{:S(2)}) copy-start(bf16[1,768,2048]{2,1,0:T(8,128)(2,1)} %param.23) | copy-start | bytes 9437188
  31.6 4.9 %collective-permute-start.13 = (bf16[9,16,128]{2,1,0:T(8,128)(2,1)S(1)}, bf16[9,16,128]{2,1,0:T(8,128)(2,1)S(1)}, u32[]{:S(2)}, u32[]{:S(2)}) collective-permute-start(bf16[9,16,128]{2,1,0:T(8,128)(2,1)S(1)} %shard_map.142.mine), channel_id=1, source_target_pairs={{0,8},{1,9},{2,10},{3,11},{4,12},{5,13},{6,14},{7,15},{8,0},{9,1},... | collective-permute-start | bytes 110600 | tf_op jit(solution)/shard_map/ppermute | solution.py:72
  36.5 1.9 %copy-start = (bf16[1,2048,768]{2,1,0:T(8,128)(2,1)S(1)}, bf16[1,2048,768]{2,1,0:T(8,128)(2,1)}, u32[]{:S(2)}) copy-start(bf16[1,2048,768]{2,1,0:T(8,128)(2,1)} %param.21) | copy-start | bytes 9437188
  36.5 2.8 %copy-start.1 = (bf16[1,2048,768]{2,1,0:T(8,128)(2,1)S(1)}, bf16[1,2048,768]{2,1,0:T(8,128)(2,1)}, u32[]{:S(2)}) copy-start(bf16[1,2048,768]{2,1,0:T(8,128)(2,1)} %param.22) | copy-start | bytes 9437188
  37.0 1.3 %collective-permute-start.14 = (bf16[8,16,128]{2,1,0:T(8,128)(2,1)S(1)}, bf16[8,16,128]{2,1,0:T(8,128)(2,1)S(1)}, u32[]{:S(2)}, u32[]{:S(2)}) collective-permute-start(bf16[8,16,128]{2,1,0:T(8,128)(2,1)S(1)} %get-tuple-element.34.mine), channel_id=1, source_target_pairs={{0,1},{1,0},{2,3},{3,2},{4,5},{5,4},{6,7},{7,6},{8,9},{9,8},{10,11... | collective-permute-start | bytes 98312 | tf_op jit(solution)/shard_map/ppermute | solution.py:72

commit v10 on v9

--- a/solution.py
+++ b/solution.py
@@ -22,10 +22,10 @@
 
 floor_score = -1e30
 epsilon = 1e-06
-FILL = 1000
+FILL = 20
 TOKEN = 1500
 MERGE = 1600
-JOIN = 800
+JOIN = 1600
 
 VMEM = pl.BlockSpec(memory_space=pltpu.VMEM)
 SMEM = pl.BlockSpec(memory_space=pltpu.SMEM)
@@ -199,7 +199,7 @@
     return top, own_weight + other_weight, acc
 
 
-def attend_kernel(lengths, mine, theirs, cache, keep, send, *, far):
+def attend_kernel(after, lengths, mine, theirs, cache, keep, send, *, far):
     me = lax.axis_index("exp")
     sequences, block, _ = cache.shape
     rows = 2 * QUERY_HEADS
@@ -325,36 +325,44 @@
     out[...] = line.astype(bf16)
 
 
-def lora_pack_kernel(after, model, inner, *outs):
-    low, first = lax.axis_index("exp") % NEAR, lax.axis_index("grp") == 0
-    ranks, split, most = model.shape[1], model.shape[1] // 2, outs[0].shape[1] - model.shape[1] // 2
+def without(index, bit):
+    return (index // (2 * bit)) * bit + index % bit
+
+
+def lora_pack_kernel(after, model, inner, keep, send, *, bit):
+    me, first = lax.axis_index("exp"), lax.axis_index("grp") == 0
+    ranks, split = model.shape[1], model.shape[1] // 2
+    most = keep.shape[1] - split
     rest = inner.shape[1] - most
-    for k, out in enumerate(outs):
+    for out in (keep, send):
         out[:, split:, ranks:] = jnp.zeros((out.shape[0], most, HEAD_WIDTH - ranks), out.dtype)
-        for z in range(out.shape[0]):
-            at = z * NEAR + (low ^ k)
-            out[z, :split] = jnp.where(first, model[at, :split], model[at, split:])
-            lower = inner[at, most:]
-            if rest < most:
-                pad = jnp.zeros((most - rest, ranks), out.dtype)
-                lower = jnp.concatenate([lower, pad], axis=0)
-            out[z, split:, :ranks] = jnp.where(first, inner[at, :most], lower)
-
-
-def lora_turn_kernel(after, *refs):
+    for d in range(model.shape[0]):
+        out, at, source = (send if d & bit else keep), without(d, bit), me ^ d
+        out[at, :split] = jnp.where(first, model[source, :split], model[source, split:])
+        lower = inner[source, most:]
+        if rest < most:
+            pad = jnp.zeros((most - rest, ranks), out.dtype)
+            lower = jnp.concatenate([lower, pad], axis=0)
+        out[at, split:, :ranks] = jnp.where(first, inner[source, :most], lower)
+
+
+def lora_turn_kernel(after, kept, got, keep, send, *, bit, following):
+    for d in range(2 * kept.shape[0]):
+        value = (got if d & bit else kept)[without(d, bit)]
+        (send if d & following else keep)[without(d, following)] = value
+
+
+def lora_spread_kernel(after, kept, got, *outs, bit):
+    for d in range(2 * kept.shape[0]):
+        outs[d // NEAR][d % NEAR] = (got if d & bit else kept)[without(d, bit)]
+
+
+def lora_order_kernel(after, *refs):
     me = lax.axis_index("exp")
-    low, high = me % NEAR, me // NEAR
-    got, outs = refs[:NEAR], refs[NEAR:]
-    for j, out in enumerate(outs):
-        for k, ref in enumerate(got):
-            out[low ^ k] = ref[high ^ j]
-
-
-def lora_order_kernel(after, *refs):
-    high = lax.axis_index("exp") // NEAR
     got, out = refs[:-1], refs[-1]
     for j, ref in enumerate(got):
-        out[pl.ds((high ^ j) * NEAR, NEAR)] = ref[...]
+        for l in range(NEAR):
+            out[me ^ (j * NEAR + l)] = ref[l]
 
 
 def lora_join_kernel(mine, theirs, model, inner):
@@ -381,27 +389,35 @@
         return [model[0], inner[0]], True
     far = n // NEAR
     block = (ranks // 2 + pad16(inner_width // 2), HEAD_WIDTH)
-    packed = call(
-        lora_pack_kernel,
-        (shape((far,) + block, bf16),) * NEAR,
+    halves = (shape((n // 2,) + block, bf16),) * 2
+    keep, send = call(
+        functools.partial(lora_pack_kernel, bit=2),
+        halves,
         [VMEM] * 3,
         marks[0],
         adapter_model,
         inner,
         nanos=FILL,
     )
-    turned = call(
-        lora_turn_kernel,
-        (shape((NEAR,) + block, bf16),) * far,
-        [VMEM] * (1 + NEAR),
+    keep, send = call(
+        functools.partial(lora_turn_kernel, bit=2, following=1),
+        halves,
+        [VMEM] * 3,
+        marks[1],
+        keep,
+        swap(send, n, 2),
+        nanos=FILL,
+    )
+    spread = call(
+        functools.partial(lora_spread_kernel, bit=1),
+        (shape((NEAR,) + block, bf16),) * (n // NEAR),
+        [VMEM] * 3,
         marks[2],
-        packed[0],
-        swap(hold(packed[1], marks[1]), n, 1),
-        swap(packed[2], n, 2),
-        swap(hold(packed[3], marks[1]), n, 3),
+        keep,
+        swap(send, n, 1),
         nanos=FILL,
     )
-    return turned, False
+    return spread, False
 
 
 def lora_far_start(turned, n, after):
@@ -493,7 +509,8 @@
     keep, send = call(
         functools.partial(attend_kernel, far=far),
         (partial,) * 2,
-        [SMEM] + [VMEM] * 3,
+        [VMEM, SMEM] + [VMEM] * 3,
+        turned[0] if whole else arrived[1],
         lengths,
         near,
         next_near,
@@ -508,7 +525,8 @@
         expert_choice,
         router_probability,
     )
-    theirs, flip, distance, after = swap(send, n, 1), 0, 2, gates
+    theirs, flip, distance = swap(send, n, 1), 0, 2
+    after = gates if whole else arrived[-1]
     while distance < n:
         keep = call(
             functools.partial(merge_kernel, slots=slots, flip=flip),

time: 52.6 us -> 57.3 us (1.089)
  blocking collectives: 9.48 us -> 0 us
  waiting for transfers between devices: 14.1 us -> 22.5 us
  starting transfers between devices: 20 us -> 24.1 us
  local copies, waits for them, and re-layouts: 1.19 us -> 2.2 us
  Pallas kernels: 7.37 us -> 8.01 us
    all_to_all x1 -> x0, blocking collectives: 9.48 us -> none  [body(): lax.all_to_all(out, 'exp', split_axis=0, concat_axis=0, tiled=True)]
    all_to_all x0 -> x1, waiting for transfers between devices: none -> 6.69 us  [body(): lax.all_to_all(out, 'exp', split_axis=0, concat_axis=0, tiled=True)]
    all_to_all x0 -> x1, starting transfers between devices: none -> 3.96 us  [body(): lax.all_to_all(out, 'exp', split_axis=0, concat_axis=0, tiled=True)]
    ppermute x15 -> x14, waiting for transfers between devices: 13.1 us -> 15.8 us  [swap(): return lax.ppermute(value, 'exp', [(t, t ^ distance) for t in range(n)])]
    unnamed x22, local copies, waits for them, and re-layouts: 1.19 us -> 2.2 us
    ppermute x1, waiting for transfers between devices: 0.98 us -> 0.01 us  [lora_join(): lax.ppermute(ordered, 'grp', [(0, 1), (1, 0)])]
    pallas_call x20 -> x19, Pallas kernels: 7.37 us -> 8.01 us  [call(): pl.pallas_call(kernel, out_shape=shapes, in_specs=specs, out_specs=jax.tr...]
    ppermute x15 -> x14, starting transfers between devices: 18.5 us -> 18.6 us  [swap(): return lax.ppermute(value, 'exp', [(t, t ^ distance) for t in range(n)])]
  transfers between devices with their start and end apart: 16 -> 16, of which waited for: 9 -> 7; matrix products, arithmetic and copies ran while one was open for 0% -> 0% of each run, Pallas kernels for 6% -> 5%
where the time goes in v10:
time: 57.3 us; the launch traced here: 57 us
  starting transfers between devices  24.1 us (42%)
  waiting for transfers between devices  22.5 us (39%)
  Pallas kernels  8.01 us (14%)
  local copies, waits for them, and re-layouts  2.2 us (4%)
    ppermute x14, starting transfers between devices, swap(): return lax.ppermute(value, 'exp', [(t, t ^ distance) for t in range(n)])  18.6 us
    ppermute x14, waiting for transfers between devices, swap(): return lax.ppermute(value, 'exp', [(t, t ^ distance) for t in range(n)])  15.8 us
    pallas_call x19, Pallas kernels, call(): pl.pallas_call(kernel, out_shape=shapes, in_specs=specs, out_specs=jax.tr...  8.01 us
    all_to_all x1, waiting for transfers between devices, body(): lax.all_to_all(out, 'exp', split_axis=0, concat_axis=0, tiled=True)  6.69 us
    all_to_all x1, starting transfers between devices, body(): lax.all_to_all(out, 'exp', split_axis=0, concat_axis=0, tiled=True)  3.96 us
    unnamed x22, local copies, waits for them, and re-layouts  2.2 us
    ppermute x1, starting transfers between devices, lora_join(): lax.ppermute(ordered, 'grp', [(0, 1), (1, 0)])  1.56 us
  transfers between devices with their start and end apart: 16, of which 7 were waited for; matrix products, arithmetic and copies ran while one was open for 0% of the time, Pallas kernels for 5%

profile of v10, /device:TPU:0, one launch (start us, length us, event | category | flops | bytes accessed | tf_op | source)
XLA Modules:
  0.0 57.0 jit_solution(12378656381389294930)
XLA Ops:
  0.0 0.8 %shard_map.127.mine.after = bf16[1,32,128]{2,1,0:T(8,128)(2,1)S(1)} custom-call(bf16[1,2048]{1,0:T(2,128)(2,1)} %query.1, bf16[1,2048]{1,0:T(2,128)(2,1)} %resid.1), custom_call_target="tpu_custom_call" | custom-call | flops 4000000000 | tf_op jit(solution)/shard_map/pallas_call | solution.py:38
  0.8 4.1 %collective-permute-start = (bf16[1,32,128]{2,1,0:T(8,128)(2,1)S(1)}, bf16[1,32,128]{2,1,0:T(8,128)(2,1)S(1)}, u32[]{:S(2)}, u32[]{:S(2)}) collective-permute-start(bf16[1,32,128]{2,1,0:T(8,128)(2,1)S(1)} %shard_map.127.mine.after), channel_id=1, source_target_pairs={{0,8},{1,9},{2,10},{3,11},{4,12},{5,13},{6,14},{7,15},{8,0},{9,1},... | collective-permute-start | bytes 24584 | tf_op jit(solution)/shard_map/ppermute | solution.py:72
  4.9 0.1 shard_map.130
  5.0 1.6 %collective-permute-start.2 = (bf16[8,80,128]{2,1,0:T(8,128)(2,1)S(1)}, bf16[8,80,128]{2,1,0:T(8,128)(2,1)S(1)}, u32[]{:S(2)}, u32[]{:S(2)}) collective-permute-start(bf16[8,80,128]{2,1,0:T(8,128)(2,1)S(1)} %get-tuple-element.22), channel_id=1, source_target_pairs={{0,2},{1,3},{2,0},{3,1},{4,6},{5,7},{6,4},{7,5},{8,10},{9,11},{10,... | collective-permute-start | bytes 491528 | tf_op jit(solution)/shard_map/ppermute | solution.py:72
  6.6 0.0 collective-permute-done.theirs
  6.6 1.8 %collective-permute-start.1 = (bf16[2,32,128]{2,1,0:T(8,128)(2,1)S(1)}, bf16[2,32,128]{2,1,0:T(8,128)(2,1)S(1)}, u32[]{:S(2)}, u32[]{:S(2)}) collective-permute-start(bf16[2,32,128]{2,1,0:T(8,128)(2,1)S(1)} %shard_map.128.mine.after), channel_id=1, source_target_pairs={{0,4},{1,5},{2,6},{3,7},{4,0},{5,1},{6,2},{7,3},{8,12},{9,13},{10,... | collective-permute-start | bytes 49160 | tf_op jit(solution)/shard_map/ppermute | solution.py:72
  8.5 2.3 %collective-permute-done.2.got = bf16[8,80,128]{2,1,0:T(8,128)(2,1)S(1)} collective-permute-done((bf16[8,80,128]{2,1,0:T(8,128)(2,1)S(1)}, bf16[8,80,128]{2,1,0:T(8,128)(2,1)S(1)}, u32[]{:S(2)}, u32[]{:S(2)}) %collective-permute-start.2) | collective-permute-done | bytes 163872 | tf_op jit(solution)/shard_map/ppermute | solution.py:72
  10.8 0.0 copy-start.7
  10.8 0.1 collective-permute-start.3
  10.9 0.0 collective-permute-done.1.theirs
  10.9 1.6 %collective-permute-start.4 = (bf16[4,32,128]{2,1,0:T(8,128)(2,1)S(1)}, bf16[4,32,128]{2,1,0:T(8,128)(2,1)S(1)}, u32[]{:S(2)}, u32[]{:S(2)}) collective-permute-start(bf16[4,32,128]{2,1,0:T(8,128)(2,1)S(1)} %shard_map.129.after.mine), channel_id=1, source_target_pairs={{0,2},{1,3},{2,0},{3,1},{4,6},{5,7},{6,4},{7,5},{8,10},{9,11},{10,... | collective-permute-start | bytes 98312 | tf_op jit(solution)/shard_map/ppermute | solution.py:72
  12.5 0.0 collective-permute-done.3.got
  12.5 0.0 copy-start.5
  12.5 0.0 copy-start.8
  12.5 1.6 %collective-permute-start.6 = (bf16[4,80,128]{2,1,0:T(8,128)(2,1)S(1)}, bf16[4,80,128]{2,1,0:T(8,128)(2,1)S(1)}, u32[]{:S(2)}, u32[]{:S(2)}) collective-permute-start(bf16[4,80,128]{2,1,0:T(8,128)(2,1)S(1)} %get-tuple-element.28), channel_id=1, source_target_pairs={{0,4},{1,5},{2,6},{3,7},{4,0},{5,1},{6,2},{7,3},{8,12},{9,13},{10,... | collective-permute-start | bytes 245768 | tf_op jit(solution)/shard_map/ppermute | solution.py:72
  14.2 0.7 %collective-permute-done.4.theirs = bf16[4,32,128]{2,1,0:T(8,128)(2,1)S(1)} collective-permute-done((bf16[4,32,128]{2,1,0:T(8,128)(2,1)S(1)}, bf16[4,32,128]{2,1,0:T(8,128)(2,1)S(1)}, u32[]{:S(2)}, u32[]{:S(2)}) %collective-permute-start.4) | collective-permute-done | bytes 32800 | tf_op jit(solution)/shard_map/ppermute | solution.py:72
  14.9 0.1 collective-permute-start.7
  15.0 2.3 %collective-permute-start.5 = (bf16[4,80,128]{2,1,0:T(8,128)(2,1)S(1)}, bf16[4,80,128]{2,1,0:T(8,128)(2,1)S(1)}, u32[]{:S(2)}, u32[]{:S(2)}) collective-permute-start(bf16[4,80,128]{2,1,0:T(8,128)(2,1)S(1)} %shard_map.134), channel_id=1, source_target_pairs={{0,8},{1,9},{2,10},{3,11},{4,12},{5,13},{6,14},{7,15},{8,0},{9,1},... | collective-permute-start | bytes 245768 | tf_op jit(solution)/shard_map/ppermute | solution.py:72
  17.3 1.2 %shard_map.135 = (bf16[9,16,128]{2,1,0:T(8,128)(2,1)S(1)}, bf16[9,16,128]{2,1,0:T(8,128)(2,1)S(1)}) custom-call(bf16[4,80,128]{2,1,0:T(8,128)(2,1)S(1)} %collective-permute-done.6.after.refs_1_, s32[8]{0:T(128)S(1)} %copy-done.8, bf16[9,16,128]{2,1,0:T(8,128)(2,1)S(1)} %get-tuple-element.27.after.mine, ...), custom_call_target="tpu_custom_call" | custom-call | flops 8000000000 | tf_op jit(solution)/shard_map/pallas_call | solution.py:38
  18.5 0.2 collective-permute-start.8
  18.7 3.8 %collective-permute-done.5.after.refs_2_ = bf16[4,80,128]{2,1,0:T(8,128)(2,1)S(1)} collective-permute-done((bf16[4,80,128]{2,1,0:T(8,128)(2,1)S(1)}, bf16[4,80,128]{2,1,0:T(8,128)(2,1)S(1)}, u32[]{:S(2)}, u32[]{:S(2)}) %collective-permute-start.5) | collective-permute-done | bytes 81952 | tf_op jit(solution)/shard_map/ppermute | solution.py:72
  22.5 0.0 collective-permute-done.8.theirs
  22.5 0.3 shard_map.136.mine.after
  22.8 1.6 %collective-permute-start.9 = (bf16[9,16,128]{2,1,0:T(8,128)(2,1)S(1)}, bf16[9,16,128]{2,1,0:T(8,128)(2,1)S(1)}, u32[]{:S(2)}, u32[]{:S(2)}) collective-permute-start(bf16[9,16,128]{2,1,0:T(8,128)(2,1)S(1)} %shard_map.136.mine.after), channel_id=1, source_target_pairs={{0,2},{1,3},{2,0},{3,1},{4,6},{5,7},{6,4},{7,5},{8,10},{9,11},{10,... | collective-permute-start | bytes 110600 | tf_op jit(solution)/shard_map/ppermute | solution.py:72
  24.4 3.2 %collective-permute-start.10 = (bf16[4,80,128]{2,1,0:T(8,128)(2,1)S(1)}, bf16[4,80,128]{2,1,0:T(8,128)(2,1)S(1)}, u32[]{:S(2)}, u32[]{:S(2)}) collective-permute-start(bf16[4,80,128]{2,1,0:T(8,128)(2,1)S(1)} %shard_map.138), channel_id=1, source_target_pairs={{0,12},{1,13},{2,14},{3,15},{4,8},{5,9},{6,10},{7,11},{8,4},{9,5},... | collective-permute-start | bytes 245768 | tf_op jit(solution)/shard_map/ppermute | solution.py:72
  27.5 0.0 collective-permute-done.9.theirs
  27.5 0.4 shard_map.137.after.mine
  27.9 0.1 collective-permute-start.11
  27.9 3.0 %collective-permute-done.10.refs_3_ = bf16[4,80,128]{2,1,0:T(8,128)(2,1)S(1)} collective-permute-done((bf16[4,80,128]{2,1,0:T(8,128)(2,1)S(1)}, bf16[4,80,128]{2,1,0:T(8,128)(2,1)S(1)}, u32[]{:S(2)}, u32[]{:S(2)}) %collective-permute-start.10) | collective-permute-done | bytes 81952 | tf_op jit(solution)/shard_map/ppermute | solution.py:72
  31.0 1.6 %collective-permute-start.14 = (bf16[16,80,128]{2,1,0:T(8,128)(2,1)S(1)}, bf16[16,80,128]{2,1,0:T(8,128)(2,1)S(1)}, u32[]{:S(2)}, u32[]{:S(2)}) collective-permute-start(bf16[16,80,128]{2,1,0:T(8,128)(2,1)S(1)} %shard_map.139.after.mine), channel_id=1, source_target_pairs={{0,16},{16,0},{1,17},{17,1},{2,18},{18,2},{3,19},{19,3},{4,20},{20... | collective-permute-start | bytes 983048 | tf_op jit(solution)/shard_map/ppermute | solution.py:451
  32.6 0.0 collective-permute-done.11.theirs
  32.6 0.4 shard_map.140.mine
  33.0 0.3 collective-permute-start.12
  33.3 4.9 %collective-permute-done.12.theirs = bf16[9,16,128]{2,1,0:T(8,128)(2,1)S(1)} collective-permute-done((bf16[9,16,128]{2,1,0:T(8,128)(2,1)S(1)}, bf16[9,16,128]{2,1,0:T(8,128)(2,1)S(1)}, u32[]{:S(2)}, u32[]{:S(2)}) %collective-permute-start.12) | collective-permute-done | bytes 36896 | tf_op jit(solution)/shard_map/ppermute | solution.py:72
  38.2 0.4 shard_map.141
  38.6 0.0 copy-start
  38.6 0.1 collective-permute-start.13
  38.7 0.0 collective-permute-done.14.theirs
  38.7 0.1 shard_map.142
  38.8 1.0 %collective-permute-done.13.theirs = bf16[8,16,128]{2,1,0:T(8,128)(2,1)S(1)} collective-permute-done((bf16[8,16,128]{2,1,0:T(8,128)(2,1)S(1)}, bf16[8,16,128]{2,1,0:T(8,128)(2,1)S(1)}, u32[]{:S(2)}, u32[]{:S(2)}) %collective-permute-start.13) | collective-permute-done | bytes 32800 | tf_op jit(solution)/shard_map/ppermute | solution.py:72
  39.9 0.2 copy-done.1
  40.1 1.0 %copy-done.2 = bf16[1,768,2048]{2,1,0:T(8,128)(2,1)S(1)} copy-done((bf16[1,768,2048]{2,1,0:T(8,128)(2,1)S(1)}, bf16[1,768,2048]{2,1,0:T(8,128)(2,1)}, u32[]{:S(2)}) %copy-start.2) | copy-done | bytes 3145752
  41.0 1.0 %copy-done = bf16[1,2048,768]{2,1,0:T(8,128)(2,1)S(1)} copy-done((bf16[1,2048,768]{2,1,0:T(8,128)(2,1)S(1)}, bf16[1,2048,768]{2,1,0:T(8,128)(2,1)}, u32[]{:S(2)}) %copy-start) | copy-done | bytes 3145752
  42.0 3.4 %shard_map.143 = bf16[16,16,128]{2,1,0:T(8,128)(2,1)} custom-call(bf16[8,16,128]{2,1,0:T(8,128)(2,1)S(1)} %get-tuple-element.34.mine, bf16[8,16,128]{2,1,0:T(8,128)(2,1)S(1)} %collective-permute-done.13.theirs, bf16[2048,768]{1,0:T(8,128)(2,1)S(1)} %bitcast.5, bf16[2048,768]{1,0:T(8,128)(2,1)S(1)} %bitcast.6, bf16[768,2048]{1,0:T(8,128)(2,1)S(1)} %bitcast.7, ...), custom_call_target="tpu_custom_call" | custom-call | flops 1600000000 | tf_op jit(solution)/shard_map/pallas_call | solution.py:38
  45.4 4.0 %all-to-all-start = ((bf16[16,16,128]{2,1,0:T(8,128)(2,1)}), bf16[16,16,128]{2,1,0:T(8,128)(2,1)S(1)}, u32[]{:S(2)}, u32[]{:S(2)}) async-start(bf16[16,16,128]{2,1,0:T(8,128)(2,1)} %shard_map.143), calls=%async_computation | async-start | bytes 131072 | tf_op jit(solution)/shard_map/all_to_all | solution.py:578
  49.4 0.2 shard_map.144.gates
  49.6 6.7 %all-to-all-done.got = bf16[16,16,128]{2,1,0:T(8,128)(2,1)S(1)} async-done(((bf16[16,16,128]{2,1,0:T(8,128)(2,1)}), bf16[16,16,128]{2,1,0:T(8,128)(2,1)S(1)}, u32[]{:S(2)}, u32[]{:S(2)}) %all-to-all-start) | async-done | bytes 65568 | tf_op jit(solution)/shard_map/all_to_all | solution.py:578
  56.3 0.7 %shard_map.145 = bf16[1,2048]{1,0:T(2,128)(2,1)} custom-call(f32[16,128]{1,0:T(8,128)S(1)} %get-tuple-element.33.hidden, bf16[16,16,128]{2,1,0:T(8,128)(2,1)S(1)} %all-to-all-done.got, f32[1,128]{1,0:T(1,128)S(1)} %shard_map.144.gates), custom_call_target="tpu_custom_call" | custom-call | flops 1600000000 | tf_op jit(solution)/shard_map/pallas_call | solution.py:38
  (25 shorter events, 0.1 us)
Async XLA Ops:
  0.0 4.9 %copy-start.4 = (bf16[16,96,48]{1,2,0:T(8,128)(2,1)S(1)}, bf16[16,96,48]{1,2,0:T(8,128)(2,1)}, u32[]{:S(2)}) copy-start(bf16[16,96,48]{1,2,0:T(8,128)(2,1)} %param.25) | copy-start | bytes 442372
  0.0 4.9 %copy-start.3 = (bf16[16,96,128]{2,1,0:T(8,128)(2,1)S(1)}, bf16[16,96,128]{2,1,0:T(8,128)(2,1)}, u32[]{:S(2)}) copy-start(bf16[16,96,128]{2,1,0:T(8,128)(2,1)} %model.1) | copy-start | bytes 1179652
  0.8 5.8 %collective-permute-start = (bf16[1,32,128]{2,1,0:T(8,128)(2,1)S(1)}, bf16[1,32,128]{2,1,0:T(8,128)(2,1)S(1)}, u32[]{:S(2)}, u32[]{:S(2)}) collective-permute-start(bf16[1,32,128]{2,1,0:T(8,128)(2,1)S(1)} %shard_map.127.mine.after), channel_id=1, source_target_pairs={{0,8},{1,9},{2,10},{3,11},{4,12},{5,13},{6,14},{7,15},{8,0},{9,1},... | collective-permute-start | bytes 24584 | tf_op jit(solution)/shard_map/ppermute | solution.py:72
  5.0 5.7 %collective-permute-start.2 = (bf16[8,80,128]{2,1,0:T(8,128)(2,1)S(1)}, bf16[8,80,128]{2,1,0:T(8,128)(2,1)S(1)}, u32[]{:S(2)}, u32[]{:S(2)}) collective-permute-start(bf16[8,80,128]{2,1,0:T(8,128)(2,1)S(1)} %get-tuple-element.22), channel_id=1, source_target_pairs={{0,2},{1,3},{2,0},{3,1},{4,6},{5,7},{6,4},{7,5},{8,10},{9,11},{10,... | collective-permute-start | bytes 491528 | tf_op jit(solution)/shard_map/ppermute | solution.py:72
  6.6 4.3 %collective-permute-start.1 = (bf16[2,32,128]{2,1,0:T(8,128)(2,1)S(1)}, bf16[2,32,128]{2,1,0:T(8,128)(2,1)S(1)}, u32[]{:S(2)}, u32[]{:S(2)}) collective-permute-start(bf16[2,32,128]{2,1,0:T(8,128)(2,1)S(1)} %shard_map.128.mine.after), channel_id=1, source_target_pairs={{0,4},{1,5},{2,6},{3,7},{4,0},{5,1},{6,2},{7,3},{8,12},{9,13},{10,... | collective-permute-start | bytes 49160 | tf_op jit(solution)/shard_map/ppermute | solution.py:72
  10.8 4.1 %copy-start.7 = (bf16[1,512]{1,0:T(2,128)(2,1)S(1)}, bf16[1,512]{1,0:T(2,128)(2,1)}, u32[]{:S(2)}) copy-start(bf16[1,512]{1,0:T(2,128)(2,1)} %new.1) | copy-start | bytes 3076
  10.8 1.7 %collective-permute-start.3 = (bf16[8,80,128]{2,1,0:T(8,128)(2,1)S(1)}, bf16[8,80,128]{2,1,0:T(8,128)(2,1)S(1)}, u32[]{:S(2)}, u32[]{:S(2)}) collective-permute-start(bf16[8,80,128]{2,1,0:T(8,128)(2,1)S(1)} %get-tuple-element.24), channel_id=1, source_target_pairs={{0,1},{1,0},{2,3},{3,2},{4,5},{5,4},{6,7},{7,6},{8,9},{9,8},{10,11... | collective-permute-start | bytes 491528 | tf_op jit(solution)/shard_map/ppermute | solution.py:72
  10.9 4.0 %collective-permute-start.4 = (bf16[4,32,128]{2,1,0:T(8,128)(2,1)S(1)}, bf16[4,32,128]{2,1,0:T(8,128)(2,1)S(1)}, u32[]{:S(2)}, u32[]{:S(2)}) collective-permute-start(bf16[4,32,128]{2,1,0:T(8,128)(2,1)S(1)} %shard_map.129.after.mine), channel_id=1, source_target_pairs={{0,2},{1,3},{2,0},{3,1},{4,6},{5,7},{6,4},{7,5},{8,10},{9,11},{10,... | collective-permute-start | bytes 98312 | tf_op jit(solution)/shard_map/ppermute | solution.py:72
  12.5 4.8 %copy-start.5 = (bf16[8,192,512]{2,1,0:T(8,128)(2,1)S(1)}, bf16[8,192,512]{2,1,0:T(8,128)(2,1)}, u32[]{:S(2)}) copy-start(bf16[8,192,512]{2,1,0:T(8,128)(2,1)} %cache.1) | copy-start | bytes 4718596
  12.5 4.8 %copy-start.8 = (s32[8]{0:T(128)S(1)}, s32[8]{0:T(128)}, u32[]{:S(2)}) copy-start(s32[8]{0:T(128)} %lengths.1) | copy-start | bytes 100
  12.5 4.8 %collective-permute-start.6 = (bf16[4,80,128]{2,1,0:T(8,128)(2,1)S(1)}, bf16[4,80,128]{2,1,0:T(8,128)(2,1)S(1)}, u32[]{:S(2)}, u32[]{:S(2)}) collective-permute-start(bf16[4,80,128]{2,1,0:T(8,128)(2,1)S(1)} %get-tuple-element.28), channel_id=1, source_target_pairs={{0,4},{1,5},{2,6},{3,7},{4,0},{5,1},{6,2},{7,3},{8,12},{9,13},{10,... | collective-permute-start | bytes 245768 | tf_op jit(solution)/shard_map/ppermute | solution.py:72
  14.9 2.4 %collective-permute-start.7 = (bf16[9,16,128]{2,1,0:T(8,128)(2,1)S(1)}, bf16[9,16,128]{2,1,0:T(8,128)(2,1)S(1)}, u32[]{:S(2)}, u32[]{:S(2)}) collective-permute-start(bf16[9,16,128]{2,1,0:T(8,128)(2,1)S(1)} %get-tuple-element.27.after.mine), channel_id=1, source_target_pairs={{0,1},{1,0},{2,3},{3,2},{4,5},{5,4},{6,7},{7,6},{8,9},{9,8},{10,11... | collective-permute-start | bytes 110600 | tf_op jit(solution)/shard_map/ppermute | solution.py:72
  15.0 7.5 %collective-permute-start.5 = (bf16[4,80,128]{2,1,0:T(8,128)(2,1)S(1)}, bf16[4,80,128]{2,1,0:T(8,128)(2,1)S(1)}, u32[]{:S(2)}, u32[]{:S(2)}) collective-permute-start(bf16[4,80,128]{2,1,0:T(8,128)(2,1)S(1)} %shard_map.134), channel_id=1, source_target_pairs={{0,8},{1,9},{2,10},{3,11},{4,12},{5,13},{6,14},{7,15},{8,0},{9,1},... | collective-permute-start | bytes 245768 | tf_op jit(solution)/shard_map/ppermute | solution.py:72
  18.5 4.0 %collective-permute-start.8 = (bf16[9,16,128]{2,1,0:T(8,128)(2,1)S(1)}, bf16[9,16,128]{2,1,0:T(8,128)(2,1)S(1)}, u32[]{:S(2)}, u32[]{:S(2)}) collective-permute-start(bf16[9,16,128]{2,1,0:T(8,128)(2,1)S(1)} %get-tuple-element.30), channel_id=1, source_target_pairs={{0,1},{1,0},{2,3},{3,2},{4,5},{5,4},{6,7},{7,6},{8,9},{9,8},{10,11... | collective-permute-start | bytes 110600 | tf_op jit(solution)/shard_map/ppermute | solution.py:72
  22.8 4.7 %collective-permute-start.9 = (bf16[9,16,128]{2,1,0:T(8,128)(2,1)S(1)}, bf16[9,16,128]{2,1,0:T(8,128)(2,1)S(1)}, u32[]{:S(2)}, u32[]{:S(2)}) collective-permute-start(bf16[9,16,128]{2,1,0:T(8,128)(2,1)S(1)} %shard_map.136.mine.after), channel_id=1, source_target_pairs={{0,2},{1,3},{2,0},{3,1},{4,6},{5,7},{6,4},{7,5},{8,10},{9,11},{10,... | collective-permute-start | bytes 110600 | tf_op jit(solution)/shard_map/ppermute | solution.py:72
  24.4 6.6 %collective-permute-start.10 = (bf16[4,80,128]{2,1,0:T(8,128)(2,1)S(1)}, bf16[4,80,128]{2,1,0:T(8,128)(2,1)S(1)}, u32[]{:S(2)}, u32[]{:S(2)}) collective-permute-start(bf16[4,80,128]{2,1,0:T(8,128)(2,1)S(1)} %shard_map.138), channel_id=1, source_target_pairs={{0,12},{1,13},{2,14},{3,15},{4,8},{5,9},{6,10},{7,11},{8,4},{9,5},... | collective-permute-start | bytes 245768 | tf_op jit(solution)/shard_map/ppermute | solution.py:72
  27.9 10.3 %copy-start.6 = (f32[2048]{0:T(1024)S(1)}, f32[2048]{0:T(1024)}, u32[]{:S(2)}) copy-start(f32[2048]{0:T(1024)} %param.18) | copy-start | bytes 24580
  27.9 4.7 %collective-permute-start.11 = (bf16[9,16,128]{2,1,0:T(8,128)(2,1)S(1)}, bf16[9,16,128]{2,1,0:T(8,128)(2,1)S(1)}, u32[]{:S(2)}, u32[]{:S(2)}) collective-permute-start(bf16[9,16,128]{2,1,0:T(8,128)(2,1)S(1)} %shard_map.137.after.mine), channel_id=1, source_target_pairs={{0,4},{1,5},{2,6},{3,7},{4,0},{5,1},{6,2},{7,3},{8,12},{9,13},{10,... | collective-permute-start | bytes 110600 | tf_op jit(solution)/shard_map/ppermute | solution.py:72
  31.0 7.7 %collective-permute-start.14 = (bf16[16,80,128]{2,1,0:T(8,128)(2,1)S(1)}, bf16[16,80,128]{2,1,0:T(8,128)(2,1)S(1)}, u32[]{:S(2)}, u32[]{:S(2)}) collective-permute-start(bf16[16,80,128]{2,1,0:T(8,128)(2,1)S(1)} %shard_map.139.after.mine), channel_id=1, source_target_pairs={{0,16},{16,0},{1,17},{17,1},{2,18},{18,2},{3,19},{19,3},{4,20},{20... | collective-permute-start | bytes 983048 | tf_op jit(solution)/shard_map/ppermute | solution.py:451
  33.0 5.2 %collective-permute-start.12 = (bf16[9,16,128]{2,1,0:T(8,128)(2,1)S(1)}, bf16[9,16,128]{2,1,0:T(8,128)(2,1)S(1)}, u32[]{:S(2)}, u32[]{:S(2)}) collective-permute-start(bf16[9,16,128]{2,1,0:T(8,128)(2,1)S(1)} %shard_map.140.mine), channel_id=1, source_target_pairs={{0,8},{1,9},{2,10},{3,11},{4,12},{5,13},{6,14},{7,15},{8,0},{9,1},... | collective-permute-start | bytes 110600 | tf_op jit(solution)/shard_map/ppermute | solution.py:72
  38.2 1.9 %copy-start.1 = (bf16[1,2048,768]{2,1,0:T(8,128)(2,1)S(1)}, bf16[1,2048,768]{2,1,0:T(8,128)(2,1)}, u32[]{:S(2)}) copy-start(bf16[1,2048,768]{2,1,0:T(8,128)(2,1)} %param.22) | copy-start | bytes 9437188
  38.2 2.8 %copy-start.2 = (bf16[1,768,2048]{2,1,0:T(8,128)(2,1)S(1)}, bf16[1,768,2048]{2,1,0:T(8,128)(2,1)}, u32[]{:S(2)}) copy-start(bf16[1,768,2048]{2,1,0:T(8,128)(2,1)} %param.23) | copy-start | bytes 9437188
  38.6 3.4 %copy-start = (bf16[1,2048,768]{2,1,0:T(8,128)(2,1)S(1)}, bf16[1,2048,768]{2,1,0:T(8,128)(2,1)}, u32[]{:S(2)}) copy-start(bf16[1,2048,768]{2,1,0:T(8,128)(2,1)} %param.21) | copy-start | bytes 9437188
  38.6 1.3 %collective-permute-start.13 = (bf16[8,16,128]{2,1,0:T(8,128)(2,1)S(1)}, bf16[8,16,128]{2,1,0:T(8,128)(2,1)S(1)}, u32[]{:S(2)}, u32[]{:S(2)}) collective-permute-start(bf16[8,16,128]{2,1,0:T(8,128)(2,1)S(1)} %get-tuple-element.34.mine), channel_id=1, source_target_pairs={{0,1},{1,0},{2,3},{3,2},{4,5},{5,4},{6,7},{7,6},{8,9},{9,8},{10,11... | collective-permute-start | bytes 98312 | tf_op jit(solution)/shard_map/ppermute | solution.py:72
  42.0 7.3 %copy-start.9 = (s32[1,8]{1,0:T(1,128)S(1)}, s32[1,8]{1,0:T(1,128)}, u32[]{:S(2)}) copy-start(s32[1,8]{1,0:T(1,128)} %choice.1) | copy-start | bytes 100
  42.0 7.4 %copy-start.10 = (f32[1,8]{1,0:T(1,128)S(1)}, f32[1,8]{1,0:T(1,128)}, u32[]{:S(2)}) copy-start(f32[1,8]{1,0:T(1,128)} %probability.1) | copy-start | bytes 100
  45.4 10.9 %all-to-all-start = ((bf16[16,16,128]{2,1,0:T(8,128)(2,1)}), bf16[16,16,128]{2,1,0:T(8,128)(2,1)S(1)}, u32[]{:S(2)}, u32[]{:S(2)}) async-start(bf16[16,16,128]{2,1,0:T(8,128)(2,1)} %shard_map.143), calls=%async_computation | async-start | bytes 131072 | tf_op jit(solution)/shard_map/all_to_all | solution.py:578

commit v11 on v10

--- a/solution.py
+++ b/solution.py
@@ -23,8 +23,8 @@
 floor_score = -1e30
 epsilon = 1e-06
 FILL = 20
-TOKEN = 1500
-MERGE = 1600
+TOKEN = 800
+MERGE = 2500
 JOIN = 1600
 
 VMEM = pl.BlockSpec(memory_space=pltpu.VMEM)
@@ -526,7 +526,7 @@
         router_probability,
     )
     theirs, flip, distance = swap(send, n, 1), 0, 2
-    after = gates if whole else arrived[-1]
+    after = gates
     while distance < n:
         keep = call(
             functools.partial(merge_kernel, slots=slots, flip=flip),
@@ -538,6 +538,7 @@
             nanos=MERGE,
         )
         if distance == 2 and not whole:
+            after = arrived[-1]
             last = hold(turned[-1], keep)
             arrived.append(swap(last, n, n - NEAR))
         if distance == n // 4:

time: 57.3 us -> 52.8 us (0.921)
  blocking collectives: 0 us -> 11 us
  waiting for transfers between devices: 22.5 us -> 11.8 us
  starting transfers between devices: 24.1 us -> 20.9 us
  local copies, waits for them, and re-layouts: 2.2 us -> 1.3 us
  Pallas kernels: 8.01 us -> 7.38 us
    all_to_all x0 -> x1, blocking collectives: none -> 11 us  [body(): lax.all_to_all(out, 'exp', split_axis=0, concat_axis=0, tiled=True)]
    all_to_all x1 -> x0, waiting for transfers between devices: 6.69 us -> none  [body(): lax.all_to_all(out, 'exp', split_axis=0, concat_axis=0, tiled=True)]
    ppermute x14, waiting for transfers between devices: 15.8 us -> 11 us  [swap(): return lax.ppermute(value, 'exp', [(t, t ^ distance) for t in range(n)])]
    all_to_all x1 -> x0, starting transfers between devices: 3.96 us -> none  [body(): lax.all_to_all(out, 'exp', split_axis=0, concat_axis=0, tiled=True)]
    unnamed x22, local copies, waits for them, and re-layouts: 2.2 us -> 1.3 us
    ppermute x1, waiting for transfers between devices: 0.01 us -> 0.86 us  [lora_join(): lax.ppermute(ordered, 'grp', [(0, 1), (1, 0)])]
    ppermute x14, starting transfers between devices: 18.6 us -> 19.3 us  [swap(): return lax.ppermute(value, 'exp', [(t, t ^ distance) for t in range(n)])]
    pallas_call x19, Pallas kernels: 8.01 us -> 7.38 us  [call(): pl.pallas_call(kernel, out_shape=shapes, in_specs=specs, out_specs=jax.tr...]
  transfers between devices with their start and end apart: 16 -> 15, of which waited for: 7 -> 8; matrix products, arithmetic and copies ran while one was open for 0% -> 0% of each run, Pallas kernels for 5% -> 6%
where the time goes in v11:
time: 52.8 us; the launch traced here: 52.5 us
  starting transfers between devices  20.9 us (40%)
  waiting for transfers between devices  11.8 us (22%)
  blocking collectives  11 us (21%)
  Pallas kernels  7.38 us (14%)
  local copies, waits for them, and re-layouts  1.3 us (2%)
    ppermute x14, starting transfers between devices, swap(): return lax.ppermute(value, 'exp', [(t, t ^ distance) for t in range(n)])  19.3 us
    ppermute x14, waiting for transfers between devices, swap(): return lax.ppermute(value, 'exp', [(t, t ^ distance) for t in range(n)])  11 us
    all_to_all x1, blocking collectives, body(): lax.all_to_all(out, 'exp', split_axis=0, concat_axis=0, tiled=True)  11 us
    pallas_call x19, Pallas kernels, call(): pl.pallas_call(kernel, out_shape=shapes, in_specs=specs, out_specs=jax.tr...  7.38 us
    ppermute x1, starting transfers between devices, lora_join(): lax.ppermute(ordered, 'grp', [(0, 1), (1, 0)])  1.56 us
    unnamed x22, local copies, waits for them, and re-layouts  1.3 us
  transfers between devices with their start and end apart: 15, of which 8 were waited for; matrix products, arithmetic and copies ran while one was open for 0% of the time, Pallas kernels for 6%

profile of v11, /device:TPU:0, one launch (start us, length us, event | category | flops | bytes accessed | tf_op | source)
XLA Modules:
  0.0 52.5 jit_solution(5364974940012433939)
XLA Ops:
  0.0 0.8 %shard_map.127.mine.after = bf16[1,32,128]{2,1,0:T(8,128)(2,1)S(1)} custom-call(bf16[1,2048]{1,0:T(2,128)(2,1)} %query.1, bf16[1,2048]{1,0:T(2,128)(2,1)} %resid.1), custom_call_target="tpu_custom_call" | custom-call | flops 4000000000 | tf_op jit(solution)/shard_map/pallas_call | solution.py:38
  0.8 4.1 %collective-permute-start = (bf16[1,32,128]{2,1,0:T(8,128)(2,1)S(1)}, bf16[1,32,128]{2,1,0:T(8,128)(2,1)S(1)}, u32[]{:S(2)}, u32[]{:S(2)}) collective-permute-start(bf16[1,32,128]{2,1,0:T(8,128)(2,1)S(1)} %shard_map.127.mine.after), channel_id=1, source_target_pairs={{0,8},{1,9},{2,10},{3,11},{4,12},{5,13},{6,14},{7,15},{8,0},{9,1},... | collective-permute-start | bytes 24584 | tf_op jit(solution)/shard_map/ppermute | solution.py:72
  4.9 0.1 shard_map.130
  5.0 1.6 %collective-permute-start.2 = (bf16[8,80,128]{2,1,0:T(8,128)(2,1)S(1)}, bf16[8,80,128]{2,1,0:T(8,128)(2,1)S(1)}, u32[]{:S(2)}, u32[]{:S(2)}) collective-permute-start(bf16[8,80,128]{2,1,0:T(8,128)(2,1)S(1)} %get-tuple-element.22), channel_id=1, source_target_pairs={{0,2},{1,3},{2,0},{3,1},{4,6},{5,7},{6,4},{7,5},{8,10},{9,11},{10,... | collective-permute-start | bytes 491528 | tf_op jit(solution)/shard_map/ppermute | solution.py:72
  6.6 1.8 %collective-permute-start.1 = (bf16[2,32,128]{2,1,0:T(8,128)(2,1)S(1)}, bf16[2,32,128]{2,1,0:T(8,128)(2,1)S(1)}, u32[]{:S(2)}, u32[]{:S(2)}) collective-permute-start(bf16[2,32,128]{2,1,0:T(8,128)(2,1)S(1)} %shard_map.128.mine.after), channel_id=1, source_target_pairs={{0,4},{1,5},{2,6},{3,7},{4,0},{5,1},{6,2},{7,3},{8,12},{9,13},{10,... | collective-permute-start | bytes 49160 | tf_op jit(solution)/shard_map/ppermute | solution.py:72
  8.5 2.3 %collective-permute-done.2.got = bf16[8,80,128]{2,1,0:T(8,128)(2,1)S(1)} collective-permute-done((bf16[8,80,128]{2,1,0:T(8,128)(2,1)S(1)}, bf16[8,80,128]{2,1,0:T(8,128)(2,1)S(1)}, u32[]{:S(2)}, u32[]{:S(2)}) %collective-permute-start.2) | collective-permute-done | bytes 163872 | tf_op jit(solution)/shard_map/ppermute | solution.py:72
  10.8 0.0 copy-start.7
  10.8 0.1 collective-permute-start.3
  10.9 0.0 collective-permute-done.1.theirs
  10.9 1.6 %collective-permute-start.4 = (bf16[4,32,128]{2,1,0:T(8,128)(2,1)S(1)}, bf16[4,32,128]{2,1,0:T(8,128)(2,1)S(1)}, u32[]{:S(2)}, u32[]{:S(2)}) collective-permute-start(bf16[4,32,128]{2,1,0:T(8,128)(2,1)S(1)} %shard_map.129.after.mine), channel_id=1, source_target_pairs={{0,2},{1,3},{2,0},{3,1},{4,6},{5,7},{6,4},{7,5},{8,10},{9,11},{10,... | collective-permute-start | bytes 98312 | tf_op jit(solution)/shard_map/ppermute | solution.py:72
  12.5 0.0 copy-start.5
  12.5 0.0 copy-start.8
  12.5 1.6 %collective-permute-start.6 = (bf16[4,80,128]{2,1,0:T(8,128)(2,1)S(1)}, bf16[4,80,128]{2,1,0:T(8,128)(2,1)S(1)}, u32[]{:S(2)}, u32[]{:S(2)}) collective-permute-start(bf16[4,80,128]{2,1,0:T(8,128)(2,1)S(1)} %get-tuple-element.28), channel_id=1, source_target_pairs={{0,4},{1,5},{2,6},{3,7},{4,0},{5,1},{6,2},{7,3},{8,12},{9,13},{10,... | collective-permute-start | bytes 245768 | tf_op jit(solution)/shard_map/ppermute | solution.py:72
  14.2 0.7 %collective-permute-done.4.theirs = bf16[4,32,128]{2,1,0:T(8,128)(2,1)S(1)} collective-permute-done((bf16[4,32,128]{2,1,0:T(8,128)(2,1)S(1)}, bf16[4,32,128]{2,1,0:T(8,128)(2,1)S(1)}, u32[]{:S(2)}, u32[]{:S(2)}) %collective-permute-start.4) | collective-permute-done | bytes 32800 | tf_op jit(solution)/shard_map/ppermute | solution.py:72
  14.9 0.1 collective-permute-start.7
  15.0 0.0 copy-start.9
  15.0 0.0 copy-start.10
  15.0 2.3 %collective-permute-start.5 = (bf16[4,80,128]{2,1,0:T(8,128)(2,1)S(1)}, bf16[4,80,128]{2,1,0:T(8,128)(2,1)S(1)}, u32[]{:S(2)}, u32[]{:S(2)}) collective-permute-start(bf16[4,80,128]{2,1,0:T(8,128)(2,1)S(1)} %shard_map.134), channel_id=1, source_target_pairs={{0,8},{1,9},{2,10},{3,11},{4,12},{5,13},{6,14},{7,15},{8,0},{9,1},... | collective-permute-start | bytes 245768 | tf_op jit(solution)/shard_map/ppermute | solution.py:72
  17.3 0.0 collective-permute-done.7.theirs
  17.3 0.0 collective-permute-done.6.after.refs_1_
  17.4 1.2 %shard_map.135 = (bf16[9,16,128]{2,1,0:T(8,128)(2,1)S(1)}, bf16[9,16,128]{2,1,0:T(8,128)(2,1)S(1)}) custom-call(bf16[4,80,128]{2,1,0:T(8,128)(2,1)S(1)} %collective-permute-done.6.after.refs_1_, s32[8]{0:T(128)S(1)} %copy-done.8, bf16[9,16,128]{2,1,0:T(8,128)(2,1)S(1)} %get-tuple-element.27.after.mine, ...), custom_call_target="tpu_custom_call" | custom-call | flops 8000000000 | tf_op jit(solution)/shard_map/pallas_call | solution.py:38
  18.5 0.2 collective-permute-start.8
  18.8 0.2 shard_map.136.after.gates
  19.0 0.8 %collective-permute-done.8.theirs = bf16[9,16,128]{2,1,0:T(8,128)(2,1)S(1)} collective-permute-done((bf16[9,16,128]{2,1,0:T(8,128)(2,1)S(1)}, bf16[9,16,128]{2,1,0:T(8,128)(2,1)S(1)}, u32[]{:S(2)}, u32[]{:S(2)}) %collective-permute-start.8) | collective-permute-done | bytes 36896 | tf_op jit(solution)/shard_map/ppermute | solution.py:72
  19.8 0.3 shard_map.137.mine.after
  20.1 1.6 %collective-permute-start.9 = (bf16[9,16,128]{2,1,0:T(8,128)(2,1)S(1)}, bf16[9,16,128]{2,1,0:T(8,128)(2,1)S(1)}, u32[]{:S(2)}, u32[]{:S(2)}) collective-permute-start(bf16[9,16,128]{2,1,0:T(8,128)(2,1)S(1)} %shard_map.137.mine.after), channel_id=1, source_target_pairs={{0,2},{1,3},{2,0},{3,1},{4,6},{5,7},{6,4},{7,5},{8,10},{9,11},{10,... | collective-permute-start | bytes 110600 | tf_op jit(solution)/shard_map/ppermute | solution.py:72
  21.6 2.1 %collective-permute-start.10 = (bf16[4,80,128]{2,1,0:T(8,128)(2,1)S(1)}, bf16[4,80,128]{2,1,0:T(8,128)(2,1)S(1)}, u32[]{:S(2)}, u32[]{:S(2)}) collective-permute-start(bf16[4,80,128]{2,1,0:T(8,128)(2,1)S(1)} %shard_map.139), channel_id=1, source_target_pairs={{0,12},{1,13},{2,14},{3,15},{4,8},{5,9},{6,10},{7,11},{8,4},{9,5},... | collective-permute-start | bytes 245768 | tf_op jit(solution)/shard_map/ppermute | solution.py:72
  23.7 0.0 collective-permute-done.5.after.refs_2_
  23.7 0.3 collective-permute-done.9.theirs
  24.1 0.4 shard_map.138.after.mine
  24.4 1.6 %collective-permute-start.11 = (bf16[9,16,128]{2,1,0:T(8,128)(2,1)S(1)}, bf16[9,16,128]{2,1,0:T(8,128)(2,1)S(1)}, u32[]{:S(2)}, u32[]{:S(2)}) collective-permute-start(bf16[9,16,128]{2,1,0:T(8,128)(2,1)S(1)} %shard_map.138.after.mine), channel_id=1, source_target_pairs={{0,4},{1,5},{2,6},{3,7},{4,0},{5,1},{6,2},{7,3},{8,12},{9,13},{10,... | collective-permute-start | bytes 110600 | tf_op jit(solution)/shard_map/ppermute | solution.py:72
  26.0 2.2 %collective-permute-done.10.refs_3_ = bf16[4,80,128]{2,1,0:T(8,128)(2,1)S(1)} collective-permute-done((bf16[4,80,128]{2,1,0:T(8,128)(2,1)S(1)}, bf16[4,80,128]{2,1,0:T(8,128)(2,1)S(1)}, u32[]{:S(2)}, u32[]{:S(2)}) %collective-permute-start.10) | collective-permute-done | bytes 81952 | tf_op jit(solution)/shard_map/ppermute | solution.py:72
  28.3 0.0 copy-start.6
  28.3 1.6 %collective-permute-start.14 = (bf16[16,80,128]{2,1,0:T(8,128)(2,1)S(1)}, bf16[16,80,128]{2,1,0:T(8,128)(2,1)S(1)}, u32[]{:S(2)}, u32[]{:S(2)}) collective-permute-start(bf16[16,80,128]{2,1,0:T(8,128)(2,1)S(1)} %shard_map.140.after.mine), channel_id=1, source_target_pairs={{0,16},{16,0},{1,17},{17,1},{2,18},{18,2},{3,19},{19,3},{4,20},{20... | collective-permute-start | bytes 983048 | tf_op jit(solution)/shard_map/ppermute | solution.py:451
  29.9 0.4 shard_map.141.mine
  30.3 0.5 collective-permute-start.12
  30.8 4.4 %collective-permute-done.12.theirs = bf16[9,16,128]{2,1,0:T(8,128)(2,1)S(1)} collective-permute-done((bf16[9,16,128]{2,1,0:T(8,128)(2,1)S(1)}, bf16[9,16,128]{2,1,0:T(8,128)(2,1)S(1)}, u32[]{:S(2)}, u32[]{:S(2)}) %collective-permute-start.12) | collective-permute-done | bytes 36896 | tf_op jit(solution)/shard_map/ppermute | solution.py:72
  35.2 0.4 shard_map.142
  35.6 0.0 copy-start
  35.6 0.1 collective-permute-start.13
  35.7 0.9 %collective-permute-done.14.theirs = bf16[16,80,128]{2,1,0:T(8,128)(2,1)S(1)} collective-permute-done((bf16[16,80,128]{2,1,0:T(8,128)(2,1)S(1)}, bf16[16,80,128]{2,1,0:T(8,128)(2,1)S(1)}, u32[]{:S(2)}, u32[]{:S(2)}) %collective-permute-start.14) | collective-permute-done | bytes 327712 | tf_op jit(solution)/shard_map/ppermute | solution.py:451
  36.5 0.1 shard_map.143
  36.7 0.2 collective-permute-done.13.theirs
  36.9 0.2 copy-done.1
  37.1 1.1 %copy-done = bf16[1,2048,768]{2,1,0:T(8,128)(2,1)S(1)} copy-done((bf16[1,2048,768]{2,1,0:T(8,128)(2,1)S(1)}, bf16[1,2048,768]{2,1,0:T(8,128)(2,1)}, u32[]{:S(2)}) %copy-start) | copy-done | bytes 3145752
  38.1 2.8 %shard_map.144 = bf16[16,16,128]{2,1,0:T(8,128)(2,1)S(1)} custom-call(bf16[8,16,128]{2,1,0:T(8,128)(2,1)S(1)} %get-tuple-element.34.mine, bf16[8,16,128]{2,1,0:T(8,128)(2,1)S(1)} %collective-permute-done.13.theirs, bf16[2048,768]{1,0:T(8,128)(2,1)S(1)} %bitcast.5, bf16[2048,768]{1,0:T(8,128)(2,1)S(1)} %bitcast.6, bf16[768,2048]{1,0:T(8,128)(2,1)S(1)} %bitcast.7, ...), custom_call_target="tpu_custom_call" | custom-call | flops 1600000000 | tf_op jit(solution)/shard_map/pallas_call | solution.py:38
  40.9 11.0 %all_to_all.5.got = bf16[16,16,128]{2,1,0:T(8,128)(2,1)S(1)} all-to-all(bf16[16,16,128]{2,1,0:T(8,128)(2,1)S(1)} %shard_map.144), channel_id=1, replica_groups=mesh['grp'=2,'exp'=16] {'exp'}, dimensions={0} | all-to-all | bytes 131072 | tf_op jit(solution)/shard_map/all_to_all | solution.py:579
  51.8 0.7 %shard_map.145 = bf16[1,2048]{1,0:T(2,128)(2,1)} custom-call(f32[16,128]{1,0:T(8,128)S(1)} %get-tuple-element.33.hidden, bf16[16,16,128]{2,1,0:T(8,128)(2,1)S(1)} %all_to_all.5.got, f32[1,128]{1,0:T(1,128)S(1)} %shard_map.136.after.gates), custom_call_target="tpu_custom_call" | custom-call | flops 1600000000 | tf_op jit(solution)/shard_map/pallas_call | solution.py:38
  (24 shorter events, 0.1 us)
Async XLA Ops:
  0.0 4.9 %copy-start.4 = (bf16[16,96,48]{1,2,0:T(8,128)(2,1)S(1)}, bf16[16,96,48]{1,2,0:T(8,128)(2,1)}, u32[]{:S(2)}) copy-start(bf16[16,96,48]{1,2,0:T(8,128)(2,1)} %param.25) | copy-start | bytes 442372
  0.0 4.9 %copy-start.3 = (bf16[16,96,128]{2,1,0:T(8,128)(2,1)S(1)}, bf16[16,96,128]{2,1,0:T(8,128)(2,1)}, u32[]{:S(2)}) copy-start(bf16[16,96,128]{2,1,0:T(8,128)(2,1)} %model.1) | copy-start | bytes 1179652
  0.8 5.8 %collective-permute-start = (bf16[1,32,128]{2,1,0:T(8,128)(2,1)S(1)}, bf16[1,32,128]{2,1,0:T(8,128)(2,1)S(1)}, u32[]{:S(2)}, u32[]{:S(2)}) collective-permute-start(bf16[1,32,128]{2,1,0:T(8,128)(2,1)S(1)} %shard_map.127.mine.after), channel_id=1, source_target_pairs={{0,8},{1,9},{2,10},{3,11},{4,12},{5,13},{6,14},{7,15},{8,0},{9,1},... | collective-permute-start | bytes 24584 | tf_op jit(solution)/shard_map/ppermute | solution.py:72
  5.0 5.7 %collective-permute-start.2 = (bf16[8,80,128]{2,1,0:T(8,128)(2,1)S(1)}, bf16[8,80,128]{2,1,0:T(8,128)(2,1)S(1)}, u32[]{:S(2)}, u32[]{:S(2)}) collective-permute-start(bf16[8,80,128]{2,1,0:T(8,128)(2,1)S(1)} %get-tuple-element.22), channel_id=1, source_target_pairs={{0,2},{1,3},{2,0},{3,1},{4,6},{5,7},{6,4},{7,5},{8,10},{9,11},{10,... | collective-permute-start | bytes 491528 | tf_op jit(solution)/shard_map/ppermute | solution.py:72
  6.6 4.3 %collective-permute-start.1 = (bf16[2,32,128]{2,1,0:T(8,128)(2,1)S(1)}, bf16[2,32,128]{2,1,0:T(8,128)(2,1)S(1)}, u32[]{:S(2)}, u32[]{:S(2)}) collective-permute-start(bf16[2,32,128]{2,1,0:T(8,128)(2,1)S(1)} %shard_map.128.mine.after), channel_id=1, source_target_pairs={{0,4},{1,5},{2,6},{3,7},{4,0},{5,1},{6,2},{7,3},{8,12},{9,13},{10,... | collective-permute-start | bytes 49160 | tf_op jit(solution)/shard_map/ppermute | solution.py:72
  10.8 4.1 %copy-start.7 = (bf16[1,512]{1,0:T(2,128)(2,1)S(1)}, bf16[1,512]{1,0:T(2,128)(2,1)}, u32[]{:S(2)}) copy-start(bf16[1,512]{1,0:T(2,128)(2,1)} %new.1) | copy-start | bytes 3076
  10.8 1.7 %collective-permute-start.3 = (bf16[8,80,128]{2,1,0:T(8,128)(2,1)S(1)}, bf16[8,80,128]{2,1,0:T(8,128)(2,1)S(1)}, u32[]{:S(2)}, u32[]{:S(2)}) collective-permute-start(bf16[8,80,128]{2,1,0:T(8,128)(2,1)S(1)} %get-tuple-element.24), channel_id=1, source_target_pairs={{0,1},{1,0},{2,3},{3,2},{4,5},{5,4},{6,7},{7,6},{8,9},{9,8},{10,11... | collective-permute-start | bytes 491528 | tf_op jit(solution)/shard_map/ppermute | solution.py:72
  10.9 4.0 %collective-permute-start.4 = (bf16[4,32,128]{2,1,0:T(8,128)(2,1)S(1)}, bf16[4,32,128]{2,1,0:T(8,128)(2,1)S(1)}, u32[]{:S(2)}, u32[]{:S(2)}) collective-permute-start(bf16[4,32,128]{2,1,0:T(8,128)(2,1)S(1)} %shard_map.129.after.mine), channel_id=1, source_target_pairs={{0,2},{1,3},{2,0},{3,1},{4,6},{5,7},{6,4},{7,5},{8,10},{9,11},{10,... | collective-permute-start | bytes 98312 | tf_op jit(solution)/shard_map/ppermute | solution.py:72
  12.5 4.8 %copy-start.5 = (bf16[8,192,512]{2,1,0:T(8,128)(2,1)S(1)}, bf16[8,192,512]{2,1,0:T(8,128)(2,1)}, u32[]{:S(2)}) copy-start(bf16[8,192,512]{2,1,0:T(8,128)(2,1)} %cache.1) | copy-start | bytes 4718596
  12.5 4.8 %copy-start.8 = (s32[8]{0:T(128)S(1)}, s32[8]{0:T(128)}, u32[]{:S(2)}) copy-start(s32[8]{0:T(128)} %lengths.1) | copy-start | bytes 100
  12.5 4.8 %collective-permute-start.6 = (bf16[4,80,128]{2,1,0:T(8,128)(2,1)S(1)}, bf16[4,80,128]{2,1,0:T(8,128)(2,1)S(1)}, u32[]{:S(2)}, u32[]{:S(2)}) collective-permute-start(bf16[4,80,128]{2,1,0:T(8,128)(2,1)S(1)} %get-tuple-element.28), channel_id=1, source_target_pairs={{0,4},{1,5},{2,6},{3,7},{4,0},{5,1},{6,2},{7,3},{8,12},{9,13},{10,... | collective-permute-start | bytes 245768 | tf_op jit(solution)/shard_map/ppermute | solution.py:72
  14.9 2.4 %collective-permute-start.7 = (bf16[9,16,128]{2,1,0:T(8,128)(2,1)S(1)}, bf16[9,16,128]{2,1,0:T(8,128)(2,1)S(1)}, u32[]{:S(2)}, u32[]{:S(2)}) collective-permute-start(bf16[9,16,128]{2,1,0:T(8,128)(2,1)S(1)} %get-tuple-element.27.after.mine), channel_id=1, source_target_pairs={{0,1},{1,0},{2,3},{3,2},{4,5},{5,4},{6,7},{7,6},{8,9},{9,8},{10,11... | collective-permute-start | bytes 110600 | tf_op jit(solution)/shard_map/ppermute | solution.py:72
  15.0 3.8 %copy-start.9 = (s32[1,8]{1,0:T(1,128)S(1)}, s32[1,8]{1,0:T(1,128)}, u32[]{:S(2)}) copy-start(s32[1,8]{1,0:T(1,128)} %choice.1) | copy-start | bytes 100
  15.0 3.8 %copy-start.10 = (f32[1,8]{1,0:T(1,128)S(1)}, f32[1,8]{1,0:T(1,128)}, u32[]{:S(2)}) copy-start(f32[1,8]{1,0:T(1,128)} %probability.1) | copy-start | bytes 100
  15.0 8.7 %collective-permute-start.5 = (bf16[4,80,128]{2,1,0:T(8,128)(2,1)S(1)}, bf16[4,80,128]{2,1,0:T(8,128)(2,1)S(1)}, u32[]{:S(2)}, u32[]{:S(2)}) collective-permute-start(bf16[4,80,128]{2,1,0:T(8,128)(2,1)S(1)} %shard_map.134), channel_id=1, source_target_pairs={{0,8},{1,9},{2,10},{3,11},{4,12},{5,13},{6,14},{7,15},{8,0},{9,1},... | collective-permute-start | bytes 245768 | tf_op jit(solution)/shard_map/ppermute | solution.py:72
  18.5 1.3 %collective-permute-start.8 = (bf16[9,16,128]{2,1,0:T(8,128)(2,1)S(1)}, bf16[9,16,128]{2,1,0:T(8,128)(2,1)S(1)}, u32[]{:S(2)}, u32[]{:S(2)}) collective-permute-start(bf16[9,16,128]{2,1,0:T(8,128)(2,1)S(1)} %get-tuple-element.30), channel_id=1, source_target_pairs={{0,1},{1,0},{2,3},{3,2},{4,5},{5,4},{6,7},{7,6},{8,9},{9,8},{10,11... | collective-permute-start | bytes 110600 | tf_op jit(solution)/shard_map/ppermute | solution.py:72
  20.1 4.0 %collective-permute-start.9 = (bf16[9,16,128]{2,1,0:T(8,128)(2,1)S(1)}, bf16[9,16,128]{2,1,0:T(8,128)(2,1)S(1)}, u32[]{:S(2)}, u32[]{:S(2)}) collective-permute-start(bf16[9,16,128]{2,1,0:T(8,128)(2,1)S(1)} %shard_map.137.mine.after), channel_id=1, source_target_pairs={{0,2},{1,3},{2,0},{3,1},{4,6},{5,7},{6,4},{7,5},{8,10},{9,11},{10,... | collective-permute-start | bytes 110600 | tf_op jit(solution)/shard_map/ppermute | solution.py:72
  21.6 6.6 %collective-permute-start.10 = (bf16[4,80,128]{2,1,0:T(8,128)(2,1)S(1)}, bf16[4,80,128]{2,1,0:T(8,128)(2,1)S(1)}, u32[]{:S(2)}, u32[]{:S(2)}) collective-permute-start(bf16[4,80,128]{2,1,0:T(8,128)(2,1)S(1)} %shard_map.139), channel_id=1, source_target_pairs={{0,12},{1,13},{2,14},{3,15},{4,8},{5,9},{6,10},{7,11},{8,4},{9,5},... | collective-permute-start | bytes 245768 | tf_op jit(solution)/shard_map/ppermute | solution.py:72
  24.4 5.5 %collective-permute-start.11 = (bf16[9,16,128]{2,1,0:T(8,128)(2,1)S(1)}, bf16[9,16,128]{2,1,0:T(8,128)(2,1)S(1)}, u32[]{:S(2)}, u32[]{:S(2)}) collective-permute-start(bf16[9,16,128]{2,1,0:T(8,128)(2,1)S(1)} %shard_map.138.after.mine), channel_id=1, source_target_pairs={{0,4},{1,5},{2,6},{3,7},{4,0},{5,1},{6,2},{7,3},{8,12},{9,13},{10,... | collective-permute-start | bytes 110600 | tf_op jit(solution)/shard_map/ppermute | solution.py:72
  28.3 6.9 %copy-start.6 = (f32[2048]{0:T(1024)S(1)}, f32[2048]{0:T(1024)}, u32[]{:S(2)}) copy-start(f32[2048]{0:T(1024)} %param.18) | copy-start | bytes 24580
  28.3 8.2 %collective-permute-start.14 = (bf16[16,80,128]{2,1,0:T(8,128)(2,1)S(1)}, bf16[16,80,128]{2,1,0:T(8,128)(2,1)S(1)}, u32[]{:S(2)}, u32[]{:S(2)}) collective-permute-start(bf16[16,80,128]{2,1,0:T(8,128)(2,1)S(1)} %shard_map.140.after.mine), channel_id=1, source_target_pairs={{0,16},{16,0},{1,17},{17,1},{2,18},{18,2},{3,19},{19,3},{4,20},{20... | collective-permute-start | bytes 983048 | tf_op jit(solution)/shard_map/ppermute | solution.py:451
  29.9 7.0 %copy-start.2 = (bf16[1,768,2048]{2,1,0:T(8,128)(2,1)S(1)}, bf16[1,768,2048]{2,1,0:T(8,128)(2,1)}, u32[]{:S(2)}) copy-start(bf16[1,768,2048]{2,1,0:T(8,128)(2,1)} %param.23) | copy-start | bytes 9437188
  30.3 4.9 %collective-permute-start.12 = (bf16[9,16,128]{2,1,0:T(8,128)(2,1)S(1)}, bf16[9,16,128]{2,1,0:T(8,128)(2,1)S(1)}, u32[]{:S(2)}, u32[]{:S(2)}) collective-permute-start(bf16[9,16,128]{2,1,0:T(8,128)(2,1)S(1)} %shard_map.141.mine), channel_id=1, source_target_pairs={{0,8},{1,9},{2,10},{3,11},{4,12},{5,13},{6,14},{7,15},{8,0},{9,1},... | collective-permute-start | bytes 110600 | tf_op jit(solution)/shard_map/ppermute | solution.py:72
  35.2 1.9 %copy-start.1 = (bf16[1,2048,768]{2,1,0:T(8,128)(2,1)S(1)}, bf16[1,2048,768]{2,1,0:T(8,128)(2,1)}, u32[]{:S(2)}) copy-start(bf16[1,2048,768]{2,1,0:T(8,128)(2,1)} %param.22) | copy-start | bytes 9437188
  35.6 2.5 %copy-start = (bf16[1,2048,768]{2,1,0:T(8,128)(2,1)S(1)}, bf16[1,2048,768]{2,1,0:T(8,128)(2,1)}, u32[]{:S(2)}) copy-start(bf16[1,2048,768]{2,1,0:T(8,128)(2,1)} %param.21) | copy-start | bytes 9437188
  35.6 1.3 %collective-permute-start.13 = (bf16[8,16,128]{2,1,0:T(8,128)(2,1)S(1)}, bf16[8,16,128]{2,1,0:T(8,128)(2,1)S(1)}, u32[]{:S(2)}, u32[]{:S(2)}) collective-permute-start(bf16[8,16,128]{2,1,0:T(8,128)(2,1)S(1)} %get-tuple-element.34.mine), channel_id=1, source_target_pairs={{0,1},{1,0},{2,3},{3,2},{4,5},{5,4},{6,7},{7,6},{8,9},{9,8},{10,11... | collective-permute-start | bytes 98312 | tf_op jit(solution)/shard_map/ppermute | solution.py:72

commit v12 on v11

--- a/solution.py
+++ b/solution.py
@@ -357,26 +357,30 @@
         outs[d // NEAR][d % NEAR] = (got if d & bit else kept)[without(d, bit)]
 
 
-def lora_order_kernel(after, *refs):
-    me = lax.axis_index("exp")
+def lora_gather_kernel(after, *refs):
     got, out = refs[:-1], refs[-1]
     for j, ref in enumerate(got):
-        for l in range(NEAR):
-            out[me ^ (j * NEAR + l)] = ref[l]
-
-
-def lora_join_kernel(mine, theirs, model, inner):
-    first = lax.axis_index("grp") == 0
-    split = model.shape[0] // 2
-    most, width = mine.shape[1] - split, inner.shape[0] // mine.shape[0]
-    for at in range(mine.shape[0]):
-        own, other = mine[at], theirs[at]
-        halves = jnp.where(first, own, other), jnp.where(first, other, own)
-        columns = slice(at * HEAD_WIDTH, (at + 1) * HEAD_WIDTH)
-        model[:split, columns] = halves[0][:split]
-        model[split:, columns] = halves[1][:split]
-        inner[at * width : at * width + most] = halves[0][split:]
-        inner[at * width + most : (at + 1) * width] = halves[1][split : split + width - most]
+        out[j * NEAR : (j + 1) * NEAR] = ref[...]
+
+
+def lora_join_kernel(*refs):
+    me, first = lax.axis_index("exp"), lax.axis_index("grp") == 0
+    pairs, (model, inner) = refs[:-2], refs[-2:]
+    split, d = model.shape[0] // 2, 0
+    most = pairs[0].shape[1] - split
+    total = sum(mine.shape[0] for mine in pairs[::2])
+    width = inner.shape[0] // total
+    for mine, theirs in zip(pairs[::2], pairs[1::2]):
+        for k in range(mine.shape[0]):
+            own, other, at = mine[k], theirs[k], me ^ d
+            halves = jnp.where(first, own, other), jnp.where(first, other, own)
+            columns = pl.ds(pl.multiple_of(at * HEAD_WIDTH, HEAD_WIDTH), HEAD_WIDTH)
+            model[:split, columns] = halves[0][:split]
+            model[split:, columns] = halves[1][:split]
+            start = pl.multiple_of(at * width, 16)
+            inner[pl.ds(start, most)] = halves[0][split:]
+            inner[pl.ds(start + most, width - most)] = halves[1][split : split + width - most]
+            d += 1
 
 
 def lora_near(adapter_model, adapter_hidden, n, marks):
@@ -391,7 +395,7 @@
     block = (ranks // 2 + pad16(inner_width // 2), HEAD_WIDTH)
     halves = (shape((n // 2,) + block, bf16),) * 2
     keep, send = call(
-        functools.partial(lora_pack_kernel, bit=2),
+        functools.partial(lora_pack_kernel, bit=1),
         halves,
         [VMEM] * 3,
         marks[0],
@@ -400,21 +404,21 @@
         nanos=FILL,
     )
     keep, send = call(
-        functools.partial(lora_turn_kernel, bit=2, following=1),
+        functools.partial(lora_turn_kernel, bit=1, following=2),
         halves,
         [VMEM] * 3,
         marks[1],
         keep,
-        swap(send, n, 2),
+        swap(send, n, 1),
         nanos=FILL,
     )
     spread = call(
-        functools.partial(lora_spread_kernel, bit=1),
+        functools.partial(lora_spread_kernel, bit=2),
         (shape((NEAR,) + block, bf16),) * (n // NEAR),
         [VMEM] * 3,
         marks[2],
         keep,
-        swap(send, n, 1),
+        swap(send, n, 2),
         nanos=FILL,
     )
     return spread, False
@@ -427,10 +431,11 @@
     return arrived
 
 
-def lora_order(arrived, n, after):
+def lora_gather(arrived, after):
+    blocks = sum(part.shape[0] for part in arrived)
     return call(
-        lora_order_kernel,
-        shape((n,) + arrived[0].shape[1:], bf16),
+        lora_gather_kernel,
+        shape((blocks,) + arrived[0].shape[1:], bf16),
         [VMEM] * (1 + len(arrived)),
         after,
         *arrived,
@@ -438,17 +443,17 @@
     )
 
 
-def lora_join(ordered, inner_width):
-    n = ordered.shape[0]
+def lora_join(parts, inner_width):
+    pairs = [x for part in parts for x in (part, lax.ppermute(part, "grp", [(0, 1), (1, 0)]))]
+    n = sum(part.shape[0] for part in parts)
     return call(
         lora_join_kernel,
         (
             shape((3 * ADAPTER_RANK, n * HEAD_WIDTH), bf16),
             shape((n * inner_width, HEAD_WIDTH), bf16),
         ),
-        [VMEM] * 2,
-        ordered,
-        lax.ppermute(ordered, "grp", [(0, 1), (1, 0)]),
+        [VMEM] * len(pairs),
+        *pairs,
     )
 
 
@@ -541,12 +546,13 @@
             after = arrived[-1]
             last = hold(turned[-1], keep)
             arrived.append(swap(last, n, n - NEAR))
-        if distance == n // 4:
-            after = turned[0] if whole else lora_order(arrived, n, keep)
+        if distance == n // 4 and not whole:
+            after = lora_gather(arrived[:-1], keep)
+            parts = [after, hold(arrived[-1], after)]
+            after = parts[1]
         theirs = swap(keep, n, distance)
         flip = slots // distance
         distance *= 2
-    ordered = after
     hidden, normed = call(
         token_kernel,
         (shape(HEADS, f32), shape((slots,) + HEADS, bf16)),
@@ -557,7 +563,7 @@
         norm_scale_vector.reshape(HEADS),
         nanos=TOKEN,
     )
-    model, inner = turned if whole else lora_join(ordered, adapter_hidden.shape[2])
+    model, inner = turned if whole else lora_join(parts, adapter_hidden.shape[2])
     out = call(
         functools.partial(expert_kernel, far=far),
         shape((n,) + HEADS, bf16),

time: 52.8 us -> 53.8 us (1.019)
  starting transfers between devices: 20.9 us -> 24.7 us
  waiting for transfers between devices: 11.8 us -> 8.98 us
  local copies, waits for them, and re-layouts: 1.3 us -> 0.28 us
  blocking collectives: 11 us -> 12 us
    ppermute x14, waiting for transfers between devices: 11 us -> 6.98 us  [swap(): return lax.ppermute(value, 'exp', [(t, t ^ distance) for t in range(n)])]
    ppermute x14, starting transfers between devices: 19.3 us -> 21.7 us  [swap(): return lax.ppermute(value, 'exp', [(t, t ^ distance) for t in range(n)])]
    ppermute x1 -> x2, starting transfers between devices: 1.56 us -> 3.05 us  [lora_join(): lax.ppermute(part, 'grp', [(0, 1), (1, 0)])]
    ppermute x1 -> x2, waiting for transfers between devices: 0.86 us -> 1.99 us  [lora_join(): lax.ppermute(part, 'grp', [(0, 1), (1, 0)])]
    unnamed x22, local copies, waits for them, and re-layouts: 1.3 us -> 0.28 us
    all_to_all x1, blocking collectives: 11 us -> 12 us  [body(): lax.all_to_all(out, 'exp', split_axis=0, concat_axis=0, tiled=True)]
    pallas_call x19 -> x20, Pallas kernels: 7.38 us -> 7.41 us  [call(): pl.pallas_call(kernel, out_shape=shapes, in_specs=specs, out_specs=jax.tr...]
  transfers between devices with their start and end apart: 15 -> 16, of which waited for: 8 -> 9; matrix products, arithmetic and copies ran while one was open for 0% -> 0% of each run, Pallas kernels for 6% -> 6%
where the time goes in v12:
time: 53.8 us; the launch traced here: 53.6 us
  starting transfers between devices  24.7 us (46%)
  blocking collectives  12 us (22%)
  waiting for transfers between devices  8.98 us (17%)
  Pallas kernels  7.41 us (14%)
    ppermute x14, starting transfers between devices, swap(): return lax.ppermute(value, 'exp', [(t, t ^ distance) for t in range(n)])  21.7 us
    all_to_all x1, blocking collectives, body(): lax.all_to_all(out, 'exp', split_axis=0, concat_axis=0, tiled=True)  12 us
    pallas_call x20, Pallas kernels, call(): pl.pallas_call(kernel, out_shape=shapes, in_specs=specs, out_specs=jax.tr...  7.41 us
    ppermute x14, waiting for transfers between devices, swap(): return lax.ppermute(value, 'exp', [(t, t ^ distance) for t in range(n)])  6.98 us
    ppermute x2, starting transfers between devices, lora_join(): lax.ppermute(part, 'grp', [(0, 1), (1, 0)])  3.05 us
    ppermute x2, waiting for transfers between devices, lora_join(): lax.ppermute(part, 'grp', [(0, 1), (1, 0)])  1.99 us
  transfers between devices with their start and end apart: 16, of which 9 were waited for; matrix products, arithmetic and copies ran while one was open for 0% of the time, Pallas kernels for 6%

profile of v12, /device:TPU:0, one launch (start us, length us, event | category | flops | bytes accessed | tf_op | source)
XLA Modules:
  0.0 53.6 jit_solution(6993061768721516236)
XLA Ops:
  0.0 0.8 %shard_map.127.mine.after = bf16[1,32,128]{2,1,0:T(8,128)(2,1)S(1)} custom-call(bf16[1,2048]{1,0:T(2,128)(2,1)} %query.1, bf16[1,2048]{1,0:T(2,128)(2,1)} %resid.1), custom_call_target="tpu_custom_call" | custom-call | flops 4000000000 | tf_op jit(solution)/shard_map/pallas_call | solution.py:38
  0.8 4.1 %collective-permute-start = (bf16[1,32,128]{2,1,0:T(8,128)(2,1)S(1)}, bf16[1,32,128]{2,1,0:T(8,128)(2,1)S(1)}, u32[]{:S(2)}, u32[]{:S(2)}) collective-permute-start(bf16[1,32,128]{2,1,0:T(8,128)(2,1)S(1)} %shard_map.127.mine.after), channel_id=1, source_target_pairs={{0,8},{1,9},{2,10},{3,11},{4,12},{5,13},{6,14},{7,15},{8,0},{9,1},... | collective-permute-start | bytes 24584 | tf_op jit(solution)/shard_map/ppermute | solution.py:72
  4.9 0.1 shard_map.130
  5.0 0.1 collective-permute-start.2
  5.1 1.4 %collective-permute-done.theirs = bf16[1,32,128]{2,1,0:T(8,128)(2,1)S(1)} collective-permute-done((bf16[1,32,128]{2,1,0:T(8,128)(2,1)S(1)}, bf16[1,32,128]{2,1,0:T(8,128)(2,1)S(1)}, u32[]{:S(2)}, u32[]{:S(2)}) %collective-permute-start) | collective-permute-done | bytes 8224 | tf_op jit(solution)/shard_map/ppermute | solution.py:72
  6.6 1.9 %collective-permute-start.1 = (bf16[2,32,128]{2,1,0:T(8,128)(2,1)S(1)}, bf16[2,32,128]{2,1,0:T(8,128)(2,1)S(1)}, u32[]{:S(2)}, u32[]{:S(2)}) collective-permute-start(bf16[2,32,128]{2,1,0:T(8,128)(2,1)S(1)} %shard_map.128.mine.after), channel_id=1, source_target_pairs={{0,4},{1,5},{2,6},{3,7},{4,0},{5,1},{6,2},{7,3},{8,12},{9,13},{10,... | collective-permute-start | bytes 49160 | tf_op jit(solution)/shard_map/ppermute | solution.py:72
  8.5 0.0 collective-permute-done.2.got
  8.5 0.0 copy-start.7
  8.5 1.6 %collective-permute-start.3 = (bf16[8,80,128]{2,1,0:T(8,128)(2,1)S(1)}, bf16[8,80,128]{2,1,0:T(8,128)(2,1)S(1)}, u32[]{:S(2)}, u32[]{:S(2)}) collective-permute-start(bf16[8,80,128]{2,1,0:T(8,128)(2,1)S(1)} %get-tuple-element.24), channel_id=1, source_target_pairs={{0,2},{1,3},{2,0},{3,1},{4,6},{5,7},{6,4},{7,5},{8,10},{9,11},{10,... | collective-permute-start | bytes 491528 | tf_op jit(solution)/shard_map/ppermute | solution.py:72
  10.1 0.2 collective-permute-done.1.theirs
  10.3 1.8 %collective-permute-start.5 = (bf16[4,32,128]{2,1,0:T(8,128)(2,1)S(1)}, bf16[4,32,128]{2,1,0:T(8,128)(2,1)S(1)}, u32[]{:S(2)}, u32[]{:S(2)}) collective-permute-start(bf16[4,32,128]{2,1,0:T(8,128)(2,1)S(1)} %shard_map.129.after.mine), channel_id=1, source_target_pairs={{0,2},{1,3},{2,0},{3,1},{4,6},{5,7},{6,4},{7,5},{8,10},{9,11},{10,... | collective-permute-start | bytes 98312 | tf_op jit(solution)/shard_map/ppermute | solution.py:72
  12.1 1.7 %collective-permute-done.3.got = bf16[8,80,128]{2,1,0:T(8,128)(2,1)S(1)} collective-permute-done((bf16[8,80,128]{2,1,0:T(8,128)(2,1)S(1)}, bf16[8,80,128]{2,1,0:T(8,128)(2,1)S(1)}, u32[]{:S(2)}, u32[]{:S(2)}) %collective-permute-start.3) | collective-permute-done | bytes 163872 | tf_op jit(solution)/shard_map/ppermute | solution.py:72
  13.9 0.0 copy-start.5
  13.9 0.0 copy-start.8
  13.9 1.0 %collective-permute-start.4 = (bf16[4,80,128]{2,1,0:T(8,128)(2,1)S(1)}, bf16[4,80,128]{2,1,0:T(8,128)(2,1)S(1)}, u32[]{:S(2)}, u32[]{:S(2)}) collective-permute-start(bf16[4,80,128]{2,1,0:T(8,128)(2,1)S(1)} %get-tuple-element.26), channel_id=1, source_target_pairs={{0,4},{1,5},{2,6},{3,7},{4,0},{5,1},{6,2},{7,3},{8,12},{9,13},{10,... | collective-permute-start | bytes 245768 | tf_op jit(solution)/shard_map/ppermute | solution.py:72
  14.9 0.0 collective-permute-done.5.theirs
  14.9 0.1 collective-permute-start.6
  15.0 0.0 copy-start.9
  15.0 0.0 copy-start.10
  15.0 2.3 %collective-permute-start.9 = (bf16[4,80,128]{2,1,0:T(8,128)(2,1)S(1)}, bf16[4,80,128]{2,1,0:T(8,128)(2,1)S(1)}, u32[]{:S(2)}, u32[]{:S(2)}) collective-permute-start(bf16[4,80,128]{2,1,0:T(8,128)(2,1)S(1)} %shard_map.138), channel_id=1, source_target_pairs={{0,8},{1,9},{2,10},{3,11},{4,12},{5,13},{6,14},{7,15},{8,0},{9,1},... | collective-permute-start | bytes 245768 | tf_op jit(solution)/shard_map/ppermute | solution.py:72
  17.4 1.1 %collective-permute-done.4.after.refs_1_ = bf16[4,80,128]{2,1,0:T(8,128)(2,1)S(1)} collective-permute-done((bf16[4,80,128]{2,1,0:T(8,128)(2,1)S(1)}, bf16[4,80,128]{2,1,0:T(8,128)(2,1)S(1)}, u32[]{:S(2)}, u32[]{:S(2)}) %collective-permute-start.4) | collective-permute-done | bytes 81952 | tf_op jit(solution)/shard_map/ppermute | solution.py:72
  18.4 1.2 %shard_map.134 = (bf16[9,16,128]{2,1,0:T(8,128)(2,1)S(1)}, bf16[9,16,128]{2,1,0:T(8,128)(2,1)S(1)}) custom-call(bf16[4,80,128]{2,1,0:T(8,128)(2,1)S(1)} %collective-permute-done.4.after.refs_1_, s32[8]{0:T(128)S(1)} %copy-done.8, bf16[9,16,128]{2,1,0:T(8,128)(2,1)S(1)} %get-tuple-element.28.mine.after, ...), custom_call_target="tpu_custom_call" | custom-call | flops 8000000000 | tf_op jit(solution)/shard_map/pallas_call | solution.py:38
  19.6 0.0 collective-permute-start.7
  19.7 0.2 shard_map.135.after.gates
  19.9 1.0 %collective-permute-done.7.theirs = bf16[9,16,128]{2,1,0:T(8,128)(2,1)S(1)} collective-permute-done((bf16[9,16,128]{2,1,0:T(8,128)(2,1)S(1)}, bf16[9,16,128]{2,1,0:T(8,128)(2,1)S(1)}, u32[]{:S(2)}, u32[]{:S(2)}) %collective-permute-start.7) | collective-permute-done | bytes 36896 | tf_op jit(solution)/shard_map/ppermute | solution.py:72
  20.9 0.3 shard_map.136.after.mine
  21.2 1.6 %collective-permute-start.10 = (bf16[9,16,128]{2,1,0:T(8,128)(2,1)S(1)}, bf16[9,16,128]{2,1,0:T(8,128)(2,1)S(1)}, u32[]{:S(2)}, u32[]{:S(2)}) collective-permute-start(bf16[9,16,128]{2,1,0:T(8,128)(2,1)S(1)} %shard_map.136.after.mine), channel_id=1, source_target_pairs={{0,2},{1,3},{2,0},{3,1},{4,6},{5,7},{6,4},{7,5},{8,10},{9,11},{10,... | collective-permute-start | bytes 110600 | tf_op jit(solution)/shard_map/ppermute | solution.py:72
  22.7 2.6 %collective-permute-start.8 = (bf16[4,80,128]{2,1,0:T(8,128)(2,1)S(1)}, bf16[4,80,128]{2,1,0:T(8,128)(2,1)S(1)}, u32[]{:S(2)}, u32[]{:S(2)}) collective-permute-start(bf16[4,80,128]{2,1,0:T(8,128)(2,1)S(1)} %shard_map.137), channel_id=1, source_target_pairs={{0,12},{1,13},{2,14},{3,15},{4,8},{5,9},{6,10},{7,11},{8,4},{9,5},... | collective-permute-start | bytes 245768 | tf_op jit(solution)/shard_map/ppermute | solution.py:72
  25.3 0.0 collective-permute-done.10.theirs
  25.3 0.4 shard_map.139.after.mine
  25.7 1.4 %collective-permute-start.11 = (bf16[9,16,128]{2,1,0:T(8,128)(2,1)S(1)}, bf16[9,16,128]{2,1,0:T(8,128)(2,1)S(1)}, u32[]{:S(2)}, u32[]{:S(2)}) collective-permute-start(bf16[9,16,128]{2,1,0:T(8,128)(2,1)S(1)} %shard_map.139.after.mine), channel_id=1, source_target_pairs={{0,4},{1,5},{2,6},{3,7},{4,0},{5,1},{6,2},{7,3},{8,12},{9,13},{10,... | collective-permute-start | bytes 110600 | tf_op jit(solution)/shard_map/ppermute | solution.py:72
  27.0 1.6 %collective-permute-start.14 = (bf16[12,80,128]{2,1,0:T(8,128)(2,1)S(1)}, bf16[12,80,128]{2,1,0:T(8,128)(2,1)S(1)}, u32[]{:S(2)}, u32[]{:S(2)}) collective-permute-start(bf16[12,80,128]{2,1,0:T(8,128)(2,1)S(1)} %shard_map.140.after.refs_0_), channel_id=1, source_target_pairs={{0,16},{16,0},{1,17},{17,1},{2,18},{18,2},{3,19},{19,3},{4,20},{20... | collective-permute-start | bytes 737288 | tf_op jit(solution)/shard_map/ppermute | solution.py:447
  28.6 0.5 collective-permute-done.8.value
  29.1 0.6 %collective-permute-done.11.theirs = bf16[9,16,128]{2,1,0:T(8,128)(2,1)S(1)} collective-permute-done((bf16[9,16,128]{2,1,0:T(8,128)(2,1)S(1)}, bf16[9,16,128]{2,1,0:T(8,128)(2,1)S(1)}, u32[]{:S(2)}, u32[]{:S(2)}) %collective-permute-start.11) | collective-permute-done | bytes 36896 | tf_op jit(solution)/shard_map/ppermute | solution.py:72
  29.7 0.4 shard_map.142.mine
  30.0 3.2 %collective-permute-start.12 = (bf16[9,16,128]{2,1,0:T(8,128)(2,1)S(1)}, bf16[9,16,128]{2,1,0:T(8,128)(2,1)S(1)}, u32[]{:S(2)}, u32[]{:S(2)}) collective-permute-start(bf16[9,16,128]{2,1,0:T(8,128)(2,1)S(1)} %shard_map.142.mine), channel_id=1, source_target_pairs={{0,8},{1,9},{2,10},{3,11},{4,12},{5,13},{6,14},{7,15},{8,0},{9,1},... | collective-permute-start | bytes 110600 | tf_op jit(solution)/shard_map/ppermute | solution.py:72
  33.2 1.5 %collective-permute-start.15 = (bf16[4,80,128]{2,1,0:T(8,128)(2,1)S(1)}, bf16[4,80,128]{2,1,0:T(8,128)(2,1)S(1)}, u32[]{:S(2)}, u32[]{:S(2)}) collective-permute-start(bf16[4,80,128]{2,1,0:T(8,128)(2,1)S(1)} %shard_map.141.after.refs_2_), channel_id=1, source_target_pairs={{0,16},{16,0},{1,17},{17,1},{2,18},{18,2},{3,19},{19,3},{4,20},{20... | collective-permute-start | bytes 245768 | tf_op jit(solution)/shard_map/ppermute | solution.py:447
  34.7 0.4 collective-permute-done.12.theirs
  35.2 0.4 shard_map.143
  35.6 0.0 copy-start
  35.6 0.1 collective-permute-start.13
  35.7 2.0 %collective-permute-done.15.refs_3_ = bf16[4,80,128]{2,1,0:T(8,128)(2,1)S(1)} collective-permute-done((bf16[4,80,128]{2,1,0:T(8,128)(2,1)S(1)}, bf16[4,80,128]{2,1,0:T(8,128)(2,1)S(1)}, u32[]{:S(2)}, u32[]{:S(2)}) %collective-permute-start.15) | collective-permute-done | bytes 81952 | tf_op jit(solution)/shard_map/ppermute | solution.py:447
  37.7 0.2 shard_map.144
  37.9 0.0 collective-permute-done.13.theirs
  37.9 0.2 copy-done
  38.1 2.8 %shard_map.145 = bf16[16,16,128]{2,1,0:T(8,128)(2,1)S(1)} custom-call(bf16[8,16,128]{2,1,0:T(8,128)(2,1)S(1)} %get-tuple-element.34.mine, bf16[8,16,128]{2,1,0:T(8,128)(2,1)S(1)} %collective-permute-done.13.theirs, bf16[2048,768]{1,0:T(8,128)(2,1)S(1)} %bitcast.5, bf16[2048,768]{1,0:T(8,128)(2,1)S(1)} %bitcast.6, bf16[768,2048]{1,0:T(8,128)(2,1)S(1)} %bitcast.7, ...), custom_call_target="tpu_custom_call" | custom-call | flops 1600000000 | tf_op jit(solution)/shard_map/pallas_call | solution.py:38
  40.9 12.0 %all_to_all.5.got = bf16[16,16,128]{2,1,0:T(8,128)(2,1)S(1)} all-to-all(bf16[16,16,128]{2,1,0:T(8,128)(2,1)S(1)} %shard_map.145), channel_id=1, replica_groups=mesh['grp'=2,'exp'=16] {'exp'}, dimensions={0} | all-to-all | bytes 131072 | tf_op jit(solution)/shard_map/all_to_all | solution.py:585
  52.9 0.7 %shard_map.146 = bf16[1,2048]{1,0:T(2,128)(2,1)} custom-call(f32[16,128]{1,0:T(8,128)S(1)} %get-tuple-element.33.hidden, bf16[16,16,128]{2,1,0:T(8,128)(2,1)S(1)} %all_to_all.5.got, f32[1,128]{1,0:T(1,128)S(1)} %shard_map.135.after.gates), custom_call_target="tpu_custom_call" | custom-call | flops 1600000000 | tf_op jit(solution)/shard_map/pallas_call | solution.py:38
  (27 shorter events, 0.1 us)
Async XLA Ops:
  0.0 4.9 %copy-start.4 = (bf16[16,96,48]{1,2,0:T(8,128)(2,1)S(1)}, bf16[16,96,48]{1,2,0:T(8,128)(2,1)}, u32[]{:S(2)}) copy-start(bf16[16,96,48]{1,2,0:T(8,128)(2,1)} %param.25) | copy-start | bytes 442372
  0.0 4.9 %copy-start.3 = (bf16[16,96,128]{2,1,0:T(8,128)(2,1)S(1)}, bf16[16,96,128]{2,1,0:T(8,128)(2,1)}, u32[]{:S(2)}) copy-start(bf16[16,96,128]{2,1,0:T(8,128)(2,1)} %model.1) | copy-start | bytes 1179652
  0.8 5.7 %collective-permute-start = (bf16[1,32,128]{2,1,0:T(8,128)(2,1)S(1)}, bf16[1,32,128]{2,1,0:T(8,128)(2,1)S(1)}, u32[]{:S(2)}, u32[]{:S(2)}) collective-permute-start(bf16[1,32,128]{2,1,0:T(8,128)(2,1)S(1)} %shard_map.127.mine.after), channel_id=1, source_target_pairs={{0,8},{1,9},{2,10},{3,11},{4,12},{5,13},{6,14},{7,15},{8,0},{9,1},... | collective-permute-start | bytes 24584 | tf_op jit(solution)/shard_map/ppermute | solution.py:72
  5.0 3.4 %collective-permute-start.2 = (bf16[8,80,128]{2,1,0:T(8,128)(2,1)S(1)}, bf16[8,80,128]{2,1,0:T(8,128)(2,1)S(1)}, u32[]{:S(2)}, u32[]{:S(2)}) collective-permute-start(bf16[8,80,128]{2,1,0:T(8,128)(2,1)S(1)} %get-tuple-element.22), channel_id=1, source_target_pairs={{0,1},{1,0},{2,3},{3,2},{4,5},{5,4},{6,7},{7,6},{8,9},{9,8},{10,11... | collective-permute-start | bytes 491528 | tf_op jit(solution)/shard_map/ppermute | solution.py:72
  6.6 3.7 %collective-permute-start.1 = (bf16[2,32,128]{2,1,0:T(8,128)(2,1)S(1)}, bf16[2,32,128]{2,1,0:T(8,128)(2,1)S(1)}, u32[]{:S(2)}, u32[]{:S(2)}) collective-permute-start(bf16[2,32,128]{2,1,0:T(8,128)(2,1)S(1)} %shard_map.128.mine.after), channel_id=1, source_target_pairs={{0,4},{1,5},{2,6},{3,7},{4,0},{5,1},{6,2},{7,3},{8,12},{9,13},{10,... | collective-permute-start | bytes 49160 | tf_op jit(solution)/shard_map/ppermute | solution.py:72
  8.5 6.4 %copy-start.7 = (bf16[1,512]{1,0:T(2,128)(2,1)S(1)}, bf16[1,512]{1,0:T(2,128)(2,1)}, u32[]{:S(2)}) copy-start(bf16[1,512]{1,0:T(2,128)(2,1)} %new.1) | copy-start | bytes 3076
  8.5 5.4 %collective-permute-start.3 = (bf16[8,80,128]{2,1,0:T(8,128)(2,1)S(1)}, bf16[8,80,128]{2,1,0:T(8,128)(2,1)S(1)}, u32[]{:S(2)}, u32[]{:S(2)}) collective-permute-start(bf16[8,80,128]{2,1,0:T(8,128)(2,1)S(1)} %get-tuple-element.24), channel_id=1, source_target_pairs={{0,2},{1,3},{2,0},{3,1},{4,6},{5,7},{6,4},{7,5},{8,10},{9,11},{10,... | collective-permute-start | bytes 491528 | tf_op jit(solution)/shard_map/ppermute | solution.py:72
  10.3 4.6 %collective-permute-start.5 = (bf16[4,32,128]{2,1,0:T(8,128)(2,1)S(1)}, bf16[4,32,128]{2,1,0:T(8,128)(2,1)S(1)}, u32[]{:S(2)}, u32[]{:S(2)}) collective-permute-start(bf16[4,32,128]{2,1,0:T(8,128)(2,1)S(1)} %shard_map.129.after.mine), channel_id=1, source_target_pairs={{0,2},{1,3},{2,0},{3,1},{4,6},{5,7},{6,4},{7,5},{8,10},{9,11},{10,... | collective-permute-start | bytes 98312 | tf_op jit(solution)/shard_map/ppermute | solution.py:72
  13.9 4.5 %copy-start.5 = (bf16[8,192,512]{2,1,0:T(8,128)(2,1)S(1)}, bf16[8,192,512]{2,1,0:T(8,128)(2,1)}, u32[]{:S(2)}) copy-start(bf16[8,192,512]{2,1,0:T(8,128)(2,1)} %cache.1) | copy-start | bytes 4718596
  13.9 4.5 %copy-start.8 = (s32[8]{0:T(128)S(1)}, s32[8]{0:T(128)}, u32[]{:S(2)}) copy-start(s32[8]{0:T(128)} %lengths.1) | copy-start | bytes 100
  13.9 4.5 %collective-permute-start.4 = (bf16[4,80,128]{2,1,0:T(8,128)(2,1)S(1)}, bf16[4,80,128]{2,1,0:T(8,128)(2,1)S(1)}, u32[]{:S(2)}, u32[]{:S(2)}) collective-permute-start(bf16[4,80,128]{2,1,0:T(8,128)(2,1)S(1)} %get-tuple-element.26), channel_id=1, source_target_pairs={{0,4},{1,5},{2,6},{3,7},{4,0},{5,1},{6,2},{7,3},{8,12},{9,13},{10,... | collective-permute-start | bytes 245768 | tf_op jit(solution)/shard_map/ppermute | solution.py:72
  14.9 2.4 %collective-permute-start.6 = (bf16[9,16,128]{2,1,0:T(8,128)(2,1)S(1)}, bf16[9,16,128]{2,1,0:T(8,128)(2,1)S(1)}, u32[]{:S(2)}, u32[]{:S(2)}) collective-permute-start(bf16[9,16,128]{2,1,0:T(8,128)(2,1)S(1)} %get-tuple-element.28.mine.after), channel_id=1, source_target_pairs={{0,1},{1,0},{2,3},{3,2},{4,5},{5,4},{6,7},{7,6},{8,9},{9,8},{10,11... | collective-permute-start | bytes 110600 | tf_op jit(solution)/shard_map/ppermute | solution.py:72
  15.0 4.7 %copy-start.9 = (s32[1,8]{1,0:T(1,128)S(1)}, s32[1,8]{1,0:T(1,128)}, u32[]{:S(2)}) copy-start(s32[1,8]{1,0:T(1,128)} %choice.1) | copy-start | bytes 100
  15.0 4.7 %copy-start.10 = (f32[1,8]{1,0:T(1,128)S(1)}, f32[1,8]{1,0:T(1,128)}, u32[]{:S(2)}) copy-start(f32[1,8]{1,0:T(1,128)} %probability.1) | copy-start | bytes 100
  15.0 10.3 %collective-permute-start.9 = (bf16[4,80,128]{2,1,0:T(8,128)(2,1)S(1)}, bf16[4,80,128]{2,1,0:T(8,128)(2,1)S(1)}, u32[]{:S(2)}, u32[]{:S(2)}) collective-permute-start(bf16[4,80,128]{2,1,0:T(8,128)(2,1)S(1)} %shard_map.138), channel_id=1, source_target_pairs={{0,8},{1,9},{2,10},{3,11},{4,12},{5,13},{6,14},{7,15},{8,0},{9,1},... | collective-permute-start | bytes 245768 | tf_op jit(solution)/shard_map/ppermute | solution.py:72
  19.6 1.3 %collective-permute-start.7 = (bf16[9,16,128]{2,1,0:T(8,128)(2,1)S(1)}, bf16[9,16,128]{2,1,0:T(8,128)(2,1)S(1)}, u32[]{:S(2)}, u32[]{:S(2)}) collective-permute-start(bf16[9,16,128]{2,1,0:T(8,128)(2,1)S(1)} %get-tuple-element.30), channel_id=1, source_target_pairs={{0,1},{1,0},{2,3},{3,2},{4,5},{5,4},{6,7},{7,6},{8,9},{9,8},{10,11... | collective-permute-start | bytes 110600 | tf_op jit(solution)/shard_map/ppermute | solution.py:72
  21.2 4.2 %collective-permute-start.10 = (bf16[9,16,128]{2,1,0:T(8,128)(2,1)S(1)}, bf16[9,16,128]{2,1,0:T(8,128)(2,1)S(1)}, u32[]{:S(2)}, u32[]{:S(2)}) collective-permute-start(bf16[9,16,128]{2,1,0:T(8,128)(2,1)S(1)} %shard_map.136.after.mine), channel_id=1, source_target_pairs={{0,2},{1,3},{2,0},{3,1},{4,6},{5,7},{6,4},{7,5},{8,10},{9,11},{10,... | collective-permute-start | bytes 110600 | tf_op jit(solution)/shard_map/ppermute | solution.py:72
  22.7 6.3 %collective-permute-start.8 = (bf16[4,80,128]{2,1,0:T(8,128)(2,1)S(1)}, bf16[4,80,128]{2,1,0:T(8,128)(2,1)S(1)}, u32[]{:S(2)}, u32[]{:S(2)}) collective-permute-start(bf16[4,80,128]{2,1,0:T(8,128)(2,1)S(1)} %shard_map.137), channel_id=1, source_target_pairs={{0,12},{1,13},{2,14},{3,15},{4,8},{5,9},{6,10},{7,11},{8,4},{9,5},... | collective-permute-start | bytes 245768 | tf_op jit(solution)/shard_map/ppermute | solution.py:72
  25.7 4.0 %collective-permute-start.11 = (bf16[9,16,128]{2,1,0:T(8,128)(2,1)S(1)}, bf16[9,16,128]{2,1,0:T(8,128)(2,1)S(1)}, u32[]{:S(2)}, u32[]{:S(2)}) collective-permute-start(bf16[9,16,128]{2,1,0:T(8,128)(2,1)S(1)} %shard_map.139.after.mine), channel_id=1, source_target_pairs={{0,4},{1,5},{2,6},{3,7},{4,0},{5,1},{6,2},{7,3},{8,12},{9,13},{10,... | collective-permute-start | bytes 110600 | tf_op jit(solution)/shard_map/ppermute | solution.py:72
  27.0 10.6 %collective-permute-start.14 = (bf16[12,80,128]{2,1,0:T(8,128)(2,1)S(1)}, bf16[12,80,128]{2,1,0:T(8,128)(2,1)S(1)}, u32[]{:S(2)}, u32[]{:S(2)}) collective-permute-start(bf16[12,80,128]{2,1,0:T(8,128)(2,1)S(1)} %shard_map.140.after.refs_0_), channel_id=1, source_target_pairs={{0,16},{16,0},{1,17},{17,1},{2,18},{18,2},{3,19},{19,3},{4,20},{20... | collective-permute-start | bytes 737288 | tf_op jit(solution)/shard_map/ppermute | solution.py:447
  29.1 6.1 %copy-start.6 = (f32[2048]{0:T(1024)S(1)}, f32[2048]{0:T(1024)}, u32[]{:S(2)}) copy-start(f32[2048]{0:T(1024)} %param.18) | copy-start | bytes 24580
  29.7 8.2 %copy-start.2 = (bf16[1,768,2048]{2,1,0:T(8,128)(2,1)S(1)}, bf16[1,768,2048]{2,1,0:T(8,128)(2,1)}, u32[]{:S(2)}) copy-start(bf16[1,768,2048]{2,1,0:T(8,128)(2,1)} %param.23) | copy-start | bytes 9437188
  30.0 5.1 %collective-permute-start.12 = (bf16[9,16,128]{2,1,0:T(8,128)(2,1)S(1)}, bf16[9,16,128]{2,1,0:T(8,128)(2,1)S(1)}, u32[]{:S(2)}, u32[]{:S(2)}) collective-permute-start(bf16[9,16,128]{2,1,0:T(8,128)(2,1)S(1)} %shard_map.142.mine), channel_id=1, source_target_pairs={{0,8},{1,9},{2,10},{3,11},{4,12},{5,13},{6,14},{7,15},{8,0},{9,1},... | collective-permute-start | bytes 110600 | tf_op jit(solution)/shard_map/ppermute | solution.py:72
  33.2 4.4 %collective-permute-start.15 = (bf16[4,80,128]{2,1,0:T(8,128)(2,1)S(1)}, bf16[4,80,128]{2,1,0:T(8,128)(2,1)S(1)}, u32[]{:S(2)}, u32[]{:S(2)}) collective-permute-start(bf16[4,80,128]{2,1,0:T(8,128)(2,1)S(1)} %shard_map.141.after.refs_2_), channel_id=1, source_target_pairs={{0,16},{16,0},{1,17},{17,1},{2,18},{18,2},{3,19},{19,3},{4,20},{20... | collective-permute-start | bytes 245768 | tf_op jit(solution)/shard_map/ppermute | solution.py:447
  35.2 2.7 %copy-start.1 = (bf16[1,2048,768]{2,1,0:T(8,128)(2,1)S(1)}, bf16[1,2048,768]{2,1,0:T(8,128)(2,1)}, u32[]{:S(2)}) copy-start(bf16[1,2048,768]{2,1,0:T(8,128)(2,1)} %param.22) | copy-start | bytes 9437188
  35.6 2.5 %copy-start = (bf16[1,2048,768]{2,1,0:T(8,128)(2,1)S(1)}, bf16[1,2048,768]{2,1,0:T(8,128)(2,1)}, u32[]{:S(2)}) copy-start(bf16[1,2048,768]{2,1,0:T(8,128)(2,1)} %param.21) | copy-start | bytes 9437188
  35.6 2.3 %collective-permute-start.13 = (bf16[8,16,128]{2,1,0:T(8,128)(2,1)S(1)}, bf16[8,16,128]{2,1,0:T(8,128)(2,1)S(1)}, u32[]{:S(2)}, u32[]{:S(2)}) collective-permute-start(bf16[8,16,128]{2,1,0:T(8,128)(2,1)S(1)} %get-tuple-element.34.mine), channel_id=1, source_target_pairs={{0,1},{1,0},{2,3},{3,2},{4,5},{5,4},{6,7},{7,6},{8,9},{9,8},{10,11... | collective-permute-start | bytes 98312 | tf_op jit(solution)/shard_map/ppermute | solution.py:72

commit v13 on v11

--- a/solution.py
+++ b/solution.py
@@ -22,9 +22,10 @@
 
 floor_score = -1e30
 epsilon = 1e-06
+DOWN_PARTS = 4
 FILL = 20
 TOKEN = 800
-MERGE = 2500
+MERGE = 3500
 JOIN = 1600
 
 VMEM = pl.BlockSpec(memory_space=pltpu.VMEM)
@@ -282,8 +283,17 @@
     return both[: value.shape[0]] + both[value.shape[0] :]
 
 
-def expert_kernel(mine, theirs, gate_w, up_w, down_w, model, inner, out, *, far):
+def expert_kernel(mine, theirs, gate_w, up_w, down_hbm, model, inner, out, down_w, sems, *, far):
     me = lax.axis_index("exp")
+    rows = down_w.shape[0] // DOWN_PARTS
+    copies = [
+        pltpu.make_async_copy(
+            down_hbm.at[pl.ds(k * rows, rows)], down_w.at[pl.ds(k * rows, rows)], sems.at[k]
+        )
+        for k in range(DOWN_PARTS)
+    ]
+    for copy in copies:
+        copy.start()
     half = mine.shape[0]
     x = jnp.concatenate([mine[...].astype(f32), theirs[...].astype(f32)], axis=0)
     x = x.reshape(2 * half, WIDTH).astype(bf16)
@@ -296,6 +306,8 @@
     up = jnp.dot(x, up_w[...], preferred_element_type=f32)
     up = up + dot_pair(mixed[:, r:], inner[:, r : 2 * r], 1)
     act = (gate / (1.0 + jnp.exp(-gate)) * up).astype(bf16)
+    for copy in copies:
+        copy.wait()
     lowered = jnp.dot(act, inner[:, 2 * r : 3 * r], preferred_element_type=f32)
     result = jnp.dot(act, down_w[...], preferred_element_type=f32)
     result = result + dot_pair(lowered, model[2 * r :], 0)
@@ -561,15 +573,19 @@
     out = call(
         functools.partial(expert_kernel, far=far),
         shape((n,) + HEADS, bf16),
-        [VMEM] * 7,
+        [VMEM] * 4 + [HBM] + [VMEM] * 2,
         normed,
         swap(normed, n, 1),
         gate_weight[0],
         up_weight[0],
-        down_weight[0],
+        pltpu.with_memory_space_constraint(down_weight[0], pltpu.HBM),
         model,
         inner,
         limit=32,
+        scratch=[
+            pltpu.VMEM(down_weight.shape[1:], bf16),
+            pltpu.SemaphoreType.DMA((DOWN_PARTS,)),
+        ],
     )
     return call(
         finish_kernel,

time: 52.8 us -> 53.3 us (level)
    unnamed x22 -> x20, local copies, waits for them, and re-layouts: 1.3 us -> 1.3 us
where the time goes in v13:
time: 53.3 us; the launch traced here: 53 us
  starting transfers between devices  20.9 us (39%)
  waiting for transfers between devices  11.8 us (22%)
  blocking collectives  11 us (21%)
  Pallas kernels  7.89 us (15%)
  local copies, waits for them, and re-layouts  1.3 us (2%)
    ppermute x14, starting transfers between devices, swap(): return lax.ppermute(value, 'exp', [(t, t ^ distance) for t in range(n)])  19.3 us
    ppermute x14, waiting for transfers between devices, swap(): return lax.ppermute(value, 'exp', [(t, t ^ distance) for t in range(n)])  11 us
    all_to_all x1, blocking collectives, body(): lax.all_to_all(out, 'exp', split_axis=0, concat_axis=0, tiled=True)  11 us
    pallas_call x19, Pallas kernels, call(): pl.pallas_call(kernel, out_shape=shapes, in_specs=specs, out_specs=jax.tr...  7.89 us
    ppermute x1, starting transfers between devices, lora_join(): lax.ppermute(ordered, 'grp', [(0, 1), (1, 0)])  1.56 us
    unnamed x20, local copies, waits for them, and re-layouts  1.3 us
  transfers between devices with their start and end apart: 15, of which 8 were waited for; matrix products, arithmetic and copies ran while one was open for 0% of the time, Pallas kernels for 6%

profile of v13, /device:TPU:0, one launch (start us, length us, event | category | flops | bytes accessed | tf_op | source)
XLA Modules:
  0.0 53.0 jit_solution(12262821293347355484)
XLA Ops:
  0.0 0.8 %shard_map.127.mine.after = bf16[1,32,128]{2,1,0:T(8,128)(2,1)S(1)} custom-call(bf16[1,2048]{1,0:T(2,128)(2,1)} %query.1, bf16[1,2048]{1,0:T(2,128)(2,1)} %resid.1), custom_call_target="tpu_custom_call" | custom-call | flops 4000000000 | tf_op jit(solution)/shard_map/pallas_call | solution.py:39
  0.8 4.1 %collective-permute-start = (bf16[1,32,128]{2,1,0:T(8,128)(2,1)S(1)}, bf16[1,32,128]{2,1,0:T(8,128)(2,1)S(1)}, u32[]{:S(2)}, u32[]{:S(2)}) collective-permute-start(bf16[1,32,128]{2,1,0:T(8,128)(2,1)S(1)} %shard_map.127.mine.after), channel_id=1, source_target_pairs={{0,8},{1,9},{2,10},{3,11},{4,12},{5,13},{6,14},{7,15},{8,0},{9,1},... | collective-permute-start | bytes 24584 | tf_op jit(solution)/shard_map/ppermute | solution.py:73
  4.9 0.1 shard_map.130
  5.0 1.6 %collective-permute-start.2 = (bf16[8,80,128]{2,1,0:T(8,128)(2,1)S(1)}, bf16[8,80,128]{2,1,0:T(8,128)(2,1)S(1)}, u32[]{:S(2)}, u32[]{:S(2)}) collective-permute-start(bf16[8,80,128]{2,1,0:T(8,128)(2,1)S(1)} %get-tuple-element.22), channel_id=1, source_target_pairs={{0,2},{1,3},{2,0},{3,1},{4,6},{5,7},{6,4},{7,5},{8,10},{9,11},{10,... | collective-permute-start | bytes 491528 | tf_op jit(solution)/shard_map/ppermute | solution.py:73
  6.6 1.8 %collective-permute-start.1 = (bf16[2,32,128]{2,1,0:T(8,128)(2,1)S(1)}, bf16[2,32,128]{2,1,0:T(8,128)(2,1)S(1)}, u32[]{:S(2)}, u32[]{:S(2)}) collective-permute-start(bf16[2,32,128]{2,1,0:T(8,128)(2,1)S(1)} %shard_map.128.mine.after), channel_id=1, source_target_pairs={{0,4},{1,5},{2,6},{3,7},{4,0},{5,1},{6,2},{7,3},{8,12},{9,13},{10,... | collective-permute-start | bytes 49160 | tf_op jit(solution)/shard_map/ppermute | solution.py:73
  8.5 2.3 %collective-permute-done.2.got = bf16[8,80,128]{2,1,0:T(8,128)(2,1)S(1)} collective-permute-done((bf16[8,80,128]{2,1,0:T(8,128)(2,1)S(1)}, bf16[8,80,128]{2,1,0:T(8,128)(2,1)S(1)}, u32[]{:S(2)}, u32[]{:S(2)}) %collective-permute-start.2) | collective-permute-done | bytes 163872 | tf_op jit(solution)/shard_map/ppermute | solution.py:73
  10.8 0.0 copy-start.6
  10.8 0.1 collective-permute-start.3
  10.9 0.0 collective-permute-done.1.theirs
  10.9 1.6 %collective-permute-start.4 = (bf16[4,32,128]{2,1,0:T(8,128)(2,1)S(1)}, bf16[4,32,128]{2,1,0:T(8,128)(2,1)S(1)}, u32[]{:S(2)}, u32[]{:S(2)}) collective-permute-start(bf16[4,32,128]{2,1,0:T(8,128)(2,1)S(1)} %shard_map.129.after.mine), channel_id=1, source_target_pairs={{0,2},{1,3},{2,0},{3,1},{4,6},{5,7},{6,4},{7,5},{8,10},{9,11},{10,... | collective-permute-start | bytes 98312 | tf_op jit(solution)/shard_map/ppermute | solution.py:73
  12.5 0.0 copy-start.4
  12.5 0.0 copy-start.7
  12.5 1.6 %collective-permute-start.6 = (bf16[4,80,128]{2,1,0:T(8,128)(2,1)S(1)}, bf16[4,80,128]{2,1,0:T(8,128)(2,1)S(1)}, u32[]{:S(2)}, u32[]{:S(2)}) collective-permute-start(bf16[4,80,128]{2,1,0:T(8,128)(2,1)S(1)} %get-tuple-element.28), channel_id=1, source_target_pairs={{0,4},{1,5},{2,6},{3,7},{4,0},{5,1},{6,2},{7,3},{8,12},{9,13},{10,... | collective-permute-start | bytes 245768 | tf_op jit(solution)/shard_map/ppermute | solution.py:73
  14.2 0.7 %collective-permute-done.4.theirs = bf16[4,32,128]{2,1,0:T(8,128)(2,1)S(1)} collective-permute-done((bf16[4,32,128]{2,1,0:T(8,128)(2,1)S(1)}, bf16[4,32,128]{2,1,0:T(8,128)(2,1)S(1)}, u32[]{:S(2)}, u32[]{:S(2)}) %collective-permute-start.4) | collective-permute-done | bytes 32800 | tf_op jit(solution)/shard_map/ppermute | solution.py:73
  14.9 0.1 collective-permute-start.7
  15.0 0.0 copy-start.8
  15.0 0.0 copy-start.9
  15.0 2.3 %collective-permute-start.5 = (bf16[4,80,128]{2,1,0:T(8,128)(2,1)S(1)}, bf16[4,80,128]{2,1,0:T(8,128)(2,1)S(1)}, u32[]{:S(2)}, u32[]{:S(2)}) collective-permute-start(bf16[4,80,128]{2,1,0:T(8,128)(2,1)S(1)} %shard_map.134), channel_id=1, source_target_pairs={{0,8},{1,9},{2,10},{3,11},{4,12},{5,13},{6,14},{7,15},{8,0},{9,1},... | collective-permute-start | bytes 245768 | tf_op jit(solution)/shard_map/ppermute | solution.py:73
  17.3 0.0 collective-permute-done.7.theirs
  17.3 0.0 collective-permute-done.6.after.refs_1_
  17.4 1.2 %shard_map.135 = (bf16[9,16,128]{2,1,0:T(8,128)(2,1)S(1)}, bf16[9,16,128]{2,1,0:T(8,128)(2,1)S(1)}) custom-call(bf16[4,80,128]{2,1,0:T(8,128)(2,1)S(1)} %collective-permute-done.6.after.refs_1_, s32[8]{0:T(128)S(1)} %copy-done.7, bf16[9,16,128]{2,1,0:T(8,128)(2,1)S(1)} %get-tuple-element.27.after.mine, ...), custom_call_target="tpu_custom_call" | custom-call | flops 8000000000 | tf_op jit(solution)/shard_map/pallas_call | solution.py:39
  18.5 0.2 collective-permute-start.8
  18.8 0.2 shard_map.136.after.gates
  19.0 0.8 %collective-permute-done.8.theirs = bf16[9,16,128]{2,1,0:T(8,128)(2,1)S(1)} collective-permute-done((bf16[9,16,128]{2,1,0:T(8,128)(2,1)S(1)}, bf16[9,16,128]{2,1,0:T(8,128)(2,1)S(1)}, u32[]{:S(2)}, u32[]{:S(2)}) %collective-permute-start.8) | collective-permute-done | bytes 36896 | tf_op jit(solution)/shard_map/ppermute | solution.py:73
  19.8 0.3 shard_map.137.mine.after
  20.1 1.6 %collective-permute-start.9 = (bf16[9,16,128]{2,1,0:T(8,128)(2,1)S(1)}, bf16[9,16,128]{2,1,0:T(8,128)(2,1)S(1)}, u32[]{:S(2)}, u32[]{:S(2)}) collective-permute-start(bf16[9,16,128]{2,1,0:T(8,128)(2,1)S(1)} %shard_map.137.mine.after), channel_id=1, source_target_pairs={{0,2},{1,3},{2,0},{3,1},{4,6},{5,7},{6,4},{7,5},{8,10},{9,11},{10,... | collective-permute-start | bytes 110600 | tf_op jit(solution)/shard_map/ppermute | solution.py:73
  21.6 2.1 %collective-permute-start.10 = (bf16[4,80,128]{2,1,0:T(8,128)(2,1)S(1)}, bf16[4,80,128]{2,1,0:T(8,128)(2,1)S(1)}, u32[]{:S(2)}, u32[]{:S(2)}) collective-permute-start(bf16[4,80,128]{2,1,0:T(8,128)(2,1)S(1)} %shard_map.139), channel_id=1, source_target_pairs={{0,12},{1,13},{2,14},{3,15},{4,8},{5,9},{6,10},{7,11},{8,4},{9,5},... | collective-permute-start | bytes 245768 | tf_op jit(solution)/shard_map/ppermute | solution.py:73
  23.7 0.0 collective-permute-done.5.after.refs_2_
  23.7 0.3 collective-permute-done.9.theirs
  24.1 0.4 shard_map.138.after.mine
  24.4 1.6 %collective-permute-start.11 = (bf16[9,16,128]{2,1,0:T(8,128)(2,1)S(1)}, bf16[9,16,128]{2,1,0:T(8,128)(2,1)S(1)}, u32[]{:S(2)}, u32[]{:S(2)}) collective-permute-start(bf16[9,16,128]{2,1,0:T(8,128)(2,1)S(1)} %shard_map.138.after.mine), channel_id=1, source_target_pairs={{0,4},{1,5},{2,6},{3,7},{4,0},{5,1},{6,2},{7,3},{8,12},{9,13},{10,... | collective-permute-start | bytes 110600 | tf_op jit(solution)/shard_map/ppermute | solution.py:73
  26.0 2.2 %collective-permute-done.10.refs_3_ = bf16[4,80,128]{2,1,0:T(8,128)(2,1)S(1)} collective-permute-done((bf16[4,80,128]{2,1,0:T(8,128)(2,1)S(1)}, bf16[4,80,128]{2,1,0:T(8,128)(2,1)S(1)}, u32[]{:S(2)}, u32[]{:S(2)}) %collective-permute-start.10) | collective-permute-done | bytes 81952 | tf_op jit(solution)/shard_map/ppermute | solution.py:73
  28.3 0.0 copy-start.5
  28.3 1.6 %collective-permute-start.14 = (bf16[16,80,128]{2,1,0:T(8,128)(2,1)S(1)}, bf16[16,80,128]{2,1,0:T(8,128)(2,1)S(1)}, u32[]{:S(2)}, u32[]{:S(2)}) collective-permute-start(bf16[16,80,128]{2,1,0:T(8,128)(2,1)S(1)} %shard_map.140.after.mine), channel_id=1, source_target_pairs={{0,16},{16,0},{1,17},{17,1},{2,18},{18,2},{3,19},{19,3},{4,20},{20... | collective-permute-start | bytes 983048 | tf_op jit(solution)/shard_map/ppermute | solution.py:463
  29.9 0.4 shard_map.141.mine
  30.3 0.5 collective-permute-start.12
  30.8 4.4 %collective-permute-done.12.theirs = bf16[9,16,128]{2,1,0:T(8,128)(2,1)S(1)} collective-permute-done((bf16[9,16,128]{2,1,0:T(8,128)(2,1)S(1)}, bf16[9,16,128]{2,1,0:T(8,128)(2,1)S(1)}, u32[]{:S(2)}, u32[]{:S(2)}) %collective-permute-start.12) | collective-permute-done | bytes 36896 | tf_op jit(solution)/shard_map/ppermute | solution.py:73
  35.2 0.4 shard_map.142
  35.6 0.0 copy-start
  35.6 0.1 collective-permute-start.13
  35.7 0.9 %collective-permute-done.14.theirs = bf16[16,80,128]{2,1,0:T(8,128)(2,1)S(1)} collective-permute-done((bf16[16,80,128]{2,1,0:T(8,128)(2,1)S(1)}, bf16[16,80,128]{2,1,0:T(8,128)(2,1)S(1)}, u32[]{:S(2)}, u32[]{:S(2)}) %collective-permute-start.14) | collective-permute-done | bytes 327712 | tf_op jit(solution)/shard_map/ppermute | solution.py:463
  36.5 0.1 shard_map.143
  36.7 0.2 collective-permute-done.13.theirs
  36.9 0.2 copy-done.1
  37.1 1.1 %copy-done = bf16[1,2048,768]{2,1,0:T(8,128)(2,1)S(1)} copy-done((bf16[1,2048,768]{2,1,0:T(8,128)(2,1)S(1)}, bf16[1,2048,768]{2,1,0:T(8,128)(2,1)}, u32[]{:S(2)}) %copy-start) | copy-done | bytes 3145752
  38.1 3.3 %shard_map.144 = bf16[16,16,128]{2,1,0:T(8,128)(2,1)S(1)} custom-call(bf16[8,16,128]{2,1,0:T(8,128)(2,1)S(1)} %get-tuple-element.34.mine, bf16[8,16,128]{2,1,0:T(8,128)(2,1)S(1)} %collective-permute-done.13.theirs, bf16[2048,768]{1,0:T(8,128)(2,1)S(1)} %bitcast.5, bf16[2048,768]{1,0:T(8,128)(2,1)S(1)} %bitcast.6, bf16[768,2048]{1,0:T(8,128)(2,1)} %bitcast.9, ...), custom_call_target="tpu_custom_call" | custom-call | flops 1600000000 | tf_op jit(solution)/shard_map/pallas_call | solution.py:39
  41.4 11.0 %all_to_all.5.got = bf16[16,16,128]{2,1,0:T(8,128)(2,1)S(1)} all-to-all(bf16[16,16,128]{2,1,0:T(8,128)(2,1)S(1)} %shard_map.144), channel_id=1, replica_groups=mesh['grp'=2,'exp'=16] {'exp'}, dimensions={0} | all-to-all | bytes 131072 | tf_op jit(solution)/shard_map/all_to_all | solution.py:595
  52.3 0.7 %shard_map.145 = bf16[1,2048]{1,0:T(2,128)(2,1)} custom-call(f32[16,128]{1,0:T(8,128)S(1)} %get-tuple-element.33.hidden, bf16[16,16,128]{2,1,0:T(8,128)(2,1)S(1)} %all_to_all.5.got, f32[1,128]{1,0:T(1,128)S(1)} %shard_map.136.after.gates), custom_call_target="tpu_custom_call" | custom-call | flops 1600000000 | tf_op jit(solution)/shard_map/pallas_call | solution.py:39
  (22 shorter events, 0.1 us)
Async XLA Ops:
  0.0 4.9 %copy-start.3 = (bf16[16,96,48]{1,2,0:T(8,128)(2,1)S(1)}, bf16[16,96,48]{1,2,0:T(8,128)(2,1)}, u32[]{:S(2)}) copy-start(bf16[16,96,48]{1,2,0:T(8,128)(2,1)} %param.25) | copy-start | bytes 442372
  0.0 4.9 %copy-start.2 = (bf16[16,96,128]{2,1,0:T(8,128)(2,1)S(1)}, bf16[16,96,128]{2,1,0:T(8,128)(2,1)}, u32[]{:S(2)}) copy-start(bf16[16,96,128]{2,1,0:T(8,128)(2,1)} %model.1) | copy-start | bytes 1179652
  0.8 5.8 %collective-permute-start = (bf16[1,32,128]{2,1,0:T(8,128)(2,1)S(1)}, bf16[1,32,128]{2,1,0:T(8,128)(2,1)S(1)}, u32[]{:S(2)}, u32[]{:S(2)}) collective-permute-start(bf16[1,32,128]{2,1,0:T(8,128)(2,1)S(1)} %shard_map.127.mine.after), channel_id=1, source_target_pairs={{0,8},{1,9},{2,10},{3,11},{4,12},{5,13},{6,14},{7,15},{8,0},{9,1},... | collective-permute-start | bytes 24584 | tf_op jit(solution)/shard_map/ppermute | solution.py:73
  5.0 5.7 %collective-permute-start.2 = (bf16[8,80,128]{2,1,0:T(8,128)(2,1)S(1)}, bf16[8,80,128]{2,1,0:T(8,128)(2,1)S(1)}, u32[]{:S(2)}, u32[]{:S(2)}) collective-permute-start(bf16[8,80,128]{2,1,0:T(8,128)(2,1)S(1)} %get-tuple-element.22), channel_id=1, source_target_pairs={{0,2},{1,3},{2,0},{3,1},{4,6},{5,7},{6,4},{7,5},{8,10},{9,11},{10,... | collective-permute-start | bytes 491528 | tf_op jit(solution)/shard_map/ppermute | solution.py:73
  6.6 4.3 %collective-permute-start.1 = (bf16[2,32,128]{2,1,0:T(8,128)(2,1)S(1)}, bf16[2,32,128]{2,1,0:T(8,128)(2,1)S(1)}, u32[]{:S(2)}, u32[]{:S(2)}) collective-permute-start(bf16[2,32,128]{2,1,0:T(8,128)(2,1)S(1)} %shard_map.128.mine.after), channel_id=1, source_target_pairs={{0,4},{1,5},{2,6},{3,7},{4,0},{5,1},{6,2},{7,3},{8,12},{9,13},{10,... | collective-permute-start | bytes 49160 | tf_op jit(solution)/shard_map/ppermute | solution.py:73
  10.8 4.1 %copy-start.6 = (bf16[1,512]{1,0:T(2,128)(2,1)S(1)}, bf16[1,512]{1,0:T(2,128)(2,1)}, u32[]{:S(2)}) copy-start(bf16[1,512]{1,0:T(2,128)(2,1)} %new.1) | copy-start | bytes 3076
  10.8 1.7 %collective-permute-start.3 = (bf16[8,80,128]{2,1,0:T(8,128)(2,1)S(1)}, bf16[8,80,128]{2,1,0:T(8,128)(2,1)S(1)}, u32[]{:S(2)}, u32[]{:S(2)}) collective-permute-start(bf16[8,80,128]{2,1,0:T(8,128)(2,1)S(1)} %get-tuple-element.24), channel_id=1, source_target_pairs={{0,1},{1,0},{2,3},{3,2},{4,5},{5,4},{6,7},{7,6},{8,9},{9,8},{10,11... | collective-permute-start | bytes 491528 | tf_op jit(solution)/shard_map/ppermute | solution.py:73
  10.9 4.0 %collective-permute-start.4 = (bf16[4,32,128]{2,1,0:T(8,128)(2,1)S(1)}, bf16[4,32,128]{2,1,0:T(8,128)(2,1)S(1)}, u32[]{:S(2)}, u32[]{:S(2)}) collective-permute-start(bf16[4,32,128]{2,1,0:T(8,128)(2,1)S(1)} %shard_map.129.after.mine), channel_id=1, source_target_pairs={{0,2},{1,3},{2,0},{3,1},{4,6},{5,7},{6,4},{7,5},{8,10},{9,11},{10,... | collective-permute-start | bytes 98312 | tf_op jit(solution)/shard_map/ppermute | solution.py:73
  12.5 4.8 %copy-start.4 = (bf16[8,192,512]{2,1,0:T(8,128)(2,1)S(1)}, bf16[8,192,512]{2,1,0:T(8,128)(2,1)}, u32[]{:S(2)}) copy-start(bf16[8,192,512]{2,1,0:T(8,128)(2,1)} %cache.1) | copy-start | bytes 4718596
  12.5 4.8 %copy-start.7 = (s32[8]{0:T(128)S(1)}, s32[8]{0:T(128)}, u32[]{:S(2)}) copy-start(s32[8]{0:T(128)} %lengths.1) | copy-start | bytes 100
  12.5 4.8 %collective-permute-start.6 = (bf16[4,80,128]{2,1,0:T(8,128)(2,1)S(1)}, bf16[4,80,128]{2,1,0:T(8,128)(2,1)S(1)}, u32[]{:S(2)}, u32[]{:S(2)}) collective-permute-start(bf16[4,80,128]{2,1,0:T(8,128)(2,1)S(1)} %get-tuple-element.28), channel_id=1, source_target_pairs={{0,4},{1,5},{2,6},{3,7},{4,0},{5,1},{6,2},{7,3},{8,12},{9,13},{10,... | collective-permute-start | bytes 245768 | tf_op jit(solution)/shard_map/ppermute | solution.py:73
  14.9 2.4 %collective-permute-start.7 = (bf16[9,16,128]{2,1,0:T(8,128)(2,1)S(1)}, bf16[9,16,128]{2,1,0:T(8,128)(2,1)S(1)}, u32[]{:S(2)}, u32[]{:S(2)}) collective-permute-start(bf16[9,16,128]{2,1,0:T(8,128)(2,1)S(1)} %get-tuple-element.27.after.mine), channel_id=1, source_target_pairs={{0,1},{1,0},{2,3},{3,2},{4,5},{5,4},{6,7},{7,6},{8,9},{9,8},{10,11... | collective-permute-start | bytes 110600 | tf_op jit(solution)/shard_map/ppermute | solution.py:73
  15.0 3.8 %copy-start.8 = (s32[1,8]{1,0:T(1,128)S(1)}, s32[1,8]{1,0:T(1,128)}, u32[]{:S(2)}) copy-start(s32[1,8]{1,0:T(1,128)} %choice.1) | copy-start | bytes 100
  15.0 3.8 %copy-start.9 = (f32[1,8]{1,0:T(1,128)S(1)}, f32[1,8]{1,0:T(1,128)}, u32[]{:S(2)}) copy-start(f32[1,8]{1,0:T(1,128)} %probability.1) | copy-start | bytes 100
  15.0 8.7 %collective-permute-start.5 = (bf16[4,80,128]{2,1,0:T(8,128)(2,1)S(1)}, bf16[4,80,128]{2,1,0:T(8,128)(2,1)S(1)}, u32[]{:S(2)}, u32[]{:S(2)}) collective-permute-start(bf16[4,80,128]{2,1,0:T(8,128)(2,1)S(1)} %shard_map.134), channel_id=1, source_target_pairs={{0,8},{1,9},{2,10},{3,11},{4,12},{5,13},{6,14},{7,15},{8,0},{9,1},... | collective-permute-start | bytes 245768 | tf_op jit(solution)/shard_map/ppermute | solution.py:73
  18.5 1.3 %collective-permute-start.8 = (bf16[9,16,128]{2,1,0:T(8,128)(2,1)S(1)}, bf16[9,16,128]{2,1,0:T(8,128)(2,1)S(1)}, u32[]{:S(2)}, u32[]{:S(2)}) collective-permute-start(bf16[9,16,128]{2,1,0:T(8,128)(2,1)S(1)} %get-tuple-element.30), channel_id=1, source_target_pairs={{0,1},{1,0},{2,3},{3,2},{4,5},{5,4},{6,7},{7,6},{8,9},{9,8},{10,11... | collective-permute-start | bytes 110600 | tf_op jit(solution)/shard_map/ppermute | solution.py:73
  20.1 4.0 %collective-permute-start.9 = (bf16[9,16,128]{2,1,0:T(8,128)(2,1)S(1)}, bf16[9,16,128]{2,1,0:T(8,128)(2,1)S(1)}, u32[]{:S(2)}, u32[]{:S(2)}) collective-permute-start(bf16[9,16,128]{2,1,0:T(8,128)(2,1)S(1)} %shard_map.137.mine.after), channel_id=1, source_target_pairs={{0,2},{1,3},{2,0},{3,1},{4,6},{5,7},{6,4},{7,5},{8,10},{9,11},{10,... | collective-permute-start | bytes 110600 | tf_op jit(solution)/shard_map/ppermute | solution.py:73
  21.6 6.6 %collective-permute-start.10 = (bf16[4,80,128]{2,1,0:T(8,128)(2,1)S(1)}, bf16[4,80,128]{2,1,0:T(8,128)(2,1)S(1)}, u32[]{:S(2)}, u32[]{:S(2)}) collective-permute-start(bf16[4,80,128]{2,1,0:T(8,128)(2,1)S(1)} %shard_map.139), channel_id=1, source_target_pairs={{0,12},{1,13},{2,14},{3,15},{4,8},{5,9},{6,10},{7,11},{8,4},{9,5},... | collective-permute-start | bytes 245768 | tf_op jit(solution)/shard_map/ppermute | solution.py:73
  24.4 5.5 %collective-permute-start.11 = (bf16[9,16,128]{2,1,0:T(8,128)(2,1)S(1)}, bf16[9,16,128]{2,1,0:T(8,128)(2,1)S(1)}, u32[]{:S(2)}, u32[]{:S(2)}) collective-permute-start(bf16[9,16,128]{2,1,0:T(8,128)(2,1)S(1)} %shard_map.138.after.mine), channel_id=1, source_target_pairs={{0,4},{1,5},{2,6},{3,7},{4,0},{5,1},{6,2},{7,3},{8,12},{9,13},{10,... | collective-permute-start | bytes 110600 | tf_op jit(solution)/shard_map/ppermute | solution.py:73
  28.3 6.9 %copy-start.5 = (f32[2048]{0:T(1024)S(1)}, f32[2048]{0:T(1024)}, u32[]{:S(2)}) copy-start(f32[2048]{0:T(1024)} %param.18) | copy-start | bytes 24580
  28.3 8.2 %collective-permute-start.14 = (bf16[16,80,128]{2,1,0:T(8,128)(2,1)S(1)}, bf16[16,80,128]{2,1,0:T(8,128)(2,1)S(1)}, u32[]{:S(2)}, u32[]{:S(2)}) collective-permute-start(bf16[16,80,128]{2,1,0:T(8,128)(2,1)S(1)} %shard_map.140.after.mine), channel_id=1, source_target_pairs={{0,16},{16,0},{1,17},{17,1},{2,18},{18,2},{3,19},{19,3},{4,20},{20... | collective-permute-start | bytes 983048 | tf_op jit(solution)/shard_map/ppermute | solution.py:463
  30.3 4.9 %collective-permute-start.12 = (bf16[9,16,128]{2,1,0:T(8,128)(2,1)S(1)}, bf16[9,16,128]{2,1,0:T(8,128)(2,1)S(1)}, u32[]{:S(2)}, u32[]{:S(2)}) collective-permute-start(bf16[9,16,128]{2,1,0:T(8,128)(2,1)S(1)} %shard_map.141.mine), channel_id=1, source_target_pairs={{0,8},{1,9},{2,10},{3,11},{4,12},{5,13},{6,14},{7,15},{8,0},{9,1},... | collective-permute-start | bytes 110600 | tf_op jit(solution)/shard_map/ppermute | solution.py:73
  35.2 1.9 %copy-start.1 = (bf16[1,2048,768]{2,1,0:T(8,128)(2,1)S(1)}, bf16[1,2048,768]{2,1,0:T(8,128)(2,1)}, u32[]{:S(2)}) copy-start(bf16[1,2048,768]{2,1,0:T(8,128)(2,1)} %param.22) | copy-start | bytes 9437188
  35.6 2.5 %copy-start = (bf16[1,2048,768]{2,1,0:T(8,128)(2,1)S(1)}, bf16[1,2048,768]{2,1,0:T(8,128)(2,1)}, u32[]{:S(2)}) copy-start(bf16[1,2048,768]{2,1,0:T(8,128)(2,1)} %param.21) | copy-start | bytes 9437188
  35.6 1.3 %collective-permute-start.13 = (bf16[8,16,128]{2,1,0:T(8,128)(2,1)S(1)}, bf16[8,16,128]{2,1,0:T(8,128)(2,1)S(1)}, u32[]{:S(2)}, u32[]{:S(2)}) collective-permute-start(bf16[8,16,128]{2,1,0:T(8,128)(2,1)S(1)} %get-tuple-element.34.mine), channel_id=1, source_target_pairs={{0,1},{1,0},{2,3},{3,2},{4,5},{5,4},{6,7},{7,6},{8,9},{9,8},{10,11... | collective-permute-start | bytes 98312 | tf_op jit(solution)/shard_map/ppermute | solution.py:73

commit v14 on v11

--- a/solution.py
+++ b/solution.py
@@ -23,7 +23,8 @@
 floor_score = -1e30
 epsilon = 1e-06
 FILL = 20
-TOKEN = 800
+LATE = 20
+TOKEN = 50
 MERGE = 2500
 JOIN = 1600
 
@@ -449,6 +450,7 @@
         [VMEM] * 2,
         ordered,
         lax.ppermute(ordered, "grp", [(0, 1), (1, 0)]),
+        nanos=LATE,
     )
 
 

time: 52.8 us -> 51.6 us (0.977)
  local copies, waits for them, and re-layouts: 1.3 us -> 0.06 us
    unnamed x22, local copies, waits for them, and re-layouts: 1.3 us -> 0.06 us
where the time goes in v14:
time: 51.6 us; the launch traced here: 51.3 us
  starting transfers between devices  20.8 us (40%)
  waiting for transfers between devices  11.9 us (23%)
  blocking collectives  11 us (21%)
  Pallas kernels  7.38 us (14%)
    ppermute x14, starting transfers between devices, swap(): return lax.ppermute(value, 'exp', [(t, t ^ distance) for t in range(n)])  19.3 us
    ppermute x14, waiting for transfers between devices, swap(): return lax.ppermute(value, 'exp', [(t, t ^ distance) for t in range(n)])  11 us
    all_to_all x1, blocking collectives, body(): lax.all_to_all(out, 'exp', split_axis=0, concat_axis=0, tiled=True)  11 us
    pallas_call x19, Pallas kernels, call(): pl.pallas_call(kernel, out_shape=shapes, in_specs=specs, out_specs=jax.tr...  7.38 us
    ppermute x1, starting transfers between devices, lora_join(): lax.ppermute(ordered, 'grp', [(0, 1), (1, 0)])  1.56 us
  transfers between devices with their start and end apart: 15, of which 8 were waited for; matrix products, arithmetic and copies ran while one was open for 0% of the time, Pallas kernels for 6%

profile of v14, /device:TPU:0, one launch (start us, length us, event | category | flops | bytes accessed | tf_op | source)
XLA Modules:
  0.0 51.3 jit_solution(6346586249175822808)
XLA Ops:
  0.0 0.8 %shard_map.127.mine.after = bf16[1,32,128]{2,1,0:T(8,128)(2,1)S(1)} custom-call(bf16[1,2048]{1,0:T(2,128)(2,1)} %query.1, bf16[1,2048]{1,0:T(2,128)(2,1)} %resid.1), custom_call_target="tpu_custom_call" | custom-call | flops 4000000000 | tf_op jit(solution)/shard_map/pallas_call | solution.py:39
  0.8 4.1 %collective-permute-start = (bf16[1,32,128]{2,1,0:T(8,128)(2,1)S(1)}, bf16[1,32,128]{2,1,0:T(8,128)(2,1)S(1)}, u32[]{:S(2)}, u32[]{:S(2)}) collective-permute-start(bf16[1,32,128]{2,1,0:T(8,128)(2,1)S(1)} %shard_map.127.mine.after), channel_id=1, source_target_pairs={{0,8},{1,9},{2,10},{3,11},{4,12},{5,13},{6,14},{7,15},{8,0},{9,1},... | collective-permute-start | bytes 24584 | tf_op jit(solution)/shard_map/ppermute | solution.py:73
  4.9 0.1 shard_map.130
  5.0 1.6 %collective-permute-start.2 = (bf16[8,80,128]{2,1,0:T(8,128)(2,1)S(1)}, bf16[8,80,128]{2,1,0:T(8,128)(2,1)S(1)}, u32[]{:S(2)}, u32[]{:S(2)}) collective-permute-start(bf16[8,80,128]{2,1,0:T(8,128)(2,1)S(1)} %get-tuple-element.22), channel_id=1, source_target_pairs={{0,2},{1,3},{2,0},{3,1},{4,6},{5,7},{6,4},{7,5},{8,10},{9,11},{10,... | collective-permute-start | bytes 491528 | tf_op jit(solution)/shard_map/ppermute | solution.py:73
  6.6 1.8 %collective-permute-start.1 = (bf16[2,32,128]{2,1,0:T(8,128)(2,1)S(1)}, bf16[2,32,128]{2,1,0:T(8,128)(2,1)S(1)}, u32[]{:S(2)}, u32[]{:S(2)}) collective-permute-start(bf16[2,32,128]{2,1,0:T(8,128)(2,1)S(1)} %shard_map.128.mine.after), channel_id=1, source_target_pairs={{0,4},{1,5},{2,6},{3,7},{4,0},{5,1},{6,2},{7,3},{8,12},{9,13},{10,... | collective-permute-start | bytes 49160 | tf_op jit(solution)/shard_map/ppermute | solution.py:73
  8.5 2.3 %collective-permute-done.2.got = bf16[8,80,128]{2,1,0:T(8,128)(2,1)S(1)} collective-permute-done((bf16[8,80,128]{2,1,0:T(8,128)(2,1)S(1)}, bf16[8,80,128]{2,1,0:T(8,128)(2,1)S(1)}, u32[]{:S(2)}, u32[]{:S(2)}) %collective-permute-start.2) | collective-permute-done | bytes 163872 | tf_op jit(solution)/shard_map/ppermute | solution.py:73
  10.8 0.0 copy-start.7
  10.8 0.1 collective-permute-start.3
  10.9 0.0 collective-permute-done.1.theirs
  10.9 1.6 %collective-permute-start.4 = (bf16[4,32,128]{2,1,0:T(8,128)(2,1)S(1)}, bf16[4,32,128]{2,1,0:T(8,128)(2,1)S(1)}, u32[]{:S(2)}, u32[]{:S(2)}) collective-permute-start(bf16[4,32,128]{2,1,0:T(8,128)(2,1)S(1)} %shard_map.129.after.mine), channel_id=1, source_target_pairs={{0,2},{1,3},{2,0},{3,1},{4,6},{5,7},{6,4},{7,5},{8,10},{9,11},{10,... | collective-permute-start | bytes 98312 | tf_op jit(solution)/shard_map/ppermute | solution.py:73
  12.5 0.0 collective-permute-done.3.got
  12.5 0.0 copy-start.5
  12.5 0.0 copy-start.8
  12.5 1.6 %collective-permute-start.6 = (bf16[4,80,128]{2,1,0:T(8,128)(2,1)S(1)}, bf16[4,80,128]{2,1,0:T(8,128)(2,1)S(1)}, u32[]{:S(2)}, u32[]{:S(2)}) collective-permute-start(bf16[4,80,128]{2,1,0:T(8,128)(2,1)S(1)} %get-tuple-element.28), channel_id=1, source_target_pairs={{0,4},{1,5},{2,6},{3,7},{4,0},{5,1},{6,2},{7,3},{8,12},{9,13},{10,... | collective-permute-start | bytes 245768 | tf_op jit(solution)/shard_map/ppermute | solution.py:73
  14.2 0.7 %collective-permute-done.4.theirs = bf16[4,32,128]{2,1,0:T(8,128)(2,1)S(1)} collective-permute-done((bf16[4,32,128]{2,1,0:T(8,128)(2,1)S(1)}, bf16[4,32,128]{2,1,0:T(8,128)(2,1)S(1)}, u32[]{:S(2)}, u32[]{:S(2)}) %collective-permute-start.4) | collective-permute-done | bytes 32800 | tf_op jit(solution)/shard_map/ppermute | solution.py:73
  14.9 0.1 collective-permute-start.7
  15.0 0.0 copy-start.9
  15.0 0.0 copy-start.10
  15.0 2.3 %collective-permute-start.5 = (bf16[4,80,128]{2,1,0:T(8,128)(2,1)S(1)}, bf16[4,80,128]{2,1,0:T(8,128)(2,1)S(1)}, u32[]{:S(2)}, u32[]{:S(2)}) collective-permute-start(bf16[4,80,128]{2,1,0:T(8,128)(2,1)S(1)} %shard_map.134), channel_id=1, source_target_pairs={{0,8},{1,9},{2,10},{3,11},{4,12},{5,13},{6,14},{7,15},{8,0},{9,1},... | collective-permute-start | bytes 245768 | tf_op jit(solution)/shard_map/ppermute | solution.py:73
  17.3 0.0 collective-permute-done.7.theirs
  17.3 0.0 collective-permute-done.6.after.refs_1_
  17.4 1.2 %shard_map.135 = (bf16[9,16,128]{2,1,0:T(8,128)(2,1)S(1)}, bf16[9,16,128]{2,1,0:T(8,128)(2,1)S(1)}) custom-call(bf16[4,80,128]{2,1,0:T(8,128)(2,1)S(1)} %collective-permute-done.6.after.refs_1_, s32[8]{0:T(128)S(1)} %copy-done.8, bf16[9,16,128]{2,1,0:T(8,128)(2,1)S(1)} %get-tuple-element.27.after.mine, ...), custom_call_target="tpu_custom_call" | custom-call | flops 8000000000 | tf_op jit(solution)/shard_map/pallas_call | solution.py:39
  18.5 0.2 collective-permute-start.8
  18.8 0.2 shard_map.136.after.gates
  19.0 0.8 %collective-permute-done.8.theirs = bf16[9,16,128]{2,1,0:T(8,128)(2,1)S(1)} collective-permute-done((bf16[9,16,128]{2,1,0:T(8,128)(2,1)S(1)}, bf16[9,16,128]{2,1,0:T(8,128)(2,1)S(1)}, u32[]{:S(2)}, u32[]{:S(2)}) %collective-permute-start.8) | collective-permute-done | bytes 36896 | tf_op jit(solution)/shard_map/ppermute | solution.py:73
  19.8 0.3 shard_map.137.mine.after
  20.1 1.6 %collective-permute-start.9 = (bf16[9,16,128]{2,1,0:T(8,128)(2,1)S(1)}, bf16[9,16,128]{2,1,0:T(8,128)(2,1)S(1)}, u32[]{:S(2)}, u32[]{:S(2)}) collective-permute-start(bf16[9,16,128]{2,1,0:T(8,128)(2,1)S(1)} %shard_map.137.mine.after), channel_id=1, source_target_pairs={{0,2},{1,3},{2,0},{3,1},{4,6},{5,7},{6,4},{7,5},{8,10},{9,11},{10,... | collective-permute-start | bytes 110600 | tf_op jit(solution)/shard_map/ppermute | solution.py:73
  21.6 2.1 %collective-permute-start.10 = (bf16[4,80,128]{2,1,0:T(8,128)(2,1)S(1)}, bf16[4,80,128]{2,1,0:T(8,128)(2,1)S(1)}, u32[]{:S(2)}, u32[]{:S(2)}) collective-permute-start(bf16[4,80,128]{2,1,0:T(8,128)(2,1)S(1)} %shard_map.139), channel_id=1, source_target_pairs={{0,12},{1,13},{2,14},{3,15},{4,8},{5,9},{6,10},{7,11},{8,4},{9,5},... | collective-permute-start | bytes 245768 | tf_op jit(solution)/shard_map/ppermute | solution.py:73
  23.7 0.0 collective-permute-done.5.after.refs_2_
  23.7 0.3 collective-permute-done.9.theirs
  24.1 0.4 shard_map.138.after.mine
  24.4 1.6 %collective-permute-start.11 = (bf16[9,16,128]{2,1,0:T(8,128)(2,1)S(1)}, bf16[9,16,128]{2,1,0:T(8,128)(2,1)S(1)}, u32[]{:S(2)}, u32[]{:S(2)}) collective-permute-start(bf16[9,16,128]{2,1,0:T(8,128)(2,1)S(1)} %shard_map.138.after.mine), channel_id=1, source_target_pairs={{0,4},{1,5},{2,6},{3,7},{4,0},{5,1},{6,2},{7,3},{8,12},{9,13},{10,... | collective-permute-start | bytes 110600 | tf_op jit(solution)/shard_map/ppermute | solution.py:73
  26.0 2.2 %collective-permute-done.10.refs_3_ = bf16[4,80,128]{2,1,0:T(8,128)(2,1)S(1)} collective-permute-done((bf16[4,80,128]{2,1,0:T(8,128)(2,1)S(1)}, bf16[4,80,128]{2,1,0:T(8,128)(2,1)S(1)}, u32[]{:S(2)}, u32[]{:S(2)}) %collective-permute-start.10) | collective-permute-done | bytes 81952 | tf_op jit(solution)/shard_map/ppermute | solution.py:73
  28.3 0.0 copy-start
  28.3 0.0 copy-start.1
  28.3 0.0 copy-start.2
  28.4 1.6 %collective-permute-start.14 = (bf16[16,80,128]{2,1,0:T(8,128)(2,1)S(1)}, bf16[16,80,128]{2,1,0:T(8,128)(2,1)S(1)}, u32[]{:S(2)}, u32[]{:S(2)}) collective-permute-start(bf16[16,80,128]{2,1,0:T(8,128)(2,1)S(1)} %shard_map.140.after.mine), channel_id=1, source_target_pairs={{0,16},{16,0},{1,17},{17,1},{2,18},{18,2},{3,19},{19,3},{4,20},{20... | collective-permute-start | bytes 983048 | tf_op jit(solution)/shard_map/ppermute | solution.py:452
  29.9 0.4 shard_map.141.mine
  30.3 0.5 collective-permute-start.12
  30.8 4.4 %collective-permute-done.12.theirs = bf16[9,16,128]{2,1,0:T(8,128)(2,1)S(1)} collective-permute-done((bf16[9,16,128]{2,1,0:T(8,128)(2,1)S(1)}, bf16[9,16,128]{2,1,0:T(8,128)(2,1)S(1)}, u32[]{:S(2)}, u32[]{:S(2)}) %collective-permute-start.12) | collective-permute-done | bytes 36896 | tf_op jit(solution)/shard_map/ppermute | solution.py:73
  35.2 0.4 shard_map.142
  35.6 0.1 collective-permute-start.13
  35.7 0.9 %collective-permute-done.14.theirs = bf16[16,80,128]{2,1,0:T(8,128)(2,1)S(1)} collective-permute-done((bf16[16,80,128]{2,1,0:T(8,128)(2,1)S(1)}, bf16[16,80,128]{2,1,0:T(8,128)(2,1)S(1)}, u32[]{:S(2)}, u32[]{:S(2)}) %collective-permute-start.14) | collective-permute-done | bytes 327712 | tf_op jit(solution)/shard_map/ppermute | solution.py:452
  36.6 0.1 shard_map.143
  36.7 0.2 collective-permute-done.13.theirs
  36.9 2.8 %shard_map.144 = bf16[16,16,128]{2,1,0:T(8,128)(2,1)S(1)} custom-call(bf16[8,16,128]{2,1,0:T(8,128)(2,1)S(1)} %get-tuple-element.34.mine, bf16[8,16,128]{2,1,0:T(8,128)(2,1)S(1)} %collective-permute-done.13.theirs, bf16[2048,768]{1,0:T(8,128)(2,1)S(1)} %bitcast.5, bf16[2048,768]{1,0:T(8,128)(2,1)S(1)} %bitcast.6, bf16[768,2048]{1,0:T(8,128)(2,1)S(1)} %bitcast.7, ...), custom_call_target="tpu_custom_call" | custom-call | flops 1600000000 | tf_op jit(solution)/shard_map/pallas_call | solution.py:39
  39.7 11.0 %all_to_all.5.got = bf16[16,16,128]{2,1,0:T(8,128)(2,1)S(1)} all-to-all(bf16[16,16,128]{2,1,0:T(8,128)(2,1)S(1)} %shard_map.144), channel_id=1, replica_groups=mesh['grp'=2,'exp'=16] {'exp'}, dimensions={0} | all-to-all | bytes 131072 | tf_op jit(solution)/shard_map/all_to_all | solution.py:581
  50.6 0.7 %shard_map.145 = bf16[1,2048]{1,0:T(2,128)(2,1)} custom-call(f32[16,128]{1,0:T(8,128)S(1)} %get-tuple-element.33.hidden, bf16[16,16,128]{2,1,0:T(8,128)(2,1)S(1)} %all_to_all.5.got, f32[1,128]{1,0:T(1,128)S(1)} %shard_map.136.after.gates), custom_call_target="tpu_custom_call" | custom-call | flops 1600000000 | tf_op jit(solution)/shard_map/pallas_call | solution.py:39
  (24 shorter events, 0.1 us)
Async XLA Ops:
  0.0 4.9 %copy-start.4 = (bf16[16,96,48]{1,2,0:T(8,128)(2,1)S(1)}, bf16[16,96,48]{1,2,0:T(8,128)(2,1)}, u32[]{:S(2)}) copy-start(bf16[16,96,48]{1,2,0:T(8,128)(2,1)} %param.25) | copy-start | bytes 442372
  0.0 4.9 %copy-start.3 = (bf16[16,96,128]{2,1,0:T(8,128)(2,1)S(1)}, bf16[16,96,128]{2,1,0:T(8,128)(2,1)}, u32[]{:S(2)}) copy-start(bf16[16,96,128]{2,1,0:T(8,128)(2,1)} %model.1) | copy-start | bytes 1179652
  0.8 5.8 %collective-permute-start = (bf16[1,32,128]{2,1,0:T(8,128)(2,1)S(1)}, bf16[1,32,128]{2,1,0:T(8,128)(2,1)S(1)}, u32[]{:S(2)}, u32[]{:S(2)}) collective-permute-start(bf16[1,32,128]{2,1,0:T(8,128)(2,1)S(1)} %shard_map.127.mine.after), channel_id=1, source_target_pairs={{0,8},{1,9},{2,10},{3,11},{4,12},{5,13},{6,14},{7,15},{8,0},{9,1},... | collective-permute-start | bytes 24584 | tf_op jit(solution)/shard_map/ppermute | solution.py:73
  5.0 5.7 %collective-permute-start.2 = (bf16[8,80,128]{2,1,0:T(8,128)(2,1)S(1)}, bf16[8,80,128]{2,1,0:T(8,128)(2,1)S(1)}, u32[]{:S(2)}, u32[]{:S(2)}) collective-permute-start(bf16[8,80,128]{2,1,0:T(8,128)(2,1)S(1)} %get-tuple-element.22), channel_id=1, source_target_pairs={{0,2},{1,3},{2,0},{3,1},{4,6},{5,7},{6,4},{7,5},{8,10},{9,11},{10,... | collective-permute-start | bytes 491528 | tf_op jit(solution)/shard_map/ppermute | solution.py:73
  6.6 4.3 %collective-permute-start.1 = (bf16[2,32,128]{2,1,0:T(8,128)(2,1)S(1)}, bf16[2,32,128]{2,1,0:T(8,128)(2,1)S(1)}, u32[]{:S(2)}, u32[]{:S(2)}) collective-permute-start(bf16[2,32,128]{2,1,0:T(8,128)(2,1)S(1)} %shard_map.128.mine.after), channel_id=1, source_target_pairs={{0,4},{1,5},{2,6},{3,7},{4,0},{5,1},{6,2},{7,3},{8,12},{9,13},{10,... | collective-permute-start | bytes 49160 | tf_op jit(solution)/shard_map/ppermute | solution.py:73
  10.8 4.1 %copy-start.7 = (bf16[1,512]{1,0:T(2,128)(2,1)S(1)}, bf16[1,512]{1,0:T(2,128)(2,1)}, u32[]{:S(2)}) copy-start(bf16[1,512]{1,0:T(2,128)(2,1)} %new.1) | copy-start | bytes 3076
  10.8 1.7 %collective-permute-start.3 = (bf16[8,80,128]{2,1,0:T(8,128)(2,1)S(1)}, bf16[8,80,128]{2,1,0:T(8,128)(2,1)S(1)}, u32[]{:S(2)}, u32[]{:S(2)}) collective-permute-start(bf16[8,80,128]{2,1,0:T(8,128)(2,1)S(1)} %get-tuple-element.24), channel_id=1, source_target_pairs={{0,1},{1,0},{2,3},{3,2},{4,5},{5,4},{6,7},{7,6},{8,9},{9,8},{10,11... | collective-permute-start | bytes 491528 | tf_op jit(solution)/shard_map/ppermute | solution.py:73
  10.9 4.0 %collective-permute-start.4 = (bf16[4,32,128]{2,1,0:T(8,128)(2,1)S(1)}, bf16[4,32,128]{2,1,0:T(8,128)(2,1)S(1)}, u32[]{:S(2)}, u32[]{:S(2)}) collective-permute-start(bf16[4,32,128]{2,1,0:T(8,128)(2,1)S(1)} %shard_map.129.after.mine), channel_id=1, source_target_pairs={{0,2},{1,3},{2,0},{3,1},{4,6},{5,7},{6,4},{7,5},{8,10},{9,11},{10,... | collective-permute-start | bytes 98312 | tf_op jit(solution)/shard_map/ppermute | solution.py:73
  12.5 4.8 %copy-start.5 = (bf16[8,192,512]{2,1,0:T(8,128)(2,1)S(1)}, bf16[8,192,512]{2,1,0:T(8,128)(2,1)}, u32[]{:S(2)}) copy-start(bf16[8,192,512]{2,1,0:T(8,128)(2,1)} %cache.1) | copy-start | bytes 4718596
  12.5 4.8 %copy-start.8 = (s32[8]{0:T(128)S(1)}, s32[8]{0:T(128)}, u32[]{:S(2)}) copy-start(s32[8]{0:T(128)} %lengths.1) | copy-start | bytes 100
  12.5 4.8 %collective-permute-start.6 = (bf16[4,80,128]{2,1,0:T(8,128)(2,1)S(1)}, bf16[4,80,128]{2,1,0:T(8,128)(2,1)S(1)}, u32[]{:S(2)}, u32[]{:S(2)}) collective-permute-start(bf16[4,80,128]{2,1,0:T(8,128)(2,1)S(1)} %get-tuple-element.28), channel_id=1, source_target_pairs={{0,4},{1,5},{2,6},{3,7},{4,0},{5,1},{6,2},{7,3},{8,12},{9,13},{10,... | collective-permute-start | bytes 245768 | tf_op jit(solution)/shard_map/ppermute | solution.py:73
  14.9 2.4 %collective-permute-start.7 = (bf16[9,16,128]{2,1,0:T(8,128)(2,1)S(1)}, bf16[9,16,128]{2,1,0:T(8,128)(2,1)S(1)}, u32[]{:S(2)}, u32[]{:S(2)}) collective-permute-start(bf16[9,16,128]{2,1,0:T(8,128)(2,1)S(1)} %get-tuple-element.27.after.mine), channel_id=1, source_target_pairs={{0,1},{1,0},{2,3},{3,2},{4,5},{5,4},{6,7},{7,6},{8,9},{9,8},{10,11... | collective-permute-start | bytes 110600 | tf_op jit(solution)/shard_map/ppermute | solution.py:73
  15.0 3.8 %copy-start.9 = (s32[1,8]{1,0:T(1,128)S(1)}, s32[1,8]{1,0:T(1,128)}, u32[]{:S(2)}) copy-start(s32[1,8]{1,0:T(1,128)} %choice.1) | copy-start | bytes 100
  15.0 3.8 %copy-start.10 = (f32[1,8]{1,0:T(1,128)S(1)}, f32[1,8]{1,0:T(1,128)}, u32[]{:S(2)}) copy-start(f32[1,8]{1,0:T(1,128)} %probability.1) | copy-start | bytes 100
  15.0 8.7 %collective-permute-start.5 = (bf16[4,80,128]{2,1,0:T(8,128)(2,1)S(1)}, bf16[4,80,128]{2,1,0:T(8,128)(2,1)S(1)}, u32[]{:S(2)}, u32[]{:S(2)}) collective-permute-start(bf16[4,80,128]{2,1,0:T(8,128)(2,1)S(1)} %shard_map.134), channel_id=1, source_target_pairs={{0,8},{1,9},{2,10},{3,11},{4,12},{5,13},{6,14},{7,15},{8,0},{9,1},... | collective-permute-start | bytes 245768 | tf_op jit(solution)/shard_map/ppermute | solution.py:73
  18.5 1.3 %collective-permute-start.8 = (bf16[9,16,128]{2,1,0:T(8,128)(2,1)S(1)}, bf16[9,16,128]{2,1,0:T(8,128)(2,1)S(1)}, u32[]{:S(2)}, u32[]{:S(2)}) collective-permute-start(bf16[9,16,128]{2,1,0:T(8,128)(2,1)S(1)} %get-tuple-element.30), channel_id=1, source_target_pairs={{0,1},{1,0},{2,3},{3,2},{4,5},{5,4},{6,7},{7,6},{8,9},{9,8},{10,11... | collective-permute-start | bytes 110600 | tf_op jit(solution)/shard_map/ppermute | solution.py:73
  20.1 4.0 %collective-permute-start.9 = (bf16[9,16,128]{2,1,0:T(8,128)(2,1)S(1)}, bf16[9,16,128]{2,1,0:T(8,128)(2,1)S(1)}, u32[]{:S(2)}, u32[]{:S(2)}) collective-permute-start(bf16[9,16,128]{2,1,0:T(8,128)(2,1)S(1)} %shard_map.137.mine.after), channel_id=1, source_target_pairs={{0,2},{1,3},{2,0},{3,1},{4,6},{5,7},{6,4},{7,5},{8,10},{9,11},{10,... | collective-permute-start | bytes 110600 | tf_op jit(solution)/shard_map/ppermute | solution.py:73
  21.6 6.6 %collective-permute-start.10 = (bf16[4,80,128]{2,1,0:T(8,128)(2,1)S(1)}, bf16[4,80,128]{2,1,0:T(8,128)(2,1)S(1)}, u32[]{:S(2)}, u32[]{:S(2)}) collective-permute-start(bf16[4,80,128]{2,1,0:T(8,128)(2,1)S(1)} %shard_map.139), channel_id=1, source_target_pairs={{0,12},{1,13},{2,14},{3,15},{4,8},{5,9},{6,10},{7,11},{8,4},{9,5},... | collective-permute-start | bytes 245768 | tf_op jit(solution)/shard_map/ppermute | solution.py:73
  24.4 5.5 %collective-permute-start.11 = (bf16[9,16,128]{2,1,0:T(8,128)(2,1)S(1)}, bf16[9,16,128]{2,1,0:T(8,128)(2,1)S(1)}, u32[]{:S(2)}, u32[]{:S(2)}) collective-permute-start(bf16[9,16,128]{2,1,0:T(8,128)(2,1)S(1)} %shard_map.138.after.mine), channel_id=1, source_target_pairs={{0,4},{1,5},{2,6},{3,7},{4,0},{5,1},{6,2},{7,3},{8,12},{9,13},{10,... | collective-permute-start | bytes 110600 | tf_op jit(solution)/shard_map/ppermute | solution.py:73
  28.3 6.9 %copy-start.6 = (f32[2048]{0:T(1024)S(1)}, f32[2048]{0:T(1024)}, u32[]{:S(2)}) copy-start(f32[2048]{0:T(1024)} %param.18) | copy-start | bytes 24580
  28.3 8.6 %copy-start = (bf16[1,2048,768]{2,1,0:T(8,128)(2,1)S(1)}, bf16[1,2048,768]{2,1,0:T(8,128)(2,1)}, u32[]{:S(2)}) copy-start(bf16[1,2048,768]{2,1,0:T(8,128)(2,1)} %param.21) | copy-start | bytes 9437188
  28.3 8.6 %copy-start.1 = (bf16[1,2048,768]{2,1,0:T(8,128)(2,1)S(1)}, bf16[1,2048,768]{2,1,0:T(8,128)(2,1)}, u32[]{:S(2)}) copy-start(bf16[1,2048,768]{2,1,0:T(8,128)(2,1)} %param.22) | copy-start | bytes 9437188
  28.3 8.6 %copy-start.2 = (bf16[1,768,2048]{2,1,0:T(8,128)(2,1)S(1)}, bf16[1,768,2048]{2,1,0:T(8,128)(2,1)}, u32[]{:S(2)}) copy-start(bf16[1,768,2048]{2,1,0:T(8,128)(2,1)} %param.23) | copy-start | bytes 9437188
  28.4 8.2 %collective-permute-start.14 = (bf16[16,80,128]{2,1,0:T(8,128)(2,1)S(1)}, bf16[16,80,128]{2,1,0:T(8,128)(2,1)S(1)}, u32[]{:S(2)}, u32[]{:S(2)}) collective-permute-start(bf16[16,80,128]{2,1,0:T(8,128)(2,1)S(1)} %shard_map.140.after.mine), channel_id=1, source_target_pairs={{0,16},{16,0},{1,17},{17,1},{2,18},{18,2},{3,19},{19,3},{4,20},{20... | collective-permute-start | bytes 983048 | tf_op jit(solution)/shard_map/ppermute | solution.py:452
  30.3 4.9 %collective-permute-start.12 = (bf16[9,16,128]{2,1,0:T(8,128)(2,1)S(1)}, bf16[9,16,128]{2,1,0:T(8,128)(2,1)S(1)}, u32[]{:S(2)}, u32[]{:S(2)}) collective-permute-start(bf16[9,16,128]{2,1,0:T(8,128)(2,1)S(1)} %shard_map.141.mine), channel_id=1, source_target_pairs={{0,8},{1,9},{2,10},{3,11},{4,12},{5,13},{6,14},{7,15},{8,0},{9,1},... | collective-permute-start | bytes 110600 | tf_op jit(solution)/shard_map/ppermute | solution.py:73
  35.6 1.3 %collective-permute-start.13 = (bf16[8,16,128]{2,1,0:T(8,128)(2,1)S(1)}, bf16[8,16,128]{2,1,0:T(8,128)(2,1)S(1)}, u32[]{:S(2)}, u32[]{:S(2)}) collective-permute-start(bf16[8,16,128]{2,1,0:T(8,128)(2,1)S(1)} %get-tuple-element.34.mine), channel_id=1, source_target_pairs={{0,1},{1,0},{2,3},{3,2},{4,5},{5,4},{6,7},{7,6},{8,9},{9,8},{10,11... | collective-permute-start | bytes 98312 | tf_op jit(solution)/shard_map/ppermute | solution.py:73

commit v15 on v14

--- a/solution.py
+++ b/solution.py
@@ -118,17 +118,30 @@
     out[2 * half] = jnp.concatenate([fresh, rest], axis=0).astype(bf16)
 
 
-def write_stats(stats, out, slots):
+def split_three(value):
     parts = []
     for _ in range(3):
-        part = stats.astype(bf16).astype(f32)
+        part = value.astype(bf16).astype(f32)
         parts.append(part)
-        stats = stats - part
-    if stat_tiles(slots) == 1:
-        tile = parts[0]
-        for k in (1, 2):
-            tile = tile + pltpu.roll(parts[k], 2 * slots * k, 1)
-        out[slots] = tile.astype(bf16)
+        value = value - part
+    return parts
+
+
+def turned_to(value, lane):
+    return pltpu.roll(value, lane % HEAD_WIDTH, 1) if lane % HEAD_WIDTH else value
+
+
+def write_stats(groups, out, slots):
+    single = stat_tiles(slots) == 1
+    copies = 3 if single else 1
+    spread = sum(
+        turned_to(value, 2 * slots * k + at) for k in range(copies) for at, value in groups
+    )
+    parts = split_three(spread)
+    if single:
+        lanes = iota(HEADS, 1)
+        low = jnp.where(lanes < 4 * slots, parts[1], parts[2])
+        out[slots] = jnp.where(lanes < 2 * slots, parts[0], low).astype(bf16)
     else:
         for k in range(3):
             out[slots + k] = parts[k].astype(bf16)
@@ -137,14 +150,9 @@
 def read_stats(message, slots):
     if stat_tiles(slots) == 1:
         tile = message[slots].astype(f32)
-        lanes = iota(HEADS, 1)
-        stats = tile
-        for k in (1, 2):
-            stats = stats + pltpu.roll(tile, HEAD_WIDTH - 2 * slots * k, 1)
-        stats = jnp.where(lanes < 2 * slots, stats, 0.0)
-    else:
-        stats = sum(message[slots + k].astype(f32) for k in range(3))
-    return stats, pltpu.roll(stats, HEAD_WIDTH - slots, 1)
+        return [sum(turned_to(tile, -2 * slots * k - at) for k in range(3)) for at in (0, slots)]
+    stats = sum(message[slots + k].astype(f32) for k in range(3))
+    return [stats, turned_to(stats, -slots)]
 
 
 def flipped(value, flip):
@@ -173,9 +181,8 @@
 def merge_kernel(after, mine, theirs, out, *, slots, flip):
     peak, total, acc = merged(mine, theirs, slots, flip)
     lanes = iota(HEADS, 1)
-    stats = jnp.where(lanes < slots, peak, 0.0)
-    stats = stats + pltpu.roll(jnp.where(lanes < slots, total, 0.0), slots, 1)
-    write_stats(stats, out, slots)
+    peak, total = jnp.where(lanes < slots, peak, 0.0), jnp.where(lanes < slots, total, 0.0)
+    write_stats([(0, peak), (slots, total)], out, slots)
     for slot in range(slots):
         out[slot] = acc(slot).astype(bf16)
 
@@ -255,7 +262,7 @@
                 stats[k] = jnp.where(lanes == slot, t, stats[k])
                 stats[k] = jnp.where(lanes == sequences + slot, z, stats[k])
     for k, part in enumerate((keep, send)):
-        write_stats(stats[k], part, sequences)
+        write_stats([(0, stats[k])], part, sequences)
 
 
 def token_kernel(mine, theirs, residuals, scale, hidden_out, normed_out):

time: 51.6 us -> 51.5 us (level)
  no operation moved by 1% of the time
where the time goes in v15:
time: 51.5 us; the launch traced here: 51.2 us
  starting transfers between devices  20.9 us (41%)
  waiting for transfers between devices  12 us (23%)
  blocking collectives  11 us (21%)
  Pallas kernels  7.09 us (14%)
    ppermute x14, starting transfers between devices, swap(): return lax.ppermute(value, 'exp', [(t, t ^ distance) for t in range(n)])  19.3 us
    ppermute x14, waiting for transfers between devices, swap(): return lax.ppermute(value, 'exp', [(t, t ^ distance) for t in range(n)])  11 us
    all_to_all x1, blocking collectives, body(): lax.all_to_all(out, 'exp', split_axis=0, concat_axis=0, tiled=True)  11 us
    pallas_call x19, Pallas kernels, call(): pl.pallas_call(kernel, out_shape=shapes, in_specs=specs, out_specs=jax.tr...  7.09 us
    ppermute x1, starting transfers between devices, lora_join(): lax.ppermute(ordered, 'grp', [(0, 1), (1, 0)])  1.56 us
  transfers between devices with their start and end apart: 15, of which 8 were waited for; matrix products, arithmetic and copies ran while one was open for 0% of the time, Pallas kernels for 6%

profile of v15, /device:TPU:0, one launch (start us, length us, event | category | flops | bytes accessed | tf_op | source)
XLA Modules:
  0.0 51.2 jit_solution(6543908503872339672)
XLA Ops:
  0.0 0.8 %shard_map.127.mine.after = bf16[1,32,128]{2,1,0:T(8,128)(2,1)S(1)} custom-call(bf16[1,2048]{1,0:T(2,128)(2,1)} %query.1, bf16[1,2048]{1,0:T(2,128)(2,1)} %resid.1), custom_call_target="tpu_custom_call" | custom-call | flops 4000000000 | tf_op jit(solution)/shard_map/pallas_call | solution.py:39
  0.8 4.1 %collective-permute-start = (bf16[1,32,128]{2,1,0:T(8,128)(2,1)S(1)}, bf16[1,32,128]{2,1,0:T(8,128)(2,1)S(1)}, u32[]{:S(2)}, u32[]{:S(2)}) collective-permute-start(bf16[1,32,128]{2,1,0:T(8,128)(2,1)S(1)} %shard_map.127.mine.after), channel_id=1, source_target_pairs={{0,8},{1,9},{2,10},{3,11},{4,12},{5,13},{6,14},{7,15},{8,0},{9,1},... | collective-permute-start | bytes 24584 | tf_op jit(solution)/shard_map/ppermute | solution.py:73
  4.9 0.1 shard_map.130
  5.0 1.6 %collective-permute-start.2 = (bf16[8,80,128]{2,1,0:T(8,128)(2,1)S(1)}, bf16[8,80,128]{2,1,0:T(8,128)(2,1)S(1)}, u32[]{:S(2)}, u32[]{:S(2)}) collective-permute-start(bf16[8,80,128]{2,1,0:T(8,128)(2,1)S(1)} %get-tuple-element.22), channel_id=1, source_target_pairs={{0,2},{1,3},{2,0},{3,1},{4,6},{5,7},{6,4},{7,5},{8,10},{9,11},{10,... | collective-permute-start | bytes 491528 | tf_op jit(solution)/shard_map/ppermute | solution.py:73
  6.6 0.0 collective-permute-done.theirs
  6.6 1.8 %collective-permute-start.1 = (bf16[2,32,128]{2,1,0:T(8,128)(2,1)S(1)}, bf16[2,32,128]{2,1,0:T(8,128)(2,1)S(1)}, u32[]{:S(2)}, u32[]{:S(2)}) collective-permute-start(bf16[2,32,128]{2,1,0:T(8,128)(2,1)S(1)} %shard_map.128.mine.after), channel_id=1, source_target_pairs={{0,4},{1,5},{2,6},{3,7},{4,0},{5,1},{6,2},{7,3},{8,12},{9,13},{10,... | collective-permute-start | bytes 49160 | tf_op jit(solution)/shard_map/ppermute | solution.py:73
  8.5 2.3 %collective-permute-done.2.got = bf16[8,80,128]{2,1,0:T(8,128)(2,1)S(1)} collective-permute-done((bf16[8,80,128]{2,1,0:T(8,128)(2,1)S(1)}, bf16[8,80,128]{2,1,0:T(8,128)(2,1)S(1)}, u32[]{:S(2)}, u32[]{:S(2)}) %collective-permute-start.2) | collective-permute-done | bytes 163872 | tf_op jit(solution)/shard_map/ppermute | solution.py:73
  10.8 0.0 copy-start.7
  10.8 0.1 collective-permute-start.3
  10.9 0.0 collective-permute-done.1.theirs
  10.9 1.6 %collective-permute-start.4 = (bf16[4,32,128]{2,1,0:T(8,128)(2,1)S(1)}, bf16[4,32,128]{2,1,0:T(8,128)(2,1)S(1)}, u32[]{:S(2)}, u32[]{:S(2)}) collective-permute-start(bf16[4,32,128]{2,1,0:T(8,128)(2,1)S(1)} %shard_map.129.after.mine), channel_id=1, source_target_pairs={{0,2},{1,3},{2,0},{3,1},{4,6},{5,7},{6,4},{7,5},{8,10},{9,11},{10,... | collective-permute-start | bytes 98312 | tf_op jit(solution)/shard_map/ppermute | solution.py:73
  12.5 0.0 collective-permute-done.3.got
  12.5 0.0 copy-start.5
  12.5 0.0 copy-start.8
  12.5 1.6 %collective-permute-start.6 = (bf16[4,80,128]{2,1,0:T(8,128)(2,1)S(1)}, bf16[4,80,128]{2,1,0:T(8,128)(2,1)S(1)}, u32[]{:S(2)}, u32[]{:S(2)}) collective-permute-start(bf16[4,80,128]{2,1,0:T(8,128)(2,1)S(1)} %get-tuple-element.28), channel_id=1, source_target_pairs={{0,4},{1,5},{2,6},{3,7},{4,0},{5,1},{6,2},{7,3},{8,12},{9,13},{10,... | collective-permute-start | bytes 245768 | tf_op jit(solution)/shard_map/ppermute | solution.py:73
  14.2 0.7 %collective-permute-done.4.theirs = bf16[4,32,128]{2,1,0:T(8,128)(2,1)S(1)} collective-permute-done((bf16[4,32,128]{2,1,0:T(8,128)(2,1)S(1)}, bf16[4,32,128]{2,1,0:T(8,128)(2,1)S(1)}, u32[]{:S(2)}, u32[]{:S(2)}) %collective-permute-start.4) | collective-permute-done | bytes 32800 | tf_op jit(solution)/shard_map/ppermute | solution.py:73
  14.9 0.1 collective-permute-start.7
  15.0 0.0 copy-start.9
  15.0 0.0 copy-start.10
  15.0 2.3 %collective-permute-start.5 = (bf16[4,80,128]{2,1,0:T(8,128)(2,1)S(1)}, bf16[4,80,128]{2,1,0:T(8,128)(2,1)S(1)}, u32[]{:S(2)}, u32[]{:S(2)}) collective-permute-start(bf16[4,80,128]{2,1,0:T(8,128)(2,1)S(1)} %shard_map.134), channel_id=1, source_target_pairs={{0,8},{1,9},{2,10},{3,11},{4,12},{5,13},{6,14},{7,15},{8,0},{9,1},... | collective-permute-start | bytes 245768 | tf_op jit(solution)/shard_map/ppermute | solution.py:73
  17.3 0.0 collective-permute-done.7.theirs
  17.4 1.2 %shard_map.135 = (bf16[9,16,128]{2,1,0:T(8,128)(2,1)S(1)}, bf16[9,16,128]{2,1,0:T(8,128)(2,1)S(1)}) custom-call(bf16[4,80,128]{2,1,0:T(8,128)(2,1)S(1)} %collective-permute-done.6.after.refs_1_, s32[8]{0:T(128)S(1)} %copy-done.8, bf16[9,16,128]{2,1,0:T(8,128)(2,1)S(1)} %get-tuple-element.27.after.mine, ...), custom_call_target="tpu_custom_call" | custom-call | flops 8000000000 | tf_op jit(solution)/shard_map/pallas_call | solution.py:39
  18.5 0.3 collective-permute-start.8
  18.8 0.2 shard_map.136.after.gates
  19.0 0.8 %collective-permute-done.8.theirs = bf16[9,16,128]{2,1,0:T(8,128)(2,1)S(1)} collective-permute-done((bf16[9,16,128]{2,1,0:T(8,128)(2,1)S(1)}, bf16[9,16,128]{2,1,0:T(8,128)(2,1)S(1)}, u32[]{:S(2)}, u32[]{:S(2)}) %collective-permute-start.8) | collective-permute-done | bytes 36896 | tf_op jit(solution)/shard_map/ppermute | solution.py:73
  19.8 0.2 shard_map.137.mine.after
  20.0 1.6 %collective-permute-start.9 = (bf16[9,16,128]{2,1,0:T(8,128)(2,1)S(1)}, bf16[9,16,128]{2,1,0:T(8,128)(2,1)S(1)}, u32[]{:S(2)}, u32[]{:S(2)}) collective-permute-start(bf16[9,16,128]{2,1,0:T(8,128)(2,1)S(1)} %shard_map.137.mine.after), channel_id=1, source_target_pairs={{0,2},{1,3},{2,0},{3,1},{4,6},{5,7},{6,4},{7,5},{8,10},{9,11},{10,... | collective-permute-start | bytes 110600 | tf_op jit(solution)/shard_map/ppermute | solution.py:73
  21.6 2.1 %collective-permute-start.10 = (bf16[4,80,128]{2,1,0:T(8,128)(2,1)S(1)}, bf16[4,80,128]{2,1,0:T(8,128)(2,1)S(1)}, u32[]{:S(2)}, u32[]{:S(2)}) collective-permute-start(bf16[4,80,128]{2,1,0:T(8,128)(2,1)S(1)} %shard_map.139), channel_id=1, source_target_pairs={{0,12},{1,13},{2,14},{3,15},{4,8},{5,9},{6,10},{7,11},{8,4},{9,5},... | collective-permute-start | bytes 245768 | tf_op jit(solution)/shard_map/ppermute | solution.py:73
  23.7 0.0 collective-permute-done.5.after.refs_2_
  23.7 0.3 collective-permute-done.9.theirs
  24.0 0.3 shard_map.138.after.mine
  24.3 1.6 %collective-permute-start.11 = (bf16[9,16,128]{2,1,0:T(8,128)(2,1)S(1)}, bf16[9,16,128]{2,1,0:T(8,128)(2,1)S(1)}, u32[]{:S(2)}, u32[]{:S(2)}) collective-permute-start(bf16[9,16,128]{2,1,0:T(8,128)(2,1)S(1)} %shard_map.138.after.mine), channel_id=1, source_target_pairs={{0,4},{1,5},{2,6},{3,7},{4,0},{5,1},{6,2},{7,3},{8,12},{9,13},{10,... | collective-permute-start | bytes 110600 | tf_op jit(solution)/shard_map/ppermute | solution.py:73
  26.0 2.3 %collective-permute-done.10.refs_3_ = bf16[4,80,128]{2,1,0:T(8,128)(2,1)S(1)} collective-permute-done((bf16[4,80,128]{2,1,0:T(8,128)(2,1)S(1)}, bf16[4,80,128]{2,1,0:T(8,128)(2,1)S(1)}, u32[]{:S(2)}, u32[]{:S(2)}) %collective-permute-start.10) | collective-permute-done | bytes 81952 | tf_op jit(solution)/shard_map/ppermute | solution.py:73
  28.3 0.0 copy-start
  28.3 0.0 copy-start.1
  28.3 0.0 copy-start.2
  28.3 1.6 %collective-permute-start.14 = (bf16[16,80,128]{2,1,0:T(8,128)(2,1)S(1)}, bf16[16,80,128]{2,1,0:T(8,128)(2,1)S(1)}, u32[]{:S(2)}, u32[]{:S(2)}) collective-permute-start(bf16[16,80,128]{2,1,0:T(8,128)(2,1)S(1)} %shard_map.140.after.mine), channel_id=1, source_target_pairs={{0,16},{16,0},{1,17},{17,1},{2,18},{18,2},{3,19},{19,3},{4,20},{20... | collective-permute-start | bytes 983048 | tf_op jit(solution)/shard_map/ppermute | solution.py:459
  29.9 0.3 shard_map.141.mine
  30.2 0.4 collective-permute-start.12
  30.6 4.5 %collective-permute-done.12.theirs = bf16[9,16,128]{2,1,0:T(8,128)(2,1)S(1)} collective-permute-done((bf16[9,16,128]{2,1,0:T(8,128)(2,1)S(1)}, bf16[9,16,128]{2,1,0:T(8,128)(2,1)S(1)}, u32[]{:S(2)}, u32[]{:S(2)}) %collective-permute-start.12) | collective-permute-done | bytes 36896 | tf_op jit(solution)/shard_map/ppermute | solution.py:73
  35.1 0.4 shard_map.142
  35.5 0.1 collective-permute-start.13
  35.6 1.0 %collective-permute-done.14.theirs = bf16[16,80,128]{2,1,0:T(8,128)(2,1)S(1)} collective-permute-done((bf16[16,80,128]{2,1,0:T(8,128)(2,1)S(1)}, bf16[16,80,128]{2,1,0:T(8,128)(2,1)S(1)}, u32[]{:S(2)}, u32[]{:S(2)}) %collective-permute-start.14) | collective-permute-done | bytes 327712 | tf_op jit(solution)/shard_map/ppermute | solution.py:459
  36.5 0.1 shard_map.143
  36.7 0.1 collective-permute-done.13.theirs
  36.8 2.8 %shard_map.144 = bf16[16,16,128]{2,1,0:T(8,128)(2,1)S(1)} custom-call(bf16[8,16,128]{2,1,0:T(8,128)(2,1)S(1)} %get-tuple-element.34.mine, bf16[8,16,128]{2,1,0:T(8,128)(2,1)S(1)} %collective-permute-done.13.theirs, bf16[2048,768]{1,0:T(8,128)(2,1)S(1)} %bitcast.5, bf16[2048,768]{1,0:T(8,128)(2,1)S(1)} %bitcast.6, bf16[768,2048]{1,0:T(8,128)(2,1)S(1)} %bitcast.7, ...), custom_call_target="tpu_custom_call" | custom-call | flops 1600000000 | tf_op jit(solution)/shard_map/pallas_call | solution.py:39
  39.6 11.0 %all_to_all.5.got = bf16[16,16,128]{2,1,0:T(8,128)(2,1)S(1)} all-to-all(bf16[16,16,128]{2,1,0:T(8,128)(2,1)S(1)} %shard_map.144), channel_id=1, replica_groups=mesh['grp'=2,'exp'=16] {'exp'}, dimensions={0} | all-to-all | bytes 131072 | tf_op jit(solution)/shard_map/all_to_all | solution.py:588
  50.5 0.7 %shard_map.145 = bf16[1,2048]{1,0:T(2,128)(2,1)} custom-call(f32[16,128]{1,0:T(8,128)S(1)} %get-tuple-element.33.hidden, bf16[16,16,128]{2,1,0:T(8,128)(2,1)S(1)} %all_to_all.5.got, f32[1,128]{1,0:T(1,128)S(1)} %shard_map.136.after.gates), custom_call_target="tpu_custom_call" | custom-call | flops 1600000000 | tf_op jit(solution)/shard_map/pallas_call | solution.py:39
  (24 shorter events, 0.1 us)
Async XLA Ops:
  0.0 4.9 %copy-start.4 = (bf16[16,96,48]{1,2,0:T(8,128)(2,1)S(1)}, bf16[16,96,48]{1,2,0:T(8,128)(2,1)}, u32[]{:S(2)}) copy-start(bf16[16,96,48]{1,2,0:T(8,128)(2,1)} %param.25) | copy-start | bytes 442372
  0.0 4.9 %copy-start.3 = (bf16[16,96,128]{2,1,0:T(8,128)(2,1)S(1)}, bf16[16,96,128]{2,1,0:T(8,128)(2,1)}, u32[]{:S(2)}) copy-start(bf16[16,96,128]{2,1,0:T(8,128)(2,1)} %model.1) | copy-start | bytes 1179652
  0.8 5.8 %collective-permute-start = (bf16[1,32,128]{2,1,0:T(8,128)(2,1)S(1)}, bf16[1,32,128]{2,1,0:T(8,128)(2,1)S(1)}, u32[]{:S(2)}, u32[]{:S(2)}) collective-permute-start(bf16[1,32,128]{2,1,0:T(8,128)(2,1)S(1)} %shard_map.127.mine.after), channel_id=1, source_target_pairs={{0,8},{1,9},{2,10},{3,11},{4,12},{5,13},{6,14},{7,15},{8,0},{9,1},... | collective-permute-start | bytes 24584 | tf_op jit(solution)/shard_map/ppermute | solution.py:73
  5.0 5.7 %collective-permute-start.2 = (bf16[8,80,128]{2,1,0:T(8,128)(2,1)S(1)}, bf16[8,80,128]{2,1,0:T(8,128)(2,1)S(1)}, u32[]{:S(2)}, u32[]{:S(2)}) collective-permute-start(bf16[8,80,128]{2,1,0:T(8,128)(2,1)S(1)} %get-tuple-element.22), channel_id=1, source_target_pairs={{0,2},{1,3},{2,0},{3,1},{4,6},{5,7},{6,4},{7,5},{8,10},{9,11},{10,... | collective-permute-start | bytes 491528 | tf_op jit(solution)/shard_map/ppermute | solution.py:73
  6.6 4.3 %collective-permute-start.1 = (bf16[2,32,128]{2,1,0:T(8,128)(2,1)S(1)}, bf16[2,32,128]{2,1,0:T(8,128)(2,1)S(1)}, u32[]{:S(2)}, u32[]{:S(2)}) collective-permute-start(bf16[2,32,128]{2,1,0:T(8,128)(2,1)S(1)} %shard_map.128.mine.after), channel_id=1, source_target_pairs={{0,4},{1,5},{2,6},{3,7},{4,0},{5,1},{6,2},{7,3},{8,12},{9,13},{10,... | collective-permute-start | bytes 49160 | tf_op jit(solution)/shard_map/ppermute | solution.py:73
  10.8 4.1 %copy-start.7 = (bf16[1,512]{1,0:T(2,128)(2,1)S(1)}, bf16[1,512]{1,0:T(2,128)(2,1)}, u32[]{:S(2)}) copy-start(bf16[1,512]{1,0:T(2,128)(2,1)} %new.1) | copy-start | bytes 3076
  10.8 1.7 %collective-permute-start.3 = (bf16[8,80,128]{2,1,0:T(8,128)(2,1)S(1)}, bf16[8,80,128]{2,1,0:T(8,128)(2,1)S(1)}, u32[]{:S(2)}, u32[]{:S(2)}) collective-permute-start(bf16[8,80,128]{2,1,0:T(8,128)(2,1)S(1)} %get-tuple-element.24), channel_id=1, source_target_pairs={{0,1},{1,0},{2,3},{3,2},{4,5},{5,4},{6,7},{7,6},{8,9},{9,8},{10,11... | collective-permute-start | bytes 491528 | tf_op jit(solution)/shard_map/ppermute | solution.py:73
  10.9 4.0 %collective-permute-start.4 = (bf16[4,32,128]{2,1,0:T(8,128)(2,1)S(1)}, bf16[4,32,128]{2,1,0:T(8,128)(2,1)S(1)}, u32[]{:S(2)}, u32[]{:S(2)}) collective-permute-start(bf16[4,32,128]{2,1,0:T(8,128)(2,1)S(1)} %shard_map.129.after.mine), channel_id=1, source_target_pairs={{0,2},{1,3},{2,0},{3,1},{4,6},{5,7},{6,4},{7,5},{8,10},{9,11},{10,... | collective-permute-start | bytes 98312 | tf_op jit(solution)/shard_map/ppermute | solution.py:73
  12.5 4.8 %copy-start.5 = (bf16[8,192,512]{2,1,0:T(8,128)(2,1)S(1)}, bf16[8,192,512]{2,1,0:T(8,128)(2,1)}, u32[]{:S(2)}) copy-start(bf16[8,192,512]{2,1,0:T(8,128)(2,1)} %cache.1) | copy-start | bytes 4718596
  12.5 4.8 %copy-start.8 = (s32[8]{0:T(128)S(1)}, s32[8]{0:T(128)}, u32[]{:S(2)}) copy-start(s32[8]{0:T(128)} %lengths.1) | copy-start | bytes 100
  12.5 4.8 %collective-permute-start.6 = (bf16[4,80,128]{2,1,0:T(8,128)(2,1)S(1)}, bf16[4,80,128]{2,1,0:T(8,128)(2,1)S(1)}, u32[]{:S(2)}, u32[]{:S(2)}) collective-permute-start(bf16[4,80,128]{2,1,0:T(8,128)(2,1)S(1)} %get-tuple-element.28), channel_id=1, source_target_pairs={{0,4},{1,5},{2,6},{3,7},{4,0},{5,1},{6,2},{7,3},{8,12},{9,13},{10,... | collective-permute-start | bytes 245768 | tf_op jit(solution)/shard_map/ppermute | solution.py:73
  14.9 2.4 %collective-permute-start.7 = (bf16[9,16,128]{2,1,0:T(8,128)(2,1)S(1)}, bf16[9,16,128]{2,1,0:T(8,128)(2,1)S(1)}, u32[]{:S(2)}, u32[]{:S(2)}) collective-permute-start(bf16[9,16,128]{2,1,0:T(8,128)(2,1)S(1)} %get-tuple-element.27.after.mine), channel_id=1, source_target_pairs={{0,1},{1,0},{2,3},{3,2},{4,5},{5,4},{6,7},{7,6},{8,9},{9,8},{10,11... | collective-permute-start | bytes 110600 | tf_op jit(solution)/shard_map/ppermute | solution.py:73
  15.0 3.8 %copy-start.9 = (s32[1,8]{1,0:T(1,128)S(1)}, s32[1,8]{1,0:T(1,128)}, u32[]{:S(2)}) copy-start(s32[1,8]{1,0:T(1,128)} %choice.1) | copy-start | bytes 100
  15.0 3.8 %copy-start.10 = (f32[1,8]{1,0:T(1,128)S(1)}, f32[1,8]{1,0:T(1,128)}, u32[]{:S(2)}) copy-start(f32[1,8]{1,0:T(1,128)} %probability.1) | copy-start | bytes 100
  15.0 8.7 %collective-permute-start.5 = (bf16[4,80,128]{2,1,0:T(8,128)(2,1)S(1)}, bf16[4,80,128]{2,1,0:T(8,128)(2,1)S(1)}, u32[]{:S(2)}, u32[]{:S(2)}) collective-permute-start(bf16[4,80,128]{2,1,0:T(8,128)(2,1)S(1)} %shard_map.134), channel_id=1, source_target_pairs={{0,8},{1,9},{2,10},{3,11},{4,12},{5,13},{6,14},{7,15},{8,0},{9,1},... | collective-permute-start | bytes 245768 | tf_op jit(solution)/shard_map/ppermute | solution.py:73
  18.5 1.3 %collective-permute-start.8 = (bf16[9,16,128]{2,1,0:T(8,128)(2,1)S(1)}, bf16[9,16,128]{2,1,0:T(8,128)(2,1)S(1)}, u32[]{:S(2)}, u32[]{:S(2)}) collective-permute-start(bf16[9,16,128]{2,1,0:T(8,128)(2,1)S(1)} %get-tuple-element.30), channel_id=1, source_target_pairs={{0,1},{1,0},{2,3},{3,2},{4,5},{5,4},{6,7},{7,6},{8,9},{9,8},{10,11... | collective-permute-start | bytes 110600 | tf_op jit(solution)/shard_map/ppermute | solution.py:73
  20.0 4.0 %collective-permute-start.9 = (bf16[9,16,128]{2,1,0:T(8,128)(2,1)S(1)}, bf16[9,16,128]{2,1,0:T(8,128)(2,1)S(1)}, u32[]{:S(2)}, u32[]{:S(2)}) collective-permute-start(bf16[9,16,128]{2,1,0:T(8,128)(2,1)S(1)} %shard_map.137.mine.after), channel_id=1, source_target_pairs={{0,2},{1,3},{2,0},{3,1},{4,6},{5,7},{6,4},{7,5},{8,10},{9,11},{10,... | collective-permute-start | bytes 110600 | tf_op jit(solution)/shard_map/ppermute | solution.py:73
  21.6 6.7 %collective-permute-start.10 = (bf16[4,80,128]{2,1,0:T(8,128)(2,1)S(1)}, bf16[4,80,128]{2,1,0:T(8,128)(2,1)S(1)}, u32[]{:S(2)}, u32[]{:S(2)}) collective-permute-start(bf16[4,80,128]{2,1,0:T(8,128)(2,1)S(1)} %shard_map.139), channel_id=1, source_target_pairs={{0,12},{1,13},{2,14},{3,15},{4,8},{5,9},{6,10},{7,11},{8,4},{9,5},... | collective-permute-start | bytes 245768 | tf_op jit(solution)/shard_map/ppermute | solution.py:73
  24.3 5.6 %collective-permute-start.11 = (bf16[9,16,128]{2,1,0:T(8,128)(2,1)S(1)}, bf16[9,16,128]{2,1,0:T(8,128)(2,1)S(1)}, u32[]{:S(2)}, u32[]{:S(2)}) collective-permute-start(bf16[9,16,128]{2,1,0:T(8,128)(2,1)S(1)} %shard_map.138.after.mine), channel_id=1, source_target_pairs={{0,4},{1,5},{2,6},{3,7},{4,0},{5,1},{6,2},{7,3},{8,12},{9,13},{10,... | collective-permute-start | bytes 110600 | tf_op jit(solution)/shard_map/ppermute | solution.py:73
  28.3 6.9 %copy-start.6 = (f32[2048]{0:T(1024)S(1)}, f32[2048]{0:T(1024)}, u32[]{:S(2)}) copy-start(f32[2048]{0:T(1024)} %param.18) | copy-start | bytes 24580
  28.3 8.5 %copy-start = (bf16[1,2048,768]{2,1,0:T(8,128)(2,1)S(1)}, bf16[1,2048,768]{2,1,0:T(8,128)(2,1)}, u32[]{:S(2)}) copy-start(bf16[1,2048,768]{2,1,0:T(8,128)(2,1)} %param.21) | copy-start | bytes 9437188
  28.3 8.5 %copy-start.1 = (bf16[1,2048,768]{2,1,0:T(8,128)(2,1)S(1)}, bf16[1,2048,768]{2,1,0:T(8,128)(2,1)}, u32[]{:S(2)}) copy-start(bf16[1,2048,768]{2,1,0:T(8,128)(2,1)} %param.22) | copy-start | bytes 9437188
  28.3 8.5 %copy-start.2 = (bf16[1,768,2048]{2,1,0:T(8,128)(2,1)S(1)}, bf16[1,768,2048]{2,1,0:T(8,128)(2,1)}, u32[]{:S(2)}) copy-start(bf16[1,768,2048]{2,1,0:T(8,128)(2,1)} %param.23) | copy-start | bytes 9437188
  28.3 8.2 %collective-permute-start.14 = (bf16[16,80,128]{2,1,0:T(8,128)(2,1)S(1)}, bf16[16,80,128]{2,1,0:T(8,128)(2,1)S(1)}, u32[]{:S(2)}, u32[]{:S(2)}) collective-permute-start(bf16[16,80,128]{2,1,0:T(8,128)(2,1)S(1)} %shard_map.140.after.mine), channel_id=1, source_target_pairs={{0,16},{16,0},{1,17},{17,1},{2,18},{18,2},{3,19},{19,3},{4,20},{20... | collective-permute-start | bytes 983048 | tf_op jit(solution)/shard_map/ppermute | solution.py:459
  30.2 4.9 %collective-permute-start.12 = (bf16[9,16,128]{2,1,0:T(8,128)(2,1)S(1)}, bf16[9,16,128]{2,1,0:T(8,128)(2,1)S(1)}, u32[]{:S(2)}, u32[]{:S(2)}) collective-permute-start(bf16[9,16,128]{2,1,0:T(8,128)(2,1)S(1)} %shard_map.141.mine), channel_id=1, source_target_pairs={{0,8},{1,9},{2,10},{3,11},{4,12},{5,13},{6,14},{7,15},{8,0},{9,1},... | collective-permute-start | bytes 110600 | tf_op jit(solution)/shard_map/ppermute | solution.py:73
  35.5 1.3 %collective-permute-start.13 = (bf16[8,16,128]{2,1,0:T(8,128)(2,1)S(1)}, bf16[8,16,128]{2,1,0:T(8,128)(2,1)S(1)}, u32[]{:S(2)}, u32[]{:S(2)}) collective-permute-start(bf16[8,16,128]{2,1,0:T(8,128)(2,1)S(1)} %get-tuple-element.34.mine), channel_id=1, source_target_pairs={{0,1},{1,0},{2,3},{3,2},{4,5},{5,4},{6,7},{7,6},{8,9},{9,8},{10,11... | collective-permute-start | bytes 98312 | tf_op jit(solution)/shard_map/ppermute | solution.py:73

commit v16 on v15

--- a/solution.py
+++ b/solution.py
@@ -429,8 +429,9 @@
 
 
 def lora_far_start(turned, n, after):
-    arrived = [turned[0], swap(turned[1], n, NEAR)]
-    for j in range(2, len(turned) - 1):
+    most = len(turned) - 1
+    arrived = [turned[0], swap(turned[most], n, most * NEAR)]
+    for j in range(most - 1, 1, -1):
         arrived.append(swap(hold(turned[j], after), n, j * NEAR))
     return arrived
 
@@ -548,10 +549,9 @@
         )
         if distance == 2 and not whole:
             after = arrived[-1]
-            last = hold(turned[-1], keep)
-            arrived.append(swap(last, n, n - NEAR))
+            arrived.append(swap(hold(turned[1], keep), n, NEAR))
         if distance == n // 4:
-            after = turned[0] if whole else lora_order(arrived, n, keep)
+            after = turned[0] if whole else lora_order([arrived[0]] + arrived[:0:-1], n, keep)
         theirs = swap(keep, n, distance)
         flip = slots // distance
         distance *= 2

time: 51.5 us -> 53.3 us (1.035)
  starting transfers between devices: 20.9 us -> 23.3 us
  waiting for transfers between devices: 12 us -> 11.3 us
    ppermute x14, starting transfers between devices: 19.3 us -> 21.8 us  [swap(): return lax.ppermute(value, 'exp', [(t, t ^ distance) for t in range(n)])]
    ppermute x14, waiting for transfers between devices: 11 us -> 9.68 us  [swap(): return lax.ppermute(value, 'exp', [(t, t ^ distance) for t in range(n)])]
    ppermute x1, waiting for transfers between devices: 0.96 us -> 1.6 us  [lora_join(): lax.ppermute(ordered, 'grp', [(0, 1), (1, 0)])]
  transfers between devices with their start and end apart: 15 -> 15, of which waited for: 8 -> 7; matrix products, arithmetic and copies ran while one was open for 0% -> 0% of each run, Pallas kernels for 6% -> 5%
where the time goes in v16:
time: 53.3 us; the launch traced here: 53 us
  starting transfers between devices  23.3 us (44%)
  waiting for transfers between devices  11.3 us (21%)
  blocking collectives  11 us (21%)
  Pallas kernels  7.09 us (13%)
    ppermute x14, starting transfers between devices, swap(): return lax.ppermute(value, 'exp', [(t, t ^ distance) for t in range(n)])  21.8 us
    all_to_all x1, blocking collectives, body(): lax.all_to_all(out, 'exp', split_axis=0, concat_axis=0, tiled=True)  11 us
    ppermute x14, waiting for transfers between devices, swap(): return lax.ppermute(value, 'exp', [(t, t ^ distance) for t in range(n)])  9.68 us
    pallas_call x19, Pallas kernels, call(): pl.pallas_call(kernel, out_shape=shapes, in_specs=specs, out_specs=jax.tr...  7.09 us
    ppermute x1, waiting for transfers between devices, lora_join(): lax.ppermute(ordered, 'grp', [(0, 1), (1, 0)])  1.6 us
    ppermute x1, starting transfers between devices, lora_join(): lax.ppermute(ordered, 'grp', [(0, 1), (1, 0)])  1.56 us
  transfers between devices with their start and end apart: 15, of which 7 were waited for; matrix products, arithmetic and copies ran while one was open for 0% of the time, Pallas kernels for 5%

profile of v16, /device:TPU:0, one launch (start us, length us, event | category | flops | bytes accessed | tf_op | source)
XLA Modules:
  0.0 53.0 jit_solution(17715634757324770382)
XLA Ops:
  0.0 0.8 %shard_map.127.mine.after = bf16[1,32,128]{2,1,0:T(8,128)(2,1)S(1)} custom-call(bf16[1,2048]{1,0:T(2,128)(2,1)} %query.1, bf16[1,2048]{1,0:T(2,128)(2,1)} %resid.1), custom_call_target="tpu_custom_call" | custom-call | flops 4000000000 | tf_op jit(solution)/shard_map/pallas_call | solution.py:39
  0.8 4.1 %collective-permute-start = (bf16[1,32,128]{2,1,0:T(8,128)(2,1)S(1)}, bf16[1,32,128]{2,1,0:T(8,128)(2,1)S(1)}, u32[]{:S(2)}, u32[]{:S(2)}) collective-permute-start(bf16[1,32,128]{2,1,0:T(8,128)(2,1)S(1)} %shard_map.127.mine.after), channel_id=1, source_target_pairs={{0,8},{1,9},{2,10},{3,11},{4,12},{5,13},{6,14},{7,15},{8,0},{9,1},... | collective-permute-start | bytes 24584 | tf_op jit(solution)/shard_map/ppermute | solution.py:73
  4.9 0.1 shard_map.130
  5.0 1.6 %collective-permute-start.2 = (bf16[8,80,128]{2,1,0:T(8,128)(2,1)S(1)}, bf16[8,80,128]{2,1,0:T(8,128)(2,1)S(1)}, u32[]{:S(2)}, u32[]{:S(2)}) collective-permute-start(bf16[8,80,128]{2,1,0:T(8,128)(2,1)S(1)} %get-tuple-element.22), channel_id=1, source_target_pairs={{0,2},{1,3},{2,0},{3,1},{4,6},{5,7},{6,4},{7,5},{8,10},{9,11},{10,... | collective-permute-start | bytes 491528 | tf_op jit(solution)/shard_map/ppermute | solution.py:73
  6.6 0.0 collective-permute-done.theirs
  6.6 1.8 %collective-permute-start.1 = (bf16[2,32,128]{2,1,0:T(8,128)(2,1)S(1)}, bf16[2,32,128]{2,1,0:T(8,128)(2,1)S(1)}, u32[]{:S(2)}, u32[]{:S(2)}) collective-permute-start(bf16[2,32,128]{2,1,0:T(8,128)(2,1)S(1)} %shard_map.128.mine.after), channel_id=1, source_target_pairs={{0,4},{1,5},{2,6},{3,7},{4,0},{5,1},{6,2},{7,3},{8,12},{9,13},{10,... | collective-permute-start | bytes 49160 | tf_op jit(solution)/shard_map/ppermute | solution.py:73
  8.5 2.3 %collective-permute-done.2.got = bf16[8,80,128]{2,1,0:T(8,128)(2,1)S(1)} collective-permute-done((bf16[8,80,128]{2,1,0:T(8,128)(2,1)S(1)}, bf16[8,80,128]{2,1,0:T(8,128)(2,1)S(1)}, u32[]{:S(2)}, u32[]{:S(2)}) %collective-permute-start.2) | collective-permute-done | bytes 163872 | tf_op jit(solution)/shard_map/ppermute | solution.py:73
  10.8 0.0 copy-start.7
  10.8 0.1 collective-permute-start.3
  10.9 0.0 collective-permute-done.1.theirs
  10.9 1.6 %collective-permute-start.4 = (bf16[4,32,128]{2,1,0:T(8,128)(2,1)S(1)}, bf16[4,32,128]{2,1,0:T(8,128)(2,1)S(1)}, u32[]{:S(2)}, u32[]{:S(2)}) collective-permute-start(bf16[4,32,128]{2,1,0:T(8,128)(2,1)S(1)} %shard_map.129.after.mine), channel_id=1, source_target_pairs={{0,2},{1,3},{2,0},{3,1},{4,6},{5,7},{6,4},{7,5},{8,10},{9,11},{10,... | collective-permute-start | bytes 98312 | tf_op jit(solution)/shard_map/ppermute | solution.py:73
  12.5 0.0 copy-start.5
  12.5 0.0 copy-start.8
  12.5 3.3 %collective-permute-start.6 = (bf16[4,80,128]{2,1,0:T(8,128)(2,1)S(1)}, bf16[4,80,128]{2,1,0:T(8,128)(2,1)S(1)}, u32[]{:S(2)}, u32[]{:S(2)}) collective-permute-start(bf16[4,80,128]{2,1,0:T(8,128)(2,1)S(1)} %get-tuple-element.28), channel_id=1, source_target_pairs={{0,12},{1,13},{2,14},{3,15},{4,8},{5,9},{6,10},{7,11},{8,4},{9,5},... | collective-permute-start | bytes 245768 | tf_op jit(solution)/shard_map/ppermute | solution.py:73
  15.9 0.1 collective-permute-start.7
  16.0 0.0 copy-start.9
  16.0 0.0 copy-start.10
  16.0 1.3 %collective-permute-start.5 = (bf16[4,80,128]{2,1,0:T(8,128)(2,1)S(1)}, bf16[4,80,128]{2,1,0:T(8,128)(2,1)S(1)}, u32[]{:S(2)}, u32[]{:S(2)}) collective-permute-start(bf16[4,80,128]{2,1,0:T(8,128)(2,1)S(1)} %shard_map.134), channel_id=1, source_target_pairs={{0,8},{1,9},{2,10},{3,11},{4,12},{5,13},{6,14},{7,15},{8,0},{9,1},... | collective-permute-start | bytes 245768 | tf_op jit(solution)/shard_map/ppermute | solution.py:73
  17.3 0.0 collective-permute-done.7.theirs
  17.3 1.7 %collective-permute-done.6.after.refs_3_ = bf16[4,80,128]{2,1,0:T(8,128)(2,1)S(1)} collective-permute-done((bf16[4,80,128]{2,1,0:T(8,128)(2,1)S(1)}, bf16[4,80,128]{2,1,0:T(8,128)(2,1)S(1)}, u32[]{:S(2)}, u32[]{:S(2)}) %collective-permute-start.6) | collective-permute-done | bytes 81952 | tf_op jit(solution)/shard_map/ppermute | solution.py:73
  19.0 1.2 %shard_map.135 = (bf16[9,16,128]{2,1,0:T(8,128)(2,1)S(1)}, bf16[9,16,128]{2,1,0:T(8,128)(2,1)S(1)}) custom-call(bf16[4,80,128]{2,1,0:T(8,128)(2,1)S(1)} %collective-permute-done.6.after.refs_3_, s32[8]{0:T(128)S(1)} %copy-done.8, bf16[9,16,128]{2,1,0:T(8,128)(2,1)S(1)} %get-tuple-element.27.after.mine, ...), custom_call_target="tpu_custom_call" | custom-call | flops 8000000000 | tf_op jit(solution)/shard_map/pallas_call | solution.py:39
  20.2 0.1 collective-permute-start.8
  20.3 0.2 shard_map.136.after.gates
  20.5 1.0 %collective-permute-done.8.theirs = bf16[9,16,128]{2,1,0:T(8,128)(2,1)S(1)} collective-permute-done((bf16[9,16,128]{2,1,0:T(8,128)(2,1)S(1)}, bf16[9,16,128]{2,1,0:T(8,128)(2,1)S(1)}, u32[]{:S(2)}, u32[]{:S(2)}) %collective-permute-start.8) | collective-permute-done | bytes 36896 | tf_op jit(solution)/shard_map/ppermute | solution.py:73
  21.5 0.2 shard_map.137.mine.after
  21.7 1.3 %collective-permute-start.9 = (bf16[9,16,128]{2,1,0:T(8,128)(2,1)S(1)}, bf16[9,16,128]{2,1,0:T(8,128)(2,1)S(1)}, u32[]{:S(2)}, u32[]{:S(2)}) collective-permute-start(bf16[9,16,128]{2,1,0:T(8,128)(2,1)S(1)} %shard_map.137.mine.after), channel_id=1, source_target_pairs={{0,2},{1,3},{2,0},{3,1},{4,6},{5,7},{6,4},{7,5},{8,10},{9,11},{10,... | collective-permute-start | bytes 110600 | tf_op jit(solution)/shard_map/ppermute | solution.py:73
  23.0 3.8 %collective-permute-start.10 = (bf16[4,80,128]{2,1,0:T(8,128)(2,1)S(1)}, bf16[4,80,128]{2,1,0:T(8,128)(2,1)S(1)}, u32[]{:S(2)}, u32[]{:S(2)}) collective-permute-start(bf16[4,80,128]{2,1,0:T(8,128)(2,1)S(1)} %shard_map.139), channel_id=1, source_target_pairs={{0,4},{1,5},{2,6},{3,7},{4,0},{5,1},{6,2},{7,3},{8,12},{9,13},{10,... | collective-permute-start | bytes 245768 | tf_op jit(solution)/shard_map/ppermute | solution.py:73
  26.8 0.0 collective-permute-done.5.after.refs_2_
  26.8 0.0 collective-permute-done.9.theirs
  26.8 0.3 shard_map.138.after.mine
  27.1 2.0 %collective-permute-start.11 = (bf16[9,16,128]{2,1,0:T(8,128)(2,1)S(1)}, bf16[9,16,128]{2,1,0:T(8,128)(2,1)S(1)}, u32[]{:S(2)}, u32[]{:S(2)}) collective-permute-start(bf16[9,16,128]{2,1,0:T(8,128)(2,1)S(1)} %shard_map.138.after.mine), channel_id=1, source_target_pairs={{0,4},{1,5},{2,6},{3,7},{4,0},{5,1},{6,2},{7,3},{8,12},{9,13},{10,... | collective-permute-start | bytes 110600 | tf_op jit(solution)/shard_map/ppermute | solution.py:73
  29.1 0.2 collective-permute-done.10.refs_1_
  29.3 0.0 copy-start
  29.3 0.0 copy-start.1
  29.3 0.0 copy-start.2
  29.3 1.6 %collective-permute-start.14 = (bf16[16,80,128]{2,1,0:T(8,128)(2,1)S(1)}, bf16[16,80,128]{2,1,0:T(8,128)(2,1)S(1)}, u32[]{:S(2)}, u32[]{:S(2)}) collective-permute-start(bf16[16,80,128]{2,1,0:T(8,128)(2,1)S(1)} %shard_map.140.after.mine), channel_id=1, source_target_pairs={{0,16},{16,0},{1,17},{17,1},{2,18},{18,2},{3,19},{19,3},{4,20},{20... | collective-permute-start | bytes 983048 | tf_op jit(solution)/shard_map/ppermute | solution.py:460
  30.9 0.2 collective-permute-done.11.theirs
  31.1 0.3 shard_map.141.mine
  31.4 0.6 %collective-permute-start.12 = (bf16[9,16,128]{2,1,0:T(8,128)(2,1)S(1)}, bf16[9,16,128]{2,1,0:T(8,128)(2,1)S(1)}, u32[]{:S(2)}, u32[]{:S(2)}) collective-permute-start(bf16[9,16,128]{2,1,0:T(8,128)(2,1)S(1)} %shard_map.141.mine), channel_id=1, source_target_pairs={{0,8},{1,9},{2,10},{3,11},{4,12},{5,13},{6,14},{7,15},{8,0},{9,1},... | collective-permute-start | bytes 110600 | tf_op jit(solution)/shard_map/ppermute | solution.py:73
  32.0 4.3 %collective-permute-done.12.theirs = bf16[9,16,128]{2,1,0:T(8,128)(2,1)S(1)} collective-permute-done((bf16[9,16,128]{2,1,0:T(8,128)(2,1)S(1)}, bf16[9,16,128]{2,1,0:T(8,128)(2,1)S(1)}, u32[]{:S(2)}, u32[]{:S(2)}) %collective-permute-start.12) | collective-permute-done | bytes 36896 | tf_op jit(solution)/shard_map/ppermute | solution.py:73
  36.3 0.4 shard_map.142
  36.7 0.1 collective-permute-start.13
  36.8 1.6 %collective-permute-done.14.theirs = bf16[16,80,128]{2,1,0:T(8,128)(2,1)S(1)} collective-permute-done((bf16[16,80,128]{2,1,0:T(8,128)(2,1)S(1)}, bf16[16,80,128]{2,1,0:T(8,128)(2,1)S(1)}, u32[]{:S(2)}, u32[]{:S(2)}) %collective-permute-start.14) | collective-permute-done | bytes 327712 | tf_op jit(solution)/shard_map/ppermute | solution.py:460
  38.4 0.1 shard_map.143
  38.5 0.0 collective-permute-done.13.theirs
  38.5 2.8 %shard_map.144 = bf16[16,16,128]{2,1,0:T(8,128)(2,1)S(1)} custom-call(bf16[8,16,128]{2,1,0:T(8,128)(2,1)S(1)} %get-tuple-element.34.mine, bf16[8,16,128]{2,1,0:T(8,128)(2,1)S(1)} %collective-permute-done.13.theirs, bf16[2048,768]{1,0:T(8,128)(2,1)S(1)} %bitcast.5, bf16[2048,768]{1,0:T(8,128)(2,1)S(1)} %bitcast.6, bf16[768,2048]{1,0:T(8,128)(2,1)S(1)} %bitcast.7, ...), custom_call_target="tpu_custom_call" | custom-call | flops 1600000000 | tf_op jit(solution)/shard_map/pallas_call | solution.py:39
  41.3 11.0 %all_to_all.5.got = bf16[16,16,128]{2,1,0:T(8,128)(2,1)S(1)} all-to-all(bf16[16,16,128]{2,1,0:T(8,128)(2,1)S(1)} %shard_map.144), channel_id=1, replica_groups=mesh['grp'=2,'exp'=16] {'exp'}, dimensions={0} | all-to-all | bytes 131072 | tf_op jit(solution)/shard_map/all_to_all | solution.py:588
  52.3 0.7 %shard_map.145 = bf16[1,2048]{1,0:T(2,128)(2,1)} custom-call(f32[16,128]{1,0:T(8,128)S(1)} %get-tuple-element.33.hidden, bf16[16,16,128]{2,1,0:T(8,128)(2,1)S(1)} %all_to_all.5.got, f32[1,128]{1,0:T(1,128)S(1)} %shard_map.136.after.gates), custom_call_target="tpu_custom_call" | custom-call | flops 1600000000 | tf_op jit(solution)/shard_map/pallas_call | solution.py:39
  (24 shorter events, 0.1 us)
Async XLA Ops:
  0.0 4.9 %copy-start.4 = (bf16[16,96,48]{1,2,0:T(8,128)(2,1)S(1)}, bf16[16,96,48]{1,2,0:T(8,128)(2,1)}, u32[]{:S(2)}) copy-start(bf16[16,96,48]{1,2,0:T(8,128)(2,1)} %param.25) | copy-start | bytes 442372
  0.0 4.9 %copy-start.3 = (bf16[16,96,128]{2,1,0:T(8,128)(2,1)S(1)}, bf16[16,96,128]{2,1,0:T(8,128)(2,1)}, u32[]{:S(2)}) copy-start(bf16[16,96,128]{2,1,0:T(8,128)(2,1)} %model.1) | copy-start | bytes 1179652
  0.8 5.8 %collective-permute-start = (bf16[1,32,128]{2,1,0:T(8,128)(2,1)S(1)}, bf16[1,32,128]{2,1,0:T(8,128)(2,1)S(1)}, u32[]{:S(2)}, u32[]{:S(2)}) collective-permute-start(bf16[1,32,128]{2,1,0:T(8,128)(2,1)S(1)} %shard_map.127.mine.after), channel_id=1, source_target_pairs={{0,8},{1,9},{2,10},{3,11},{4,12},{5,13},{6,14},{7,15},{8,0},{9,1},... | collective-permute-start | bytes 24584 | tf_op jit(solution)/shard_map/ppermute | solution.py:73
  5.0 5.7 %collective-permute-start.2 = (bf16[8,80,128]{2,1,0:T(8,128)(2,1)S(1)}, bf16[8,80,128]{2,1,0:T(8,128)(2,1)S(1)}, u32[]{:S(2)}, u32[]{:S(2)}) collective-permute-start(bf16[8,80,128]{2,1,0:T(8,128)(2,1)S(1)} %get-tuple-element.22), channel_id=1, source_target_pairs={{0,2},{1,3},{2,0},{3,1},{4,6},{5,7},{6,4},{7,5},{8,10},{9,11},{10,... | collective-permute-start | bytes 491528 | tf_op jit(solution)/shard_map/ppermute | solution.py:73
  6.6 4.3 %collective-permute-start.1 = (bf16[2,32,128]{2,1,0:T(8,128)(2,1)S(1)}, bf16[2,32,128]{2,1,0:T(8,128)(2,1)S(1)}, u32[]{:S(2)}, u32[]{:S(2)}) collective-permute-start(bf16[2,32,128]{2,1,0:T(8,128)(2,1)S(1)} %shard_map.128.mine.after), channel_id=1, source_target_pairs={{0,4},{1,5},{2,6},{3,7},{4,0},{5,1},{6,2},{7,3},{8,12},{9,13},{10,... | collective-permute-start | bytes 49160 | tf_op jit(solution)/shard_map/ppermute | solution.py:73
  10.8 5.1 %copy-start.7 = (bf16[1,512]{1,0:T(2,128)(2,1)S(1)}, bf16[1,512]{1,0:T(2,128)(2,1)}, u32[]{:S(2)}) copy-start(bf16[1,512]{1,0:T(2,128)(2,1)} %new.1) | copy-start | bytes 3076
  10.8 1.7 %collective-permute-start.3 = (bf16[8,80,128]{2,1,0:T(8,128)(2,1)S(1)}, bf16[8,80,128]{2,1,0:T(8,128)(2,1)S(1)}, u32[]{:S(2)}, u32[]{:S(2)}) collective-permute-start(bf16[8,80,128]{2,1,0:T(8,128)(2,1)S(1)} %get-tuple-element.24), channel_id=1, source_target_pairs={{0,1},{1,0},{2,3},{3,2},{4,5},{5,4},{6,7},{7,6},{8,9},{9,8},{10,11... | collective-permute-start | bytes 491528 | tf_op jit(solution)/shard_map/ppermute | solution.py:73
  10.9 5.0 %collective-permute-start.4 = (bf16[4,32,128]{2,1,0:T(8,128)(2,1)S(1)}, bf16[4,32,128]{2,1,0:T(8,128)(2,1)S(1)}, u32[]{:S(2)}, u32[]{:S(2)}) collective-permute-start(bf16[4,32,128]{2,1,0:T(8,128)(2,1)S(1)} %shard_map.129.after.mine), channel_id=1, source_target_pairs={{0,2},{1,3},{2,0},{3,1},{4,6},{5,7},{6,4},{7,5},{8,10},{9,11},{10,... | collective-permute-start | bytes 98312 | tf_op jit(solution)/shard_map/ppermute | solution.py:73
  12.5 6.5 %copy-start.5 = (bf16[8,192,512]{2,1,0:T(8,128)(2,1)S(1)}, bf16[8,192,512]{2,1,0:T(8,128)(2,1)}, u32[]{:S(2)}) copy-start(bf16[8,192,512]{2,1,0:T(8,128)(2,1)} %cache.1) | copy-start | bytes 4718596
  12.5 6.5 %copy-start.8 = (s32[8]{0:T(128)S(1)}, s32[8]{0:T(128)}, u32[]{:S(2)}) copy-start(s32[8]{0:T(128)} %lengths.1) | copy-start | bytes 100
  12.5 6.5 %collective-permute-start.6 = (bf16[4,80,128]{2,1,0:T(8,128)(2,1)S(1)}, bf16[4,80,128]{2,1,0:T(8,128)(2,1)S(1)}, u32[]{:S(2)}, u32[]{:S(2)}) collective-permute-start(bf16[4,80,128]{2,1,0:T(8,128)(2,1)S(1)} %get-tuple-element.28), channel_id=1, source_target_pairs={{0,12},{1,13},{2,14},{3,15},{4,8},{5,9},{6,10},{7,11},{8,4},{9,5},... | collective-permute-start | bytes 245768 | tf_op jit(solution)/shard_map/ppermute | solution.py:73
  15.9 1.4 %collective-permute-start.7 = (bf16[9,16,128]{2,1,0:T(8,128)(2,1)S(1)}, bf16[9,16,128]{2,1,0:T(8,128)(2,1)S(1)}, u32[]{:S(2)}, u32[]{:S(2)}) collective-permute-start(bf16[9,16,128]{2,1,0:T(8,128)(2,1)S(1)} %get-tuple-element.27.after.mine), channel_id=1, source_target_pairs={{0,1},{1,0},{2,3},{3,2},{4,5},{5,4},{6,7},{7,6},{8,9},{9,8},{10,11... | collective-permute-start | bytes 110600 | tf_op jit(solution)/shard_map/ppermute | solution.py:73
  16.0 4.3 %copy-start.9 = (s32[1,8]{1,0:T(1,128)S(1)}, s32[1,8]{1,0:T(1,128)}, u32[]{:S(2)}) copy-start(s32[1,8]{1,0:T(1,128)} %choice.1) | copy-start | bytes 100
  16.0 4.3 %copy-start.10 = (f32[1,8]{1,0:T(1,128)S(1)}, f32[1,8]{1,0:T(1,128)}, u32[]{:S(2)}) copy-start(f32[1,8]{1,0:T(1,128)} %probability.1) | copy-start | bytes 100
  16.0 10.8 %collective-permute-start.5 = (bf16[4,80,128]{2,1,0:T(8,128)(2,1)S(1)}, bf16[4,80,128]{2,1,0:T(8,128)(2,1)S(1)}, u32[]{:S(2)}, u32[]{:S(2)}) collective-permute-start(bf16[4,80,128]{2,1,0:T(8,128)(2,1)S(1)} %shard_map.134), channel_id=1, source_target_pairs={{0,8},{1,9},{2,10},{3,11},{4,12},{5,13},{6,14},{7,15},{8,0},{9,1},... | collective-permute-start | bytes 245768 | tf_op jit(solution)/shard_map/ppermute | solution.py:73
  20.2 1.3 %collective-permute-start.8 = (bf16[9,16,128]{2,1,0:T(8,128)(2,1)S(1)}, bf16[9,16,128]{2,1,0:T(8,128)(2,1)S(1)}, u32[]{:S(2)}, u32[]{:S(2)}) collective-permute-start(bf16[9,16,128]{2,1,0:T(8,128)(2,1)S(1)} %get-tuple-element.30), channel_id=1, source_target_pairs={{0,1},{1,0},{2,3},{3,2},{4,5},{5,4},{6,7},{7,6},{8,9},{9,8},{10,11... | collective-permute-start | bytes 110600 | tf_op jit(solution)/shard_map/ppermute | solution.py:73
  21.7 5.1 %collective-permute-start.9 = (bf16[9,16,128]{2,1,0:T(8,128)(2,1)S(1)}, bf16[9,16,128]{2,1,0:T(8,128)(2,1)S(1)}, u32[]{:S(2)}, u32[]{:S(2)}) collective-permute-start(bf16[9,16,128]{2,1,0:T(8,128)(2,1)S(1)} %shard_map.137.mine.after), channel_id=1, source_target_pairs={{0,2},{1,3},{2,0},{3,1},{4,6},{5,7},{6,4},{7,5},{8,10},{9,11},{10,... | collective-permute-start | bytes 110600 | tf_op jit(solution)/shard_map/ppermute | solution.py:73
  23.0 6.2 %collective-permute-start.10 = (bf16[4,80,128]{2,1,0:T(8,128)(2,1)S(1)}, bf16[4,80,128]{2,1,0:T(8,128)(2,1)S(1)}, u32[]{:S(2)}, u32[]{:S(2)}) collective-permute-start(bf16[4,80,128]{2,1,0:T(8,128)(2,1)S(1)} %shard_map.139), channel_id=1, source_target_pairs={{0,4},{1,5},{2,6},{3,7},{4,0},{5,1},{6,2},{7,3},{8,12},{9,13},{10,... | collective-permute-start | bytes 245768 | tf_op jit(solution)/shard_map/ppermute | solution.py:73
  27.1 4.0 %collective-permute-start.11 = (bf16[9,16,128]{2,1,0:T(8,128)(2,1)S(1)}, bf16[9,16,128]{2,1,0:T(8,128)(2,1)S(1)}, u32[]{:S(2)}, u32[]{:S(2)}) collective-permute-start(bf16[9,16,128]{2,1,0:T(8,128)(2,1)S(1)} %shard_map.138.after.mine), channel_id=1, source_target_pairs={{0,4},{1,5},{2,6},{3,7},{4,0},{5,1},{6,2},{7,3},{8,12},{9,13},{10,... | collective-permute-start | bytes 110600 | tf_op jit(solution)/shard_map/ppermute | solution.py:73
  29.3 7.0 %copy-start.6 = (f32[2048]{0:T(1024)S(1)}, f32[2048]{0:T(1024)}, u32[]{:S(2)}) copy-start(f32[2048]{0:T(1024)} %param.18) | copy-start | bytes 24580
  29.3 9.2 %copy-start = (bf16[1,2048,768]{2,1,0:T(8,128)(2,1)S(1)}, bf16[1,2048,768]{2,1,0:T(8,128)(2,1)}, u32[]{:S(2)}) copy-start(bf16[1,2048,768]{2,1,0:T(8,128)(2,1)} %param.21) | copy-start | bytes 9437188
  29.3 9.2 %copy-start.1 = (bf16[1,2048,768]{2,1,0:T(8,128)(2,1)S(1)}, bf16[1,2048,768]{2,1,0:T(8,128)(2,1)}, u32[]{:S(2)}) copy-start(bf16[1,2048,768]{2,1,0:T(8,128)(2,1)} %param.22) | copy-start | bytes 9437188
  29.3 9.2 %copy-start.2 = (bf16[1,768,2048]{2,1,0:T(8,128)(2,1)S(1)}, bf16[1,768,2048]{2,1,0:T(8,128)(2,1)}, u32[]{:S(2)}) copy-start(bf16[1,768,2048]{2,1,0:T(8,128)(2,1)} %param.23) | copy-start | bytes 9437188
  29.3 9.0 %collective-permute-start.14 = (bf16[16,80,128]{2,1,0:T(8,128)(2,1)S(1)}, bf16[16,80,128]{2,1,0:T(8,128)(2,1)S(1)}, u32[]{:S(2)}, u32[]{:S(2)}) collective-permute-start(bf16[16,80,128]{2,1,0:T(8,128)(2,1)S(1)} %shard_map.140.after.mine), channel_id=1, source_target_pairs={{0,16},{16,0},{1,17},{17,1},{2,18},{18,2},{3,19},{19,3},{4,20},{20... | collective-permute-start | bytes 983048 | tf_op jit(solution)/shard_map/ppermute | solution.py:460
  31.4 4.9 %collective-permute-start.12 = (bf16[9,16,128]{2,1,0:T(8,128)(2,1)S(1)}, bf16[9,16,128]{2,1,0:T(8,128)(2,1)S(1)}, u32[]{:S(2)}, u32[]{:S(2)}) collective-permute-start(bf16[9,16,128]{2,1,0:T(8,128)(2,1)S(1)} %shard_map.141.mine), channel_id=1, source_target_pairs={{0,8},{1,9},{2,10},{3,11},{4,12},{5,13},{6,14},{7,15},{8,0},{9,1},... | collective-permute-start | bytes 110600 | tf_op jit(solution)/shard_map/ppermute | solution.py:73
  36.7 1.8 %collective-permute-start.13 = (bf16[8,16,128]{2,1,0:T(8,128)(2,1)S(1)}, bf16[8,16,128]{2,1,0:T(8,128)(2,1)S(1)}, u32[]{:S(2)}, u32[]{:S(2)}) collective-permute-start(bf16[8,16,128]{2,1,0:T(8,128)(2,1)S(1)} %get-tuple-element.34.mine), channel_id=1, source_target_pairs={{0,1},{1,0},{2,3},{3,2},{4,5},{5,4},{6,7},{7,6},{8,9},{9,8},{10,11... | collective-permute-start | bytes 98312 | tf_op jit(solution)/shard_map/ppermute | solution.py:73

commit v17 on v15

--- a/solution.py
+++ b/solution.py
@@ -279,15 +279,12 @@
 
 
 def dot_pair(value, factor, contract):
-    high = value.astype(bf16)
-    low = (value - high.astype(f32)).astype(bf16)
-    both = lax.dot_general(
-        jnp.concatenate([high, low], axis=0),
+    return lax.dot_general(
+        value.astype(bf16),
         factor,
         (((1,), (contract,)), ((), ())),
         preferred_element_type=f32,
     )
-    return both[: value.shape[0]] + both[value.shape[0] :]
 
 
 def expert_kernel(mine, theirs, gate_w, up_w, down_w, model, inner, out, *, far):

time: 51.5 us -> 51.4 us (level)
  no operation moved by 1% of the time
where the time goes in v17:
time: 51.4 us; the launch traced here: 51.2 us
  starting transfers between devices  20.9 us (41%)
  waiting for transfers between devices  12 us (23%)
  blocking collectives  11 us (21%)
  Pallas kernels  7.05 us (14%)
    ppermute x14, starting transfers between devices, swap(): return lax.ppermute(value, 'exp', [(t, t ^ distance) for t in range(n)])  19.3 us
    ppermute x14, waiting for transfers between devices, swap(): return lax.ppermute(value, 'exp', [(t, t ^ distance) for t in range(n)])  11 us
    all_to_all x1, blocking collectives, body(): lax.all_to_all(out, 'exp', split_axis=0, concat_axis=0, tiled=True)  11 us
    pallas_call x19, Pallas kernels, call(): pl.pallas_call(kernel, out_shape=shapes, in_specs=specs, out_specs=jax.tr...  7.05 us
    ppermute x1, starting transfers between devices, lora_join(): lax.ppermute(ordered, 'grp', [(0, 1), (1, 0)])  1.56 us
  transfers between devices with their start and end apart: 15, of which 8 were waited for; matrix products, arithmetic and copies ran while one was open for 0% of the time, Pallas kernels for 6%

profile of v17, /device:TPU:0, one launch (start us, length us, event | category | flops | bytes accessed | tf_op | source)
XLA Modules:
  0.0 51.2 jit_solution(6658720327554240496)
XLA Ops:
  0.0 0.8 %shard_map.127.mine.after = bf16[1,32,128]{2,1,0:T(8,128)(2,1)S(1)} custom-call(bf16[1,2048]{1,0:T(2,128)(2,1)} %query.1, bf16[1,2048]{1,0:T(2,128)(2,1)} %resid.1), custom_call_target="tpu_custom_call" | custom-call | flops 4000000000 | tf_op jit(solution)/shard_map/pallas_call | solution.py:39
  0.8 4.1 %collective-permute-start = (bf16[1,32,128]{2,1,0:T(8,128)(2,1)S(1)}, bf16[1,32,128]{2,1,0:T(8,128)(2,1)S(1)}, u32[]{:S(2)}, u32[]{:S(2)}) collective-permute-start(bf16[1,32,128]{2,1,0:T(8,128)(2,1)S(1)} %shard_map.127.mine.after), channel_id=1, source_target_pairs={{0,8},{1,9},{2,10},{3,11},{4,12},{5,13},{6,14},{7,15},{8,0},{9,1},... | collective-permute-start | bytes 24584 | tf_op jit(solution)/shard_map/ppermute | solution.py:73
  4.9 0.1 shard_map.130
  5.0 1.6 %collective-permute-start.2 = (bf16[8,80,128]{2,1,0:T(8,128)(2,1)S(1)}, bf16[8,80,128]{2,1,0:T(8,128)(2,1)S(1)}, u32[]{:S(2)}, u32[]{:S(2)}) collective-permute-start(bf16[8,80,128]{2,1,0:T(8,128)(2,1)S(1)} %get-tuple-element.22), channel_id=1, source_target_pairs={{0,2},{1,3},{2,0},{3,1},{4,6},{5,7},{6,4},{7,5},{8,10},{9,11},{10,... | collective-permute-start | bytes 491528 | tf_op jit(solution)/shard_map/ppermute | solution.py:73
  6.6 0.0 collective-permute-done.theirs
  6.6 1.8 %collective-permute-start.1 = (bf16[2,32,128]{2,1,0:T(8,128)(2,1)S(1)}, bf16[2,32,128]{2,1,0:T(8,128)(2,1)S(1)}, u32[]{:S(2)}, u32[]{:S(2)}) collective-permute-start(bf16[2,32,128]{2,1,0:T(8,128)(2,1)S(1)} %shard_map.128.mine.after), channel_id=1, source_target_pairs={{0,4},{1,5},{2,6},{3,7},{4,0},{5,1},{6,2},{7,3},{8,12},{9,13},{10,... | collective-permute-start | bytes 49160 | tf_op jit(solution)/shard_map/ppermute | solution.py:73
  8.5 2.3 %collective-permute-done.2.got = bf16[8,80,128]{2,1,0:T(8,128)(2,1)S(1)} collective-permute-done((bf16[8,80,128]{2,1,0:T(8,128)(2,1)S(1)}, bf16[8,80,128]{2,1,0:T(8,128)(2,1)S(1)}, u32[]{:S(2)}, u32[]{:S(2)}) %collective-permute-start.2) | collective-permute-done | bytes 163872 | tf_op jit(solution)/shard_map/ppermute | solution.py:73
  10.8 0.0 copy-start.7
  10.8 0.1 collective-permute-start.3
  10.9 0.0 collective-permute-done.1.theirs
  10.9 1.6 %collective-permute-start.4 = (bf16[4,32,128]{2,1,0:T(8,128)(2,1)S(1)}, bf16[4,32,128]{2,1,0:T(8,128)(2,1)S(1)}, u32[]{:S(2)}, u32[]{:S(2)}) collective-permute-start(bf16[4,32,128]{2,1,0:T(8,128)(2,1)S(1)} %shard_map.129.after.mine), channel_id=1, source_target_pairs={{0,2},{1,3},{2,0},{3,1},{4,6},{5,7},{6,4},{7,5},{8,10},{9,11},{10,... | collective-permute-start | bytes 98312 | tf_op jit(solution)/shard_map/ppermute | solution.py:73
  12.5 0.0 copy-start.5
  12.5 0.0 copy-start.8
  12.5 1.6 %collective-permute-start.6 = (bf16[4,80,128]{2,1,0:T(8,128)(2,1)S(1)}, bf16[4,80,128]{2,1,0:T(8,128)(2,1)S(1)}, u32[]{:S(2)}, u32[]{:S(2)}) collective-permute-start(bf16[4,80,128]{2,1,0:T(8,128)(2,1)S(1)} %get-tuple-element.28), channel_id=1, source_target_pairs={{0,4},{1,5},{2,6},{3,7},{4,0},{5,1},{6,2},{7,3},{8,12},{9,13},{10,... | collective-permute-start | bytes 245768 | tf_op jit(solution)/shard_map/ppermute | solution.py:73
  14.2 0.7 %collective-permute-done.4.theirs = bf16[4,32,128]{2,1,0:T(8,128)(2,1)S(1)} collective-permute-done((bf16[4,32,128]{2,1,0:T(8,128)(2,1)S(1)}, bf16[4,32,128]{2,1,0:T(8,128)(2,1)S(1)}, u32[]{:S(2)}, u32[]{:S(2)}) %collective-permute-start.4) | collective-permute-done | bytes 32800 | tf_op jit(solution)/shard_map/ppermute | solution.py:73
  14.9 0.1 collective-permute-start.7
  15.0 0.0 copy-start.9
  15.0 0.0 copy-start.10
  15.0 2.3 %collective-permute-start.5 = (bf16[4,80,128]{2,1,0:T(8,128)(2,1)S(1)}, bf16[4,80,128]{2,1,0:T(8,128)(2,1)S(1)}, u32[]{:S(2)}, u32[]{:S(2)}) collective-permute-start(bf16[4,80,128]{2,1,0:T(8,128)(2,1)S(1)} %shard_map.134), channel_id=1, source_target_pairs={{0,8},{1,9},{2,10},{3,11},{4,12},{5,13},{6,14},{7,15},{8,0},{9,1},... | collective-permute-start | bytes 245768 | tf_op jit(solution)/shard_map/ppermute | solution.py:73
  17.3 0.0 collective-permute-done.7.theirs
  17.3 0.0 collective-permute-done.6.after.refs_1_
  17.4 1.2 %shard_map.135 = (bf16[9,16,128]{2,1,0:T(8,128)(2,1)S(1)}, bf16[9,16,128]{2,1,0:T(8,128)(2,1)S(1)}) custom-call(bf16[4,80,128]{2,1,0:T(8,128)(2,1)S(1)} %collective-permute-done.6.after.refs_1_, s32[8]{0:T(128)S(1)} %copy-done.8, bf16[9,16,128]{2,1,0:T(8,128)(2,1)S(1)} %get-tuple-element.27.after.mine, ...), custom_call_target="tpu_custom_call" | custom-call | flops 8000000000 | tf_op jit(solution)/shard_map/pallas_call | solution.py:39
  18.5 0.3 collective-permute-start.8
  18.8 0.2 shard_map.136.after.gates
  19.0 0.8 %collective-permute-done.8.theirs = bf16[9,16,128]{2,1,0:T(8,128)(2,1)S(1)} collective-permute-done((bf16[9,16,128]{2,1,0:T(8,128)(2,1)S(1)}, bf16[9,16,128]{2,1,0:T(8,128)(2,1)S(1)}, u32[]{:S(2)}, u32[]{:S(2)}) %collective-permute-start.8) | collective-permute-done | bytes 36896 | tf_op jit(solution)/shard_map/ppermute | solution.py:73
  19.8 0.2 shard_map.137.mine.after
  20.0 1.6 %collective-permute-start.9 = (bf16[9,16,128]{2,1,0:T(8,128)(2,1)S(1)}, bf16[9,16,128]{2,1,0:T(8,128)(2,1)S(1)}, u32[]{:S(2)}, u32[]{:S(2)}) collective-permute-start(bf16[9,16,128]{2,1,0:T(8,128)(2,1)S(1)} %shard_map.137.mine.after), channel_id=1, source_target_pairs={{0,2},{1,3},{2,0},{3,1},{4,6},{5,7},{6,4},{7,5},{8,10},{9,11},{10,... | collective-permute-start | bytes 110600 | tf_op jit(solution)/shard_map/ppermute | solution.py:73
  21.6 2.1 %collective-permute-start.10 = (bf16[4,80,128]{2,1,0:T(8,128)(2,1)S(1)}, bf16[4,80,128]{2,1,0:T(8,128)(2,1)S(1)}, u32[]{:S(2)}, u32[]{:S(2)}) collective-permute-start(bf16[4,80,128]{2,1,0:T(8,128)(2,1)S(1)} %shard_map.139), channel_id=1, source_target_pairs={{0,12},{1,13},{2,14},{3,15},{4,8},{5,9},{6,10},{7,11},{8,4},{9,5},... | collective-permute-start | bytes 245768 | tf_op jit(solution)/shard_map/ppermute | solution.py:73
  23.7 0.3 collective-permute-done.9.theirs
  24.0 0.3 shard_map.138.after.mine
  24.3 1.6 %collective-permute-start.11 = (bf16[9,16,128]{2,1,0:T(8,128)(2,1)S(1)}, bf16[9,16,128]{2,1,0:T(8,128)(2,1)S(1)}, u32[]{:S(2)}, u32[]{:S(2)}) collective-permute-start(bf16[9,16,128]{2,1,0:T(8,128)(2,1)S(1)} %shard_map.138.after.mine), channel_id=1, source_target_pairs={{0,4},{1,5},{2,6},{3,7},{4,0},{5,1},{6,2},{7,3},{8,12},{9,13},{10,... | collective-permute-start | bytes 110600 | tf_op jit(solution)/shard_map/ppermute | solution.py:73
  26.0 2.3 %collective-permute-done.10.refs_3_ = bf16[4,80,128]{2,1,0:T(8,128)(2,1)S(1)} collective-permute-done((bf16[4,80,128]{2,1,0:T(8,128)(2,1)S(1)}, bf16[4,80,128]{2,1,0:T(8,128)(2,1)S(1)}, u32[]{:S(2)}, u32[]{:S(2)}) %collective-permute-start.10) | collective-permute-done | bytes 81952 | tf_op jit(solution)/shard_map/ppermute | solution.py:73
  28.3 0.0 copy-start
  28.3 0.0 copy-start.1
  28.3 0.0 copy-start.2
  28.3 1.6 %collective-permute-start.14 = (bf16[16,80,128]{2,1,0:T(8,128)(2,1)S(1)}, bf16[16,80,128]{2,1,0:T(8,128)(2,1)S(1)}, u32[]{:S(2)}, u32[]{:S(2)}) collective-permute-start(bf16[16,80,128]{2,1,0:T(8,128)(2,1)S(1)} %shard_map.140.after.mine), channel_id=1, source_target_pairs={{0,16},{16,0},{1,17},{17,1},{2,18},{18,2},{3,19},{19,3},{4,20},{20... | collective-permute-start | bytes 983048 | tf_op jit(solution)/shard_map/ppermute | solution.py:456
  29.9 0.0 collective-permute-done.11.theirs
  29.9 0.3 shard_map.141.mine
  30.2 0.4 collective-permute-start.12
  30.6 4.5 %collective-permute-done.12.theirs = bf16[9,16,128]{2,1,0:T(8,128)(2,1)S(1)} collective-permute-done((bf16[9,16,128]{2,1,0:T(8,128)(2,1)S(1)}, bf16[9,16,128]{2,1,0:T(8,128)(2,1)S(1)}, u32[]{:S(2)}, u32[]{:S(2)}) %collective-permute-start.12) | collective-permute-done | bytes 36896 | tf_op jit(solution)/shard_map/ppermute | solution.py:73
  35.1 0.4 shard_map.142
  35.5 0.1 collective-permute-start.13
  35.6 1.0 %collective-permute-done.14.theirs = bf16[16,80,128]{2,1,0:T(8,128)(2,1)S(1)} collective-permute-done((bf16[16,80,128]{2,1,0:T(8,128)(2,1)S(1)}, bf16[16,80,128]{2,1,0:T(8,128)(2,1)S(1)}, u32[]{:S(2)}, u32[]{:S(2)}) %collective-permute-start.14) | collective-permute-done | bytes 327712 | tf_op jit(solution)/shard_map/ppermute | solution.py:456
  36.5 0.1 shard_map.143
  36.7 0.1 collective-permute-done.13.theirs
  36.8 2.7 %shard_map.144 = bf16[16,16,128]{2,1,0:T(8,128)(2,1)S(1)} custom-call(bf16[8,16,128]{2,1,0:T(8,128)(2,1)S(1)} %get-tuple-element.34.mine, bf16[8,16,128]{2,1,0:T(8,128)(2,1)S(1)} %collective-permute-done.13.theirs, bf16[2048,768]{1,0:T(8,128)(2,1)S(1)} %bitcast.5, bf16[2048,768]{1,0:T(8,128)(2,1)S(1)} %bitcast.6, bf16[768,2048]{1,0:T(8,128)(2,1)S(1)} %bitcast.7, ...), custom_call_target="tpu_custom_call" | custom-call | flops 1600000000 | tf_op jit(solution)/shard_map/pallas_call | solution.py:39
  39.5 11.0 %all_to_all.5.got = bf16[16,16,128]{2,1,0:T(8,128)(2,1)S(1)} all-to-all(bf16[16,16,128]{2,1,0:T(8,128)(2,1)S(1)} %shard_map.144), channel_id=1, replica_groups=mesh['grp'=2,'exp'=16] {'exp'}, dimensions={0} | all-to-all | bytes 131072 | tf_op jit(solution)/shard_map/all_to_all | solution.py:585
  50.5 0.7 %shard_map.145 = bf16[1,2048]{1,0:T(2,128)(2,1)} custom-call(f32[16,128]{1,0:T(8,128)S(1)} %get-tuple-element.33.hidden, bf16[16,16,128]{2,1,0:T(8,128)(2,1)S(1)} %all_to_all.5.got, f32[1,128]{1,0:T(1,128)S(1)} %shard_map.136.after.gates), custom_call_target="tpu_custom_call" | custom-call | flops 1600000000 | tf_op jit(solution)/shard_map/pallas_call | solution.py:39
  (24 shorter events, 0.1 us)
Async XLA Ops:
  0.0 4.9 %copy-start.4 = (bf16[16,96,48]{1,2,0:T(8,128)(2,1)S(1)}, bf16[16,96,48]{1,2,0:T(8,128)(2,1)}, u32[]{:S(2)}) copy-start(bf16[16,96,48]{1,2,0:T(8,128)(2,1)} %param.25) | copy-start | bytes 442372
  0.0 4.9 %copy-start.3 = (bf16[16,96,128]{2,1,0:T(8,128)(2,1)S(1)}, bf16[16,96,128]{2,1,0:T(8,128)(2,1)}, u32[]{:S(2)}) copy-start(bf16[16,96,128]{2,1,0:T(8,128)(2,1)} %model.1) | copy-start | bytes 1179652
  0.8 5.8 %collective-permute-start = (bf16[1,32,128]{2,1,0:T(8,128)(2,1)S(1)}, bf16[1,32,128]{2,1,0:T(8,128)(2,1)S(1)}, u32[]{:S(2)}, u32[]{:S(2)}) collective-permute-start(bf16[1,32,128]{2,1,0:T(8,128)(2,1)S(1)} %shard_map.127.mine.after), channel_id=1, source_target_pairs={{0,8},{1,9},{2,10},{3,11},{4,12},{5,13},{6,14},{7,15},{8,0},{9,1},... | collective-permute-start | bytes 24584 | tf_op jit(solution)/shard_map/ppermute | solution.py:73
  5.0 5.7 %collective-permute-start.2 = (bf16[8,80,128]{2,1,0:T(8,128)(2,1)S(1)}, bf16[8,80,128]{2,1,0:T(8,128)(2,1)S(1)}, u32[]{:S(2)}, u32[]{:S(2)}) collective-permute-start(bf16[8,80,128]{2,1,0:T(8,128)(2,1)S(1)} %get-tuple-element.22), channel_id=1, source_target_pairs={{0,2},{1,3},{2,0},{3,1},{4,6},{5,7},{6,4},{7,5},{8,10},{9,11},{10,... | collective-permute-start | bytes 491528 | tf_op jit(solution)/shard_map/ppermute | solution.py:73
  6.6 4.3 %collective-permute-start.1 = (bf16[2,32,128]{2,1,0:T(8,128)(2,1)S(1)}, bf16[2,32,128]{2,1,0:T(8,128)(2,1)S(1)}, u32[]{:S(2)}, u32[]{:S(2)}) collective-permute-start(bf16[2,32,128]{2,1,0:T(8,128)(2,1)S(1)} %shard_map.128.mine.after), channel_id=1, source_target_pairs={{0,4},{1,5},{2,6},{3,7},{4,0},{5,1},{6,2},{7,3},{8,12},{9,13},{10,... | collective-permute-start | bytes 49160 | tf_op jit(solution)/shard_map/ppermute | solution.py:73
  10.8 4.1 %copy-start.7 = (bf16[1,512]{1,0:T(2,128)(2,1)S(1)}, bf16[1,512]{1,0:T(2,128)(2,1)}, u32[]{:S(2)}) copy-start(bf16[1,512]{1,0:T(2,128)(2,1)} %new.1) | copy-start | bytes 3076
  10.8 1.7 %collective-permute-start.3 = (bf16[8,80,128]{2,1,0:T(8,128)(2,1)S(1)}, bf16[8,80,128]{2,1,0:T(8,128)(2,1)S(1)}, u32[]{:S(2)}, u32[]{:S(2)}) collective-permute-start(bf16[8,80,128]{2,1,0:T(8,128)(2,1)S(1)} %get-tuple-element.24), channel_id=1, source_target_pairs={{0,1},{1,0},{2,3},{3,2},{4,5},{5,4},{6,7},{7,6},{8,9},{9,8},{10,11... | collective-permute-start | bytes 491528 | tf_op jit(solution)/shard_map/ppermute | solution.py:73
  10.9 4.0 %collective-permute-start.4 = (bf16[4,32,128]{2,1,0:T(8,128)(2,1)S(1)}, bf16[4,32,128]{2,1,0:T(8,128)(2,1)S(1)}, u32[]{:S(2)}, u32[]{:S(2)}) collective-permute-start(bf16[4,32,128]{2,1,0:T(8,128)(2,1)S(1)} %shard_map.129.after.mine), channel_id=1, source_target_pairs={{0,2},{1,3},{2,0},{3,1},{4,6},{5,7},{6,4},{7,5},{8,10},{9,11},{10,... | collective-permute-start | bytes 98312 | tf_op jit(solution)/shard_map/ppermute | solution.py:73
  12.5 4.8 %copy-start.5 = (bf16[8,192,512]{2,1,0:T(8,128)(2,1)S(1)}, bf16[8,192,512]{2,1,0:T(8,128)(2,1)}, u32[]{:S(2)}) copy-start(bf16[8,192,512]{2,1,0:T(8,128)(2,1)} %cache.1) | copy-start | bytes 4718596
  12.5 4.8 %copy-start.8 = (s32[8]{0:T(128)S(1)}, s32[8]{0:T(128)}, u32[]{:S(2)}) copy-start(s32[8]{0:T(128)} %lengths.1) | copy-start | bytes 100
  12.5 4.8 %collective-permute-start.6 = (bf16[4,80,128]{2,1,0:T(8,128)(2,1)S(1)}, bf16[4,80,128]{2,1,0:T(8,128)(2,1)S(1)}, u32[]{:S(2)}, u32[]{:S(2)}) collective-permute-start(bf16[4,80,128]{2,1,0:T(8,128)(2,1)S(1)} %get-tuple-element.28), channel_id=1, source_target_pairs={{0,4},{1,5},{2,6},{3,7},{4,0},{5,1},{6,2},{7,3},{8,12},{9,13},{10,... | collective-permute-start | bytes 245768 | tf_op jit(solution)/shard_map/ppermute | solution.py:73
  14.9 2.4 %collective-permute-start.7 = (bf16[9,16,128]{2,1,0:T(8,128)(2,1)S(1)}, bf16[9,16,128]{2,1,0:T(8,128)(2,1)S(1)}, u32[]{:S(2)}, u32[]{:S(2)}) collective-permute-start(bf16[9,16,128]{2,1,0:T(8,128)(2,1)S(1)} %get-tuple-element.27.after.mine), channel_id=1, source_target_pairs={{0,1},{1,0},{2,3},{3,2},{4,5},{5,4},{6,7},{7,6},{8,9},{9,8},{10,11... | collective-permute-start | bytes 110600 | tf_op jit(solution)/shard_map/ppermute | solution.py:73
  15.0 3.8 %copy-start.9 = (s32[1,8]{1,0:T(1,128)S(1)}, s32[1,8]{1,0:T(1,128)}, u32[]{:S(2)}) copy-start(s32[1,8]{1,0:T(1,128)} %choice.1) | copy-start | bytes 100
  15.0 3.8 %copy-start.10 = (f32[1,8]{1,0:T(1,128)S(1)}, f32[1,8]{1,0:T(1,128)}, u32[]{:S(2)}) copy-start(f32[1,8]{1,0:T(1,128)} %probability.1) | copy-start | bytes 100
  15.0 8.7 %collective-permute-start.5 = (bf16[4,80,128]{2,1,0:T(8,128)(2,1)S(1)}, bf16[4,80,128]{2,1,0:T(8,128)(2,1)S(1)}, u32[]{:S(2)}, u32[]{:S(2)}) collective-permute-start(bf16[4,80,128]{2,1,0:T(8,128)(2,1)S(1)} %shard_map.134), channel_id=1, source_target_pairs={{0,8},{1,9},{2,10},{3,11},{4,12},{5,13},{6,14},{7,15},{8,0},{9,1},... | collective-permute-start | bytes 245768 | tf_op jit(solution)/shard_map/ppermute | solution.py:73
  18.5 1.3 %collective-permute-start.8 = (bf16[9,16,128]{2,1,0:T(8,128)(2,1)S(1)}, bf16[9,16,128]{2,1,0:T(8,128)(2,1)S(1)}, u32[]{:S(2)}, u32[]{:S(2)}) collective-permute-start(bf16[9,16,128]{2,1,0:T(8,128)(2,1)S(1)} %get-tuple-element.30), channel_id=1, source_target_pairs={{0,1},{1,0},{2,3},{3,2},{4,5},{5,4},{6,7},{7,6},{8,9},{9,8},{10,11... | collective-permute-start | bytes 110600 | tf_op jit(solution)/shard_map/ppermute | solution.py:73
  20.0 4.0 %collective-permute-start.9 = (bf16[9,16,128]{2,1,0:T(8,128)(2,1)S(1)}, bf16[9,16,128]{2,1,0:T(8,128)(2,1)S(1)}, u32[]{:S(2)}, u32[]{:S(2)}) collective-permute-start(bf16[9,16,128]{2,1,0:T(8,128)(2,1)S(1)} %shard_map.137.mine.after), channel_id=1, source_target_pairs={{0,2},{1,3},{2,0},{3,1},{4,6},{5,7},{6,4},{7,5},{8,10},{9,11},{10,... | collective-permute-start | bytes 110600 | tf_op jit(solution)/shard_map/ppermute | solution.py:73
  21.6 6.7 %collective-permute-start.10 = (bf16[4,80,128]{2,1,0:T(8,128)(2,1)S(1)}, bf16[4,80,128]{2,1,0:T(8,128)(2,1)S(1)}, u32[]{:S(2)}, u32[]{:S(2)}) collective-permute-start(bf16[4,80,128]{2,1,0:T(8,128)(2,1)S(1)} %shard_map.139), channel_id=1, source_target_pairs={{0,12},{1,13},{2,14},{3,15},{4,8},{5,9},{6,10},{7,11},{8,4},{9,5},... | collective-permute-start | bytes 245768 | tf_op jit(solution)/shard_map/ppermute | solution.py:73
  24.3 5.6 %collective-permute-start.11 = (bf16[9,16,128]{2,1,0:T(8,128)(2,1)S(1)}, bf16[9,16,128]{2,1,0:T(8,128)(2,1)S(1)}, u32[]{:S(2)}, u32[]{:S(2)}) collective-permute-start(bf16[9,16,128]{2,1,0:T(8,128)(2,1)S(1)} %shard_map.138.after.mine), channel_id=1, source_target_pairs={{0,4},{1,5},{2,6},{3,7},{4,0},{5,1},{6,2},{7,3},{8,12},{9,13},{10,... | collective-permute-start | bytes 110600 | tf_op jit(solution)/shard_map/ppermute | solution.py:73
  28.3 6.9 %copy-start.6 = (f32[2048]{0:T(1024)S(1)}, f32[2048]{0:T(1024)}, u32[]{:S(2)}) copy-start(f32[2048]{0:T(1024)} %param.18) | copy-start | bytes 24580
  28.3 8.5 %copy-start = (bf16[1,2048,768]{2,1,0:T(8,128)(2,1)S(1)}, bf16[1,2048,768]{2,1,0:T(8,128)(2,1)}, u32[]{:S(2)}) copy-start(bf16[1,2048,768]{2,1,0:T(8,128)(2,1)} %param.21) | copy-start | bytes 9437188
  28.3 8.5 %copy-start.1 = (bf16[1,2048,768]{2,1,0:T(8,128)(2,1)S(1)}, bf16[1,2048,768]{2,1,0:T(8,128)(2,1)}, u32[]{:S(2)}) copy-start(bf16[1,2048,768]{2,1,0:T(8,128)(2,1)} %param.22) | copy-start | bytes 9437188
  28.3 8.5 %copy-start.2 = (bf16[1,768,2048]{2,1,0:T(8,128)(2,1)S(1)}, bf16[1,768,2048]{2,1,0:T(8,128)(2,1)}, u32[]{:S(2)}) copy-start(bf16[1,768,2048]{2,1,0:T(8,128)(2,1)} %param.23) | copy-start | bytes 9437188
  28.3 8.2 %collective-permute-start.14 = (bf16[16,80,128]{2,1,0:T(8,128)(2,1)S(1)}, bf16[16,80,128]{2,1,0:T(8,128)(2,1)S(1)}, u32[]{:S(2)}, u32[]{:S(2)}) collective-permute-start(bf16[16,80,128]{2,1,0:T(8,128)(2,1)S(1)} %shard_map.140.after.mine), channel_id=1, source_target_pairs={{0,16},{16,0},{1,17},{17,1},{2,18},{18,2},{3,19},{19,3},{4,20},{20... | collective-permute-start | bytes 983048 | tf_op jit(solution)/shard_map/ppermute | solution.py:456
  30.2 4.9 %collective-permute-start.12 = (bf16[9,16,128]{2,1,0:T(8,128)(2,1)S(1)}, bf16[9,16,128]{2,1,0:T(8,128)(2,1)S(1)}, u32[]{:S(2)}, u32[]{:S(2)}) collective-permute-start(bf16[9,16,128]{2,1,0:T(8,128)(2,1)S(1)} %shard_map.141.mine), channel_id=1, source_target_pairs={{0,8},{1,9},{2,10},{3,11},{4,12},{5,13},{6,14},{7,15},{8,0},{9,1},... | collective-permute-start | bytes 110600 | tf_op jit(solution)/shard_map/ppermute | solution.py:73
  35.5 1.3 %collective-permute-start.13 = (bf16[8,16,128]{2,1,0:T(8,128)(2,1)S(1)}, bf16[8,16,128]{2,1,0:T(8,128)(2,1)S(1)}, u32[]{:S(2)}, u32[]{:S(2)}) collective-permute-start(bf16[8,16,128]{2,1,0:T(8,128)(2,1)S(1)} %get-tuple-element.34.mine), channel_id=1, source_target_pairs={{0,1},{1,0},{2,3},{3,2},{4,5},{5,4},{6,7},{7,6},{8,9},{9,8},{10,11... | collective-permute-start | bytes 98312 | tf_op jit(solution)/shard_map/ppermute | solution.py:73
